TPU v7x, 128 devices: a whole 4x4x4 slice. The times are simulated.
128 devices in a mesh: pop: 8 (over z, core), mp: 16 (over x, y).
Axes of the slice: x: 4, y: 4, z: 4, core: 2. Of those that a mesh axis runs over, the one named last changes fastest.
Arguments:
- weight: bfloat16 [4096, 16384], P(None, 'mp'), may hold values from -0.09375 to 0.09375
- layer_input: bfloat16 [16384, 4096], P('pop', 'mp'), may hold values from -17 to 17
- cotangent: bfloat16 [16384, 16384], P('pop', 'mp'), may hold values from -6 to 6
- factor_left: bfloat16 [128, 4096], replicated, may hold values from -6 to 6
- factor_right: bfloat16 [128, 16384], P(None, 'mp'), may hold values from -6 to 6
- seeds: int32 [128], P('pop'), may hold values from 0 to 127, each once
Outputs:
- estimate: float32 [4096, 16384], P('pop', 'mp')
- fitness: float32 [128], P('pop')
Inputs may be any that keep to these rules, and one draw needn't show every extreme that they name: seeds is a permutation: each table row belongs to exactly one member.
All inputs are finite; a program needn't handle non-finite values.
Results may differ from a plain program's by a relative error of at most 0.0003.
Values may be sent and summed in bfloat16 or wider, within the bound.
No kernel may reach another device: no remote copies, remote signals or barrier semaphores. Data moves between devices by JAX's collectives and lax.ppermute only.
A program may use at most 128 MiB of HBM per device.

v0:
```python
import math

import jax
import jax.numpy as jnp
from jax import lax
from jax.sharding import PartitionSpec as P

D = 4096
FF = 16384
TOK = 128


perturb_scale = 0.25
epsilon = 1e-05


def per_device(weight, layer_input, cotangent, factor_left, factor_right, seeds):
    members = factor_left.shape[0]
    owned_count = seeds.shape[0]
    shard_width = weight.shape[1]
    left_own = factor_left[seeds]
    right_own = factor_right[seeds]
    shard_piece = lax.all_gather(layer_input, "mp", axis=1, tiled=True)
    extent = shard_piece.shape[1]
    base_sum = jnp.dot(shard_piece, weight, preferred_element_type=jnp.float32)
    grouped = shard_piece.reshape(owned_count, TOK, extent)
    projected = jnp.einsum("mtd,md->mt", grouped, left_own, preferred_element_type=jnp.float32)
    base_sum, projected = (base_sum, projected)
    preact = (
        base_sum.reshape(owned_count, TOK, shard_width)
        + (projected * (perturb_scale / math.sqrt(D)))[:, :, None]
        * right_own.astype(jnp.float32)[:, None, :]
    )
    squared = jnp.square(jax.nn.relu(preact))
    partial_value = -jnp.sum(
        cotangent.reshape(owned_count, TOK, shard_width).astype(jnp.float32) * squared, axis=(1, 2)
    ) / math.sqrt(TOK * FF)
    placement = (seeds[:, None] == jnp.arange(members, dtype=jnp.int32)[None, :]).astype(
        jnp.float32
    )
    fitness_own = lax.psum(partial_value, "mp")
    fitness_table = lax.psum(jnp.sum(placement * fitness_own[:, None], 0), "pop")
    average = jnp.mean(fitness_table)
    variance = jnp.mean(jnp.square(fitness_table - average))
    shaped = (fitness_table - average) / jnp.sqrt(variance + epsilon)
    weights_table = shaped / math.sqrt(members)
    row_share = weight.shape[0] // lax.axis_size("pop")
    offset = lax.axis_index("pop") * row_share
    left_block = (
        lax.dynamic_slice_in_dim(factor_left, offset, row_share, 1).astype(jnp.float32)
        * weights_table[:, None]
    )
    estimate = jnp.dot(
        left_block.T, factor_right.astype(jnp.float32), precision=lax.Precision.HIGHEST
    )
    return (estimate, fitness_own)


def solution(mesh):
    placed = (P(None, "mp"), P("pop", "mp"), P("pop", "mp"), P(), P(None, "mp"), P("pop"))
    return jax.shard_map(
        per_device,
        mesh=mesh,
        in_specs=placed,
        out_specs=(P("pop", "mp"), P("pop")),
        check_vma=False,
    )
```

profile of v0, /device:TPU:1, one launch (start us, length us, event | category | flops | bytes accessed | tf_op | source)
XLA Modules:
  0.0 238.0 jit_solution(3255359181978484932)
XLA Ops:
  7.2 0.0 copy-start
  7.2 0.0 all-gather.2.cloned.1.call-start
  7.2 0.7 all-gather.2.cloned.1.call-update
  7.9 0.7 compare_select_fusion
  8.6 2.1 gather_fusion
  10.7 0.0 copy-done
  10.7 0.6 gather_fusion.1
  11.3 0.1 copy.11
  11.4 6.5 %copy.10 = bf16[2048,1024]{0,1:T(8,128)(2,1)} copy(bf16[2048,1024]{1,0:T(8,128)(2,1)} %param.8) | data formatting | bytes 8388608 | tf_op args[2]
  17.9 115.5 %all-gather.2.cloned.1.call-done = bf16[2048,4096]{1,0:T(8,128)(2,1)} async-done(((bf16[2048,256]{1,0:T(8,128)(2,1)}), bf16[2048,4096]{1,0:T(8,128)(2,1)}) %all-gather.2.cloned.1.call-update) | async-done | bytes 16777232 | tf_op jit(solution)/shard_map/all_gather | solution.py:23
  133.4 8.0 %fusion.5 = f32[16,1,128]{2,1,0:T(1,128)S(1)} fusion(bf16[16,128,4096]{2,1,0:T(8,128)(2,1)} %bitcast.27, bf16[16,4096,1]{1,0,2:T(8,128)(2,1)S(1)} %bitcast.29), kind=kOutput, calls=%fused_computation.8 | convolution fusion | flops 16777216 | bytes 16916480 | tf_op jit(solution)/shard_map/mtd,md->mt/dot_general | solution.py:27
  141.4 5.9 %mul.52 = f32[16,128,1024]{1,0,2:T(8,128)} broadcast(f32[16,1024]{0,1:T(8,128)S(1)} %copy.11), dimensions={0,2} | broadcast | bytes 8454144 | tf_op jit(solution)/shard_map/mul | solution.py:31
  147.3 0.0 copy-start.1
  147.3 26.1 %fusion.4 = f32[2048]{0:T(1024)S(1)} fusion(f32[128,8,16,128]{3,2,1,0:T(8,128)} %bitcast.28, bf16[2048,1024]{0,1:T(8,128)(2,1)} %copy.10, bf16[2048,4096]{1,0:T(8,128)(2,1)} %all-gather.2.cloned.1.call-done, bf16[4096,1024]{1,0:T(8,128)(2,1)} %param.6, f32[2048]{0:T(1024)S(1)} %multiply_bitcast_fusion), kind=kOutput, calls=%fused_computation.7 | convolution fusion | flops 17194547200 | bytes 37765120 | tf_op jit(solution)/shard_map/dot_general | solution.py:25
  173.5 0.1 bitcast_reduce_fusion
  173.6 30.9 %psum.14 = f32[16]{0:T(128)S(1)} all-reduce(f32[16]{0:T(128)S(1)} %negate_multiply_fusion), channel_id=1, replica_groups=mesh['pop'=8,'mp'=16] {'mp'}, use_global_device_ids=true, to_apply=%region_2.3 | all-reduce | flops 16 | bytes 128 | tf_op jit(solution)/shard_map/psum | solution.py:41
  204.5 0.0 copy-done.1
  204.5 0.0 copy-start.2
  204.5 0.1 select_reduce_fusion
  204.6 20.6 %psum.15 = f32[128]{0:T(128)S(1)} all-reduce(f32[128]{0:T(128)S(1)} %select_reduce_fusion), channel_id=1, replica_groups=mesh['pop'=8,'mp'=16] {'pop'}, use_global_device_ids=true, to_apply=%region_4.5 | all-reduce | flops 128 | bytes 1024 | tf_op jit(solution)/shard_map/psum | solution.py:42
  225.2 0.6 reduce_sum.47
  226.5 0.6 multiply_reduce_fusion
  227.8 3.3 %fusion.7 = f32[512,1024]{1,0:T(8,128)} fusion(bf16[128,1024]{1,0:T(8,128)(2,1)S(1)} %copy-done, f32[128]{0:T(128)S(1)} %divide_multiply_fusion, bf16[128,4096]{1,0:T(8,128)(2,1)} %param.9, s32[]{:T(128)S(6)} %select_n.7), kind=kOutput, calls=%fused_computation.10 | convolution fusion | flops 805437440 | bytes 2490884 | tf_op jit(solution)/shard_map/dot_general | solution.py:53
  231.1 0.0 copy-done.2
  (4 shorter events, 0.0 us)
Async XLA Ops:
  7.2 3.5 %copy-start = (bf16[128,1024]{1,0:T(8,128)(2,1)S(1)}, bf16[128,1024]{1,0:T(8,128)(2,1)}, u32[]{:S(2)}) copy-start(bf16[128,1024]{1,0:T(8,128)(2,1)} %param.10) | copy-start | bytes 786436
  7.2 126.2 %all-gather.2.cloned.1.call-start = ((), (), s32[]{:S(2)}) async-start(), calls=%async_computation | async-start | bytes 17825792 | tf_op jit(solution)/shard_map/all_gather | solution.py:23
  147.3 57.2 %copy-start.1 = (s32[16]{0:T(128)S(1)}, s32[16]{0:T(128)}, u32[]{:S(2)}) copy-start(s32[16]{0:T(128)} %param.11) | copy-start | bytes 196
  204.5 26.6 %copy-start.2 = (f32[16]{0:T(128)}, f32[16]{0:T(128)S(1)}, u32[]{:S(2)}) copy-start(f32[16]{0:T(128)S(1)} %psum.14) | copy-start | bytes 196
Sparse Core Ops, SparseCore 0:
  10.1 123.2 all-gather.1
where the time goes:
time: 238 us
  waiting for transfers between devices  116 us (49%)
  blocking collectives  51.6 us (22%)
  matrix products  37.5 us (16%)
  between operations  15.4 us (6%)
  local copies, waits for them, and re-layouts  15.2 us (6%)
    all_gather x1, waiting for transfers between devices, per_device(): shard_piece = lax.all_gather(layer_input, 'mp', axis=1, tiled=True)  115 us
    psum x1, blocking collectives, per_device(): fitness_own = lax.psum(partial_value, 'mp')  30.9 us
    dot_general x1, matrix products, per_device(): base_sum = jnp.dot(shard_piece, weight, preferred_element_type=jnp.float32)  26.1 us
    psum x1, blocking collectives, per_device(): lax.psum(jnp.sum(placement * fitness_own[:, None], 0), 'pop')  20.6 us
    dot_general x1, matrix products, per_device(): jnp.einsum('mtd,md->mt', grouped, left_own, preferred_element_type=jnp.fl...  8.04 us
    unnamed x7, local copies, waits for them, and re-layouts  6.49 us
    mul x1, local copies, waits for them, and re-layouts, per_device(): (projected * (perturb_scale / math.sqrt(D)))[:, :, None]  5.88 us
  transfers between devices with their start and end apart: 1, of which 1 were waited for; matrix products, arithmetic and copies ran while one was open for 4% of the time, Pallas kernels for 0%

commit v1 on v0

v1 whole, which is shorter than its diff:
```python
import functools
import math

import jax
import jax.numpy as jnp
from jax import lax
from jax.experimental import pallas as pl
from jax.experimental.pallas import tpu as pltpu
from jax.sharding import PartitionSpec as P

D = 4096
FF = 16384
TOK = 128
SIDE = 4

perturb_scale = 0.25
epsilon = 1e-05

ROWS_PER_CHUNK = 512
COLS = 256
LANES = 128


def shift(piece, dx, dy):
    perm = [
        (x * SIDE + y, ((x + dx) % SIDE) * SIDE + (y + dy) % SIDE)
        for x in range(SIDE)
        for y in range(SIDE)
    ]
    return lax.ppermute(piece, "mp", perm)


def gather_chunk(piece, x_first):
    step = (lambda a, k: shift(a, k, 0)) if x_first else (lambda a, k: shift(a, 0, k))
    leap = (lambda a, k: shift(a, 0, k)) if x_first else (lambda a, k: shift(a, k, 0))
    block = jnp.concatenate([piece] + [step(piece, k) for k in range(1, SIDE)], axis=1)
    return [block] + [leap(block, k) for k in range(1, SIDE)]


def score_kernel(members, x0, x1, x2, x3, w_ref, left_ref, right_ref, cot_ref, pick_ref, out_ref, proj_ref):
    blocks = (x0, x1, x2, x3)
    col = pl.program_id(0)

    @pl.when(col == 0)
    def _():
        total = jnp.zeros(proj_ref.shape, jnp.float32)
        for j in range(SIDE):
            total += jnp.dot(blocks[j][...], left_ref[j], preferred_element_type=jnp.float32)
        proj_ref[...] = jnp.sum(
            jnp.where(pick_ref[...] > 0, total, 0.0), axis=1, keepdims=True
        ) * (perturb_scale / math.sqrt(D)) + jnp.zeros(proj_ref.shape, jnp.float32)
        out_ref[...] = jnp.zeros(out_ref.shape, jnp.float32)

    base = jnp.dot(x0[...], w_ref[0], preferred_element_type=jnp.float32)
    for j in range(1, SIDE):
        base += jnp.dot(blocks[j][...], w_ref[j], preferred_element_type=jnp.float32)
    for m in range(members):
        rows = slice(m * TOK, (m + 1) * TOK)
        proj = proj_ref[rows, :]
        right = right_ref[m : m + 1, :].astype(jnp.float32)
        for g in range(COLS // LANES):
            cols = slice(g * LANES, (g + 1) * LANES)
            act = jnp.maximum(base[rows, cols] + proj * right[:, cols], 0.0)
            term = cot_ref[rows, cols].astype(jnp.float32) * (act * act)
            out_ref[m : m + 1, :] += jnp.sum(term, axis=0, keepdims=True)


def score_chunk(blocks, w_perm, left_perm, right_rows, cot, pick, chunk):
    rows, extent = blocks[0].shape
    width = w_perm.shape[2]
    members = rows // TOK
    return pl.pallas_call(
        functools.partial(score_kernel, members),
        grid=(width // COLS,),
        in_specs=[pl.BlockSpec((rows, extent), lambda n: (0, 0))] * SIDE
        + [
            pl.BlockSpec((SIDE, extent, COLS), lambda n: (0, 0, n)),
            pl.BlockSpec((SIDE, extent, LANES), lambda n: (0, 0, 0)),
            pl.BlockSpec((members, COLS), lambda n: (0, n)),
            pl.BlockSpec((rows, COLS), lambda n: (chunk, n)),
            pl.BlockSpec((rows, LANES), lambda n: (0, 0)),
        ],
        out_specs=pl.BlockSpec((members, LANES), lambda n: (0, 0)),
        out_shape=jax.ShapeDtypeStruct((members, LANES), jnp.float32),
        scratch_shapes=[pltpu.VMEM((rows, LANES), jnp.float32)],
        compiler_params=pltpu.CompilerParams(vmem_limit_bytes=48 * 1024 * 1024),
        cost_estimate=pl.CostEstimate(
            flops=2 * rows * SIDE * extent * width,
            bytes_accessed=2 * SIDE * extent * (rows + width) + 2 * rows * width,
            transcendentals=0,
        ),
    )(*blocks, w_perm, left_perm, right_rows, cot, pick)


def reorder(array, x_first):
    here = lax.axis_index("mp")
    x, y = here // SIDE, here % SIDE
    width = array.shape[0] // (SIDE * SIDE)
    groups = []
    for j in range(SIDE):
        parts = []
        for i in range(SIDE):
            dx, dy = (i, j) if x_first else (j, i)
            source = lax.rem(x + SIDE - dx, SIDE) * SIDE + lax.rem(y + SIDE - dy, SIDE)
            parts.append(lax.dynamic_slice_in_dim(array, source * width, width, 0))
        groups.append(jnp.concatenate(parts, axis=0))
    return jnp.stack(groups)


def per_device(weight, layer_input, cotangent, factor_left, factor_right, seeds):
    members = factor_left.shape[0]
    owned = seeds.shape[0]
    rows = layer_input.shape[0]
    chunks = rows // ROWS_PER_CHUNK
    group = ROWS_PER_CHUNK // TOK

    orders = [c % 2 == 0 for c in range(chunks)]
    gathered = [
        gather_chunk(layer_input[c * ROWS_PER_CHUNK : (c + 1) * ROWS_PER_CHUNK], orders[c])
        for c in range(chunks)
    ]

    placement = (seeds[:, None] == jnp.arange(members, dtype=jnp.int32)[None, :]).astype(jnp.float32)
    picked = placement.astype(jnp.bfloat16)
    left_own = jnp.dot(factor_left.T, picked.T, preferred_element_type=jnp.float32).astype(jnp.bfloat16)
    left_own = jnp.pad(left_own, ((0, 0), (0, LANES - owned)))
    right_own = jnp.dot(picked, factor_right, preferred_element_type=jnp.float32).astype(jnp.bfloat16)
    w_perm = {o: reorder(weight, o) for o in (True, False)}
    left_perm = {o: reorder(left_own, o) for o in (True, False)}

    sums = []
    for c in range(chunks):
        member = c * group + jnp.arange(ROWS_PER_CHUNK, dtype=jnp.int32) // TOK
        pick = (member[:, None] == jnp.arange(LANES, dtype=jnp.int32)[None, :]).astype(jnp.float32)
        sums.append(
            score_chunk(
                gathered[c],
                w_perm[orders[c]],
                left_perm[orders[c]],
                right_own[c * group : (c + 1) * group],
                cotangent,
                pick,
                c,
            )
        )
    partial = -jnp.sum(jnp.concatenate(sums, axis=0), axis=1) / math.sqrt(TOK * FF)
    table = jnp.sum(placement * partial[:, None], 0)

    everywhere = ("pop", "mp")
    devices = lax.axis_size("pop") * lax.axis_size("mp")
    copies = jnp.broadcast_to(table[None, :], (devices, members))
    fitness_table = jnp.sum(lax.all_to_all(copies, everywhere, 0, 0, tiled=True), 0)
    fitness_own = jnp.sum(placement * fitness_table[None, :], 1)

    average = jnp.mean(fitness_table)
    variance = jnp.mean(jnp.square(fitness_table - average))
    shaped = (fitness_table - average) / jnp.sqrt(variance + epsilon)
    weights_table = shaped / math.sqrt(members)
    row_share = weight.shape[0] // lax.axis_size("pop")
    offset = lax.axis_index("pop") * row_share
    left_block = (
        lax.dynamic_slice_in_dim(factor_left, offset, row_share, 1).astype(jnp.float32)
        * weights_table[:, None]
    )
    estimate = jnp.dot(
        left_block.T, factor_right.astype(jnp.float32), precision=lax.Precision.HIGHEST
    )
    return (estimate, fitness_own)


def solution(mesh):
    placed = (P(None, "mp"), P("pop", "mp"), P("pop", "mp"), P(), P(None, "mp"), P("pop"))
    return jax.shard_map(
        per_device,
        mesh=mesh,
        in_specs=placed,
        out_specs=(P("pop", "mp"), P("pop")),
        check_vma=False,
    )
```

time: 238 us -> 224 us (0.941)
  blocking collectives: 51.6 us -> 0 us
  starting transfers between devices: 0.04 us -> 41.9 us
  Pallas kernels: 0 us -> 35.4 us
  matrix products: 37.5 us -> 3.83 us
  between operations: 15.4 us -> 2.31 us
  other arithmetic: 2.09 us -> 13.5 us
  local copies, waits for them, and re-layouts: 15.2 us -> 9.98 us
    all_gather x1 -> x0, waiting for transfers between devices: 115 us -> none  [per_device(): shard_piece = lax.all_gather(layer_input, 'mp', axis=1, tiled=True)]
    ppermute x0 -> x24, waiting for transfers between devices: none -> 107 us  [shift(): return lax.ppermute(piece, 'mp', perm)]
    psum x2 -> x0, blocking collectives: 51.6 us -> none  [the longest x1 30.9 us: per_device(): fitness_own = lax.psum(partial_value, 'mp')]
    pallas_call x0 -> x4, Pallas kernels: none -> 35.4 us  [score_chunk(): pl.pallas_call(functools.partial(score_kernel, members), grid=(width // C...]
    dot_general x2, matrix products: 34.2 us -> 0.5 us  [the longest x1 0.29 us: per_device(): jnp.dot(factor_left.T, picked.T, preferred_element_type=jnp.float32)]
    ppermute x0 -> x24, starting transfers between devices: none -> 27.2 us  [shift(): return lax.ppermute(piece, 'mp', perm)]
    all_to_all x0 -> x1, starting transfers between devices: none -> 14.7 us  [per_device(): lax.all_to_all(copies, everywhere, 0, 0, tiled=True)]
    all_to_all x0 -> x1, waiting for transfers between devices: none -> 9.5 us  [per_device(): lax.all_to_all(copies, everywhere, 0, 0, tiled=True)]
  transfers between devices with their start and end apart: 1 -> 25, of which waited for: 1 -> 11; matrix products, arithmetic and copies ran while one was open for 4% -> 8% of each run, Pallas kernels for 0% -> 12%
where the time goes in v1:
time: 224 us
  waiting for transfers between devices  117 us (52%)
  starting transfers between devices  41.9 us (19%)
  Pallas kernels  35.4 us (16%)
  other arithmetic  13.5 us (6%)
  local copies, waits for them, and re-layouts  9.98 us (4%)
  matrix products  3.83 us (2%)
  between operations  2.31 us (1%)
    ppermute x24, waiting for transfers between devices, shift(): return lax.ppermute(piece, 'mp', perm)  107 us
    pallas_call x4, Pallas kernels, score_chunk(): pl.pallas_call(functools.partial(score_kernel, members), grid=(width // C...  35.4 us
    ppermute x24, starting transfers between devices, shift(): return lax.ppermute(piece, 'mp', perm)  27.2 us
    all_to_all x1, starting transfers between devices, per_device(): lax.all_to_all(copies, everywhere, 0, 0, tiled=True)  14.7 us
    all_to_all x1, waiting for transfers between devices, per_device(): lax.all_to_all(copies, everywhere, 0, 0, tiled=True)  9.5 us
    another operation x6, other arithmetic, reorder(): return jnp.stack(groups)  9.22 us
    dynamic_slice x4, local copies, waits for them, and re-layouts, reorder(): parts.append(lax.dynamic_slice_in_dim(array, source * width, width, 0))  5.25 us
  transfers between devices with their start and end apart: 25, of which 11 were waited for; matrix products, arithmetic and copies ran while one was open for 8% of the time, Pallas kernels for 12%

profile of v1, /device:TPU:1, one launch (start us, length us, event | category | flops | bytes accessed | tf_op | source)
XLA Modules:
  0.0 223.8 jit_solution(8677887863897260284)
XLA Ops:
  2.0 2.1 collective-permute-start
  4.1 2.5 %collective-permute-start.1 = (bf16[512,256]{1,0:T(8,128)(2,1)S(1)}, bf16[512,256]{1,0:T(8,128)(2,1)}, u32[]{:S(2)}, u32[]{:S(2)}) collective-permute-start(bf16[512,256]{1,0:T(8,128)(2,1)S(1)} %get-tuple-element.20), channel_id=1, source_target_pairs={{0,8},{1,9},{2,10},{3,11},{4,12},{5,13},{6,14},{7,15},{8,0},{9,1},... | collective-permute-start | bytes 786440 | tf_op jit(solution)/shard_map/ppermute | solution.py:30
  9.0 2.6 %collective-permute-start.7 = (bf16[512,256]{1,0:T(8,128)(2,1)S(1)}, bf16[512,256]{1,0:T(8,128)(2,1)S(1)}, u32[]{:S(2)}, u32[]{:S(2)}) collective-permute-start(bf16[512,256]{1,0:T(8,128)(2,1)S(1)} %get-tuple-element.21), channel_id=1, source_target_pairs={{0,2},{1,3},{2,0},{3,1},{4,6},{5,7},{6,4},{7,5},{8,10},{9,11},{10,... | collective-permute-start | bytes 786440 | tf_op jit(solution)/shard_map/ppermute | solution.py:30
  12.2 5.0 %constant_dynamic-slice_fusion.27 = (bf16[256,1024]{1,0:T(8,128)(2,1)S(1)}, bf16[256,1024]{1,0:T(8,128)(2,1)S(1)}, bf16[256,1024]{1,0:T(8,128)(2,1)S(1)}, bf16[2...) fusion(bf16[4096,1024]{1,0:T(8,128)(2,1)} %param.6, ...), kind=kLoop, calls=%fused_computation.102 | loop fusion | bytes 16777280 | tf_op jit(solution)/shard_map/dynamic_slice | solution.py:105
  19.6 6.3 %pad_maximum_fusion = (bf16[4,1024,1024]{2,1,0:T(8,128)(2,1)}, bf16[4,1024,1024]{2,1,0:T(8,128)(2,1)}) fusion(bf16[1,1024,1024]{2,1,0:T(8,128)(2,1)S(1)} %get-tuple-element.46, bf16[1,1024,1024]{2,1,0:T(8,128)(2,1)S(1)} %get-tuple-element.44, bf16[1,1024,1024]{2,1,0:T(8,128)(2,1)S(1)} %get-tuple-element.42, bf16[1,1024,1024]{2,1,0:T(8,128)(2,1)S(1)} %get-tuple-element.40, ...), kind=kLoop, calls=%fused_computation | loop fusion | flops 25165824 | bytes 33554432 | tf_op jit(solution)/shard_map/stack | solution.py:107
  33.6 6.3 %collective-permute-done.12 = bf16[512,256]{1,0:T(8,128)(2,1)S(1)} collective-permute-done((bf16[512,256]{1,0:T(8,128)(2,1)S(1)}, bf16[512,256]{1,0:T(8,128)(2,1)S(1)}, u32[]{:S(2)}, u32[]{:S(2)}) %collective-permute-start.12) | collective-permute-done | bytes 262176 | tf_op jit(solution)/shard_map/ppermute | solution.py:30
  39.9 2.3 %collective-permute-start.18 = (bf16[512,256]{1,0:T(8,128)(2,1)S(1)}, bf16[512,256]{1,0:T(8,128)(2,1)S(1)}, u32[]{:S(2)}, u32[]{:S(2)}) collective-permute-start(bf16[512,256]{1,0:T(8,128)(2,1)S(1)} %get-tuple-element.22), channel_id=1, source_target_pairs={{0,1},{1,2},{2,3},{3,0},{4,5},{5,6},{6,7},{7,4},{8,9},{9,10},{10,1... | collective-permute-start | bytes 786440 | tf_op jit(solution)/shard_map/ppermute | solution.py:30
  45.9 35.9 %collective-permute-done.18 = bf16[512,256]{1,0:T(8,128)(2,1)S(1)} collective-permute-done((bf16[512,256]{1,0:T(8,128)(2,1)S(1)}, bf16[512,256]{1,0:T(8,128)(2,1)S(1)}, u32[]{:S(2)}, u32[]{:S(2)}) %collective-permute-start.18) | collective-permute-done | bytes 262176 | tf_op jit(solution)/shard_map/ppermute | solution.py:30
  81.8 3.3 %collective-permute-done.19 = bf16[512,256]{1,0:T(8,128)(2,1)S(1)} collective-permute-done((bf16[512,256]{1,0:T(8,128)(2,1)S(1)}, bf16[512,256]{1,0:T(8,128)(2,1)S(1)}, u32[]{:S(2)}, u32[]{:S(2)}) %collective-permute-start.19) | collective-permute-done | bytes 262176 | tf_op jit(solution)/shard_map/ppermute | solution.py:30
  85.6 1.7 collective-permute-start.16
  87.3 2.0 collective-permute-start.17
  89.7 9.0 %collective-permute-done.5.x3 = bf16[512,1024]{1,0:T(8,128)(2,1)S(1)} collective-permute-done((bf16[512,1024]{1,0:T(8,128)(2,1)S(1)}, bf16[512,1024]{1,0:T(8,128)(2,1)S(1)}, u32[]{:S(2)}, u32[]{:S(2)}) %collective-permute-start.5) | collective-permute-done | bytes 1048608 | tf_op jit(solution)/shard_map/ppermute | solution.py:30
  99.3 7.6 %collective-permute-done.10.x2 = bf16[512,1024]{1,0:T(8,128)(2,1)S(1)} collective-permute-done((bf16[512,1024]{1,0:T(8,128)(2,1)S(1)}, bf16[512,1024]{1,0:T(8,128)(2,1)S(1)}, u32[]{:S(2)}, u32[]{:S(2)}) %collective-permute-start.10) | collective-permute-done | bytes 1048608 | tf_op jit(solution)/shard_map/ppermute | solution.py:30
  107.9 21.4 %collective-permute-done.16.x2 = bf16[512,1024]{1,0:T(8,128)(2,1)S(1)} collective-permute-done((bf16[512,1024]{1,0:T(8,128)(2,1)S(1)}, bf16[512,1024]{1,0:T(8,128)(2,1)S(1)}, u32[]{:S(2)}, u32[]{:S(2)}) %collective-permute-start.16) | collective-permute-done | bytes 1048608 | tf_op jit(solution)/shard_map/ppermute | solution.py:30
  129.3 2.7 %collective-permute-start.22 = (bf16[512,1024]{1,0:T(8,128)(2,1)S(1)}, bf16[512,1024]{1,0:T(8,128)(2,1)}, u32[]{:S(2)}, u32[]{:S(2)}) collective-permute-start(bf16[512,1024]{1,0:T(8,128)(2,1)S(1)} %pad_maximum_fusion.15.x0), channel_id=1, source_target_pairs={{0,8},{1,9},{2,10},{3,11},{4,12},{5,13},{6,14},{7,15},{8,0},{9,1},... | collective-permute-start | bytes 3145736 | tf_op jit(solution)/shard_map/ppermute | solution.py:30
  132.0 11.8 %collective-permute-done.17.x3 = bf16[512,1024]{1,0:T(8,128)(2,1)S(1)} collective-permute-done((bf16[512,1024]{1,0:T(8,128)(2,1)S(1)}, bf16[512,1024]{1,0:T(8,128)(2,1)S(1)}, u32[]{:S(2)}, u32[]{:S(2)}) %collective-permute-start.17) | collective-permute-done | bytes 1048608 | tf_op jit(solution)/shard_map/ppermute | solution.py:30
  145.3 8.5 %shard_map.77 = f32[4,128]{1,0:T(4,128)S(1)} custom-call(bf16[512,1024]{1,0:T(8,128)(2,1)S(1)} %pad_maximum_fusion.10.x0, bf16[512,1024]{1,0:T(8,128)(2,1)S(1)} %collective-permute-done.3.x1, bf16[512,1024]{1,0:T(8,128)(2,1)S(1)} %collective-permute-done.4.x2, bf16[512,1024]{1,0:T(8,128)(2,1)S(1)} %collective-permute-done.5.x3, ...), custom_call_target="tpu_custom_call" | custom-call | flops 4294967296 | bytes 13631488 | tf_op jit(solution)/shard_map/pallas_call | solution.py:72
  155.1 8.5 %shard_map.79 = f32[4,128]{1,0:T(4,128)S(1)} custom-call(bf16[512,1024]{1,0:T(8,128)(2,1)S(1)} %pad_maximum_fusion.14.x0, bf16[512,1024]{1,0:T(8,128)(2,1)S(1)} %collective-permute-done.15.x1, bf16[512,1024]{1,0:T(8,128)(2,1)S(1)} %collective-permute-done.16.x2, bf16[512,1024]{1,0:T(8,128)(2,1)S(1)} %copy-done.2, ...), custom_call_target="tpu_custom_call" | custom-call | flops 4294967296 | bytes 13631488 | tf_op jit(solution)/shard_map/pallas_call | solution.py:72
  163.6 8.9 %shard_map.78 = f32[4,128]{1,0:T(4,128)S(1)} custom-call(bf16[512,1024]{1,0:T(8,128)(2,1)S(1)} %pad_maximum_fusion.12.x0, bf16[512,1024]{1,0:T(8,128)(2,1)} %collective-permute-done.9.x1, bf16[512,1024]{1,0:T(8,128)(2,1)S(1)} %collective-permute-done.10.x2, bf16[512,1024]{1,0:T(8,128)(2,1)S(1)} %collective-permute-done.11.x3, ...), custom_call_target="tpu_custom_call" | custom-call | flops 4294967296 | bytes 13631488 | tf_op jit(solution)/shard_map/pallas_call | solution.py:72
  172.5 10.1 %collective-permute-done.23.x3 = bf16[512,1024]{1,0:T(8,128)(2,1)} collective-permute-done((bf16[512,1024]{1,0:T(8,128)(2,1)S(1)}, bf16[512,1024]{1,0:T(8,128)(2,1)}, u32[]{:S(2)}, u32[]{:S(2)}) %collective-permute-start.23) | collective-permute-done | bytes 1048608 | tf_op jit(solution)/shard_map/ppermute | solution.py:30
  182.6 9.5 %shard_map.80 = f32[4,128]{1,0:T(4,128)S(1)} custom-call(bf16[512,1024]{1,0:T(8,128)(2,1)S(1)} %pad_maximum_fusion.15.x0, bf16[512,1024]{1,0:T(8,128)(2,1)} %collective-permute-done.21.x1, bf16[512,1024]{1,0:T(8,128)(2,1)} %collective-permute-done.22.x2, bf16[512,1024]{1,0:T(8,128)(2,1)} %collective-permute-done.23.x3, ...), custom_call_target="tpu_custom_call" | custom-call | flops 4294967296 | bytes 13631488 | tf_op jit(solution)/shard_map/pallas_call | solution.py:72
  193.0 14.7 %all-to-all-start = ((f32[128,1,128]{2,1,0:T(1,128)}), f32[128,1,128]{2,1,0:T(1,128)S(1)}, u32[]{:S(2)}, u32[]{:S(2)}) async-start(f32[128,1,128]{2,1,0:T(1,128)} %broadcast_in_dim.2), calls=%async_computation | async-start | bytes 131072 | tf_op jit(solution)/shard_map/all_to_all | solution.py:152
  207.7 9.5 %all-to-all-done = f32[128,1,128]{2,1,0:T(1,128)S(1)} async-done(((f32[128,1,128]{2,1,0:T(1,128)}), f32[128,1,128]{2,1,0:T(1,128)S(1)}, u32[]{:S(2)}, u32[]{:S(2)}) %all-to-all-start) | async-done | bytes 65568 | tf_op jit(solution)/shard_map/all_to_all | solution.py:152
  220.5 3.3 %fusion.36 = f32[512,1024]{1,0:T(8,128)} fusion(bf16[128,1024]{1,0:T(8,128)(2,1)S(1)} %copy-done, f32[128]{0:T(128)S(1)} %divide_multiply_fusion, bf16[128,4096]{1,0:T(8,128)(2,1)} %param.9, s32[]{:T(128)S(6)} %select_n.146), kind=kOutput, calls=%fused_computation.62 | convolution fusion | flops 805437440 | bytes 2490884 | tf_op jit(solution)/shard_map/dot_general | solution.py:165
  (76 shorter events, 25.9 us)
Async XLA Ops:
  2.0 24.6 %collective-permute-start = (bf16[512,256]{1,0:T(8,128)(2,1)S(1)}, bf16[512,256]{1,0:T(8,128)(2,1)}, u32[]{:S(2)}, u32[]{:S(2)}) collective-permute-start(bf16[512,256]{1,0:T(8,128)(2,1)S(1)} %get-tuple-element.20), channel_id=1, source_target_pairs={{0,4},{1,5},{2,6},{3,7},{4,8},{5,9},{6,10},{7,11},{8,12},{9,13},{1... | collective-permute-start | bytes 786440 | tf_op jit(solution)/shard_map/ppermute | solution.py:30
  4.1 23.6 %collective-permute-start.1 = (bf16[512,256]{1,0:T(8,128)(2,1)S(1)}, bf16[512,256]{1,0:T(8,128)(2,1)}, u32[]{:S(2)}, u32[]{:S(2)}) collective-permute-start(bf16[512,256]{1,0:T(8,128)(2,1)S(1)} %get-tuple-element.20), channel_id=1, source_target_pairs={{0,8},{1,9},{2,10},{3,11},{4,12},{5,13},{6,14},{7,15},{8,0},{9,1},... | collective-permute-start | bytes 786440 | tf_op jit(solution)/shard_map/ppermute | solution.py:30
  6.6 21.2 %collective-permute-start.2 = (bf16[512,256]{1,0:T(8,128)(2,1)S(1)}, bf16[512,256]{1,0:T(8,128)(2,1)}, u32[]{:S(2)}, u32[]{:S(2)}) collective-permute-start(bf16[512,256]{1,0:T(8,128)(2,1)S(1)} %get-tuple-element.20), channel_id=1, source_target_pairs={{0,12},{1,13},{2,14},{3,15},{4,0},{5,1},{6,2},{7,3},{8,4},{9,5},{1... | collective-permute-start | bytes 786440 | tf_op jit(solution)/shard_map/ppermute | solution.py:30
  7.7 22.7 %collective-permute-start.6 = (bf16[512,256]{1,0:T(8,128)(2,1)S(1)}, bf16[512,256]{1,0:T(8,128)(2,1)S(1)}, u32[]{:S(2)}, u32[]{:S(2)}) collective-permute-start(bf16[512,256]{1,0:T(8,128)(2,1)S(1)} %get-tuple-element.21), channel_id=1, source_target_pairs={{0,1},{1,2},{2,3},{3,0},{4,5},{5,6},{6,7},{7,4},{8,9},{9,10},{10,1... | collective-permute-start | bytes 786440 | tf_op jit(solution)/shard_map/ppermute | solution.py:30
  9.0 21.8 %collective-permute-start.7 = (bf16[512,256]{1,0:T(8,128)(2,1)S(1)}, bf16[512,256]{1,0:T(8,128)(2,1)S(1)}, u32[]{:S(2)}, u32[]{:S(2)}) collective-permute-start(bf16[512,256]{1,0:T(8,128)(2,1)S(1)} %get-tuple-element.21), channel_id=1, source_target_pairs={{0,2},{1,3},{2,0},{3,1},{4,6},{5,7},{6,4},{7,5},{8,10},{9,11},{10,... | collective-permute-start | bytes 786440 | tf_op jit(solution)/shard_map/ppermute | solution.py:30
  29.0 56.6 %collective-permute-start.3 = (bf16[512,1024]{1,0:T(8,128)(2,1)S(1)}, bf16[512,1024]{1,0:T(8,128)(2,1)S(1)}, u32[]{:S(2)}, u32[]{:S(2)}) collective-permute-start(bf16[512,1024]{1,0:T(8,128)(2,1)S(1)} %pad_maximum_fusion.10.x0), channel_id=1, source_target_pairs={{0,1},{1,2},{2,3},{3,0},{4,5},{5,6},{6,7},{7,4},{8,9},{9,10},{10,1... | collective-permute-start | bytes 3145736 | tf_op jit(solution)/shard_map/ppermute | solution.py:30
  29.5 57.8 %collective-permute-start.4 = (bf16[512,1024]{1,0:T(8,128)(2,1)S(1)}, bf16[512,1024]{1,0:T(8,128)(2,1)S(1)}, u32[]{:S(2)}, u32[]{:S(2)}) collective-permute-start(bf16[512,1024]{1,0:T(8,128)(2,1)S(1)} %pad_maximum_fusion.10.x0), channel_id=1, source_target_pairs={{0,2},{1,3},{2,0},{3,1},{4,6},{5,7},{6,4},{7,5},{8,10},{9,11},{10,... | collective-permute-start | bytes 3145736 | tf_op jit(solution)/shard_map/ppermute | solution.py:30
  30.4 9.5 %collective-permute-start.12 = (bf16[512,256]{1,0:T(8,128)(2,1)S(1)}, bf16[512,256]{1,0:T(8,128)(2,1)S(1)}, u32[]{:S(2)}, u32[]{:S(2)}) collective-permute-start(bf16[512,256]{1,0:T(8,128)(2,1)S(1)} %get-tuple-element.23), channel_id=1, source_target_pairs={{0,4},{1,5},{2,6},{3,7},{4,8},{5,9},{6,10},{7,11},{8,12},{9,13},{1... | collective-permute-start | bytes 786440 | tf_op jit(solution)/shard_map/ppermute | solution.py:30
  30.8 11.4 %collective-permute-start.13 = (bf16[512,256]{1,0:T(8,128)(2,1)S(1)}, bf16[512,256]{1,0:T(8,128)(2,1)S(1)}, u32[]{:S(2)}, u32[]{:S(2)}) collective-permute-start(bf16[512,256]{1,0:T(8,128)(2,1)S(1)} %get-tuple-element.23), channel_id=1, source_target_pairs={{0,8},{1,9},{2,10},{3,11},{4,12},{5,13},{6,14},{7,15},{8,0},{9,1},... | collective-permute-start | bytes 786440 | tf_op jit(solution)/shard_map/ppermute | solution.py:30
  32.4 11.9 %collective-permute-start.14 = (bf16[512,256]{1,0:T(8,128)(2,1)S(1)}, bf16[512,256]{1,0:T(8,128)(2,1)S(1)}, u32[]{:S(2)}, u32[]{:S(2)}) collective-permute-start(bf16[512,256]{1,0:T(8,128)(2,1)S(1)} %get-tuple-element.23), channel_id=1, source_target_pairs={{0,12},{1,13},{2,14},{3,15},{4,0},{5,1},{6,2},{7,3},{8,4},{9,5},{1... | collective-permute-start | bytes 786440 | tf_op jit(solution)/shard_map/ppermute | solution.py:30
  39.9 41.9 %collective-permute-start.18 = (bf16[512,256]{1,0:T(8,128)(2,1)S(1)}, bf16[512,256]{1,0:T(8,128)(2,1)S(1)}, u32[]{:S(2)}, u32[]{:S(2)}) collective-permute-start(bf16[512,256]{1,0:T(8,128)(2,1)S(1)} %get-tuple-element.22), channel_id=1, source_target_pairs={{0,1},{1,2},{2,3},{3,0},{4,5},{5,6},{6,7},{7,4},{8,9},{9,10},{10,1... | collective-permute-start | bytes 786440 | tf_op jit(solution)/shard_map/ppermute | solution.py:30
  42.2 42.9 %collective-permute-start.19 = (bf16[512,256]{1,0:T(8,128)(2,1)S(1)}, bf16[512,256]{1,0:T(8,128)(2,1)S(1)}, u32[]{:S(2)}, u32[]{:S(2)}) collective-permute-start(bf16[512,256]{1,0:T(8,128)(2,1)S(1)} %get-tuple-element.22), channel_id=1, source_target_pairs={{0,2},{1,3},{2,0},{3,1},{4,6},{5,7},{6,4},{7,5},{8,10},{9,11},{10,... | collective-permute-start | bytes 786440 | tf_op jit(solution)/shard_map/ppermute | solution.py:30
  44.3 41.2 %collective-permute-start.20 = (bf16[512,256]{1,0:T(8,128)(2,1)S(1)}, bf16[512,256]{1,0:T(8,128)(2,1)S(1)}, u32[]{:S(2)}, u32[]{:S(2)}) collective-permute-start(bf16[512,256]{1,0:T(8,128)(2,1)S(1)} %get-tuple-element.22), channel_id=1, source_target_pairs={{0,3},{1,0},{2,1},{3,2},{4,7},{5,4},{6,5},{7,6},{8,11},{9,8},{10,9... | collective-permute-start | bytes 786440 | tf_op jit(solution)/shard_map/ppermute | solution.py:30
  81.8 16.9 %collective-permute-start.5 = (bf16[512,1024]{1,0:T(8,128)(2,1)S(1)}, bf16[512,1024]{1,0:T(8,128)(2,1)S(1)}, u32[]{:S(2)}, u32[]{:S(2)}) collective-permute-start(bf16[512,1024]{1,0:T(8,128)(2,1)S(1)} %pad_maximum_fusion.10.x0), channel_id=1, source_target_pairs={{0,3},{1,0},{2,1},{3,2},{4,7},{5,4},{6,5},{7,6},{8,11},{9,8},{10,9... | collective-permute-start | bytes 3145736 | tf_op jit(solution)/shard_map/ppermute | solution.py:30
  85.2 21.7 %collective-permute-start.10 = (bf16[512,1024]{1,0:T(8,128)(2,1)S(1)}, bf16[512,1024]{1,0:T(8,128)(2,1)S(1)}, u32[]{:S(2)}, u32[]{:S(2)}) collective-permute-start(bf16[512,1024]{1,0:T(8,128)(2,1)S(1)} %pad_maximum_fusion.12.x0), channel_id=1, source_target_pairs={{0,8},{1,9},{2,10},{3,11},{4,12},{5,13},{6,14},{7,15},{8,0},{9,1},... | collective-permute-start | bytes 3145736 | tf_op jit(solution)/shard_map/ppermute | solution.py:30
  85.5 22.1 %collective-permute-start.15 = (bf16[512,1024]{1,0:T(8,128)(2,1)S(1)}, bf16[512,1024]{1,0:T(8,128)(2,1)S(1)}, u32[]{:S(2)}, u32[]{:S(2)}) collective-permute-start(bf16[512,1024]{1,0:T(8,128)(2,1)S(1)} %pad_maximum_fusion.14.x0), channel_id=1, source_target_pairs={{0,1},{1,2},{2,3},{3,0},{4,5},{5,6},{6,7},{7,4},{8,9},{9,10},{10,1... | collective-permute-start | bytes 3145736 | tf_op jit(solution)/shard_map/ppermute | solution.py:30
  85.6 43.7 %collective-permute-start.16 = (bf16[512,1024]{1,0:T(8,128)(2,1)S(1)}, bf16[512,1024]{1,0:T(8,128)(2,1)S(1)}, u32[]{:S(2)}, u32[]{:S(2)}) collective-permute-start(bf16[512,1024]{1,0:T(8,128)(2,1)S(1)} %pad_maximum_fusion.14.x0), channel_id=1, source_target_pairs={{0,2},{1,3},{2,0},{3,1},{4,6},{5,7},{6,4},{7,5},{8,10},{9,11},{10,... | collective-permute-start | bytes 3145736 | tf_op jit(solution)/shard_map/ppermute | solution.py:30
  87.3 56.5 %collective-permute-start.17 = (bf16[512,1024]{1,0:T(8,128)(2,1)S(1)}, bf16[512,1024]{1,0:T(8,128)(2,1)S(1)}, u32[]{:S(2)}, u32[]{:S(2)}) collective-permute-start(bf16[512,1024]{1,0:T(8,128)(2,1)S(1)} %pad_maximum_fusion.14.x0), channel_id=1, source_target_pairs={{0,3},{1,0},{2,1},{3,2},{4,7},{5,4},{6,5},{7,6},{8,11},{9,8},{10,9... | collective-permute-start | bytes 3145736 | tf_op jit(solution)/shard_map/ppermute | solution.py:30
  98.7 64.9 %collective-permute-start.11 = (bf16[512,1024]{1,0:T(8,128)(2,1)S(1)}, bf16[512,1024]{1,0:T(8,128)(2,1)S(1)}, u32[]{:S(2)}, u32[]{:S(2)}) collective-permute-start(bf16[512,1024]{1,0:T(8,128)(2,1)S(1)} %pad_maximum_fusion.12.x0), channel_id=1, source_target_pairs={{0,12},{1,13},{2,14},{3,15},{4,0},{5,1},{6,2},{7,3},{8,4},{9,5},{1... | collective-permute-start | bytes 3145736 | tf_op jit(solution)/shard_map/ppermute | solution.py:30
  106.9 56.7 %collective-permute-start.9 = (bf16[512,1024]{1,0:T(8,128)(2,1)S(1)}, bf16[512,1024]{1,0:T(8,128)(2,1)}, u32[]{:S(2)}, u32[]{:S(2)}) collective-permute-start(bf16[512,1024]{1,0:T(8,128)(2,1)S(1)} %pad_maximum_fusion.12.x0), channel_id=1, source_target_pairs={{0,4},{1,5},{2,6},{3,7},{4,8},{5,9},{6,10},{7,11},{8,12},{9,13},{1... | collective-permute-start | bytes 3145736 | tf_op jit(solution)/shard_map/ppermute | solution.py:30
  107.7 64.8 %collective-permute-start.21 = (bf16[512,1024]{1,0:T(8,128)(2,1)S(1)}, bf16[512,1024]{1,0:T(8,128)(2,1)}, u32[]{:S(2)}, u32[]{:S(2)}) collective-permute-start(bf16[512,1024]{1,0:T(8,128)(2,1)S(1)} %pad_maximum_fusion.15.x0), channel_id=1, source_target_pairs={{0,4},{1,5},{2,6},{3,7},{4,8},{5,9},{6,10},{7,11},{8,12},{9,13},{1... | collective-permute-start | bytes 3145736 | tf_op jit(solution)/shard_map/ppermute | solution.py:30
  129.3 43.2 %collective-permute-start.22 = (bf16[512,1024]{1,0:T(8,128)(2,1)S(1)}, bf16[512,1024]{1,0:T(8,128)(2,1)}, u32[]{:S(2)}, u32[]{:S(2)}) collective-permute-start(bf16[512,1024]{1,0:T(8,128)(2,1)S(1)} %pad_maximum_fusion.15.x0), channel_id=1, source_target_pairs={{0,8},{1,9},{2,10},{3,11},{4,12},{5,13},{6,14},{7,15},{8,0},{9,1},... | collective-permute-start | bytes 3145736 | tf_op jit(solution)/shard_map/ppermute | solution.py:30
  144.8 37.8 %collective-permute-start.23 = (bf16[512,1024]{1,0:T(8,128)(2,1)S(1)}, bf16[512,1024]{1,0:T(8,128)(2,1)}, u32[]{:S(2)}, u32[]{:S(2)}) collective-permute-start(bf16[512,1024]{1,0:T(8,128)(2,1)S(1)} %pad_maximum_fusion.15.x0), channel_id=1, source_target_pairs={{0,12},{1,13},{2,14},{3,15},{4,0},{5,1},{6,2},{7,3},{8,4},{9,5},{1... | collective-permute-start | bytes 3145736 | tf_op jit(solution)/shard_map/ppermute | solution.py:30
  193.0 24.2 %all-to-all-start = ((f32[128,1,128]{2,1,0:T(1,128)}), f32[128,1,128]{2,1,0:T(1,128)S(1)}, u32[]{:S(2)}, u32[]{:S(2)}) async-start(f32[128,1,128]{2,1,0:T(1,128)} %broadcast_in_dim.2), calls=%async_computation | async-start | bytes 131072 | tf_op jit(solution)/shard_map/all_to_all | solution.py:152
  (6 other events, 41.4 us)

commit v2 on v0

v2 whole, which is shorter than its diff:
```python
import functools
import math

import jax
import jax.numpy as jnp
from jax import lax
from jax.experimental import pallas as pl
from jax.experimental.pallas import tpu as pltpu
from jax.sharding import PartitionSpec as P

D = 4096
FF = 16384
TOK = 128
SIDE = 4
STEPS = (0, 1, -1, 2)

perturb_scale = 0.25
epsilon = 1e-05

COLS = 256
LANES = 128


def shift(piece, dx, dy):
    perm = [
        (x * SIDE + y, ((x + dx) % SIDE) * SIDE + (y + dy) % SIDE)
        for x in range(SIDE)
        for y in range(SIDE)
    ]
    return lax.ppermute(piece, "mp", perm)


def one_ring(piece, along_x):
    step = (lambda a, k: shift(a, k, 0)) if along_x else (lambda a, k: shift(a, 0, k))
    half = piece.shape[0] // 2
    back, ahead = step(piece, 1), step(piece, -1)
    return back, ahead, step(back[:half], 1), step(ahead[half:], -1)


def near_kernel(idx_ref, b0, b1, b2, left_ref, *rest):
    w_refs, (out_ref, proj_ref) = rest[:-2], rest[-2:]
    blocks = (b0, b1, b2)

    @pl.when(pl.program_id(0) == 0)
    def _():
        total = jnp.dot(b0[...], left_ref[0], preferred_element_type=jnp.float32)
        for j in (1, 2):
            total += jnp.dot(blocks[j][...], left_ref[j], preferred_element_type=jnp.float32)
        proj_ref[...] = total

    total = None
    for j in range(3):
        w = jnp.concatenate([r[...] for r in w_refs[j * SIDE : (j + 1) * SIDE]], axis=0)
        part = jnp.dot(blocks[j][...], w, preferred_element_type=jnp.float32)
        total = part if total is None else total + part
    out_ref[...] = total


def w_specs(count, first, width):
    return [
        pl.BlockSpec((width, COLS), functools.partial(lambda k, n, idx: (idx[k], n), first + k))
        for k in range(count)
    ]


def near(blocks, idx, left_perm, weight):
    rows, extent = blocks[0].shape
    columns = weight.shape[1]
    whole = lambda n, idx: (0, 0)
    return pl.pallas_call(
        near_kernel,
        grid_spec=pltpu.PrefetchScalarGridSpec(
            num_scalar_prefetch=1,
            grid=(columns // COLS,),
            in_specs=[pl.BlockSpec((rows, extent), whole)] * 3
            + [pl.BlockSpec((3, extent, LANES), lambda n, idx: (0, 0, 0))]
            + w_specs(3 * SIDE, 0, extent // SIDE),
            out_specs=[
                pl.BlockSpec((rows, COLS), lambda n, idx: (0, n)),
                pl.BlockSpec((rows, LANES), whole),
            ],
        ),
        out_shape=[
            jax.ShapeDtypeStruct((rows, columns), jnp.float32),
            jax.ShapeDtypeStruct((rows, LANES), jnp.float32),
        ],
        compiler_params=pltpu.CompilerParams(vmem_limit_bytes=48 * 1024 * 1024),
        cost_estimate=pl.CostEstimate(
            flops=6 * rows * extent * columns,
            bytes_accessed=6 * extent * (rows + columns) + 4 * rows * columns,
            transcendentals=0,
        ),
    )(idx, *blocks, left_perm[:3], *([weight] * (3 * SIDE)))


def far_kernel(first, idx_ref, x_ref, left_ref, near_ref, near_proj_ref, right_ref, cot_ref, *rest):
    w_refs, (out_ref, proj_ref) = rest[:-2], rest[-2:]
    rows = x_ref.shape[0]

    @pl.when(pl.program_id(0) == 0)
    def _():
        total = near_proj_ref[...] + jnp.dot(
            x_ref[...], left_ref[0], preferred_element_type=jnp.float32
        )
        for m in range(rows // TOK):
            span = slice(m * TOK, (m + 1) * TOK)
            proj_ref[span, :] = jnp.broadcast_to(
                total[span, first + m : first + m + 1] * (perturb_scale / math.sqrt(D)),
                (TOK, LANES),
            )
        out_ref[...] = jnp.zeros(out_ref.shape, jnp.float32)

    w = jnp.concatenate([r[...] for r in w_refs], axis=0)
    base = near_ref[...] + jnp.dot(x_ref[...], w, preferred_element_type=jnp.float32)
    for m in range(rows // TOK):
        span = slice(m * TOK, (m + 1) * TOK)
        proj = proj_ref[span, :]
        right = right_ref[first + m : first + m + 1, :]
        sums = jnp.zeros((1, LANES), jnp.float32)
        for g in range(COLS // LANES):
            cols = slice(g * LANES, (g + 1) * LANES)
            act = jnp.maximum(base[span, cols] + proj * right[:, cols], 0.0)
            term = cot_ref[span, cols].astype(jnp.float32) * (act * act)
            sums += jnp.sum(term, axis=0, keepdims=True)
        out_ref[m : m + 1, :] += sums


def far(x, near_row, row, idx, left_perm, weight, near_sum, near_proj, right_own, cot):
    rows, extent = x.shape
    columns = weight.shape[1]
    members = rows // TOK
    whole = lambda n, idx: (0, 0)
    return pl.pallas_call(
        functools.partial(far_kernel, row // TOK),
        grid_spec=pltpu.PrefetchScalarGridSpec(
            num_scalar_prefetch=1,
            grid=(columns // COLS,),
            in_specs=[
                pl.BlockSpec((rows, extent), whole),
                pl.BlockSpec((1, extent, LANES), lambda n, idx: (3, 0, 0)),
                pl.BlockSpec((rows, COLS), lambda n, idx: (near_row // rows, n)),
                pl.BlockSpec((rows, LANES), lambda n, idx: (near_row // rows, 0)),
                pl.BlockSpec((right_own.shape[0], COLS), lambda n, idx: (0, n)),
                pl.BlockSpec((rows, COLS), lambda n, idx: (row // rows, n)),
            ]
            + w_specs(SIDE, 3 * SIDE, extent // SIDE),
            out_specs=pl.BlockSpec((members, LANES), whole),
            scratch_shapes=[pltpu.VMEM((rows, LANES), jnp.float32)],
        ),
        out_shape=jax.ShapeDtypeStruct((members, LANES), jnp.float32),
        compiler_params=pltpu.CompilerParams(vmem_limit_bytes=48 * 1024 * 1024),
        cost_estimate=pl.CostEstimate(
            flops=2 * rows * extent * columns,
            bytes_accessed=2 * extent * (rows + columns) + 6 * rows * columns,
            transcendentals=0,
        ),
    )(idx, x, left_perm, near_sum, near_proj, right_own, cot, *([weight] * SIDE))


def sources(x_first):
    here = lax.axis_index("mp")
    x, y = here // SIDE, here % SIDE
    steps = jnp.array(STEPS, dtype=jnp.int32)
    if x_first:
        index = ((x - steps[None, :]) % SIDE) * SIDE + (y - steps[:, None]) % SIDE
    else:
        index = ((x - steps[:, None]) % SIDE) * SIDE + (y - steps[None, :]) % SIDE
    return index.reshape(-1).astype(jnp.int32)


def per_device(weight, layer_input, cotangent, factor_left, factor_right, seeds):
    members = factor_left.shape[0]
    owned = seeds.shape[0]
    rows = layer_input.shape[0]
    half = rows // 2
    quarter = rows // 4

    pieces = {True: layer_input[:half], False: layer_input[half:]}
    rings = {}
    for o in (True, False):
        back, ahead, far0, far1 = one_ring(pieces[o], o)
        block = jnp.concatenate(
            [pieces[o], back, ahead, jnp.concatenate([far0, far1], axis=0)], axis=1
        )
        rings[o] = (block,) + one_ring(block, not o)

    placement = (seeds[:, None] == jnp.arange(members, dtype=jnp.int32)[None, :]).astype(jnp.float32)
    picked = placement.astype(jnp.bfloat16)
    left_own = jnp.dot(factor_left.T, picked.T, preferred_element_type=jnp.float32).astype(jnp.bfloat16)
    left_own = jnp.pad(left_own, ((0, 0), (0, LANES - owned)))
    right_own = jnp.dot(picked, factor_right, preferred_element_type=jnp.float32)
    width = layer_input.shape[1]

    sums = []
    for o in (True, False):
        idx = sources(o)
        left_perm = jnp.take(left_own.reshape(-1, width, LANES), idx, axis=0).reshape(
            SIDE, SIDE * width, LANES
        )
        block, back, ahead, far0, far1 = rings[o]
        near_sum, near_proj = near((block, back, ahead), idx, left_perm, weight)
        for k, piece in enumerate((far0, far1)):
            row = (0 if o else half) + k * quarter
            sums.append(
                far(
                    piece, k * quarter, row, idx, left_perm, weight,
                    near_sum, near_proj, right_own, cotangent,
                )
            )
    partial = -jnp.sum(jnp.concatenate(sums, axis=0), axis=1) / math.sqrt(TOK * FF)
    table = jnp.sum(placement * partial[:, None], 0)

    everywhere = ("pop", "mp")
    devices = lax.axis_size("pop") * lax.axis_size("mp")
    copies = jnp.broadcast_to(table[None, :], (devices, members))
    fitness_table = jnp.sum(lax.all_to_all(copies, everywhere, 0, 0, tiled=True), 0)
    fitness_own = jnp.sum(placement * fitness_table[None, :], 1)

    average = jnp.mean(fitness_table)
    variance = jnp.mean(jnp.square(fitness_table - average))
    shaped = (fitness_table - average) / jnp.sqrt(variance + epsilon)
    weights_table = shaped / math.sqrt(members)
    row_share = weight.shape[0] // lax.axis_size("pop")
    offset = lax.axis_index("pop") * row_share
    left_block = (
        lax.dynamic_slice_in_dim(factor_left, offset, row_share, 1).astype(jnp.float32)
        * weights_table[:, None]
    )
    estimate = jnp.dot(
        left_block.T, factor_right.astype(jnp.float32), precision=lax.Precision.HIGHEST
    )
    return (estimate, fitness_own)


def solution(mesh):
    placed = (P(None, "mp"), P("pop", "mp"), P("pop", "mp"), P(), P(None, "mp"), P("pop"))
    return jax.shard_map(
        per_device,
        mesh=mesh,
        in_specs=placed,
        out_specs=(P("pop", "mp"), P("pop")),
        check_vma=False,
    )
```

time: 238 us -> 166 us (0.70)
  waiting for transfers between devices: 116 us -> 44.3 us
  blocking collectives: 51.6 us -> 0 us
  Pallas kernels: 0 us -> 50 us
  matrix products: 37.5 us -> 3.82 us
  starting transfers between devices: 0.04 us -> 32.6 us
  between operations: 15.4 us -> 2.26 us
  other arithmetic: 2.09 us -> 10.3 us
  local copies, waits for them, and re-layouts: 15.2 us -> 21.8 us
    all_gather x1 -> x0, waiting for transfers between devices: 115 us -> none  [per_device(): shard_piece = lax.all_gather(layer_input, 'mp', axis=1, tiled=True)]
    psum x2 -> x0, blocking collectives: 51.6 us -> none  [the longest x1 30.9 us: per_device(): fitness_own = lax.psum(partial_value, 'mp')]
    pallas_call x0 -> x6, Pallas kernels: none -> 50 us  [the longest x2 28.9 us: near(): pl.pallas_call(near_kernel, grid_spec=pltpu.PrefetchScalarGridSpec(num_sc...]
    ppermute x0 -> x16, waiting for transfers between devices: none -> 34.8 us  [shift(): return lax.ppermute(piece, 'mp', perm)]
    dot_general x2, matrix products: 34.2 us -> 0.49 us  [the longest x1 0.29 us: per_device(): jnp.dot(factor_left.T, picked.T, preferred_element_type=jnp.float32)]
    ppermute x0 -> x16, starting transfers between devices: none -> 22.9 us  [shift(): return lax.ppermute(piece, 'mp', perm)]
    slice x0 -> x11, local copies, waits for them, and re-layouts: none -> 13.5 us  [the longest x8 11.2 us: one_ring(): return (back, ahead, step(back[:half], 1), step(ahead[half:], -1))]
    all_to_all x0 -> x1, starting transfers between devices: none -> 9.69 us  [per_device(): lax.all_to_all(copies, everywhere, 0, 0, tiled=True)]
  transfers between devices with their start and end apart: 1 -> 17, of which waited for: 1 -> 3; matrix products, arithmetic and copies ran while one was open for 4% -> 17% of each run, Pallas kernels for 0% -> 27%
where the time goes in v2:
time: 166 us; the launch traced here: 165 us
  Pallas kernels  50 us (30%)
  waiting for transfers between devices  44.3 us (27%)
  starting transfers between devices  32.6 us (20%)
  local copies, waits for them, and re-layouts  21.8 us (13%)
  other arithmetic  10.3 us (6%)
  matrix products  3.82 us (2%)
  between operations  2.26 us (1%)
    ppermute x16, waiting for transfers between devices, shift(): return lax.ppermute(piece, 'mp', perm)  34.8 us
    pallas_call x2, Pallas kernels, near(): pl.pallas_call(near_kernel, grid_spec=pltpu.PrefetchScalarGridSpec(num_sc...  28.9 us
    ppermute x16, starting transfers between devices, shift(): return lax.ppermute(piece, 'mp', perm)  22.9 us
    pallas_call x4, Pallas kernels, far(): pl.pallas_call(functools.partial(far_kernel, row // TOK), grid_spec=pltpu...  21.1 us
    slice x8, local copies, waits for them, and re-layouts, one_ring(): return (back, ahead, step(back[:half], 1), step(ahead[half:], -1))  11.2 us
    all_to_all x1, starting transfers between devices, per_device(): lax.all_to_all(copies, everywhere, 0, 0, tiled=True)  9.69 us
    all_to_all x1, waiting for transfers between devices, per_device(): lax.all_to_all(copies, everywhere, 0, 0, tiled=True)  9.5 us
    concatenate x2, other arithmetic, per_device(): jnp.concatenate([pieces[o], back, ahead, jnp.concatenate([far0, far1], ax...  4.65 us
  transfers between devices with their start and end apart: 17, of which 3 were waited for; matrix products, arithmetic and copies ran while one was open for 17% of the time, Pallas kernels for 27%

profile of v2, /device:TPU:1, one launch (start us, length us, event | category | flops | bytes accessed | tf_op | source)
XLA Modules:
  0.0 165.1 jit_solution(4336882339985048033)
XLA Ops:
  2.0 2.1 %collective-permute-start = (bf16[1024,256]{1,0:T(8,128)(2,1)S(1)}, bf16[1024,256]{1,0:T(8,128)(2,1)S(1)}, u32[]{:S(2)}, u32[]{:S(2)}) collective-permute-start(bf16[1024,256]{1,0:T(8,128)(2,1)S(1)} %get-tuple-element.13), channel_id=1, source_target_pairs={{0,4},{1,5},{2,6},{3,7},{4,8},{5,9},{6,10},{7,11},{8,12},{9,13},{1... | collective-permute-start | bytes 1572872 | tf_op jit(solution)/shard_map/ppermute | solution.py:30
  8.3 8.3 %collective-permute-done = bf16[1024,256]{1,0:T(8,128)(2,1)S(1)} collective-permute-done((bf16[1024,256]{1,0:T(8,128)(2,1)S(1)}, bf16[1024,256]{1,0:T(8,128)(2,1)S(1)}, u32[]{:S(2)}, u32[]{:S(2)}) %collective-permute-start) | collective-permute-done | bytes 524320 | tf_op jit(solution)/shard_map/ppermute | solution.py:30
  18.4 2.4 %collective-permute-start.3 = (bf16[512,256]{1,0:T(8,128)(2,1)}, bf16[512,256]{1,0:T(8,128)(2,1)}, u32[]{:S(2)}, u32[]{:S(2)}) collective-permute-start(bf16[512,256]{1,0:T(8,128)(2,1)} %slice.61), channel_id=1, source_target_pairs={{0,12},{1,13},{2,14},{3,15},{4,0},{5,1},{6,2},{7,3},{8,4},{9,5},{1... | collective-permute-start | bytes 786440 | tf_op jit(solution)/shard_map/ppermute | solution.py:30
  26.3 1.8 %maximum_maximum_fusion.b0 = bf16[1024,1024]{1,0:T(8,128)(2,1)S(1)} fusion(bf16[512,256]{1,0:T(8,128)(2,1)} %collective-permute-done.3, bf16[512,256]{1,0:T(8,128)(2,1)} %collective-permute-done.2, bf16[1024,256]{1,0:T(8,128)(2,1)} %copy-done.9, bf16[1024,256]{1,0:T(8,128)(2,1)} %copy-done.8, bf16[1024,256]{1,0:T(8,128)(2,1)S(1)} %get-tuple-element.13), kind=kLoop, calls=%fused_computation.4 | loop fusion | flops 10485760 | bytes 4194304 | tf_op jit(solution)/shard_map/concatenate | solution.py:182
  28.5 2.3 %collective-permute-start.6 = (bf16[1024,1024]{1,0:T(8,128)(2,1)S(1)}, bf16[1024,1024]{1,0:T(8,128)(2,1)}, u32[]{:S(2)}, u32[]{:S(2)}) collective-permute-start(bf16[1024,1024]{1,0:T(8,128)(2,1)S(1)} %maximum_maximum_fusion.b0), channel_id=1, source_target_pairs={{0,3},{1,0},{2,1},{3,2},{4,7},{5,4},{6,5},{7,6},{8,11},{9,8},{10,9... | collective-permute-start | bytes 6291464 | tf_op jit(solution)/shard_map/ppermute | solution.py:30
  30.8 2.9 %maximum_maximum_fusion.1.b0 = bf16[1024,1024]{1,0:T(8,128)(2,1)} fusion(bf16[512,256]{1,0:T(8,128)(2,1)} %collective-permute-done.11, bf16[512,256]{1,0:T(8,128)(2,1)} %collective-permute-done.10, bf16[1024,256]{1,0:T(8,128)(2,1)S(1)} %copy-done.7, bf16[1024,256]{1,0:T(8,128)(2,1)S(1)} %copy-done.5, bf16[1024,256]{1,0:T(8,128)(2,1)S(1)} %get-tuple-element.14), kind=kLoop, calls=%fused_computation.5 | loop fusion | flops 10485760 | bytes 4194304 | tf_op jit(solution)/shard_map/concatenate | solution.py:182
  33.7 2.7 %collective-permute-start.14 = (bf16[1024,1024]{1,0:T(8,128)(2,1)}, bf16[1024,1024]{1,0:T(8,128)(2,1)}, u32[]{:S(2)}, u32[]{:S(2)}) collective-permute-start(bf16[1024,1024]{1,0:T(8,128)(2,1)} %maximum_maximum_fusion.1.b0), channel_id=1, source_target_pairs={{0,12},{1,13},{2,14},{3,15},{4,0},{5,1},{6,2},{7,3},{8,4},{9,5},{1... | collective-permute-start | bytes 6291464 | tf_op jit(solution)/shard_map/ppermute | solution.py:30
  39.5 1.7 %gather_fusion = bf16[16,256,128]{2,1,0:T(8,128)(2,1)} fusion(bf16[16,256,128]{2,1,0:T(8,128)(2,1)S(1)} %bitcast.18, s32[1024]{0:T(1024)S(1)} %pad_clamp_fusion.1), kind=kCustom, calls=%fused_computation.clone | custom fusion | bytes 2097216 | tf_op jit(solution)/shard_map/jit(_take)/gather | solution.py:197
  43.6 2.9 %gather_fusion.1 = bf16[16,256,128]{2,1,0:T(8,128)(2,1)} fusion(bf16[16,256,128]{2,1,0:T(8,128)(2,1)} %bitcast.19, s32[1024]{0:T(1024)S(1)} %pad_clamp_fusion), kind=kCustom, calls=%fused_computation.1.clone | custom fusion | bytes 2097216 | tf_op jit(solution)/shard_map/jit(_take)/gather | solution.py:197
  48.2 26.5 %collective-permute-done.4.b1 = bf16[1024,1024]{1,0:T(8,128)(2,1)} collective-permute-done((bf16[1024,1024]{1,0:T(8,128)(2,1)S(1)}, bf16[1024,1024]{1,0:T(8,128)(2,1)}, u32[]{:S(2)}, u32[]{:S(2)}) %collective-permute-start.4) | collective-permute-done | bytes 2097184 | tf_op jit(solution)/shard_map/ppermute | solution.py:30
  74.7 2.3 %slice.62 = bf16[512,1024]{1,0:T(8,128)(2,1)} slice(bf16[1024,1024]{1,0:T(8,128)(2,1)} %collective-permute-done.4.b1), slice={[0:512], [0:1024]} | slice | bytes 2097152 | tf_op jit(solution)/shard_map/slice | solution.py:37
  77.8 2.2 %slice.64 = bf16[512,1024]{1,0:T(8,128)(2,1)} slice(bf16[1024,1024]{1,0:T(8,128)(2,1)} %collective-permute-done.6.b2), slice={[512:1024], [0:1024]} | slice | bytes 2097152 | tf_op jit(solution)/shard_map/slice | solution.py:37
  80.0 1.9 %collective-permute-start.7 = (bf16[512,1024]{1,0:T(8,128)(2,1)}, bf16[512,1024]{1,0:T(8,128)(2,1)S(1)}, u32[]{:S(2)}, u32[]{:S(2)}) collective-permute-start(bf16[512,1024]{1,0:T(8,128)(2,1)} %slice.64), channel_id=1, source_target_pairs={{0,3},{1,0},{2,1},{3,2},{4,7},{5,4},{6,5},{7,6},{8,11},{9,8},{10,9... | collective-permute-start | bytes 3145736 | tf_op jit(solution)/shard_map/ppermute | solution.py:30
  83.3 2.3 %slice.69 = bf16[512,1024]{1,0:T(8,128)(2,1)} slice(bf16[1024,1024]{1,0:T(8,128)(2,1)} %collective-permute-done.14.b2), slice={[512:1024], [0:1024]} | slice | bytes 2097152 | tf_op jit(solution)/shard_map/slice | solution.py:37
  85.7 2.7 %collective-permute-start.15 = (bf16[512,1024]{1,0:T(8,128)(2,1)}, bf16[512,1024]{1,0:T(8,128)(2,1)S(1)}, u32[]{:S(2)}, u32[]{:S(2)}) collective-permute-start(bf16[512,1024]{1,0:T(8,128)(2,1)} %slice.69), channel_id=1, source_target_pairs={{0,12},{1,13},{2,14},{3,15},{4,0},{5,1},{6,2},{7,3},{8,4},{9,5},{1... | collective-permute-start | bytes 3145736 | tf_op jit(solution)/shard_map/ppermute | solution.py:30
  88.3 14.1 %shard_map.95 = (f32[1024,1024]{1,0:T(8,128)}, f32[1024,128]{1,0:T(8,128)S(1)}) custom-call(s32[16]{0:T(128)S(1)} %add.82.idx_ref, bf16[1024,1024]{1,0:T(8,128)(2,1)S(1)} %maximum_maximum_fusion.b0, bf16[1024,1024]{1,0:T(8,128)(2,1)} %collective-permute-done.4.b1, bf16[1024,1024]{1,0:T(8,128)(2,1)} %collective-permute-done.6.b2, ...), custom_call_target="tpu_custom_call" | custom-call | flops 6442450944 | bytes 16777216 | tf_op jit(solution)/shard_map/pallas_call | solution.py:70
  102.4 14.7 %shard_map.98 = (f32[1024,1024]{1,0:T(8,128)}, f32[1024,128]{1,0:T(8,128)S(1)}) custom-call(s32[16]{0:T(128)S(1)} %add.88.idx_ref, bf16[1024,1024]{1,0:T(8,128)(2,1)} %maximum_maximum_fusion.1.b0, bf16[1024,1024]{1,0:T(8,128)(2,1)} %collective-permute-done.12.b1, bf16[1024,1024]{1,0:T(8,128)(2,1)} %collective-permute-done.14.b2, ...), custom_call_target="tpu_custom_call" | custom-call | flops 6442450944 | bytes 16777216 | tf_op jit(solution)/shard_map/pallas_call | solution.py:70
  117.2 5.3 %shard_map.96 = f32[4,128]{1,0:T(4,128)S(1)} custom-call(s32[16]{0:T(128)S(1)} %add.82.idx_ref, bf16[512,1024]{1,0:T(8,128)(2,1)S(1)} %collective-permute-done.5.x_ref, bf16[4,1024,128]{2,1,0:T(8,128)(2,1)S(1)} %bitcast.14, f32[1024,1024]{1,0:T(8,128)} %get-tuple-element.7.near_ref, f32[1024,128]{1,0:T(8,128)S(1)} %get-tuple-element.8.near_proj_ref, ...), custom_call_target="tpu_custom_call" | custom-call | flops 1073741824 | bytes 6291456 | tf_op jit(solution)/shard_map/pallas_call | solution.py:133
  122.5 5.3 %shard_map.97 = f32[4,128]{1,0:T(4,128)S(1)} custom-call(s32[16]{0:T(128)S(1)} %add.82.idx_ref, bf16[512,1024]{1,0:T(8,128)(2,1)S(1)} %collective-permute-done.7.x_ref, bf16[4,1024,128]{2,1,0:T(8,128)(2,1)S(1)} %bitcast.15, f32[1024,1024]{1,0:T(8,128)} %get-tuple-element.7.near_ref, f32[1024,128]{1,0:T(8,128)S(1)} %get-tuple-element.8.near_proj_ref, ...), custom_call_target="tpu_custom_call" | custom-call | flops 1073741824 | bytes 6291456 | tf_op jit(solution)/shard_map/pallas_call | solution.py:133
  127.8 5.3 %shard_map.99 = f32[4,128]{1,0:T(4,128)S(1)} custom-call(s32[16]{0:T(128)S(1)} %add.88.idx_ref, bf16[512,1024]{1,0:T(8,128)(2,1)S(1)} %collective-permute-done.13.x_ref, bf16[4,1024,128]{2,1,0:T(8,128)(2,1)S(1)} %bitcast.12, f32[1024,1024]{1,0:T(8,128)} %get-tuple-element.9.near_ref, f32[1024,128]{1,0:T(8,128)S(1)} %get-tuple-element.10.near_proj_ref, ...), custom_call_target="tpu_custom_call" | custom-call | flops 1073741824 | bytes 6291456 | tf_op jit(solution)/shard_map/pallas_call | solution.py:133
  133.1 5.3 %shard_map.100 = f32[4,128]{1,0:T(4,128)S(1)} custom-call(s32[16]{0:T(128)S(1)} %add.88.idx_ref, bf16[512,1024]{1,0:T(8,128)(2,1)S(1)} %collective-permute-done.15.x_ref, bf16[4,1024,128]{2,1,0:T(8,128)(2,1)S(1)} %bitcast.13, f32[1024,1024]{1,0:T(8,128)} %get-tuple-element.9.near_ref, f32[1024,128]{1,0:T(8,128)S(1)} %get-tuple-element.10.near_proj_ref, ...), custom_call_target="tpu_custom_call" | custom-call | flops 1073741824 | bytes 6291456 | tf_op jit(solution)/shard_map/pallas_call | solution.py:133
  139.3 9.7 %all-to-all-start = ((f32[128,1,128]{2,1,0:T(1,128)}), f32[128,1,128]{2,1,0:T(1,128)S(1)}, u32[]{:S(2)}, u32[]{:S(2)}) async-start(f32[128,1,128]{2,1,0:T(1,128)} %broadcast_in_dim.11), calls=%async_computation | async-start | bytes 131072 | tf_op jit(solution)/shard_map/all_to_all | solution.py:216
  149.0 9.5 %all-to-all-done = f32[128,1,128]{2,1,0:T(1,128)S(1)} async-done(((f32[128,1,128]{2,1,0:T(1,128)}), f32[128,1,128]{2,1,0:T(1,128)S(1)}, u32[]{:S(2)}, u32[]{:S(2)}) %all-to-all-start) | async-done | bytes 65568 | tf_op jit(solution)/shard_map/all_to_all | solution.py:216
  161.7 3.3 %fusion.1 = f32[512,1024]{1,0:T(8,128)} fusion(bf16[128,1024]{1,0:T(8,128)(2,1)S(1)} %copy-done, f32[128]{0:T(128)S(1)} %divide_multiply_fusion, bf16[128,4096]{1,0:T(8,128)(2,1)} %param.13, s32[]{:T(128)S(6)} %select_n.48), kind=kOutput, calls=%fused_computation.8 | convolution fusion | flops 805437440 | bytes 2490884 | tf_op jit(solution)/shard_map/dot_general | solution.py:229
  (78 shorter events, 25.4 us)
Async XLA Ops:
  0.6 47.4 %copy-start = (bf16[128,1024]{1,0:T(8,128)(2,1)S(1)}, bf16[128,1024]{1,0:T(8,128)(2,1)}, u32[]{:S(2)}) copy-start(bf16[128,1024]{1,0:T(8,128)(2,1)} %param.14) | copy-start | bytes 786436
  2.0 14.6 %collective-permute-start = (bf16[1024,256]{1,0:T(8,128)(2,1)S(1)}, bf16[1024,256]{1,0:T(8,128)(2,1)S(1)}, u32[]{:S(2)}, u32[]{:S(2)}) collective-permute-start(bf16[1024,256]{1,0:T(8,128)(2,1)S(1)} %get-tuple-element.13), channel_id=1, source_target_pairs={{0,4},{1,5},{2,6},{3,7},{4,8},{5,9},{6,10},{7,11},{8,12},{9,13},{1... | collective-permute-start | bytes 1572872 | tf_op jit(solution)/shard_map/ppermute | solution.py:30
  4.1 13.5 %collective-permute-start.1 = (bf16[1024,256]{1,0:T(8,128)(2,1)S(1)}, bf16[1024,256]{1,0:T(8,128)(2,1)S(1)}, u32[]{:S(2)}, u32[]{:S(2)}) collective-permute-start(bf16[1024,256]{1,0:T(8,128)(2,1)S(1)} %get-tuple-element.13), channel_id=1, source_target_pairs={{0,12},{1,13},{2,14},{3,15},{4,0},{5,1},{6,2},{7,3},{8,4},{9,5},{1... | collective-permute-start | bytes 1572872 | tf_op jit(solution)/shard_map/ppermute | solution.py:30
  5.4 16.0 %collective-permute-start.8 = (bf16[1024,256]{1,0:T(8,128)(2,1)S(1)}, bf16[1024,256]{1,0:T(8,128)(2,1)S(1)}, u32[]{:S(2)}, u32[]{:S(2)}) collective-permute-start(bf16[1024,256]{1,0:T(8,128)(2,1)S(1)} %get-tuple-element.14), channel_id=1, source_target_pairs={{0,1},{1,2},{2,3},{3,0},{4,5},{5,6},{6,7},{7,4},{8,9},{9,10},{10,1... | collective-permute-start | bytes 1572872 | tf_op jit(solution)/shard_map/ppermute | solution.py:30
  6.8 17.0 %collective-permute-start.9 = (bf16[1024,256]{1,0:T(8,128)(2,1)S(1)}, bf16[1024,256]{1,0:T(8,128)(2,1)S(1)}, u32[]{:S(2)}, u32[]{:S(2)}) collective-permute-start(bf16[1024,256]{1,0:T(8,128)(2,1)S(1)} %get-tuple-element.14), channel_id=1, source_target_pairs={{0,3},{1,0},{2,1},{3,2},{4,7},{5,4},{6,5},{7,6},{8,11},{9,8},{10,9... | collective-permute-start | bytes 1572872 | tf_op jit(solution)/shard_map/ppermute | solution.py:30
  16.5 9.7 %copy-start.8 = (bf16[1024,256]{1,0:T(8,128)(2,1)}, bf16[1024,256]{1,0:T(8,128)(2,1)S(1)}, u32[]{:S(2)}) copy-start(bf16[1024,256]{1,0:T(8,128)(2,1)S(1)} %collective-permute-done) | copy-start | bytes 1572868
  17.3 8.9 %collective-permute-start.2 = (bf16[512,256]{1,0:T(8,128)(2,1)}, bf16[512,256]{1,0:T(8,128)(2,1)}, u32[]{:S(2)}, u32[]{:S(2)}) collective-permute-start(bf16[512,256]{1,0:T(8,128)(2,1)} %slice.60), channel_id=1, source_target_pairs={{0,4},{1,5},{2,6},{3,7},{4,8},{5,9},{6,10},{7,11},{8,12},{9,13},{1... | collective-permute-start | bytes 786440 | tf_op jit(solution)/shard_map/ppermute | solution.py:30
  17.6 8.6 %copy-start.9 = (bf16[1024,256]{1,0:T(8,128)(2,1)}, bf16[1024,256]{1,0:T(8,128)(2,1)S(1)}, u32[]{:S(2)}) copy-start(bf16[1024,256]{1,0:T(8,128)(2,1)S(1)} %collective-permute-done.1) | copy-start | bytes 1572868
  18.4 7.9 %collective-permute-start.3 = (bf16[512,256]{1,0:T(8,128)(2,1)}, bf16[512,256]{1,0:T(8,128)(2,1)}, u32[]{:S(2)}, u32[]{:S(2)}) collective-permute-start(bf16[512,256]{1,0:T(8,128)(2,1)} %slice.61), channel_id=1, source_target_pairs={{0,12},{1,13},{2,14},{3,15},{4,0},{5,1},{6,2},{7,3},{8,4},{9,5},{1... | collective-permute-start | bytes 786440 | tf_op jit(solution)/shard_map/ppermute | solution.py:30
  21.4 4.7 %copy-start.4 = (bf16[1024,256]{1,0:T(8,128)(2,1)}, bf16[1024,256]{1,0:T(8,128)(2,1)S(1)}, u32[]{:S(2)}) copy-start(bf16[1024,256]{1,0:T(8,128)(2,1)S(1)} %collective-permute-done.8) | copy-start | bytes 1572868
  22.2 8.6 %collective-permute-start.10 = (bf16[512,256]{1,0:T(8,128)(2,1)}, bf16[512,256]{1,0:T(8,128)(2,1)}, u32[]{:S(2)}, u32[]{:S(2)}) collective-permute-start(bf16[512,256]{1,0:T(8,128)(2,1)} %slice.65), channel_id=1, source_target_pairs={{0,1},{1,2},{2,3},{3,0},{4,5},{5,6},{6,7},{7,4},{8,9},{9,10},{10,1... | collective-permute-start | bytes 786440 | tf_op jit(solution)/shard_map/ppermute | solution.py:30
  24.6 6.2 %collective-permute-start.11 = (bf16[512,256]{1,0:T(8,128)(2,1)}, bf16[512,256]{1,0:T(8,128)(2,1)}, u32[]{:S(2)}, u32[]{:S(2)}) collective-permute-start(bf16[512,256]{1,0:T(8,128)(2,1)} %slice.66), channel_id=1, source_target_pairs={{0,3},{1,0},{2,1},{3,2},{4,7},{5,4},{6,5},{7,6},{8,11},{9,8},{10,9... | collective-permute-start | bytes 786440 | tf_op jit(solution)/shard_map/ppermute | solution.py:30
  26.2 10.2 %copy-start.3 = (bf16[128,4096]{1,0:T(8,128)(2,1)S(1)}, bf16[128,4096]{1,0:T(8,128)(2,1)}, u32[]{:S(2)}) copy-start(bf16[128,4096]{1,0:T(8,128)(2,1)} %param.13) | copy-start | bytes 3145732
  26.2 10.2 %copy-start.10 = (s32[16]{0:T(128)S(1)}, s32[16]{0:T(128)}, u32[]{:S(2)}) copy-start(s32[16]{0:T(128)} %param.15) | copy-start | bytes 196
  28.1 46.7 %collective-permute-start.4 = (bf16[1024,1024]{1,0:T(8,128)(2,1)S(1)}, bf16[1024,1024]{1,0:T(8,128)(2,1)}, u32[]{:S(2)}, u32[]{:S(2)}) collective-permute-start(bf16[1024,1024]{1,0:T(8,128)(2,1)S(1)} %maximum_maximum_fusion.b0), channel_id=1, source_target_pairs={{0,1},{1,2},{2,3},{3,0},{4,5},{5,6},{6,7},{7,4},{8,9},{9,10},{10,1... | collective-permute-start | bytes 6291464 | tf_op jit(solution)/shard_map/ppermute | solution.py:30
  28.5 49.3 %collective-permute-start.6 = (bf16[1024,1024]{1,0:T(8,128)(2,1)S(1)}, bf16[1024,1024]{1,0:T(8,128)(2,1)}, u32[]{:S(2)}, u32[]{:S(2)}) collective-permute-start(bf16[1024,1024]{1,0:T(8,128)(2,1)S(1)} %maximum_maximum_fusion.b0), channel_id=1, source_target_pairs={{0,3},{1,0},{2,1},{3,2},{4,7},{5,4},{6,5},{7,6},{8,11},{9,8},{10,9... | collective-permute-start | bytes 6291464 | tf_op jit(solution)/shard_map/ppermute | solution.py:30
  33.7 48.2 %collective-permute-start.12 = (bf16[1024,1024]{1,0:T(8,128)(2,1)}, bf16[1024,1024]{1,0:T(8,128)(2,1)}, u32[]{:S(2)}, u32[]{:S(2)}) collective-permute-start(bf16[1024,1024]{1,0:T(8,128)(2,1)} %maximum_maximum_fusion.1.b0), channel_id=1, source_target_pairs={{0,4},{1,5},{2,6},{3,7},{4,8},{5,9},{6,10},{7,11},{8,12},{9,13},{1... | collective-permute-start | bytes 6291464 | tf_op jit(solution)/shard_map/ppermute | solution.py:30
  33.7 49.6 %collective-permute-start.14 = (bf16[1024,1024]{1,0:T(8,128)(2,1)}, bf16[1024,1024]{1,0:T(8,128)(2,1)}, u32[]{:S(2)}, u32[]{:S(2)}) collective-permute-start(bf16[1024,1024]{1,0:T(8,128)(2,1)} %maximum_maximum_fusion.1.b0), channel_id=1, source_target_pairs={{0,12},{1,13},{2,14},{3,15},{4,0},{5,1},{6,2},{7,3},{8,4},{9,5},{1... | collective-permute-start | bytes 6291464 | tf_op jit(solution)/shard_map/ppermute | solution.py:30
  48.2 40.1 %copy-start.1 = (bf16[12,256,128]{2,1,0:T(8,128)(2,1)S(1)}, bf16[12,256,128]{2,1,0:T(8,128)(2,1)}, u32[]{:S(2)}) copy-start(bf16[12,256,128]{2,1,0:T(8,128)(2,1)} %slice.63) | copy-start | bytes 2359300
  77.0 40.2 %collective-permute-start.5 = (bf16[512,1024]{1,0:T(8,128)(2,1)}, bf16[512,1024]{1,0:T(8,128)(2,1)S(1)}, u32[]{:S(2)}, u32[]{:S(2)}) collective-permute-start(bf16[512,1024]{1,0:T(8,128)(2,1)} %slice.62), channel_id=1, source_target_pairs={{0,1},{1,2},{2,3},{3,0},{4,5},{5,6},{6,7},{7,4},{8,9},{9,10},{10,1... | collective-permute-start | bytes 3145736 | tf_op jit(solution)/shard_map/ppermute | solution.py:30
  80.0 42.5 %collective-permute-start.7 = (bf16[512,1024]{1,0:T(8,128)(2,1)}, bf16[512,1024]{1,0:T(8,128)(2,1)S(1)}, u32[]{:S(2)}, u32[]{:S(2)}) collective-permute-start(bf16[512,1024]{1,0:T(8,128)(2,1)} %slice.64), channel_id=1, source_target_pairs={{0,3},{1,0},{2,1},{3,2},{4,7},{5,4},{6,5},{7,6},{8,11},{9,8},{10,9... | collective-permute-start | bytes 3145736 | tf_op jit(solution)/shard_map/ppermute | solution.py:30
  83.2 44.6 %collective-permute-start.13 = (bf16[512,1024]{1,0:T(8,128)(2,1)S(1)}, bf16[512,1024]{1,0:T(8,128)(2,1)S(1)}, u32[]{:S(2)}, u32[]{:S(2)}) collective-permute-start(bf16[512,1024]{1,0:T(8,128)(2,1)S(1)} %slice.67), channel_id=1, source_target_pairs={{0,4},{1,5},{2,6},{3,7},{4,8},{5,9},{6,10},{7,11},{8,12},{9,13},{1... | collective-permute-start | bytes 3145736 | tf_op jit(solution)/shard_map/ppermute | solution.py:30
  85.7 47.4 %collective-permute-start.15 = (bf16[512,1024]{1,0:T(8,128)(2,1)}, bf16[512,1024]{1,0:T(8,128)(2,1)S(1)}, u32[]{:S(2)}, u32[]{:S(2)}) collective-permute-start(bf16[512,1024]{1,0:T(8,128)(2,1)} %slice.69), channel_id=1, source_target_pairs={{0,12},{1,13},{2,14},{3,15},{4,0},{5,1},{6,2},{7,3},{8,4},{9,5},{1... | collective-permute-start | bytes 3145736 | tf_op jit(solution)/shard_map/ppermute | solution.py:30
  139.3 19.2 %all-to-all-start = ((f32[128,1,128]{2,1,0:T(1,128)}), f32[128,1,128]{2,1,0:T(1,128)S(1)}, u32[]{:S(2)}, u32[]{:S(2)}) async-start(f32[128,1,128]{2,1,0:T(1,128)} %broadcast_in_dim.11), calls=%async_computation | async-start | bytes 131072 | tf_op jit(solution)/shard_map/all_to_all | solution.py:216
  (4 other events, 13.3 us)

commit v3 on v0

v3 whole, which is shorter than its diff:
```python
import functools
import math

import jax
import jax.numpy as jnp
from jax import lax
from jax.experimental import pallas as pl
from jax.experimental.pallas import tpu as pltpu
from jax.sharding import PartitionSpec as P

D = 4096
FF = 16384
TOK = 128
SIDE = 4
STEPS = (0, 1, -1, 2)

perturb_scale = 0.25
epsilon = 1e-05

COLS = 256
LANES = 128
VMEM_LIMIT = 56 * 1024 * 1024


def shift(piece, dx, dy):
    perm = [
        (x * SIDE + y, ((x + dx) % SIDE) * SIDE + (y + dy) % SIDE)
        for x in range(SIDE)
        for y in range(SIDE)
    ]
    return lax.ppermute(piece, "mp", perm)


def first_ring(piece, along_x):
    step = (lambda a, k: shift(a, k, 0)) if along_x else (lambda a, k: shift(a, 0, k))
    half = piece.shape[0] // 2
    back, ahead = step(piece, 1), step(piece, -1)
    return back, ahead, step(back[:half], 1), step(ahead[half:], -1)


def stage_kernel(started, final, first, idx_ref, *refs):
    refs = list(refs)
    xs = [refs.pop(0) for _ in range(2)]
    w_refs = [[refs.pop(0) for _ in range(SIDE)] for _ in range(2)]
    left_refs = [[refs.pop(0) for _ in range(SIDE)] for _ in range(2)]
    sum_ref, sum_proj_ref = (refs.pop(0), refs.pop(0)) if started else (None, None)
    right_ref, cot_ref = (refs.pop(0), refs.pop(0)) if final else (None, None)
    out_ref, proj_ref = refs
    rows = xs[0].shape[0]

    @pl.when(pl.program_id(0) == 0)
    def _():
        for h in range(2):
            span = slice(h * rows, (h + 1) * rows)
            left = jnp.concatenate([r[...] for r in left_refs[h]], axis=0)
            total = jnp.dot(xs[h][...], left, preferred_element_type=jnp.float32)
            if started:
                total += sum_proj_ref[span, :]
            if not final:
                proj_ref[span, :] = total
                continue
            for m in range(rows // TOK):
                token = slice(m * TOK, (m + 1) * TOK)
                slot = first + h * (rows // TOK) + m
                proj_ref[h * rows + m * TOK : h * rows + (m + 1) * TOK, :] = jnp.broadcast_to(
                    total[token, slot : slot + 1] * (perturb_scale / math.sqrt(D)), (TOK, LANES)
                )
        if final:
            out_ref[...] = jnp.zeros(out_ref.shape, jnp.float32)

    for h in range(2):
        span = slice(h * rows, (h + 1) * rows)
        w = jnp.concatenate([r[...] for r in w_refs[h]], axis=0)
        base = jnp.dot(xs[h][...], w, preferred_element_type=jnp.float32)
        if started:
            base += sum_ref[span, :]
        if not final:
            out_ref[span, :] = base
            continue
        for m in range(rows // TOK):
            token = slice(m * TOK, (m + 1) * TOK)
            there = slice(h * rows + m * TOK, h * rows + (m + 1) * TOK)
            slot = h * (rows // TOK) + m
            proj = proj_ref[there, :]
            right = right_ref[first + slot : first + slot + 1, :]
            sums = jnp.zeros((1, LANES), jnp.float32)
            for g in range(COLS // LANES):
                cols = slice(g * LANES, (g + 1) * LANES)
                act = jnp.maximum(base[token, cols] + proj * right[:, cols], 0.0)
                term = cot_ref[there, cols].astype(jnp.float32) * (act * act)
                sums += jnp.sum(term, axis=0, keepdims=True)
            out_ref[slot : slot + 1, :] += sums


def stage(pieces, groups, idx, weight, left_own, sums, score=None):
    rows, extent = pieces[0].shape
    columns = weight.shape[1]
    width = extent // SIDE
    whole = lambda n, idx: (0, 0)
    block = pl.BlockSpec((2 * rows, COLS), lambda n, idx: (0, n))
    lane = pl.BlockSpec((2 * rows, LANES), whole)
    in_specs = [pl.BlockSpec((rows, extent), whole)] * 2
    operands = list(pieces)
    for array, size, moves in ((weight, COLS, 1), (left_own, LANES, 0)):
        for group in groups:
            for k in range(SIDE):
                place = functools.partial(
                    lambda at, moves, n, idx: (idx[at], n * moves), group * SIDE + k, moves
                )
                in_specs.append(pl.BlockSpec((width, size), place))
                operands.append(array)
    if sums is not None:
        in_specs += [block, lane]
        operands += list(sums)
    first = 0
    if score is None:
        out_specs, scratch = [block, lane], []
        out_shape = [
            jax.ShapeDtypeStruct((2 * rows, columns), jnp.float32),
            jax.ShapeDtypeStruct((2 * rows, LANES), jnp.float32),
        ]
    else:
        right_own, cot, part = score
        members = 2 * rows // TOK
        first = part * members
        in_specs += [
            pl.BlockSpec((right_own.shape[0], COLS), lambda n, idx: (0, n)),
            pl.BlockSpec((2 * rows, COLS), lambda n, idx: (part, n)),
        ]
        operands += [right_own, cot]
        out_specs = pl.BlockSpec((members, LANES), whole)
        out_shape = jax.ShapeDtypeStruct((members, LANES), jnp.float32)
        scratch = [pltpu.VMEM((2 * rows, LANES), jnp.float32)]
    return pl.pallas_call(
        functools.partial(stage_kernel, sums is not None, score is not None, first),
        grid_spec=pltpu.PrefetchScalarGridSpec(
            num_scalar_prefetch=1,
            grid=(columns // COLS,),
            in_specs=in_specs,
            out_specs=out_specs,
            scratch_shapes=scratch,
        ),
        out_shape=out_shape,
        compiler_params=pltpu.CompilerParams(vmem_limit_bytes=VMEM_LIMIT),
        cost_estimate=pl.CostEstimate(
            flops=4 * rows * extent * columns,
            bytes_accessed=4 * extent * (rows + columns) + 16 * rows * columns,
            transcendentals=0,
        ),
    )(idx, *operands)


def finish_kernel(owned, at_ref, tables_ref, seat_ref, left_ref, right_ref, est_ref, fit_ref):
    members = tables_ref.shape[1]
    row = jnp.sum(tables_ref[...], axis=0, keepdims=True)
    shape = (members, members)
    same = lax.broadcasted_iota(jnp.int32, shape, 0) == lax.broadcasted_iota(jnp.int32, shape, 1)
    column = jnp.sum(
        jnp.where(same, jnp.broadcast_to(row, shape), 0.0), axis=1, keepdims=True
    )
    fit_ref[...] = jnp.sum(seat_ref[...] * column, axis=0, keepdims=True)[:, :owned]
    average = jnp.sum(row) / members
    variance = jnp.sum(jnp.square(row - average)) / members
    spread = jnp.sqrt(jnp.full((members, 1), variance + epsilon, jnp.float32))
    weights = (column - average) / spread / math.sqrt(members)
    scaled = left_ref[...].astype(jnp.float32) * weights
    high = scaled.astype(jnp.bfloat16)
    rest = scaled - high.astype(jnp.float32)
    middle = rest.astype(jnp.bfloat16)
    low = (rest - middle.astype(jnp.float32)).astype(jnp.bfloat16)
    total = None
    for term in (low, middle, high):
        part = lax.dot_general(
            term, right_ref[...], (((0,), (0,)), ((), ())), preferred_element_type=jnp.float32
        )
        total = part if total is None else total + part
    est_ref[...] = total


def finish(at, tables, seat, factor_left, factor_right, owned, row_share):
    devices, members = tables.shape
    columns = factor_right.shape[1]
    return pl.pallas_call(
        functools.partial(finish_kernel, owned),
        grid_spec=pltpu.PrefetchScalarGridSpec(
            num_scalar_prefetch=1,
            grid=(1,),
            in_specs=[
                pl.BlockSpec((devices, members), lambda n, at: (0, 0)),
                pl.BlockSpec((members, LANES), lambda n, at: (0, 0)),
                pl.BlockSpec((members, row_share), lambda n, at: (0, at[0])),
                pl.BlockSpec((members, columns), lambda n, at: (0, 0)),
            ],
            out_specs=[
                pl.BlockSpec((row_share, columns), lambda n, at: (0, 0)),
                pl.BlockSpec((1, owned), lambda n, at: (0, 0)),
            ],
        ),
        out_shape=[
            jax.ShapeDtypeStruct((row_share, columns), jnp.float32),
            jax.ShapeDtypeStruct((1, owned), jnp.float32),
        ],
        compiler_params=pltpu.CompilerParams(vmem_limit_bytes=VMEM_LIMIT),
    )(at, tables, seat, factor_left, factor_right)


def sources(x_first):
    here = lax.axis_index("mp")
    x, y = here // SIDE, here % SIDE
    steps = jnp.array(STEPS, dtype=jnp.int32)
    if x_first:
        index = ((x - steps[None, :]) % SIDE) * SIDE + (y - steps[:, None]) % SIDE
    else:
        index = ((x - steps[:, None]) % SIDE) * SIDE + (y - steps[None, :]) % SIDE
    return index.reshape(-1).astype(jnp.int32)


def per_device(weight, layer_input, cotangent, factor_left, factor_right, seeds):
    members = factor_left.shape[0]
    owned = seeds.shape[0]
    rows = layer_input.shape[0]
    half = rows // 2
    quarter = rows // 4

    pieces = {True: layer_input[:half], False: layer_input[half:]}
    blocks = {}
    for o in (True, False):
        back, ahead, far0, far1 = first_ring(pieces[o], o)
        blocks[o] = [
            jnp.concatenate([pieces[o][s], back[s], ahead[s], far], axis=1)
            for s, far in ((slice(0, quarter), far0), (slice(quarter, half), far1))
        ]

    slots = jnp.pad(seeds, (0, LANES - owned), constant_values=-1)
    seat = slots[None, :] == jnp.arange(members, dtype=jnp.int32)[:, None]
    picked = seat.astype(jnp.bfloat16)
    contract = (((0,), (0,)), ((), ()))
    left_own = lax.dot_general(
        factor_left, picked, contract, preferred_element_type=jnp.float32
    ).astype(jnp.bfloat16)
    right_own = lax.dot_general(
        picked[:, :owned], factor_right, contract, preferred_element_type=jnp.float32
    )

    both = (True, False)
    ways = (1, -1)
    idx = {o: sources(o) for o in both}
    score = {o: (right_own, cotangent, 0 if o else 1) for o in both}

    def send(arrays, o, sense):
        return [
            shift(a, 0, sense * way) if o else shift(a, sense * way, 0)
            for a, way in zip(arrays, ways)
        ]

    near = {o: send(blocks[o], o, 1) for o in both}
    sums = {o: stage(blocks[o], (0, 0), idx[o], weight, left_own, None) for o in both}
    near, sums = lax.optimization_barrier((near, sums))
    far = {o: send(near[o], o, 1) for o in both}
    sums = {o: stage(near[o], (1, 2), idx[o], weight, left_own, sums[o]) for o in both}
    far, sums, blocks = lax.optimization_barrier((far, sums, blocks))
    other = {o: send(blocks[o], o, -1) for o in both}
    sums = {o: stage(far[o], (3, 3), idx[o], weight, left_own, sums[o]) for o in both}
    scores = [
        stage(other[o], (2, 1), idx[o], weight, left_own, sums[o], score[o]) for o in both
    ]
    partial = -jnp.sum(jnp.concatenate(scores, axis=0), axis=1) / math.sqrt(TOK * FF)
    seated = seat[:, :owned].astype(jnp.float32)
    table = jnp.sum(seated * partial[None, :], 1)

    everywhere = ("pop", "mp")
    devices = lax.axis_size("pop") * lax.axis_size("mp")
    copies = jnp.broadcast_to(table[None, :], (devices, members))
    tables = lax.all_to_all(copies, everywhere, 0, 0, tiled=True)
    row_share = weight.shape[0] // lax.axis_size("pop")
    at = lax.axis_index("pop").astype(jnp.int32).reshape(1)
    estimate, fitness = finish(
        at, tables, seat.astype(jnp.float32), factor_left, factor_right, owned, row_share
    )
    return (estimate, fitness.reshape(owned))


def solution(mesh):
    placed = (P(None, "mp"), P("pop", "mp"), P("pop", "mp"), P(), P(None, "mp"), P("pop"))
    return jax.shard_map(
        per_device,
        mesh=mesh,
        in_specs=placed,
        out_specs=(P("pop", "mp"), P("pop")),
        check_vma=False,
    )
```

time: 238 us -> 158 us (0.66)
  waiting for transfers between devices: 116 us -> 18.1 us
  Pallas kernels: 0 us -> 82.2 us
  blocking collectives: 51.6 us -> 0 us
  starting transfers between devices: 0.04 us -> 43.7 us
  matrix products: 37.5 us -> 3.56 us
  between operations: 15.4 us -> 1.02 us
  local copies, waits for them, and re-layouts: 15.2 us -> 5.68 us
    all_gather x1 -> x0, waiting for transfers between devices: 115 us -> none  [per_device(): shard_piece = lax.all_gather(layer_input, 'mp', axis=1, tiled=True)]
    pallas_call x0 -> x9, Pallas kernels: none -> 82.2 us  [the longest x8 78.5 us: stage(): pl.pallas_call(functools.partial(stage_kernel, sums is not None, score is...]
    psum x2 -> x0, blocking collectives: 51.6 us -> none  [the longest x1 30.9 us: per_device(): fitness_own = lax.psum(partial_value, 'mp')]
    dot_general x3 -> x2, matrix products: 37.5 us -> 3.56 us  [the longest x1 2.74 us: per_device(): lax.dot_general(factor_left, picked, contract, preferred_element_type=jnp...]
    ppermute x0 -> x20, starting transfers between devices: none -> 27.8 us  [shift(): return lax.ppermute(piece, 'mp', perm)]
    all_to_all x0 -> x1, starting transfers between devices: none -> 15.9 us  [per_device(): tables = lax.all_to_all(copies, everywhere, 0, 0, tiled=True)]
    all_to_all x0 -> x1, waiting for transfers between devices: none -> 9.5 us  [per_device(): tables = lax.all_to_all(copies, everywhere, 0, 0, tiled=True)]
    ppermute x0 -> x20, waiting for transfers between devices: none -> 8.6 us  [shift(): return lax.ppermute(piece, 'mp', perm)]
  transfers between devices with their start and end apart: 1 -> 21, of which waited for: 1 -> 4; matrix products, arithmetic and copies ran while one was open for 4% -> 5% of each run, Pallas kernels for 0% -> 44%
where the time goes in v3:
time: 158 us; the launch traced here: 157 us
  Pallas kernels  82.2 us (52%)
  starting transfers between devices  43.7 us (28%)
  waiting for transfers between devices  18.1 us (11%)
  local copies, waits for them, and re-layouts  5.68 us (4%)
  matrix products  3.56 us (2%)
  other arithmetic  3.13 us (2%)
    pallas_call x8, Pallas kernels, stage(): pl.pallas_call(functools.partial(stage_kernel, sums is not None, score is...  78.5 us
    ppermute x20, starting transfers between devices, shift(): return lax.ppermute(piece, 'mp', perm)  27.8 us
    all_to_all x1, starting transfers between devices, per_device(): tables = lax.all_to_all(copies, everywhere, 0, 0, tiled=True)  15.9 us
    all_to_all x1, waiting for transfers between devices, per_device(): tables = lax.all_to_all(copies, everywhere, 0, 0, tiled=True)  9.5 us
    ppermute x20, waiting for transfers between devices, shift(): return lax.ppermute(piece, 'mp', perm)  8.6 us
    pallas_call x1, Pallas kernels, finish(): pl.pallas_call(functools.partial(finish_kernel, owned), grid_spec=pltpu.P...  3.7 us
  transfers between devices with their start and end apart: 21, of which 4 were waited for; matrix products, arithmetic and copies ran while one was open for 5% of the time, Pallas kernels for 44%

profile of v3, /device:TPU:1, one launch (start us, length us, event | category | flops | bytes accessed | tf_op | source)
XLA Modules:
  0.0 157.3 jit_solution(4851097778626385333)
XLA Ops:
  0.6 2.1 %fusion.9 = (bf16[1024,256]{1,0:T(8,128)(2,1)}, bf16[1024,256]{1,0:T(8,128)(2,1)S(1)}) fusion(bf16[2048,256]{1,0:T(8,128)(2,1)} %param.9), kind=kLoop, calls=%fused_computation.26 | loop fusion | bytes 2097152 | tf_op jit(solution)/shard_map/slice | solution.py:225
  2.8 2.0 %collective-permute-start.6 = (bf16[1024,256]{1,0:T(8,128)(2,1)}, bf16[1024,256]{1,0:T(8,128)(2,1)S(1)}, u32[]{:S(2)}, u32[]{:S(2)}) collective-permute-start(bf16[1024,256]{1,0:T(8,128)(2,1)} %get-tuple-element.74), channel_id=1, source_target_pairs={{0,4},{1,5},{2,6},{3,7},{4,8},{5,9},{6,10},{7,11},{8,12},{9,13},{1... | collective-permute-start | bytes 1572872 | tf_op jit(solution)/shard_map/ppermute | solution.py:31
  4.8 1.3 collective-permute-start.7
  6.1 2.9 %collective-permute-start.1 = (bf16[1024,256]{1,0:T(8,128)(2,1)S(1)}, bf16[1024,256]{1,0:T(8,128)(2,1)S(1)}, u32[]{:S(2)}, u32[]{:S(2)}) collective-permute-start(bf16[1024,256]{1,0:T(8,128)(2,1)S(1)} %get-tuple-element.75), channel_id=1, source_target_pairs={{0,3},{1,0},{2,1},{3,2},{4,7},{5,4},{6,5},{7,6},{8,11},{9,8},{10,9... | collective-permute-start | bytes 1572872 | tf_op jit(solution)/shard_map/ppermute | solution.py:31
  9.8 7.7 %collective-permute-done.6 = bf16[1024,256]{1,0:T(8,128)(2,1)S(1)} collective-permute-done((bf16[1024,256]{1,0:T(8,128)(2,1)}, bf16[1024,256]{1,0:T(8,128)(2,1)S(1)}, u32[]{:S(2)}, u32[]{:S(2)}) %collective-permute-start.6) | collective-permute-done | bytes 524320 | tf_op jit(solution)/shard_map/ppermute | solution.py:31
  18.0 2.4 %collective-permute-start.10 = (bf16[512,256]{1,0:T(8,128)(2,1)S(1)}, bf16[512,256]{1,0:T(8,128)(2,1)S(1)}, u32[]{:S(2)}, u32[]{:S(2)}) collective-permute-start(bf16[512,256]{1,0:T(8,128)(2,1)S(1)} %get-tuple-element.78), channel_id=1, source_target_pairs={{0,12},{1,13},{2,14},{3,15},{4,0},{5,1},{6,2},{7,3},{8,4},{9,5},{1... | collective-permute-start | bytes 786440 | tf_op jit(solution)/shard_map/ppermute | solution.py:31
  20.4 3.1 %collective-permute-start.4 = (bf16[512,256]{1,0:T(8,128)(2,1)S(1)}, bf16[512,256]{1,0:T(8,128)(2,1)S(1)}, u32[]{:S(2)}, u32[]{:S(2)}) collective-permute-start(bf16[512,256]{1,0:T(8,128)(2,1)S(1)} %get-tuple-element.82), channel_id=1, source_target_pairs={{0,3},{1,0},{2,1},{3,2},{4,7},{5,4},{6,5},{7,6},{8,11},{9,8},{10,9... | collective-permute-start | bytes 786440 | tf_op jit(solution)/shard_map/ppermute | solution.py:31
  24.2 3.3 %collective-permute-start.11 = (bf16[512,1024]{1,0:T(8,128)(2,1)S(1)}, bf16[512,1024]{1,0:T(8,128)(2,1)}, u32[]{:S(2)}, u32[]{:S(2)}) collective-permute-start(bf16[512,1024]{1,0:T(8,128)(2,1)S(1)} %pad_maximum_fusion.3.refs_1_), channel_id=1, source_target_pairs={{0,3},{1,0},{2,1},{3,2},{4,7},{5,4},{6,5},{7,6},{8,11},{9,8},{10,9... | collective-permute-start | bytes 3145736 | tf_op jit(solution)/shard_map/ppermute | solution.py:31
  27.9 3.5 %collective-permute-start.5 = (bf16[512,1024]{1,0:T(8,128)(2,1)S(1)}, bf16[512,1024]{1,0:T(8,128)(2,1)}, u32[]{:S(2)}, u32[]{:S(2)}) collective-permute-start(bf16[512,1024]{1,0:T(8,128)(2,1)S(1)} %pad_maximum_fusion.1.refs_1_), channel_id=1, source_target_pairs={{0,12},{1,13},{2,14},{3,15},{4,0},{5,1},{6,2},{7,3},{8,4},{9,5},{1... | collective-permute-start | bytes 3145736 | tf_op jit(solution)/shard_map/ppermute | solution.py:31
  33.8 2.7 %fusion.refs_10_.refs_11_.refs_12_.refs_13_.refs_14_.refs_15_.refs_16_.refs_17_ = bf16[4096,128]{1,0:T(8,128)(2,1)} fusion(bf16[128,4096]{1,0:T(8,128)(2,1)} %left_ref.1, s32[128]{0:T(128)S(1)} %pad.4), kind=kOutput, calls=%fused_computation.1 | convolution fusion | flops 134758400 | bytes 2097664 | tf_op jit(solution)/shard_map/dot_general | solution.py:238
  36.6 8.8 %shard_map.96 = (f32[1024,1024]{1,0:T(8,128)}, f32[1024,128]{1,0:T(8,128)}) custom-call(s32[16]{0:T(128)} %add.72.idx_ref, bf16[512,1024]{1,0:T(8,128)(2,1)} %copy-done.4, bf16[512,1024]{1,0:T(8,128)(2,1)} %copy-done, bf16[4096,1024]{1,0:T(8,128)(2,1)} %refs_9_.15, bf16[4096,1024]{1,0:T(8,128)(2,1)} %refs_9_.15, bf16[4096,1024]{1,0:T(8,128)(2,1)} %refs_9_.15, ...), custom_call_target="tpu_custom_call" | custom-call | flops 2147483648 | bytes 14680064 | tf_op jit(solution)/shard_map/pallas_call | solution.py:134
  45.4 8.8 %shard_map.95 = (f32[1024,1024]{1,0:T(8,128)}, f32[1024,128]{1,0:T(8,128)}) custom-call(s32[16]{0:T(128)} %add.78.idx_ref, bf16[512,1024]{1,0:T(8,128)(2,1)} %pad_maximum_fusion.refs_0_, bf16[512,1024]{1,0:T(8,128)(2,1)} %copy-done.2, bf16[4096,1024]{1,0:T(8,128)(2,1)} %refs_9_.15, bf16[4096,1024]{1,0:T(8,128)(2,1)} %refs_9_.15, ...), custom_call_target="tpu_custom_call" | custom-call | flops 2147483648 | bytes 14680064 | tf_op jit(solution)/shard_map/pallas_call | solution.py:134
  54.7 2.7 %collective-permute-start.13 = (bf16[512,1024]{1,0:T(8,128)(2,1)}, bf16[512,1024]{1,0:T(8,128)(2,1)S(1)}, u32[]{:S(2)}, u32[]{:S(2)}) collective-permute-start(bf16[512,1024]{1,0:T(8,128)(2,1)} %collective-permute-done.5.refs_1_), channel_id=1, source_target_pairs={{0,12},{1,13},{2,14},{3,15},{4,0},{5,1},{6,2},{7,3},{8,4},{9,5},{1... | collective-permute-start | bytes 3145736 | tf_op jit(solution)/shard_map/ppermute | solution.py:31
  57.7 2.7 %collective-permute-start.15 = (bf16[512,1024]{1,0:T(8,128)(2,1)}, bf16[512,1024]{1,0:T(8,128)(2,1)S(1)}, u32[]{:S(2)}, u32[]{:S(2)}) collective-permute-start(bf16[512,1024]{1,0:T(8,128)(2,1)} %collective-permute-done.11.refs_1_), channel_id=1, source_target_pairs={{0,3},{1,0},{2,1},{3,2},{4,7},{5,4},{6,5},{7,6},{8,11},{9,8},{10,9... | collective-permute-start | bytes 3145736 | tf_op jit(solution)/shard_map/ppermute | solution.py:31
  60.4 10.1 %shard_map.98 = (f32[1024,1024]{1,0:T(8,128)}, f32[1024,128]{1,0:T(8,128)}) custom-call(s32[16]{0:T(128)} %add.72.idx_ref, bf16[512,1024]{1,0:T(8,128)(2,1)} %collective-permute-done.9.refs_0_, bf16[512,1024]{1,0:T(8,128)(2,1)} %collective-permute-done.11.refs_1_, bf16[4096,1024]{1,0:T(8,128)(2,1)} %refs_9_.15, bf16[4096,1024]{1,0:T(8,128)(2,1)} %refs_9_.15, ...), custom_call_target="tpu_custom_call" | custom-call | flops 2147483648 | bytes 14680064 | tf_op jit(solution)/shard_map/pallas_call | solution.py:134
  70.5 10.3 %shard_map.97 = (f32[1024,1024]{1,0:T(8,128)}, f32[1024,128]{1,0:T(8,128)}) custom-call(s32[16]{0:T(128)} %add.78.idx_ref, bf16[512,1024]{1,0:T(8,128)(2,1)} %collective-permute-done.3.refs_0_, bf16[512,1024]{1,0:T(8,128)(2,1)} %collective-permute-done.5.refs_1_, bf16[4096,1024]{1,0:T(8,128)(2,1)} %refs_9_.15, bf16[4096,1024]{1,0:T(8,128)(2,1)} %refs_9_.15, ...), custom_call_target="tpu_custom_call" | custom-call | flops 2147483648 | bytes 14680064 | tf_op jit(solution)/shard_map/pallas_call | solution.py:134
  80.9 1.5 collective-permute-start.16
  85.3 10.5 %shard_map.99 = (f32[1024,1024]{1,0:T(8,128)}, f32[1024,128]{1,0:T(8,128)}) custom-call(s32[16]{0:T(128)} %add.72.idx_ref, bf16[512,1024]{1,0:T(8,128)(2,1)} %copy-done.9, bf16[512,1024]{1,0:T(8,128)(2,1)} %copy-done.10, bf16[4096,1024]{1,0:T(8,128)(2,1)} %refs_9_.15, bf16[4096,1024]{1,0:T(8,128)(2,1)} %refs_9_.15, bf16[4096,1024]{1,0:T(8,128)(2,1)} %refs_9_.15, ...), custom_call_target="tpu_custom_call" | custom-call | flops 2147483648 | bytes 14680064 | tf_op jit(solution)/shard_map/pallas_call | solution.py:134
  95.8 10.4 %shard_map.101 = (f32[1024,1024]{1,0:T(8,128)}, f32[1024,128]{1,0:T(8,128)}) custom-call(s32[16]{0:T(128)} %add.78.idx_ref, bf16[512,1024]{1,0:T(8,128)(2,1)} %copy-done.7, bf16[512,1024]{1,0:T(8,128)(2,1)} %copy-done.8, bf16[4096,1024]{1,0:T(8,128)(2,1)} %refs_9_.15, bf16[4096,1024]{1,0:T(8,128)(2,1)} %refs_9_.15, bf16[4096,1024]{1,0:T(8,128)(2,1)} %refs_9_.15, ...), custom_call_target="tpu_custom_call" | custom-call | flops 2147483648 | bytes 14680064 | tf_op jit(solution)/shard_map/pallas_call | solution.py:134
  106.2 9.9 %shard_map.100 = f32[8,128]{1,0:T(8,128)} custom-call(s32[16]{0:T(128)} %add.72.idx_ref, bf16[512,1024]{1,0:T(8,128)(2,1)} %collective-permute-done.16.refs_0_, bf16[512,1024]{1,0:T(8,128)(2,1)} %collective-permute-done.17.refs_1_, bf16[4096,1024]{1,0:T(8,128)(2,1)} %refs_9_.15, bf16[4096,1024]{1,0:T(8,128)(2,1)} %refs_9_.15, bf16[4096,1024]{1,0:T(8,128)(2,1)} %refs_9_.15, ...), custom_call_target="tpu_custom_call" | custom-call | flops 2147483648 | bytes 14680064 | tf_op jit(solution)/shard_map/pallas_call | solution.py:134
  116.1 9.9 %shard_map.102 = f32[8,128]{1,0:T(8,128)} custom-call(s32[16]{0:T(128)} %add.78.idx_ref, bf16[512,1024]{1,0:T(8,128)(2,1)} %collective-permute-done.18.refs_0_, bf16[512,1024]{1,0:T(8,128)(2,1)} %collective-permute-done.19.refs_1_, bf16[4096,1024]{1,0:T(8,128)(2,1)} %refs_9_.15, bf16[4096,1024]{1,0:T(8,128)(2,1)} %refs_9_.15, bf16[4096,1024]{1,0:T(8,128)(2,1)} %refs_9_.15, ...), custom_call_target="tpu_custom_call" | custom-call | flops 2147483648 | bytes 14680064 | tf_op jit(solution)/shard_map/pallas_call | solution.py:134
  127.6 15.9 %all-to-all-start = ((f32[128,1,128]{2,1,0:T(1,128)}), f32[128,1,128]{2,1,0:T(1,128)S(1)}, u32[]{:S(2)}, u32[]{:S(2)}) async-start(f32[128,1,128]{2,1,0:T(1,128)} %broadcast_in_dim.2), calls=%async_computation | async-start | bytes 131072 | tf_op jit(solution)/shard_map/all_to_all | solution.py:274
  143.5 9.5 %all-to-all-done = f32[128,1,128]{2,1,0:T(1,128)S(1)} async-done(((f32[128,1,128]{2,1,0:T(1,128)}), f32[128,1,128]{2,1,0:T(1,128)S(1)}, u32[]{:S(2)}, u32[]{:S(2)}) %all-to-all-start) | async-done | bytes 65568 | tf_op jit(solution)/shard_map/all_to_all | solution.py:274
  153.6 3.7 %shard_map.103 = (f32[512,1024]{1,0:T(8,128)}, f32[1,16]{1,0:T(1,128)}) custom-call(s32[1]{0:T(128)} %bitcast.at_ref, f32[128,128]{1,0:T(8,128)} %bitcast.7, f32[128,128]{1,0:T(8,128)} %get-tuple-element.86.seat_ref, bf16[128,4096]{1,0:T(8,128)(2,1)} %left_ref.1, bf16[128,1024]{1,0:T(8,128)(2,1)} %right_ref.1), custom_call_target="tpu_custom_call" | custom-call | tf_op jit(solution)/shard_map/pallas_call | solution.py:183
  (83 shorter events, 10.8 us)
Async XLA Ops:
  2.8 14.7 %collective-permute-start.6 = (bf16[1024,256]{1,0:T(8,128)(2,1)}, bf16[1024,256]{1,0:T(8,128)(2,1)S(1)}, u32[]{:S(2)}, u32[]{:S(2)}) collective-permute-start(bf16[1024,256]{1,0:T(8,128)(2,1)} %get-tuple-element.74), channel_id=1, source_target_pairs={{0,4},{1,5},{2,6},{3,7},{4,8},{5,9},{6,10},{7,11},{8,12},{9,13},{1... | collective-permute-start | bytes 1572872 | tf_op jit(solution)/shard_map/ppermute | solution.py:31
  4.8 13.1 %collective-permute-start.7 = (bf16[1024,256]{1,0:T(8,128)(2,1)}, bf16[1024,256]{1,0:T(8,128)(2,1)S(1)}, u32[]{:S(2)}, u32[]{:S(2)}) collective-permute-start(bf16[1024,256]{1,0:T(8,128)(2,1)} %get-tuple-element.74), channel_id=1, source_target_pairs={{0,12},{1,13},{2,14},{3,15},{4,0},{5,1},{6,2},{7,3},{8,4},{9,5},{1... | collective-permute-start | bytes 1572872 | tf_op jit(solution)/shard_map/ppermute | solution.py:31
  6.1 14.3 %collective-permute-start.1 = (bf16[1024,256]{1,0:T(8,128)(2,1)S(1)}, bf16[1024,256]{1,0:T(8,128)(2,1)S(1)}, u32[]{:S(2)}, u32[]{:S(2)}) collective-permute-start(bf16[1024,256]{1,0:T(8,128)(2,1)S(1)} %get-tuple-element.75), channel_id=1, source_target_pairs={{0,3},{1,0},{2,1},{3,2},{4,7},{5,4},{6,5},{7,6},{8,11},{9,8},{10,9... | collective-permute-start | bytes 1572872 | tf_op jit(solution)/shard_map/ppermute | solution.py:31
  9.0 14.5 %collective-permute-start = (bf16[1024,256]{1,0:T(8,128)(2,1)S(1)}, bf16[1024,256]{1,0:T(8,128)(2,1)S(1)}, u32[]{:S(2)}, u32[]{:S(2)}) collective-permute-start(bf16[1024,256]{1,0:T(8,128)(2,1)S(1)} %get-tuple-element.75), channel_id=1, source_target_pairs={{0,1},{1,2},{2,3},{3,0},{4,5},{5,6},{6,7},{7,4},{8,9},{9,10},{10,1... | collective-permute-start | bytes 1572872 | tf_op jit(solution)/shard_map/ppermute | solution.py:31
  17.5 9.9 %collective-permute-start.8 = (bf16[512,256]{1,0:T(8,128)(2,1)S(1)}, bf16[512,256]{1,0:T(8,128)(2,1)S(1)}, u32[]{:S(2)}, u32[]{:S(2)}) collective-permute-start(bf16[512,256]{1,0:T(8,128)(2,1)S(1)} %get-tuple-element.77), channel_id=1, source_target_pairs={{0,4},{1,5},{2,6},{3,7},{4,8},{5,9},{6,10},{7,11},{8,12},{9,13},{1... | collective-permute-start | bytes 786440 | tf_op jit(solution)/shard_map/ppermute | solution.py:31
  18.0 6.1 %collective-permute-start.10 = (bf16[512,256]{1,0:T(8,128)(2,1)S(1)}, bf16[512,256]{1,0:T(8,128)(2,1)S(1)}, u32[]{:S(2)}, u32[]{:S(2)}) collective-permute-start(bf16[512,256]{1,0:T(8,128)(2,1)S(1)} %get-tuple-element.78), channel_id=1, source_target_pairs={{0,12},{1,13},{2,14},{3,15},{4,0},{5,1},{6,2},{7,3},{8,4},{9,5},{1... | collective-permute-start | bytes 786440 | tf_op jit(solution)/shard_map/ppermute | solution.py:31
  20.4 7.2 %collective-permute-start.4 = (bf16[512,256]{1,0:T(8,128)(2,1)S(1)}, bf16[512,256]{1,0:T(8,128)(2,1)S(1)}, u32[]{:S(2)}, u32[]{:S(2)}) collective-permute-start(bf16[512,256]{1,0:T(8,128)(2,1)S(1)} %get-tuple-element.82), channel_id=1, source_target_pairs={{0,3},{1,0},{2,1},{3,2},{4,7},{5,4},{6,5},{7,6},{8,11},{9,8},{10,9... | collective-permute-start | bytes 786440 | tf_op jit(solution)/shard_map/ppermute | solution.py:31
  23.6 7.7 %collective-permute-start.2 = (bf16[512,256]{1,0:T(8,128)(2,1)S(1)}, bf16[512,256]{1,0:T(8,128)(2,1)S(1)}, u32[]{:S(2)}, u32[]{:S(2)}) collective-permute-start(bf16[512,256]{1,0:T(8,128)(2,1)S(1)} %get-tuple-element.81), channel_id=1, source_target_pairs={{0,1},{1,2},{2,3},{3,0},{4,5},{5,6},{6,7},{7,4},{8,9},{9,10},{10,1... | collective-permute-start | bytes 786440 | tf_op jit(solution)/shard_map/ppermute | solution.py:31
  24.2 30.0 %collective-permute-start.11 = (bf16[512,1024]{1,0:T(8,128)(2,1)S(1)}, bf16[512,1024]{1,0:T(8,128)(2,1)}, u32[]{:S(2)}, u32[]{:S(2)}) collective-permute-start(bf16[512,1024]{1,0:T(8,128)(2,1)S(1)} %pad_maximum_fusion.3.refs_1_), channel_id=1, source_target_pairs={{0,3},{1,0},{2,1},{3,2},{4,7},{5,4},{6,5},{7,6},{8,11},{9,8},{10,9... | collective-permute-start | bytes 3145736 | tf_op jit(solution)/shard_map/ppermute | solution.py:31
  27.6 26.6 %collective-permute-start.9 = (bf16[512,1024]{1,0:T(8,128)(2,1)S(1)}, bf16[512,1024]{1,0:T(8,128)(2,1)}, u32[]{:S(2)}, u32[]{:S(2)}) collective-permute-start(bf16[512,1024]{1,0:T(8,128)(2,1)S(1)} %pad_maximum_fusion.2.refs_0_), channel_id=1, source_target_pairs={{0,1},{1,2},{2,3},{3,0},{4,5},{5,6},{6,7},{7,4},{8,9},{9,10},{10,1... | collective-permute-start | bytes 3145736 | tf_op jit(solution)/shard_map/ppermute | solution.py:31
  27.9 26.3 %collective-permute-start.5 = (bf16[512,1024]{1,0:T(8,128)(2,1)S(1)}, bf16[512,1024]{1,0:T(8,128)(2,1)}, u32[]{:S(2)}, u32[]{:S(2)}) collective-permute-start(bf16[512,1024]{1,0:T(8,128)(2,1)S(1)} %pad_maximum_fusion.1.refs_1_), channel_id=1, source_target_pairs={{0,12},{1,13},{2,14},{3,15},{4,0},{5,1},{6,2},{7,3},{8,4},{9,5},{1... | collective-permute-start | bytes 3145736 | tf_op jit(solution)/shard_map/ppermute | solution.py:31
  32.5 22.2 %collective-permute-start.3 = (bf16[512,1024]{1,0:T(8,128)(2,1)}, bf16[512,1024]{1,0:T(8,128)(2,1)}, u32[]{:S(2)}, u32[]{:S(2)}) collective-permute-start(bf16[512,1024]{1,0:T(8,128)(2,1)} %pad_maximum_fusion.refs_0_), channel_id=1, source_target_pairs={{0,4},{1,5},{2,6},{3,7},{4,8},{5,9},{6,10},{7,11},{8,12},{9,13},{1... | collective-permute-start | bytes 3145736 | tf_op jit(solution)/shard_map/ppermute | solution.py:31
  54.7 26.1 %collective-permute-start.12 = (bf16[512,1024]{1,0:T(8,128)(2,1)}, bf16[512,1024]{1,0:T(8,128)(2,1)S(1)}, u32[]{:S(2)}, u32[]{:S(2)}) collective-permute-start(bf16[512,1024]{1,0:T(8,128)(2,1)} %collective-permute-done.3.refs_0_), channel_id=1, source_target_pairs={{0,4},{1,5},{2,6},{3,7},{4,8},{5,9},{6,10},{7,11},{8,12},{9,13},{1... | collective-permute-start | bytes 3145736 | tf_op jit(solution)/shard_map/ppermute | solution.py:31
  54.7 26.1 %collective-permute-start.13 = (bf16[512,1024]{1,0:T(8,128)(2,1)}, bf16[512,1024]{1,0:T(8,128)(2,1)S(1)}, u32[]{:S(2)}, u32[]{:S(2)}) collective-permute-start(bf16[512,1024]{1,0:T(8,128)(2,1)} %collective-permute-done.5.refs_1_), channel_id=1, source_target_pairs={{0,12},{1,13},{2,14},{3,15},{4,0},{5,1},{6,2},{7,3},{8,4},{9,5},{1... | collective-permute-start | bytes 3145736 | tf_op jit(solution)/shard_map/ppermute | solution.py:31
  57.4 23.4 %collective-permute-start.14 = (bf16[512,1024]{1,0:T(8,128)(2,1)}, bf16[512,1024]{1,0:T(8,128)(2,1)S(1)}, u32[]{:S(2)}, u32[]{:S(2)}) collective-permute-start(bf16[512,1024]{1,0:T(8,128)(2,1)} %collective-permute-done.9.refs_0_), channel_id=1, source_target_pairs={{0,1},{1,2},{2,3},{3,0},{4,5},{5,6},{6,7},{7,4},{8,9},{9,10},{10,1... | collective-permute-start | bytes 3145736 | tf_op jit(solution)/shard_map/ppermute | solution.py:31
  57.7 23.1 %collective-permute-start.15 = (bf16[512,1024]{1,0:T(8,128)(2,1)}, bf16[512,1024]{1,0:T(8,128)(2,1)S(1)}, u32[]{:S(2)}, u32[]{:S(2)}) collective-permute-start(bf16[512,1024]{1,0:T(8,128)(2,1)} %collective-permute-done.11.refs_1_), channel_id=1, source_target_pairs={{0,3},{1,0},{2,1},{3,2},{4,7},{5,4},{6,5},{7,6},{8,11},{9,8},{10,9... | collective-permute-start | bytes 3145736 | tf_op jit(solution)/shard_map/ppermute | solution.py:31
  70.5 14.0 %copy-start.11 = (bf16[128,1024]{1,0:T(8,128)(2,1)S(1)}, bf16[128,1024]{1,0:T(8,128)(2,1)}, u32[]{:S(2)}) copy-start(bf16[128,1024]{1,0:T(8,128)(2,1)} %right_ref.1) | copy-start | bytes 786436
  80.8 15.0 %copy-start.7 = (bf16[512,1024]{1,0:T(8,128)(2,1)}, bf16[512,1024]{1,0:T(8,128)(2,1)S(1)}, u32[]{:S(2)}) copy-start(bf16[512,1024]{1,0:T(8,128)(2,1)S(1)} %collective-permute-done.12.refs_0_) | copy-start | bytes 3145732
  80.8 15.0 %copy-start.8 = (bf16[512,1024]{1,0:T(8,128)(2,1)}, bf16[512,1024]{1,0:T(8,128)(2,1)S(1)}, u32[]{:S(2)}) copy-start(bf16[512,1024]{1,0:T(8,128)(2,1)S(1)} %collective-permute-done.13.refs_1_) | copy-start | bytes 3145732
  80.9 25.3 %collective-permute-start.16 = (bf16[512,1024]{1,0:T(8,128)(2,1)S(1)}, bf16[512,1024]{1,0:T(8,128)(2,1)}, u32[]{:S(2)}, u32[]{:S(2)}) collective-permute-start(bf16[512,1024]{1,0:T(8,128)(2,1)S(1)} %copy-done.5), channel_id=1, source_target_pairs={{0,3},{1,0},{2,1},{3,2},{4,7},{5,4},{6,5},{7,6},{8,11},{9,8},{10,9... | collective-permute-start | bytes 3145736 | tf_op jit(solution)/shard_map/ppermute | solution.py:31
  82.4 23.8 %collective-permute-start.17 = (bf16[512,1024]{1,0:T(8,128)(2,1)S(1)}, bf16[512,1024]{1,0:T(8,128)(2,1)}, u32[]{:S(2)}, u32[]{:S(2)}) collective-permute-start(bf16[512,1024]{1,0:T(8,128)(2,1)S(1)} %copy-done.1), channel_id=1, source_target_pairs={{0,1},{1,2},{2,3},{3,0},{4,5},{5,6},{6,7},{7,4},{8,9},{9,10},{10,1... | collective-permute-start | bytes 3145736 | tf_op jit(solution)/shard_map/ppermute | solution.py:31
  82.4 33.7 %collective-permute-start.18 = (bf16[512,1024]{1,0:T(8,128)(2,1)}, bf16[512,1024]{1,0:T(8,128)(2,1)}, u32[]{:S(2)}, u32[]{:S(2)}) collective-permute-start(bf16[512,1024]{1,0:T(8,128)(2,1)} %pad_maximum_fusion.refs_0_), channel_id=1, source_target_pairs={{0,12},{1,13},{2,14},{3,15},{4,0},{5,1},{6,2},{7,3},{8,4},{9,5},{1... | collective-permute-start | bytes 3145736 | tf_op jit(solution)/shard_map/ppermute | solution.py:31
  83.2 32.9 %collective-permute-start.19 = (bf16[512,1024]{1,0:T(8,128)(2,1)S(1)}, bf16[512,1024]{1,0:T(8,128)(2,1)}, u32[]{:S(2)}, u32[]{:S(2)}) collective-permute-start(bf16[512,1024]{1,0:T(8,128)(2,1)S(1)} %copy-done.3), channel_id=1, source_target_pairs={{0,4},{1,5},{2,6},{3,7},{4,8},{5,9},{6,10},{7,11},{8,12},{9,13},{1... | collective-permute-start | bytes 3145736 | tf_op jit(solution)/shard_map/ppermute | solution.py:31
  127.6 25.4 %all-to-all-start = ((f32[128,1,128]{2,1,0:T(1,128)}), f32[128,1,128]{2,1,0:T(1,128)S(1)}, u32[]{:S(2)}, u32[]{:S(2)}) async-start(f32[128,1,128]{2,1,0:T(1,128)} %broadcast_in_dim.2), calls=%async_computation | async-start | bytes 131072 | tf_op jit(solution)/shard_map/all_to_all | solution.py:274
  (14 other events, 94.2 us)

commit v4 on v3

--- a/solution.py
+++ b/solution.py
@@ -19,7 +19,7 @@
 
 COLS = 256
 LANES = 128
-VMEM_LIMIT = 56 * 1024 * 1024
+VMEM_LIMIT = 48 * 1024 * 1024
 
 
 def shift(piece, dx, dy):
@@ -38,51 +38,61 @@
     return back, ahead, step(back[:half], 1), step(ahead[half:], -1)
 
 
-def stage_kernel(started, final, first, idx_ref, *refs):
+def stage_kernel(terms, started, final, idx_ref, *refs):
     refs = list(refs)
-    xs = [refs.pop(0) for _ in range(2)]
-    w_refs = [[refs.pop(0) for _ in range(SIDE)] for _ in range(2)]
-    left_refs = [[refs.pop(0) for _ in range(SIDE)] for _ in range(2)]
+    xs = [[refs.pop(0) for _ in block] for block in terms]
+    w_ref, left_ref = refs.pop(0), refs.pop(0)
     sum_ref, sum_proj_ref = (refs.pop(0), refs.pop(0)) if started else (None, None)
     right_ref, cot_ref = (refs.pop(0), refs.pop(0)) if final else (None, None)
     out_ref, proj_ref = refs
-    rows = xs[0].shape[0]
+    rows, extent = xs[0][0].shape
+    width = extent // SIDE
+    members = rows // TOK
+
+    def product(b, ref):
+        total = None
+        for x_ref, place in zip(xs[b], terms[b]):
+            parts = [
+                ref[pl.ds(pl.multiple_of(idx_ref[place + k] * width, width), width), :]
+                for k in range(SIDE)
+            ]
+            part = jnp.dot(
+                x_ref[...], jnp.concatenate(parts, axis=0), preferred_element_type=jnp.float32
+            )
+            total = part if total is None else total + part
+        return total
 
     @pl.when(pl.program_id(0) == 0)
     def _():
-        for h in range(2):
-            span = slice(h * rows, (h + 1) * rows)
-            left = jnp.concatenate([r[...] for r in left_refs[h]], axis=0)
-            total = jnp.dot(xs[h][...], left, preferred_element_type=jnp.float32)
+        for b in range(len(terms)):
+            total = product(b, left_ref)
             if started:
-                total += sum_proj_ref[span, :]
+                total += sum_proj_ref[b * rows : (b + 1) * rows, :]
             if not final:
-                proj_ref[span, :] = total
+                proj_ref[b * rows : (b + 1) * rows, :] = total
                 continue
-            for m in range(rows // TOK):
-                token = slice(m * TOK, (m + 1) * TOK)
-                slot = first + h * (rows // TOK) + m
-                proj_ref[h * rows + m * TOK : h * rows + (m + 1) * TOK, :] = jnp.broadcast_to(
-                    total[token, slot : slot + 1] * (perturb_scale / math.sqrt(D)), (TOK, LANES)
+            for m in range(members):
+                slot = b * members + m
+                one = total[m * TOK : (m + 1) * TOK, slot : slot + 1]
+                proj_ref[slot * TOK : (slot + 1) * TOK, :] = jnp.broadcast_to(
+                    one * (perturb_scale / math.sqrt(D)), (TOK, LANES)
                 )
         if final:
             out_ref[...] = jnp.zeros(out_ref.shape, jnp.float32)
 
-    for h in range(2):
-        span = slice(h * rows, (h + 1) * rows)
-        w = jnp.concatenate([r[...] for r in w_refs[h]], axis=0)
-        base = jnp.dot(xs[h][...], w, preferred_element_type=jnp.float32)
+    for b in range(len(terms)):
+        base = product(b, w_ref)
         if started:
-            base += sum_ref[span, :]
+            base += sum_ref[b * rows : (b + 1) * rows, :]
         if not final:
-            out_ref[span, :] = base
+            out_ref[b * rows : (b + 1) * rows, :] = base
             continue
-        for m in range(rows // TOK):
+        for m in range(members):
+            slot = b * members + m
             token = slice(m * TOK, (m + 1) * TOK)
-            there = slice(h * rows + m * TOK, h * rows + (m + 1) * TOK)
-            slot = h * (rows // TOK) + m
+            there = slice(slot * TOK, (slot + 1) * TOK)
             proj = proj_ref[there, :]
-            right = right_ref[first + slot : first + slot + 1, :]
+            right = right_ref[slot : slot + 1, :]
             sums = jnp.zeros((1, LANES), jnp.float32)
             for g in range(COLS // LANES):
                 cols = slice(g * LANES, (g + 1) * LANES)
@@ -92,47 +102,41 @@
             out_ref[slot : slot + 1, :] += sums
 
 
-def stage(pieces, groups, idx, weight, left_own, sums, score=None):
-    rows, extent = pieces[0].shape
-    columns = weight.shape[1]
-    width = extent // SIDE
+def stage(blocks, idx, weight, left_own, sums=None, score=None):
+    terms = tuple(tuple(place for _, place in block) for block in blocks)
+    rows, extent = blocks[0][0][0].shape
+    total = rows * len(blocks)
+    depth, columns = weight.shape
     whole = lambda n, idx: (0, 0)
-    block = pl.BlockSpec((2 * rows, COLS), lambda n, idx: (0, n))
-    lane = pl.BlockSpec((2 * rows, LANES), whole)
-    in_specs = [pl.BlockSpec((rows, extent), whole)] * 2
-    operands = list(pieces)
-    for array, size, moves in ((weight, COLS, 1), (left_own, LANES, 0)):
-        for group in groups:
-            for k in range(SIDE):
-                place = functools.partial(
-                    lambda at, moves, n, idx: (idx[at], n * moves), group * SIDE + k, moves
-                )
-                in_specs.append(pl.BlockSpec((width, size), place))
-                operands.append(array)
+    tile = lambda n, idx: (0, n)
+    once = pl.Buffered(1)
+    operands = [piece for block in blocks for piece, _ in block]
+    in_specs = [pl.BlockSpec((rows, extent), whole, pipeline_mode=once)] * len(operands)
+    in_specs += [
+        pl.BlockSpec((depth, COLS), tile),
+        pl.BlockSpec((depth, LANES), whole, pipeline_mode=once),
+    ]
+    operands += [weight, left_own]
+    block = pl.BlockSpec((total, COLS), tile)
     if sums is not None:
-        in_specs += [block, lane]
+        in_specs += [block, pl.BlockSpec((total, LANES), whole, pipeline_mode=once)]
         operands += list(sums)
-    first = 0
     if score is None:
-        out_specs, scratch = [block, lane], []
+        out_specs, scratch = [block, pl.BlockSpec((total, LANES), whole)], []
         out_shape = [
-            jax.ShapeDtypeStruct((2 * rows, columns), jnp.float32),
-            jax.ShapeDtypeStruct((2 * rows, LANES), jnp.float32),
+            jax.ShapeDtypeStruct((total, columns), jnp.float32),
+            jax.ShapeDtypeStruct((total, LANES), jnp.float32),
         ]
     else:
-        right_own, cot, part = score
-        members = 2 * rows // TOK
-        first = part * members
-        in_specs += [
-            pl.BlockSpec((right_own.shape[0], COLS), lambda n, idx: (0, n)),
-            pl.BlockSpec((2 * rows, COLS), lambda n, idx: (part, n)),
-        ]
-        operands += [right_own, cot]
+        members = total // TOK
+        in_specs += [pl.BlockSpec((members, COLS), tile), block]
+        operands += list(score)
         out_specs = pl.BlockSpec((members, LANES), whole)
         out_shape = jax.ShapeDtypeStruct((members, LANES), jnp.float32)
-        scratch = [pltpu.VMEM((2 * rows, LANES), jnp.float32)]
+        scratch = [pltpu.VMEM((total, LANES), jnp.float32)]
+    flops = 2 * sum(len(t) for t in terms) * rows * extent * columns
     return pl.pallas_call(
-        functools.partial(stage_kernel, sums is not None, score is not None, first),
+        functools.partial(stage_kernel, terms, sums is not None, score is not None),
         grid_spec=pltpu.PrefetchScalarGridSpec(
             num_scalar_prefetch=1,
             grid=(columns // COLS,),
@@ -143,9 +147,7 @@
         out_shape=out_shape,
         compiler_params=pltpu.CompilerParams(vmem_limit_bytes=VMEM_LIMIT),
         cost_estimate=pl.CostEstimate(
-            flops=4 * rows * extent * columns,
-            bytes_accessed=4 * extent * (rows + columns) + 16 * rows * columns,
-            transcendentals=0,
+            flops=flops, bytes_accessed=flops // 256, transcendentals=0
         ),
     )(idx, *operands)
 
@@ -244,8 +246,7 @@
 
     both = (True, False)
     ways = (1, -1)
-    idx = {o: sources(o) for o in both}
-    score = {o: (right_own, cotangent, 0 if o else 1) for o in both}
+    idx = jnp.concatenate([sources(o) for o in both])
 
     def send(arrays, o, sense):
         return [
@@ -253,18 +254,23 @@
             for a, way in zip(arrays, ways)
         ]
 
+    def terms(*given):
+        out = []
+        for base, o in ((0, True), (SIDE * SIDE, False)):
+            for h in range(2):
+                out.append([(arrays[o][h], base + SIDE * groups[h]) for arrays, groups in given])
+        return out
+
     near = {o: send(blocks[o], o, 1) for o in both}
-    sums = {o: stage(blocks[o], (0, 0), idx[o], weight, left_own, None) for o in both}
-    near, sums = lax.optimization_barrier((near, sums))
     far = {o: send(near[o], o, 1) for o in both}
-    sums = {o: stage(near[o], (1, 2), idx[o], weight, left_own, sums[o]) for o in both}
+    sums = stage(terms((blocks, (0, 0)), (near, (1, 2))), idx, weight, left_own)
     far, sums, blocks = lax.optimization_barrier((far, sums, blocks))
     other = {o: send(blocks[o], o, -1) for o in both}
-    sums = {o: stage(far[o], (3, 3), idx[o], weight, left_own, sums[o]) for o in both}
-    scores = [
-        stage(other[o], (2, 1), idx[o], weight, left_own, sums[o], score[o]) for o in both
-    ]
-    partial = -jnp.sum(jnp.concatenate(scores, axis=0), axis=1) / math.sqrt(TOK * FF)
+    sums = stage(terms((far, (3, 3))), idx, weight, left_own, sums)
+    scores = stage(
+        terms((other, (2, 1))), idx, weight, left_own, sums, (right_own, cotangent)
+    )
+    partial = -jnp.sum(scores, axis=1) / math.sqrt(TOK * FF)
     seated = seat[:, :owned].astype(jnp.float32)
     table = jnp.sum(seated * partial[None, :], 1)
 

time: 158 us -> 138 us (0.87)
  Pallas kernels: 82.2 us -> 47.4 us
  waiting for transfers between devices: 18.1 us -> 43.2 us
  starting transfers between devices: 43.7 us -> 37.6 us
  matrix products: 3.56 us -> 1.69 us
    pallas_call x8 -> x3, Pallas kernels: 78.5 us -> 44.8 us  [stage(): pl.pallas_call(functools.partial(stage_kernel, terms, sums is not None, s...]
    ppermute x20, waiting for transfers between devices: 8.6 us -> 33.7 us  [shift(): return lax.ppermute(piece, 'mp', perm)]
    all_to_all x1, starting transfers between devices: 15.9 us -> 12.6 us  [per_device(): tables = lax.all_to_all(copies, everywhere, 0, 0, tiled=True)]
    ppermute x20, starting transfers between devices: 27.8 us -> 25 us  [shift(): return lax.ppermute(piece, 'mp', perm)]
  transfers between devices with their start and end apart: 21 -> 21, of which waited for: 4 -> 8; matrix products, arithmetic and copies ran while one was open for 5% -> 3% of each run, Pallas kernels for 44% -> 23%
where the time goes in v4:
time: 138 us
  Pallas kernels  47.4 us (34%)
  waiting for transfers between devices  43.2 us (31%)
  starting transfers between devices  37.6 us (27%)
  local copies, waits for them, and re-layouts  4.41 us (3%)
  other arithmetic  2.89 us (2%)
  matrix products  1.69 us (1%)
    pallas_call x3, Pallas kernels, stage(): pl.pallas_call(functools.partial(stage_kernel, terms, sums is not None, s...  44.8 us
    ppermute x20, waiting for transfers between devices, shift(): return lax.ppermute(piece, 'mp', perm)  33.7 us
    ppermute x20, starting transfers between devices, shift(): return lax.ppermute(piece, 'mp', perm)  25 us
    all_to_all x1, starting transfers between devices, per_device(): tables = lax.all_to_all(copies, everywhere, 0, 0, tiled=True)  12.6 us
    all_to_all x1, waiting for transfers between devices, per_device(): tables = lax.all_to_all(copies, everywhere, 0, 0, tiled=True)  9.5 us
  transfers between devices with their start and end apart: 21, of which 8 were waited for; matrix products, arithmetic and copies ran while one was open for 3% of the time, Pallas kernels for 23%

profile of v4, /device:TPU:1, one launch (start us, length us, event | category | flops | bytes accessed | tf_op | source)
XLA Modules:
  0.0 138.0 jit_solution(5296497689578048354)
XLA Ops:
  0.6 1.4 fusion.9
  2.0 2.1 %collective-permute-start.8 = (bf16[1024,256]{1,0:T(8,128)(2,1)S(1)}, bf16[1024,256]{1,0:T(8,128)(2,1)S(1)}, u32[]{:S(2)}, u32[]{:S(2)}) collective-permute-start(bf16[1024,256]{1,0:T(8,128)(2,1)S(1)} %get-tuple-element.38), channel_id=1, source_target_pairs={{0,4},{1,5},{2,6},{3,7},{4,8},{5,9},{6,10},{7,11},{8,12},{9,13},{1... | collective-permute-start | bytes 1572872 | tf_op jit(solution)/shard_map/ppermute | solution.py:31
  4.1 1.3 collective-permute-start.9
  5.5 2.9 %collective-permute-start.1 = (bf16[1024,256]{1,0:T(8,128)(2,1)S(1)}, bf16[1024,256]{1,0:T(8,128)(2,1)S(1)}, u32[]{:S(2)}, u32[]{:S(2)}) collective-permute-start(bf16[1024,256]{1,0:T(8,128)(2,1)S(1)} %get-tuple-element.39), channel_id=1, source_target_pairs={{0,3},{1,0},{2,1},{3,2},{4,7},{5,4},{6,5},{7,6},{8,11},{9,8},{10,9... | collective-permute-start | bytes 1572872 | tf_op jit(solution)/shard_map/ppermute | solution.py:31
  8.4 8.2 %collective-permute-done.8 = bf16[1024,256]{1,0:T(8,128)(2,1)S(1)} collective-permute-done((bf16[1024,256]{1,0:T(8,128)(2,1)S(1)}, bf16[1024,256]{1,0:T(8,128)(2,1)S(1)}, u32[]{:S(2)}, u32[]{:S(2)}) %collective-permute-start.8) | collective-permute-done | bytes 524320 | tf_op jit(solution)/shard_map/ppermute | solution.py:31
  17.1 2.4 %collective-permute-start.13 = (bf16[512,256]{1,0:T(8,128)(2,1)S(1)}, bf16[512,256]{1,0:T(8,128)(2,1)S(1)}, u32[]{:S(2)}, u32[]{:S(2)}) collective-permute-start(bf16[512,256]{1,0:T(8,128)(2,1)S(1)} %get-tuple-element.42), channel_id=1, source_target_pairs={{0,12},{1,13},{2,14},{3,15},{4,0},{5,1},{6,2},{7,3},{8,4},{9,5},{1... | collective-permute-start | bytes 786440 | tf_op jit(solution)/shard_map/ppermute | solution.py:31
  19.5 3.1 %collective-permute-start.5 = (bf16[512,256]{1,0:T(8,128)(2,1)S(1)}, bf16[512,256]{1,0:T(8,128)(2,1)S(1)}, u32[]{:S(2)}, u32[]{:S(2)}) collective-permute-start(bf16[512,256]{1,0:T(8,128)(2,1)S(1)} %get-tuple-element.46), channel_id=1, source_target_pairs={{0,3},{1,0},{2,1},{3,2},{4,7},{5,4},{6,5},{7,6},{8,11},{9,8},{10,9... | collective-permute-start | bytes 786440 | tf_op jit(solution)/shard_map/ppermute | solution.py:31
  22.8 1.3 collective-permute-done.10
  24.2 1.8 %collective-permute-start.11 = (bf16[512,1024]{1,0:T(8,128)(2,1)S(1)}, bf16[512,1024]{1,0:T(8,128)(2,1)}, u32[]{:S(2)}, u32[]{:S(2)}) collective-permute-start(bf16[512,1024]{1,0:T(8,128)(2,1)S(1)} %pad_maximum_fusion.2.refs_0_), channel_id=1, source_target_pairs={{0,1},{1,2},{2,3},{3,0},{4,5},{5,6},{6,7},{7,4},{8,9},{9,10},{10,1... | collective-permute-start | bytes 3145736 | tf_op jit(solution)/shard_map/ppermute | solution.py:31
  26.1 1.5 %collective-permute-start.14 = (bf16[512,1024]{1,0:T(8,128)(2,1)S(1)}, bf16[512,1024]{1,0:T(8,128)(2,1)}, u32[]{:S(2)}, u32[]{:S(2)}) collective-permute-start(bf16[512,1024]{1,0:T(8,128)(2,1)S(1)} %pad_maximum_fusion.3.refs_2_), channel_id=1, source_target_pairs={{0,3},{1,0},{2,1},{3,2},{4,7},{5,4},{6,5},{7,6},{8,11},{9,8},{10,9... | collective-permute-start | bytes 3145736 | tf_op jit(solution)/shard_map/ppermute | solution.py:31
  27.7 1.1 pad_maximum_fusion.1.refs_6_
  28.8 2.3 %collective-permute-start.6 = (bf16[512,1024]{1,0:T(8,128)(2,1)}, bf16[512,1024]{1,0:T(8,128)(2,1)}, u32[]{:S(2)}, u32[]{:S(2)}) collective-permute-start(bf16[512,1024]{1,0:T(8,128)(2,1)} %pad_maximum_fusion.1.refs_6_), channel_id=1, source_target_pairs={{0,12},{1,13},{2,14},{3,15},{4,0},{5,1},{6,2},{7,3},{8,4},{9,5},{1... | collective-permute-start | bytes 3145736 | tf_op jit(solution)/shard_map/ppermute | solution.py:31
  31.1 1.1 pad_maximum_fusion.refs_4_
  32.5 19.4 %collective-permute-done.11.refs_1_ = bf16[512,1024]{1,0:T(8,128)(2,1)} collective-permute-done((bf16[512,1024]{1,0:T(8,128)(2,1)S(1)}, bf16[512,1024]{1,0:T(8,128)(2,1)}, u32[]{:S(2)}, u32[]{:S(2)}) %collective-permute-start.11) | collective-permute-done | bytes 1048608 | tf_op jit(solution)/shard_map/ppermute | solution.py:31
  52.0 2.7 %collective-permute-start.15 = (bf16[512,1024]{1,0:T(8,128)(2,1)}, bf16[512,1024]{1,0:T(8,128)(2,1)S(1)}, u32[]{:S(2)}, u32[]{:S(2)}) collective-permute-start(bf16[512,1024]{1,0:T(8,128)(2,1)} %collective-permute-done.14.refs_3_), channel_id=1, source_target_pairs={{0,3},{1,0},{2,1},{3,2},{4,7},{5,4},{6,5},{7,6},{8,11},{9,8},{10,9... | collective-permute-start | bytes 3145736 | tf_op jit(solution)/shard_map/ppermute | solution.py:31
  56.1 1.5 %fusion.refs_9_.refs_5_ = bf16[4096,128]{1,0:T(8,128)(2,1)} fusion(bf16[128,4096]{1,0:T(8,128)(2,1)S(1)} %copy-done.1, s32[128]{0:T(128)S(1)} %pad.4), kind=kOutput, calls=%fused_computation.1 | convolution fusion | flops 134758400 | bytes 2097664 | tf_op jit(solution)/shard_map/dot_general | solution.py:240
  57.6 17.5 %shard_map.95 = (f32[2048,1024]{1,0:T(8,128)}, f32[2048,128]{1,0:T(8,128)S(1)}) custom-call(s32[32]{0:T(128)S(1)} %pad_add_fusion.idx_ref, bf16[512,1024]{1,0:T(8,128)(2,1)S(1)} %pad_maximum_fusion.2.refs_0_, bf16[512,1024]{1,0:T(8,128)(2,1)} %collective-permute-done.11.refs_1_, bf16[512,1024]{1,0:T(8,128)(2,1)S(1)} %pad_maximum_fusion.3.refs_2_, ...), custom_call_target="tpu_custom_call" | custom-call | flops 8589934592 | bytes 33554432 | tf_op jit(solution)/shard_map/pallas_call | solution.py:138
  80.0 14.9 %shard_map.96 = (f32[2048,1024]{1,0:T(8,128)}, f32[2048,128]{1,0:T(8,128)S(1)}) custom-call(s32[32]{0:T(128)S(1)} %pad_add_fusion.idx_ref, bf16[512,1024]{1,0:T(8,128)(2,1)S(1)} %collective-permute-done.12.refs_0_, bf16[512,1024]{1,0:T(8,128)(2,1)S(1)} %collective-permute-done.15.refs_1_, bf16[512,1024]{1,0:T(8,128)(2,1)S(1)} %collective-permute-done.4.refs_2_, ...), custom_call_target="tpu_custom_call" | custom-call | flops 4294967296 | bytes 16777216 | tf_op jit(solution)/shard_map/pallas_call | solution.py:138
  96.3 1.4 collective-permute-done.17.refs_1_
  97.7 2.3 %collective-permute-done.19.refs_3_ = bf16[512,1024]{1,0:T(8,128)(2,1)S(1)} collective-permute-done((bf16[512,1024]{1,0:T(8,128)(2,1)}, bf16[512,1024]{1,0:T(8,128)(2,1)S(1)}, u32[]{:S(2)}, u32[]{:S(2)}) %collective-permute-start.19) | collective-permute-done | bytes 1048608 | tf_op jit(solution)/shard_map/ppermute | solution.py:31
  100.0 12.4 %shard_map.97 = f32[16,128]{1,0:T(8,128)S(1)} custom-call(s32[32]{0:T(128)S(1)} %pad_add_fusion.idx_ref, bf16[512,1024]{1,0:T(8,128)(2,1)S(1)} %collective-permute-done.16.refs_0_, bf16[512,1024]{1,0:T(8,128)(2,1)S(1)} %collective-permute-done.17.refs_1_, bf16[512,1024]{1,0:T(8,128)(2,1)S(1)} %collective-permute-done.18.refs_2_, ...), custom_call_target="tpu_custom_call" | custom-call | flops 4294967296 | bytes 16777216 | tf_op jit(solution)/shard_map/pallas_call | solution.py:138
  113.3 12.6 %all-to-all-start = ((f32[128,1,128]{2,1,0:T(1,128)}), f32[128,1,128]{2,1,0:T(1,128)S(1)}, u32[]{:S(2)}, u32[]{:S(2)}) async-start(f32[128,1,128]{2,1,0:T(1,128)} %broadcast_in_dim.2), calls=%async_computation | async-start | bytes 131072 | tf_op jit(solution)/shard_map/all_to_all | solution.py:280
  125.9 9.5 %all-to-all-done = f32[128,1,128]{2,1,0:T(1,128)S(1)} async-done(((f32[128,1,128]{2,1,0:T(1,128)}), f32[128,1,128]{2,1,0:T(1,128)S(1)}, u32[]{:S(2)}, u32[]{:S(2)}) %all-to-all-start) | async-done | bytes 65568 | tf_op jit(solution)/shard_map/all_to_all | solution.py:280
  135.4 2.6 %shard_map.98 = (f32[512,1024]{1,0:T(8,128)}, f32[1,16]{1,0:T(1,128)}) custom-call(s32[1]{0:T(128)} %bitcast.at_ref, f32[128,128]{1,0:T(8,128)S(1)} %bitcast.7, f32[128,128]{1,0:T(8,128)S(1)} %get-tuple-element.50.seat_ref, bf16[128,4096]{1,0:T(8,128)(2,1)S(1)} %copy-done.1, bf16[128,1024]{1,0:T(8,128)(2,1)S(1)} %copy-done.4), custom_call_target="tpu_custom_call" | custom-call | tf_op jit(solution)/shard_map/pallas_call | solution.py:185
  (61 shorter events, 10.0 us)
Async XLA Ops:
  2.0 14.6 %collective-permute-start.8 = (bf16[1024,256]{1,0:T(8,128)(2,1)S(1)}, bf16[1024,256]{1,0:T(8,128)(2,1)S(1)}, u32[]{:S(2)}, u32[]{:S(2)}) collective-permute-start(bf16[1024,256]{1,0:T(8,128)(2,1)S(1)} %get-tuple-element.38), channel_id=1, source_target_pairs={{0,4},{1,5},{2,6},{3,7},{4,8},{5,9},{6,10},{7,11},{8,12},{9,13},{1... | collective-permute-start | bytes 1572872 | tf_op jit(solution)/shard_map/ppermute | solution.py:31
  4.1 12.9 %collective-permute-start.9 = (bf16[1024,256]{1,0:T(8,128)(2,1)S(1)}, bf16[1024,256]{1,0:T(8,128)(2,1)S(1)}, u32[]{:S(2)}, u32[]{:S(2)}) collective-permute-start(bf16[1024,256]{1,0:T(8,128)(2,1)S(1)} %get-tuple-element.38), channel_id=1, source_target_pairs={{0,12},{1,13},{2,14},{3,15},{4,0},{5,1},{6,2},{7,3},{8,4},{9,5},{1... | collective-permute-start | bytes 1572872 | tf_op jit(solution)/shard_map/ppermute | solution.py:31
  5.5 14.0 %collective-permute-start.1 = (bf16[1024,256]{1,0:T(8,128)(2,1)S(1)}, bf16[1024,256]{1,0:T(8,128)(2,1)S(1)}, u32[]{:S(2)}, u32[]{:S(2)}) collective-permute-start(bf16[1024,256]{1,0:T(8,128)(2,1)S(1)} %get-tuple-element.39), channel_id=1, source_target_pairs={{0,3},{1,0},{2,1},{3,2},{4,7},{5,4},{6,5},{7,6},{8,11},{9,8},{10,9... | collective-permute-start | bytes 1572872 | tf_op jit(solution)/shard_map/ppermute | solution.py:31
  8.3 14.3 %collective-permute-start = (bf16[1024,256]{1,0:T(8,128)(2,1)S(1)}, bf16[1024,256]{1,0:T(8,128)(2,1)S(1)}, u32[]{:S(2)}, u32[]{:S(2)}) collective-permute-start(bf16[1024,256]{1,0:T(8,128)(2,1)S(1)} %get-tuple-element.39), channel_id=1, source_target_pairs={{0,1},{1,2},{2,3},{3,0},{4,5},{5,6},{6,7},{7,4},{8,9},{9,10},{10,1... | collective-permute-start | bytes 1572872 | tf_op jit(solution)/shard_map/ppermute | solution.py:31
  16.6 7.4 %collective-permute-start.10 = (bf16[512,256]{1,0:T(8,128)(2,1)S(1)}, bf16[512,256]{1,0:T(8,128)(2,1)S(1)}, u32[]{:S(2)}, u32[]{:S(2)}) collective-permute-start(bf16[512,256]{1,0:T(8,128)(2,1)S(1)} %get-tuple-element.41), channel_id=1, source_target_pairs={{0,4},{1,5},{2,6},{3,7},{4,8},{5,9},{6,10},{7,11},{8,12},{9,13},{1... | collective-permute-start | bytes 786440 | tf_op jit(solution)/shard_map/ppermute | solution.py:31
  17.1 8.9 %collective-permute-start.13 = (bf16[512,256]{1,0:T(8,128)(2,1)S(1)}, bf16[512,256]{1,0:T(8,128)(2,1)S(1)}, u32[]{:S(2)}, u32[]{:S(2)}) collective-permute-start(bf16[512,256]{1,0:T(8,128)(2,1)S(1)} %get-tuple-element.42), channel_id=1, source_target_pairs={{0,12},{1,13},{2,14},{3,15},{4,0},{5,1},{6,2},{7,3},{8,4},{9,5},{1... | collective-permute-start | bytes 786440 | tf_op jit(solution)/shard_map/ppermute | solution.py:31
  19.5 8.1 %collective-permute-start.5 = (bf16[512,256]{1,0:T(8,128)(2,1)S(1)}, bf16[512,256]{1,0:T(8,128)(2,1)S(1)}, u32[]{:S(2)}, u32[]{:S(2)}) collective-permute-start(bf16[512,256]{1,0:T(8,128)(2,1)S(1)} %get-tuple-element.46), channel_id=1, source_target_pairs={{0,3},{1,0},{2,1},{3,2},{4,7},{5,4},{6,5},{7,6},{8,11},{9,8},{10,9... | collective-permute-start | bytes 786440 | tf_op jit(solution)/shard_map/ppermute | solution.py:31
  22.7 8.4 %collective-permute-start.2 = (bf16[512,256]{1,0:T(8,128)(2,1)S(1)}, bf16[512,256]{1,0:T(8,128)(2,1)S(1)}, u32[]{:S(2)}, u32[]{:S(2)}) collective-permute-start(bf16[512,256]{1,0:T(8,128)(2,1)S(1)} %get-tuple-element.45), channel_id=1, source_target_pairs={{0,1},{1,2},{2,3},{3,0},{4,5},{5,6},{6,7},{7,4},{8,9},{9,10},{10,1... | collective-permute-start | bytes 786440 | tf_op jit(solution)/shard_map/ppermute | solution.py:31
  24.2 27.8 %collective-permute-start.11 = (bf16[512,1024]{1,0:T(8,128)(2,1)S(1)}, bf16[512,1024]{1,0:T(8,128)(2,1)}, u32[]{:S(2)}, u32[]{:S(2)}) collective-permute-start(bf16[512,1024]{1,0:T(8,128)(2,1)S(1)} %pad_maximum_fusion.2.refs_0_), channel_id=1, source_target_pairs={{0,1},{1,2},{2,3},{3,0},{4,5},{5,6},{6,7},{7,4},{8,9},{9,10},{10,1... | collective-permute-start | bytes 3145736 | tf_op jit(solution)/shard_map/ppermute | solution.py:31
  26.1 25.9 %collective-permute-start.14 = (bf16[512,1024]{1,0:T(8,128)(2,1)S(1)}, bf16[512,1024]{1,0:T(8,128)(2,1)}, u32[]{:S(2)}, u32[]{:S(2)}) collective-permute-start(bf16[512,1024]{1,0:T(8,128)(2,1)S(1)} %pad_maximum_fusion.3.refs_2_), channel_id=1, source_target_pairs={{0,3},{1,0},{2,1},{3,2},{4,7},{5,4},{6,5},{7,6},{8,11},{9,8},{10,9... | collective-permute-start | bytes 3145736 | tf_op jit(solution)/shard_map/ppermute | solution.py:31
  27.6 28.5 %copy-start.1 = (bf16[128,4096]{1,0:T(8,128)(2,1)S(1)}, bf16[128,4096]{1,0:T(8,128)(2,1)}, u32[]{:S(2)}) copy-start(bf16[128,4096]{1,0:T(8,128)(2,1)} %left_ref.1) | copy-start | bytes 3145732
  28.8 25.9 %collective-permute-start.6 = (bf16[512,1024]{1,0:T(8,128)(2,1)}, bf16[512,1024]{1,0:T(8,128)(2,1)}, u32[]{:S(2)}, u32[]{:S(2)}) collective-permute-start(bf16[512,1024]{1,0:T(8,128)(2,1)} %pad_maximum_fusion.1.refs_6_), channel_id=1, source_target_pairs={{0,12},{1,13},{2,14},{3,15},{4,0},{5,1},{6,2},{7,3},{8,4},{9,5},{1... | collective-permute-start | bytes 3145736 | tf_op jit(solution)/shard_map/ppermute | solution.py:31
  32.2 22.9 %collective-permute-start.3 = (bf16[512,1024]{1,0:T(8,128)(2,1)}, bf16[512,1024]{1,0:T(8,128)(2,1)}, u32[]{:S(2)}, u32[]{:S(2)}) collective-permute-start(bf16[512,1024]{1,0:T(8,128)(2,1)} %pad_maximum_fusion.refs_4_), channel_id=1, source_target_pairs={{0,4},{1,5},{2,6},{3,7},{4,8},{5,9},{6,10},{7,11},{8,12},{9,13},{1... | collective-permute-start | bytes 3145736 | tf_op jit(solution)/shard_map/ppermute | solution.py:31
  52.0 24.2 %collective-permute-start.12 = (bf16[512,1024]{1,0:T(8,128)(2,1)}, bf16[512,1024]{1,0:T(8,128)(2,1)S(1)}, u32[]{:S(2)}, u32[]{:S(2)}) collective-permute-start(bf16[512,1024]{1,0:T(8,128)(2,1)} %collective-permute-done.11.refs_1_), channel_id=1, source_target_pairs={{0,1},{1,2},{2,3},{3,0},{4,5},{5,6},{6,7},{7,4},{8,9},{9,10},{10,1... | collective-permute-start | bytes 3145736 | tf_op jit(solution)/shard_map/ppermute | solution.py:31
  52.0 24.1 %collective-permute-start.15 = (bf16[512,1024]{1,0:T(8,128)(2,1)}, bf16[512,1024]{1,0:T(8,128)(2,1)S(1)}, u32[]{:S(2)}, u32[]{:S(2)}) collective-permute-start(bf16[512,1024]{1,0:T(8,128)(2,1)} %collective-permute-done.14.refs_3_), channel_id=1, source_target_pairs={{0,3},{1,0},{2,1},{3,2},{4,7},{5,4},{6,5},{7,6},{8,11},{9,8},{10,9... | collective-permute-start | bytes 3145736 | tf_op jit(solution)/shard_map/ppermute | solution.py:31
  54.6 21.5 %collective-permute-start.7 = (bf16[512,1024]{1,0:T(8,128)(2,1)}, bf16[512,1024]{1,0:T(8,128)(2,1)S(1)}, u32[]{:S(2)}, u32[]{:S(2)}) collective-permute-start(bf16[512,1024]{1,0:T(8,128)(2,1)} %collective-permute-done.6.refs_7_), channel_id=1, source_target_pairs={{0,12},{1,13},{2,14},{3,15},{4,0},{5,1},{6,2},{7,3},{8,4},{9,5},{1... | collective-permute-start | bytes 3145736 | tf_op jit(solution)/shard_map/ppermute | solution.py:31
  55.0 21.8 %collective-permute-start.4 = (bf16[512,1024]{1,0:T(8,128)(2,1)}, bf16[512,1024]{1,0:T(8,128)(2,1)S(1)}, u32[]{:S(2)}, u32[]{:S(2)}) collective-permute-start(bf16[512,1024]{1,0:T(8,128)(2,1)} %collective-permute-done.3.refs_5_), channel_id=1, source_target_pairs={{0,4},{1,5},{2,6},{3,7},{4,8},{5,9},{6,10},{7,11},{8,12},{9,13},{1... | collective-permute-start | bytes 3145736 | tf_op jit(solution)/shard_map/ppermute | solution.py:31
  57.6 22.2 %copy-start.4 = (bf16[128,1024]{1,0:T(8,128)(2,1)S(1)}, bf16[128,1024]{1,0:T(8,128)(2,1)}, u32[]{:S(2)}) copy-start(bf16[128,1024]{1,0:T(8,128)(2,1)} %right_ref.1) | copy-start | bytes 786436
  76.8 19.5 %collective-permute-start.16 = (bf16[512,1024]{1,0:T(8,128)(2,1)S(1)}, bf16[512,1024]{1,0:T(8,128)(2,1)S(1)}, u32[]{:S(2)}, u32[]{:S(2)}) collective-permute-start(bf16[512,1024]{1,0:T(8,128)(2,1)S(1)} %pad_maximum_fusion.2.refs_0_), channel_id=1, source_target_pairs={{0,3},{1,0},{2,1},{3,2},{4,7},{5,4},{6,5},{7,6},{8,11},{9,8},{10,9... | collective-permute-start | bytes 3145736 | tf_op jit(solution)/shard_map/ppermute | solution.py:31
  77.3 20.4 %collective-permute-start.17 = (bf16[512,1024]{1,0:T(8,128)(2,1)S(1)}, bf16[512,1024]{1,0:T(8,128)(2,1)S(1)}, u32[]{:S(2)}, u32[]{:S(2)}) collective-permute-start(bf16[512,1024]{1,0:T(8,128)(2,1)S(1)} %pad_maximum_fusion.3.refs_2_), channel_id=1, source_target_pairs={{0,1},{1,2},{2,3},{3,0},{4,5},{5,6},{6,7},{7,4},{8,9},{9,10},{10,1... | collective-permute-start | bytes 3145736 | tf_op jit(solution)/shard_map/ppermute | solution.py:31
  78.3 19.4 %collective-permute-start.18 = (bf16[512,1024]{1,0:T(8,128)(2,1)}, bf16[512,1024]{1,0:T(8,128)(2,1)S(1)}, u32[]{:S(2)}, u32[]{:S(2)}) collective-permute-start(bf16[512,1024]{1,0:T(8,128)(2,1)} %pad_maximum_fusion.refs_4_), channel_id=1, source_target_pairs={{0,12},{1,13},{2,14},{3,15},{4,0},{5,1},{6,2},{7,3},{8,4},{9,5},{1... | collective-permute-start | bytes 3145736 | tf_op jit(solution)/shard_map/ppermute | solution.py:31
  79.2 20.7 %collective-permute-start.19 = (bf16[512,1024]{1,0:T(8,128)(2,1)}, bf16[512,1024]{1,0:T(8,128)(2,1)S(1)}, u32[]{:S(2)}, u32[]{:S(2)}) collective-permute-start(bf16[512,1024]{1,0:T(8,128)(2,1)} %pad_maximum_fusion.1.refs_6_), channel_id=1, source_target_pairs={{0,4},{1,5},{2,6},{3,7},{4,8},{5,9},{6,10},{7,11},{8,12},{9,13},{1... | collective-permute-start | bytes 3145736 | tf_op jit(solution)/shard_map/ppermute | solution.py:31
  80.0 19.9 %copy-start = (bf16[4096,128]{1,0:T(8,128)(2,1)S(1)}, bf16[4096,128]{1,0:T(8,128)(2,1)}, u32[]{:S(2)}) copy-start(bf16[4096,128]{1,0:T(8,128)(2,1)} %fusion.refs_9_.refs_5_) | copy-start | bytes 3145732
  113.3 22.1 %all-to-all-start = ((f32[128,1,128]{2,1,0:T(1,128)}), f32[128,1,128]{2,1,0:T(1,128)S(1)}, u32[]{:S(2)}, u32[]{:S(2)}) async-start(f32[128,1,128]{2,1,0:T(1,128)} %broadcast_in_dim.2), calls=%async_computation | async-start | bytes 131072 | tf_op jit(solution)/shard_map/all_to_all | solution.py:280
  (5 other events, 19.0 us)

commit v5 on v4

--- a/solution.py
+++ b/solution.py
@@ -19,7 +19,7 @@
 
 COLS = 256
 LANES = 128
-VMEM_LIMIT = 48 * 1024 * 1024
+VMEM_LIMITS = (36 << 20, 26 << 20, 20 << 20)
 
 
 def shift(piece, dx, dy):
@@ -41,7 +41,9 @@
 def stage_kernel(terms, started, final, idx_ref, *refs):
     refs = list(refs)
     xs = [[refs.pop(0) for _ in block] for block in terms]
-    w_ref, left_ref = refs.pop(0), refs.pop(0)
+    w_ref = None if final else refs.pop(0)
+    w_refs = {t[0]: [refs.pop(0) for _ in range(SIDE)] for t in dict.fromkeys(terms)} if final else {}
+    left_ref = refs.pop(0)
     sum_ref, sum_proj_ref = (refs.pop(0), refs.pop(0)) if started else (None, None)
     right_ref, cot_ref = (refs.pop(0), refs.pop(0)) if final else (None, None)
     out_ref, proj_ref = refs
@@ -52,10 +54,13 @@
     def product(b, ref):
         total = None
         for x_ref, place in zip(xs[b], terms[b]):
-            parts = [
-                ref[pl.ds(pl.multiple_of(idx_ref[place + k] * width, width), width), :]
-                for k in range(SIDE)
-            ]
+            if ref is None:
+                parts = [part[...] for part in w_refs[place]]
+            else:
+                parts = [
+                    ref[pl.ds(pl.multiple_of(idx_ref[place + k] * width, width), width), :]
+                    for k in range(SIDE)
+                ]
             part = jnp.dot(
                 x_ref[...], jnp.concatenate(parts, axis=0), preferred_element_type=jnp.float32
             )
@@ -102,7 +107,7 @@
             out_ref[slot : slot + 1, :] += sums
 
 
-def stage(blocks, idx, weight, left_own, sums=None, score=None):
+def stage(blocks, idx, weight, left_own, limit, sums=None, score=None):
     terms = tuple(tuple(place for _, place in block) for block in blocks)
     rows, extent = blocks[0][0][0].shape
     total = rows * len(blocks)
@@ -112,11 +117,17 @@
     once = pl.Buffered(1)
     operands = [piece for block in blocks for piece, _ in block]
     in_specs = [pl.BlockSpec((rows, extent), whole, pipeline_mode=once)] * len(operands)
-    in_specs += [
-        pl.BlockSpec((depth, COLS), tile),
-        pl.BlockSpec((depth, LANES), whole, pipeline_mode=once),
-    ]
-    operands += [weight, left_own]
+    if score is None:
+        in_specs.append(pl.BlockSpec((depth, COLS), tile))
+        operands.append(weight)
+    else:
+        for (place,) in dict.fromkeys(terms):
+            for k in range(SIDE):
+                row = functools.partial(lambda at, n, idx: (idx[at], n), place + k)
+                in_specs.append(pl.BlockSpec((extent // SIDE, COLS), row))
+                operands.append(weight)
+    in_specs.append(pl.BlockSpec((depth, LANES), whole, pipeline_mode=once))
+    operands.append(left_own)
     block = pl.BlockSpec((total, COLS), tile)
     if sums is not None:
         in_specs += [block, pl.BlockSpec((total, LANES), whole, pipeline_mode=once)]
@@ -145,7 +156,7 @@
             scratch_shapes=scratch,
         ),
         out_shape=out_shape,
-        compiler_params=pltpu.CompilerParams(vmem_limit_bytes=VMEM_LIMIT),
+        compiler_params=pltpu.CompilerParams(vmem_limit_bytes=limit),
         cost_estimate=pl.CostEstimate(
             flops=flops, bytes_accessed=flops // 256, transcendentals=0
         ),
@@ -202,7 +213,7 @@
             jax.ShapeDtypeStruct((row_share, columns), jnp.float32),
             jax.ShapeDtypeStruct((1, owned), jnp.float32),
         ],
-        compiler_params=pltpu.CompilerParams(vmem_limit_bytes=VMEM_LIMIT),
+        compiler_params=pltpu.CompilerParams(vmem_limit_bytes=VMEM_LIMITS[2]),
     )(at, tables, seat, factor_left, factor_right)
 
 
@@ -262,13 +273,14 @@
         return out
 
     near = {o: send(blocks[o], o, 1) for o in both}
+    near, blocks = lax.optimization_barrier((near, blocks))
+    other = {o: send(blocks[o], o, -1) for o in both}
+    sums = stage(terms((blocks, (0, 0)), (near, (1, 2))), idx, weight, left_own, VMEM_LIMITS[0])
+    other, sums, near = lax.optimization_barrier((other, sums, near))
     far = {o: send(near[o], o, 1) for o in both}
-    sums = stage(terms((blocks, (0, 0)), (near, (1, 2))), idx, weight, left_own)
-    far, sums, blocks = lax.optimization_barrier((far, sums, blocks))
-    other = {o: send(blocks[o], o, -1) for o in both}
-    sums = stage(terms((far, (3, 3))), idx, weight, left_own, sums)
+    sums = stage(terms((other, (2, 1))), idx, weight, left_own, VMEM_LIMITS[1], sums)
     scores = stage(
-        terms((other, (2, 1))), idx, weight, left_own, sums, (right_own, cotangent)
+        terms((far, (3, 3))), idx, weight, left_own, VMEM_LIMITS[2], sums, (right_own, cotangent)
     )
     partial = -jnp.sum(scores, axis=1) / math.sqrt(TOK * FF)
     seated = seat[:, :owned].astype(jnp.float32)

time: 138 us -> 141 us (1.022)
  Pallas kernels: 47.4 us -> 41.3 us
  starting transfers between devices: 37.6 us -> 43.1 us
  waiting for transfers between devices: 43.2 us -> 47 us
    pallas_call x3, Pallas kernels: 44.8 us -> 38.7 us  [stage(): pl.pallas_call(functools.partial(stage_kernel, terms, sums is not None, s...]
    ppermute x20, waiting for transfers between devices: 33.7 us -> 37.5 us  [shift(): return lax.ppermute(piece, 'mp', perm)]
    all_to_all x1, starting transfers between devices: 12.6 us -> 15.3 us  [per_device(): tables = lax.all_to_all(copies, everywhere, 0, 0, tiled=True)]
    ppermute x20, starting transfers between devices: 25 us -> 27.7 us  [shift(): return lax.ppermute(piece, 'mp', perm)]
  transfers between devices with their start and end apart: 21 -> 21, of which waited for: 8 -> 9; matrix products, arithmetic and copies ran while one was open for 3% -> 3% of each run, Pallas kernels for 23% -> 20%
where the time goes in v5:
time: 141 us
  waiting for transfers between devices  47 us (33%)
  starting transfers between devices  43.1 us (31%)
  Pallas kernels  41.3 us (29%)
  local copies, waits for them, and re-layouts  4.68 us (3%)
  other arithmetic  2.88 us (2%)
    pallas_call x3, Pallas kernels, stage(): pl.pallas_call(functools.partial(stage_kernel, terms, sums is not None, s...  38.7 us
    ppermute x20, waiting for transfers between devices, shift(): return lax.ppermute(piece, 'mp', perm)  37.5 us
    ppermute x20, starting transfers between devices, shift(): return lax.ppermute(piece, 'mp', perm)  27.7 us
    all_to_all x1, starting transfers between devices, per_device(): tables = lax.all_to_all(copies, everywhere, 0, 0, tiled=True)  15.3 us
    all_to_all x1, waiting for transfers between devices, per_device(): tables = lax.all_to_all(copies, everywhere, 0, 0, tiled=True)  9.5 us
  transfers between devices with their start and end apart: 21, of which 9 were waited for; matrix products, arithmetic and copies ran while one was open for 3% of the time, Pallas kernels for 20%

profile of v5, /device:TPU:1, one launch (start us, length us, event | category | flops | bytes accessed | tf_op | source)
XLA Modules:
  0.0 140.6 jit_solution(1705879981357755724)
XLA Ops:
  0.6 1.4 fusion.9
  2.0 3.4 %collective-permute-start.7 = (bf16[1024,256]{1,0:T(8,128)(2,1)S(1)}, bf16[1024,256]{1,0:T(8,128)(2,1)S(1)}, u32[]{:S(2)}, u32[]{:S(2)}) collective-permute-start(bf16[1024,256]{1,0:T(8,128)(2,1)S(1)} %get-tuple-element.54), channel_id=1, source_target_pairs={{0,12},{1,13},{2,14},{3,15},{4,0},{5,1},{6,2},{7,3},{8,4},{9,5},{1... | collective-permute-start | bytes 1572872 | tf_op jit(solution)/shard_map/ppermute | solution.py:31
  5.4 2.7 %collective-permute-start.1 = (bf16[1024,256]{1,0:T(8,128)(2,1)S(1)}, bf16[1024,256]{1,0:T(8,128)(2,1)S(1)}, u32[]{:S(2)}, u32[]{:S(2)}) collective-permute-start(bf16[1024,256]{1,0:T(8,128)(2,1)S(1)} %get-tuple-element.55), channel_id=1, source_target_pairs={{0,3},{1,0},{2,1},{3,2},{4,7},{5,4},{6,5},{7,6},{8,11},{9,8},{10,9... | collective-permute-start | bytes 1572872 | tf_op jit(solution)/shard_map/ppermute | solution.py:31
  8.2 7.8 %collective-permute-done.7 = bf16[1024,256]{1,0:T(8,128)(2,1)S(1)} collective-permute-done((bf16[1024,256]{1,0:T(8,128)(2,1)S(1)}, bf16[1024,256]{1,0:T(8,128)(2,1)S(1)}, u32[]{:S(2)}, u32[]{:S(2)}) %collective-permute-start.7) | collective-permute-done | bytes 524320 | tf_op jit(solution)/shard_map/ppermute | solution.py:31
  16.0 3.5 %collective-permute-start.10 = (bf16[512,256]{1,0:T(8,128)(2,1)S(1)}, bf16[512,256]{1,0:T(8,128)(2,1)S(1)}, u32[]{:S(2)}, u32[]{:S(2)}) collective-permute-start(bf16[512,256]{1,0:T(8,128)(2,1)S(1)} %get-tuple-element.58), channel_id=1, source_target_pairs={{0,12},{1,13},{2,14},{3,15},{4,0},{5,1},{6,2},{7,3},{8,4},{9,5},{1... | collective-permute-start | bytes 786440 | tf_op jit(solution)/shard_map/ppermute | solution.py:31
  19.7 2.8 %collective-permute-start.4 = (bf16[512,256]{1,0:T(8,128)(2,1)S(1)}, bf16[512,256]{1,0:T(8,128)(2,1)S(1)}, u32[]{:S(2)}, u32[]{:S(2)}) collective-permute-start(bf16[512,256]{1,0:T(8,128)(2,1)S(1)} %get-tuple-element.62), channel_id=1, source_target_pairs={{0,3},{1,0},{2,1},{3,2},{4,7},{5,4},{6,5},{7,6},{8,11},{9,8},{10,9... | collective-permute-start | bytes 786440 | tf_op jit(solution)/shard_map/ppermute | solution.py:31
  23.7 2.8 %collective-permute-start.11 = (bf16[512,1024]{1,0:T(8,128)(2,1)S(1)}, bf16[512,1024]{1,0:T(8,128)(2,1)}, u32[]{:S(2)}, u32[]{:S(2)}) collective-permute-start(bf16[512,1024]{1,0:T(8,128)(2,1)S(1)} %pad_maximum_fusion.3.refs_2_), channel_id=1, source_target_pairs={{0,3},{1,0},{2,1},{3,2},{4,7},{5,4},{6,5},{7,6},{8,11},{9,8},{10,9... | collective-permute-start | bytes 3145736 | tf_op jit(solution)/shard_map/ppermute | solution.py:31
  26.9 1.4 collective-permute-start.9
  29.4 1.9 %collective-permute-start.5 = (bf16[512,1024]{1,0:T(8,128)(2,1)}, bf16[512,1024]{1,0:T(8,128)(2,1)}, u32[]{:S(2)}, u32[]{:S(2)}) collective-permute-start(bf16[512,1024]{1,0:T(8,128)(2,1)} %pad_maximum_fusion.1.refs_6_), channel_id=1, source_target_pairs={{0,12},{1,13},{2,14},{3,15},{4,0},{5,1},{6,2},{7,3},{8,4},{9,5},{1... | collective-permute-start | bytes 3145736 | tf_op jit(solution)/shard_map/ppermute | solution.py:31
  32.7 16.8 %collective-permute-done.11.refs_3_ = bf16[512,1024]{1,0:T(8,128)(2,1)} collective-permute-done((bf16[512,1024]{1,0:T(8,128)(2,1)S(1)}, bf16[512,1024]{1,0:T(8,128)(2,1)}, u32[]{:S(2)}, u32[]{:S(2)}) %collective-permute-start.11) | collective-permute-done | bytes 1048608 | tf_op jit(solution)/shard_map/ppermute | solution.py:31
  49.5 3.1 %collective-permute-done.9.refs_1_ = bf16[512,1024]{1,0:T(8,128)(2,1)} collective-permute-done((bf16[512,1024]{1,0:T(8,128)(2,1)S(1)}, bf16[512,1024]{1,0:T(8,128)(2,1)}, u32[]{:S(2)}, u32[]{:S(2)}) %collective-permute-start.9) | collective-permute-done | bytes 1048608 | tf_op jit(solution)/shard_map/ppermute | solution.py:31
  52.6 2.9 %collective-permute-done.3.refs_5_ = bf16[512,1024]{1,0:T(8,128)(2,1)} collective-permute-done((bf16[512,1024]{1,0:T(8,128)(2,1)}, bf16[512,1024]{1,0:T(8,128)(2,1)}, u32[]{:S(2)}, u32[]{:S(2)}) %collective-permute-start.3) | collective-permute-done | bytes 1048608 | tf_op jit(solution)/shard_map/ppermute | solution.py:31
  55.5 1.5 %collective-permute-start.13 = (bf16[512,1024]{1,0:T(8,128)(2,1)}, bf16[512,1024]{1,0:T(8,128)(2,1)S(1)}, u32[]{:S(2)}, u32[]{:S(2)}) collective-permute-start(bf16[512,1024]{1,0:T(8,128)(2,1)} %pad_maximum_fusion.1.refs_6_), channel_id=1, source_target_pairs={{0,4},{1,5},{2,6},{3,7},{4,8},{5,9},{6,10},{7,11},{8,12},{9,13},{1... | collective-permute-start | bytes 3145736 | tf_op jit(solution)/shard_map/ppermute | solution.py:31
  57.0 2.3 %collective-permute-start.14 = (bf16[512,1024]{1,0:T(8,128)(2,1)S(1)}, bf16[512,1024]{1,0:T(8,128)(2,1)S(1)}, u32[]{:S(2)}, u32[]{:S(2)}) collective-permute-start(bf16[512,1024]{1,0:T(8,128)(2,1)S(1)} %pad_maximum_fusion.2.refs_0_), channel_id=1, source_target_pairs={{0,3},{1,0},{2,1},{3,2},{4,7},{5,4},{6,5},{7,6},{8,11},{9,8},{10,9... | collective-permute-start | bytes 3145736 | tf_op jit(solution)/shard_map/ppermute | solution.py:31
  59.9 17.7 %shard_map.95 = (f32[2048,1024]{1,0:T(8,128)}, f32[2048,128]{1,0:T(8,128)S(1)}) custom-call(s32[32]{0:T(128)S(1)} %pad_add_fusion.idx_ref, bf16[512,1024]{1,0:T(8,128)(2,1)S(1)} %pad_maximum_fusion.2.refs_0_, bf16[512,1024]{1,0:T(8,128)(2,1)} %collective-permute-done.9.refs_1_, bf16[512,1024]{1,0:T(8,128)(2,1)S(1)} %pad_maximum_fusion.3.refs_2_, ...), custom_call_target="tpu_custom_call" | custom-call | flops 8589934592 | bytes 33554432 | tf_op jit(solution)/shard_map/pallas_call | solution.py:149
  78.6 1.4 %collective-permute-done.15.refs_1_ = bf16[512,1024]{1,0:T(8,128)(2,1)S(1)} collective-permute-done((bf16[512,1024]{1,0:T(8,128)(2,1)S(1)}, bf16[512,1024]{1,0:T(8,128)(2,1)S(1)}, u32[]{:S(2)}, u32[]{:S(2)}) %collective-permute-start.15) | collective-permute-done | bytes 1048608 | tf_op jit(solution)/shard_map/ppermute | solution.py:31
  80.1 2.7 %collective-permute-start.17 = (bf16[512,1024]{1,0:T(8,128)(2,1)}, bf16[512,1024]{1,0:T(8,128)(2,1)S(1)}, u32[]{:S(2)}, u32[]{:S(2)}) collective-permute-start(bf16[512,1024]{1,0:T(8,128)(2,1)} %collective-permute-done.11.refs_3_), channel_id=1, source_target_pairs={{0,3},{1,0},{2,1},{3,2},{4,7},{5,4},{6,5},{7,6},{8,11},{9,8},{10,9... | collective-permute-start | bytes 3145736 | tf_op jit(solution)/shard_map/ppermute | solution.py:31
  83.0 2.4 %collective-permute-start.19 = (bf16[512,1024]{1,0:T(8,128)(2,1)}, bf16[512,1024]{1,0:T(8,128)(2,1)S(1)}, u32[]{:S(2)}, u32[]{:S(2)}) collective-permute-start(bf16[512,1024]{1,0:T(8,128)(2,1)} %collective-permute-done.5.refs_7_), channel_id=1, source_target_pairs={{0,12},{1,13},{2,14},{3,15},{4,0},{5,1},{6,2},{7,3},{8,4},{9,5},{1... | collective-permute-start | bytes 3145736 | tf_op jit(solution)/shard_map/ppermute | solution.py:31
  86.9 10.5 %shard_map.96 = (f32[2048,1024]{1,0:T(8,128)S(1)}, f32[2048,128]{1,0:T(8,128)S(1)}) custom-call(s32[32]{0:T(128)S(1)} %pad_add_fusion.idx_ref, bf16[512,1024]{1,0:T(8,128)(2,1)S(1)} %collective-permute-done.14.refs_0_, bf16[512,1024]{1,0:T(8,128)(2,1)S(1)} %collective-permute-done.15.refs_1_, bf16[512,1024]{1,0:T(8,128)(2,1)S(1)} %collective-permute-done.12.refs_2_, ...), custom_call_target="tpu_custom_call" | custom-call | flops 4294967296 | bytes 16777216 | tf_op jit(solution)/shard_map/pallas_call | solution.py:149
  97.5 4.2 %collective-permute-done.16.refs_0_ = bf16[512,1024]{1,0:T(8,128)(2,1)S(1)} collective-permute-done((bf16[512,1024]{1,0:T(8,128)(2,1)}, bf16[512,1024]{1,0:T(8,128)(2,1)S(1)}, u32[]{:S(2)}, u32[]{:S(2)}) %collective-permute-start.16) | collective-permute-done | bytes 1048608 | tf_op jit(solution)/shard_map/ppermute | solution.py:31
  101.7 10.4 %shard_map.97 = f32[16,128]{1,0:T(8,128)S(1)} custom-call(s32[32]{0:T(128)S(1)} %pad_add_fusion.idx_ref, bf16[512,1024]{1,0:T(8,128)(2,1)S(1)} %collective-permute-done.16.refs_0_, bf16[512,1024]{1,0:T(8,128)(2,1)S(1)} %collective-permute-done.17.refs_1_, bf16[512,1024]{1,0:T(8,128)(2,1)S(1)} %collective-permute-done.18.refs_2_, ...), custom_call_target="tpu_custom_call" | custom-call | flops 4294967296 | bytes 16777216 | tf_op jit(solution)/shard_map/pallas_call | solution.py:149
  113.1 15.3 %all-to-all-start = ((f32[128,1,128]{2,1,0:T(1,128)}), f32[128,1,128]{2,1,0:T(1,128)S(1)}, u32[]{:S(2)}, u32[]{:S(2)}) async-start(f32[128,1,128]{2,1,0:T(1,128)} %broadcast_in_dim.2), calls=%async_computation | async-start | bytes 131072 | tf_op jit(solution)/shard_map/all_to_all | solution.py:292
  128.4 9.5 %all-to-all-done = f32[128,1,128]{2,1,0:T(1,128)S(1)} async-done(((f32[128,1,128]{2,1,0:T(1,128)}), f32[128,1,128]{2,1,0:T(1,128)S(1)}, u32[]{:S(2)}, u32[]{:S(2)}) %all-to-all-start) | async-done | bytes 65568 | tf_op jit(solution)/shard_map/all_to_all | solution.py:292
  137.9 2.6 %shard_map.98 = (f32[512,1024]{1,0:T(8,128)}, f32[1,16]{1,0:T(1,128)}) custom-call(s32[1]{0:T(128)} %bitcast.at_ref, f32[128,128]{1,0:T(8,128)S(1)} %bitcast.9, f32[128,128]{1,0:T(8,128)S(1)} %get-tuple-element.66.seat_ref, bf16[128,4096]{1,0:T(8,128)(2,1)S(1)} %copy-done.1, bf16[128,1024]{1,0:T(8,128)(2,1)S(1)} %copy-done.4), custom_call_target="tpu_custom_call" | custom-call | tf_op jit(solution)/shard_map/pallas_call | solution.py:196
  (66 shorter events, 8.7 us)
Async XLA Ops:
  2.0 14.0 %collective-permute-start.7 = (bf16[1024,256]{1,0:T(8,128)(2,1)S(1)}, bf16[1024,256]{1,0:T(8,128)(2,1)S(1)}, u32[]{:S(2)}, u32[]{:S(2)}) collective-permute-start(bf16[1024,256]{1,0:T(8,128)(2,1)S(1)} %get-tuple-element.54), channel_id=1, source_target_pairs={{0,12},{1,13},{2,14},{3,15},{4,0},{5,1},{6,2},{7,3},{8,4},{9,5},{1... | collective-permute-start | bytes 1572872 | tf_op jit(solution)/shard_map/ppermute | solution.py:31
  5.4 14.1 %collective-permute-start.6 = (bf16[1024,256]{1,0:T(8,128)(2,1)S(1)}, bf16[1024,256]{1,0:T(8,128)(2,1)S(1)}, u32[]{:S(2)}, u32[]{:S(2)}) collective-permute-start(bf16[1024,256]{1,0:T(8,128)(2,1)S(1)} %get-tuple-element.54), channel_id=1, source_target_pairs={{0,4},{1,5},{2,6},{3,7},{4,8},{5,9},{6,10},{7,11},{8,12},{9,13},{1... | collective-permute-start | bytes 1572872 | tf_op jit(solution)/shard_map/ppermute | solution.py:31
  5.4 14.2 %collective-permute-start.1 = (bf16[1024,256]{1,0:T(8,128)(2,1)S(1)}, bf16[1024,256]{1,0:T(8,128)(2,1)S(1)}, u32[]{:S(2)}, u32[]{:S(2)}) collective-permute-start(bf16[1024,256]{1,0:T(8,128)(2,1)S(1)} %get-tuple-element.55), channel_id=1, source_target_pairs={{0,3},{1,0},{2,1},{3,2},{4,7},{5,4},{6,5},{7,6},{8,11},{9,8},{10,9... | collective-permute-start | bytes 1572872 | tf_op jit(solution)/shard_map/ppermute | solution.py:31
  8.1 14.4 %collective-permute-start = (bf16[1024,256]{1,0:T(8,128)(2,1)S(1)}, bf16[1024,256]{1,0:T(8,128)(2,1)S(1)}, u32[]{:S(2)}, u32[]{:S(2)}) collective-permute-start(bf16[1024,256]{1,0:T(8,128)(2,1)S(1)} %get-tuple-element.55), channel_id=1, source_target_pairs={{0,1},{1,2},{2,3},{3,0},{4,5},{5,6},{6,7},{7,4},{8,9},{9,10},{10,1... | collective-permute-start | bytes 1572872 | tf_op jit(solution)/shard_map/ppermute | solution.py:31
  16.0 7.5 %collective-permute-start.10 = (bf16[512,256]{1,0:T(8,128)(2,1)S(1)}, bf16[512,256]{1,0:T(8,128)(2,1)S(1)}, u32[]{:S(2)}, u32[]{:S(2)}) collective-permute-start(bf16[512,256]{1,0:T(8,128)(2,1)S(1)} %get-tuple-element.58), channel_id=1, source_target_pairs={{0,12},{1,13},{2,14},{3,15},{4,0},{5,1},{6,2},{7,3},{8,4},{9,5},{1... | collective-permute-start | bytes 786440 | tf_op jit(solution)/shard_map/ppermute | solution.py:31
  19.5 7.3 %collective-permute-start.8 = (bf16[512,256]{1,0:T(8,128)(2,1)S(1)}, bf16[512,256]{1,0:T(8,128)(2,1)S(1)}, u32[]{:S(2)}, u32[]{:S(2)}) collective-permute-start(bf16[512,256]{1,0:T(8,128)(2,1)S(1)} %get-tuple-element.57), channel_id=1, source_target_pairs={{0,4},{1,5},{2,6},{3,7},{4,8},{5,9},{6,10},{7,11},{8,12},{9,13},{1... | collective-permute-start | bytes 786440 | tf_op jit(solution)/shard_map/ppermute | solution.py:31
  19.7 8.6 %collective-permute-start.4 = (bf16[512,256]{1,0:T(8,128)(2,1)S(1)}, bf16[512,256]{1,0:T(8,128)(2,1)S(1)}, u32[]{:S(2)}, u32[]{:S(2)}) collective-permute-start(bf16[512,256]{1,0:T(8,128)(2,1)S(1)} %get-tuple-element.62), channel_id=1, source_target_pairs={{0,3},{1,0},{2,1},{3,2},{4,7},{5,4},{6,5},{7,6},{8,11},{9,8},{10,9... | collective-permute-start | bytes 786440 | tf_op jit(solution)/shard_map/ppermute | solution.py:31
  22.5 8.8 %collective-permute-start.2 = (bf16[512,256]{1,0:T(8,128)(2,1)S(1)}, bf16[512,256]{1,0:T(8,128)(2,1)S(1)}, u32[]{:S(2)}, u32[]{:S(2)}) collective-permute-start(bf16[512,256]{1,0:T(8,128)(2,1)S(1)} %get-tuple-element.61), channel_id=1, source_target_pairs={{0,1},{1,2},{2,3},{3,0},{4,5},{5,6},{6,7},{7,4},{8,9},{9,10},{10,1... | collective-permute-start | bytes 786440 | tf_op jit(solution)/shard_map/ppermute | solution.py:31
  23.7 25.8 %collective-permute-start.11 = (bf16[512,1024]{1,0:T(8,128)(2,1)S(1)}, bf16[512,1024]{1,0:T(8,128)(2,1)}, u32[]{:S(2)}, u32[]{:S(2)}) collective-permute-start(bf16[512,1024]{1,0:T(8,128)(2,1)S(1)} %pad_maximum_fusion.3.refs_2_), channel_id=1, source_target_pairs={{0,3},{1,0},{2,1},{3,2},{4,7},{5,4},{6,5},{7,6},{8,11},{9,8},{10,9... | collective-permute-start | bytes 3145736 | tf_op jit(solution)/shard_map/ppermute | solution.py:31
  26.9 25.7 %collective-permute-start.9 = (bf16[512,1024]{1,0:T(8,128)(2,1)S(1)}, bf16[512,1024]{1,0:T(8,128)(2,1)}, u32[]{:S(2)}, u32[]{:S(2)}) collective-permute-start(bf16[512,1024]{1,0:T(8,128)(2,1)S(1)} %pad_maximum_fusion.2.refs_0_), channel_id=1, source_target_pairs={{0,1},{1,2},{2,3},{3,0},{4,5},{5,6},{6,7},{7,4},{8,9},{9,10},{10,1... | collective-permute-start | bytes 3145736 | tf_op jit(solution)/shard_map/ppermute | solution.py:31
  28.3 31.0 %copy-start.1 = (bf16[128,4096]{1,0:T(8,128)(2,1)S(1)}, bf16[128,4096]{1,0:T(8,128)(2,1)}, u32[]{:S(2)}) copy-start(bf16[128,4096]{1,0:T(8,128)(2,1)} %left_ref.1) | copy-start | bytes 3145732
  29.4 23.2 %collective-permute-start.5 = (bf16[512,1024]{1,0:T(8,128)(2,1)}, bf16[512,1024]{1,0:T(8,128)(2,1)}, u32[]{:S(2)}, u32[]{:S(2)}) collective-permute-start(bf16[512,1024]{1,0:T(8,128)(2,1)} %pad_maximum_fusion.1.refs_6_), channel_id=1, source_target_pairs={{0,12},{1,13},{2,14},{3,15},{4,0},{5,1},{6,2},{7,3},{8,4},{9,5},{1... | collective-permute-start | bytes 3145736 | tf_op jit(solution)/shard_map/ppermute | solution.py:31
  32.4 23.2 %collective-permute-start.3 = (bf16[512,1024]{1,0:T(8,128)(2,1)}, bf16[512,1024]{1,0:T(8,128)(2,1)}, u32[]{:S(2)}, u32[]{:S(2)}) collective-permute-start(bf16[512,1024]{1,0:T(8,128)(2,1)} %pad_maximum_fusion.refs_4_), channel_id=1, source_target_pairs={{0,4},{1,5},{2,6},{3,7},{4,8},{5,9},{6,10},{7,11},{8,12},{9,13},{1... | collective-permute-start | bytes 3145736 | tf_op jit(solution)/shard_map/ppermute | solution.py:31
  55.5 23.1 %collective-permute-start.12 = (bf16[512,1024]{1,0:T(8,128)(2,1)}, bf16[512,1024]{1,0:T(8,128)(2,1)S(1)}, u32[]{:S(2)}, u32[]{:S(2)}) collective-permute-start(bf16[512,1024]{1,0:T(8,128)(2,1)} %pad_maximum_fusion.refs_4_), channel_id=1, source_target_pairs={{0,12},{1,13},{2,14},{3,15},{4,0},{5,1},{6,2},{7,3},{8,4},{9,5},{1... | collective-permute-start | bytes 3145736 | tf_op jit(solution)/shard_map/ppermute | solution.py:31
  55.5 23.1 %collective-permute-start.13 = (bf16[512,1024]{1,0:T(8,128)(2,1)}, bf16[512,1024]{1,0:T(8,128)(2,1)S(1)}, u32[]{:S(2)}, u32[]{:S(2)}) collective-permute-start(bf16[512,1024]{1,0:T(8,128)(2,1)} %pad_maximum_fusion.1.refs_6_), channel_id=1, source_target_pairs={{0,4},{1,5},{2,6},{3,7},{4,8},{5,9},{6,10},{7,11},{8,12},{9,13},{1... | collective-permute-start | bytes 3145736 | tf_op jit(solution)/shard_map/ppermute | solution.py:31
  57.0 21.6 %collective-permute-start.14 = (bf16[512,1024]{1,0:T(8,128)(2,1)S(1)}, bf16[512,1024]{1,0:T(8,128)(2,1)S(1)}, u32[]{:S(2)}, u32[]{:S(2)}) collective-permute-start(bf16[512,1024]{1,0:T(8,128)(2,1)S(1)} %pad_maximum_fusion.2.refs_0_), channel_id=1, source_target_pairs={{0,3},{1,0},{2,1},{3,2},{4,7},{5,4},{6,5},{7,6},{8,11},{9,8},{10,9... | collective-permute-start | bytes 3145736 | tf_op jit(solution)/shard_map/ppermute | solution.py:31
  59.3 20.8 %collective-permute-start.15 = (bf16[512,1024]{1,0:T(8,128)(2,1)S(1)}, bf16[512,1024]{1,0:T(8,128)(2,1)S(1)}, u32[]{:S(2)}, u32[]{:S(2)}) collective-permute-start(bf16[512,1024]{1,0:T(8,128)(2,1)S(1)} %pad_maximum_fusion.3.refs_2_), channel_id=1, source_target_pairs={{0,1},{1,2},{2,3},{3,0},{4,5},{5,6},{6,7},{7,4},{8,9},{9,10},{10,1... | collective-permute-start | bytes 3145736 | tf_op jit(solution)/shard_map/ppermute | solution.py:31
  59.3 26.4 %slice-start = ((s8[8388608]{0:T(1024)(128)(4,1)}), s8[4194304]{0:T(1024)(128)(4,1)S(1)}, s32[]{:S(2)}) async-start(s8[8388608]{0:T(1024)(128)(4,1)} %bitcast.7), calls=%async_computation.1 | async-start | bytes 8388608
  59.9 25.8 %slice-start.1 = ((s8[8388608]{0:T(1024)(128)(4,1)}), s8[4194304]{0:T(1024)(128)(4,1)S(1)}, s32[]{:S(2)}) async-start(s8[8388608]{0:T(1024)(128)(4,1)} %bitcast.7), calls=%async_computation.2 | async-start | bytes 8388608
  80.1 21.6 %collective-permute-start.16 = (bf16[512,1024]{1,0:T(8,128)(2,1)}, bf16[512,1024]{1,0:T(8,128)(2,1)S(1)}, u32[]{:S(2)}, u32[]{:S(2)}) collective-permute-start(bf16[512,1024]{1,0:T(8,128)(2,1)} %collective-permute-done.9.refs_1_), channel_id=1, source_target_pairs={{0,1},{1,2},{2,3},{3,0},{4,5},{5,6},{6,7},{7,4},{8,9},{9,10},{10,1... | collective-permute-start | bytes 3145736 | tf_op jit(solution)/shard_map/ppermute | solution.py:31
  80.1 21.6 %collective-permute-start.17 = (bf16[512,1024]{1,0:T(8,128)(2,1)}, bf16[512,1024]{1,0:T(8,128)(2,1)S(1)}, u32[]{:S(2)}, u32[]{:S(2)}) collective-permute-start(bf16[512,1024]{1,0:T(8,128)(2,1)} %collective-permute-done.11.refs_3_), channel_id=1, source_target_pairs={{0,3},{1,0},{2,1},{3,2},{4,7},{5,4},{6,5},{7,6},{8,11},{9,8},{10,9... | collective-permute-start | bytes 3145736 | tf_op jit(solution)/shard_map/ppermute | solution.py:31
  82.8 18.9 %collective-permute-start.18 = (bf16[512,1024]{1,0:T(8,128)(2,1)}, bf16[512,1024]{1,0:T(8,128)(2,1)S(1)}, u32[]{:S(2)}, u32[]{:S(2)}) collective-permute-start(bf16[512,1024]{1,0:T(8,128)(2,1)} %collective-permute-done.3.refs_5_), channel_id=1, source_target_pairs={{0,4},{1,5},{2,6},{3,7},{4,8},{5,9},{6,10},{7,11},{8,12},{9,13},{1... | collective-permute-start | bytes 3145736 | tf_op jit(solution)/shard_map/ppermute | solution.py:31
  83.0 18.7 %collective-permute-start.19 = (bf16[512,1024]{1,0:T(8,128)(2,1)}, bf16[512,1024]{1,0:T(8,128)(2,1)S(1)}, u32[]{:S(2)}, u32[]{:S(2)}) collective-permute-start(bf16[512,1024]{1,0:T(8,128)(2,1)} %collective-permute-done.5.refs_7_), channel_id=1, source_target_pairs={{0,12},{1,13},{2,14},{3,15},{4,0},{5,1},{6,2},{7,3},{8,4},{9,5},{1... | collective-permute-start | bytes 3145736 | tf_op jit(solution)/shard_map/ppermute | solution.py:31
  113.1 24.8 %all-to-all-start = ((f32[128,1,128]{2,1,0:T(1,128)}), f32[128,1,128]{2,1,0:T(1,128)S(1)}, u32[]{:S(2)}, u32[]{:S(2)}) async-start(f32[128,1,128]{2,1,0:T(1,128)} %broadcast_in_dim.2), calls=%async_computation | async-start | bytes 131072 | tf_op jit(solution)/shard_map/all_to_all | solution.py:292
  (7 other events, 58.6 us)

commit v6 on v5

--- a/solution.py
+++ b/solution.py
@@ -19,7 +19,8 @@
 
 COLS = 256
 LANES = 128
-VMEM_LIMITS = (36 << 20, 26 << 20, 20 << 20)
+FEW = 2
+VMEM_LIMITS = (26 << 20, 20 << 20, 20 << 20, 20 << 20)
 
 
 def shift(piece, dx, dy):
@@ -38,14 +39,16 @@
     return back, ahead, step(back[:half], 1), step(ahead[half:], -1)
 
 
-def stage_kernel(terms, started, final, idx_ref, *refs):
+def stage_kernel(terms, slots, started, final, idx_ref, *refs):
     refs = list(refs)
     xs = [[refs.pop(0) for _ in block] for block in terms]
-    w_ref = None if final else refs.pop(0)
-    w_refs = {t[0]: [refs.pop(0) for _ in range(SIDE)] for t in dict.fromkeys(terms)} if final else {}
+    places = dict.fromkeys(place for block in terms for place in block)
+    w_refs = {p: [refs.pop(0) for _ in range(SIDE)] for p in places} if len(places) <= FEW else {}
+    w_ref = None if w_refs else refs.pop(0)
     left_ref = refs.pop(0)
     sum_ref, sum_proj_ref = (refs.pop(0), refs.pop(0)) if started else (None, None)
-    right_ref, cot_ref = (refs.pop(0), refs.pop(0)) if final else (None, None)
+    right_ref = refs.pop(0) if final else None
+    cot_refs = [refs.pop(0) for _ in terms] if final else None
     out_ref, proj_ref = refs
     rows, extent = xs[0][0].shape
     width = extent // SIDE
@@ -77,9 +80,9 @@
                 proj_ref[b * rows : (b + 1) * rows, :] = total
                 continue
             for m in range(members):
-                slot = b * members + m
+                slot, local = slots[b] + m, b * members + m
                 one = total[m * TOK : (m + 1) * TOK, slot : slot + 1]
-                proj_ref[slot * TOK : (slot + 1) * TOK, :] = jnp.broadcast_to(
+                proj_ref[local * TOK : (local + 1) * TOK, :] = jnp.broadcast_to(
                     one * (perturb_scale / math.sqrt(D)), (TOK, LANES)
                 )
         if final:
@@ -93,21 +96,20 @@
             out_ref[b * rows : (b + 1) * rows, :] = base
             continue
         for m in range(members):
-            slot = b * members + m
+            slot, local = slots[b] + m, b * members + m
             token = slice(m * TOK, (m + 1) * TOK)
-            there = slice(slot * TOK, (slot + 1) * TOK)
-            proj = proj_ref[there, :]
+            proj = proj_ref[local * TOK : (local + 1) * TOK, :]
             right = right_ref[slot : slot + 1, :]
             sums = jnp.zeros((1, LANES), jnp.float32)
             for g in range(COLS // LANES):
                 cols = slice(g * LANES, (g + 1) * LANES)
                 act = jnp.maximum(base[token, cols] + proj * right[:, cols], 0.0)
-                term = cot_ref[there, cols].astype(jnp.float32) * (act * act)
+                term = cot_refs[b][token, cols].astype(jnp.float32) * (act * act)
                 sums += jnp.sum(term, axis=0, keepdims=True)
             out_ref[slot : slot + 1, :] += sums
 
 
-def stage(blocks, idx, weight, left_own, limit, sums=None, score=None):
+def stage(blocks, idx, weight, left_own, limit, sums=None, score=None, slots=None):
     terms = tuple(tuple(place for _, place in block) for block in blocks)
     rows, extent = blocks[0][0][0].shape
     total = rows * len(blocks)
@@ -117,11 +119,12 @@
     once = pl.Buffered(1)
     operands = [piece for block in blocks for piece, _ in block]
     in_specs = [pl.BlockSpec((rows, extent), whole, pipeline_mode=once)] * len(operands)
-    if score is None:
+    places = dict.fromkeys(place for block in terms for place in block)
+    if len(places) > FEW:
         in_specs.append(pl.BlockSpec((depth, COLS), tile))
         operands.append(weight)
     else:
-        for (place,) in dict.fromkeys(terms):
+        for place in places:
             for k in range(SIDE):
                 row = functools.partial(lambda at, n, idx: (idx[at], n), place + k)
                 in_specs.append(pl.BlockSpec((extent // SIDE, COLS), row))
@@ -139,15 +142,21 @@
             jax.ShapeDtypeStruct((total, LANES), jnp.float32),
         ]
     else:
-        members = total // TOK
-        in_specs += [pl.BlockSpec((members, COLS), tile), block]
-        operands += list(score)
+        right_own, cot = score
+        members = right_own.shape[0]
+        in_specs.append(pl.BlockSpec((members, COLS), tile))
+        operands.append(right_own)
+        for slot in slots:
+            in_specs.append(
+                pl.BlockSpec((rows, COLS), functools.partial(lambda at, n, idx: (at, n), slot * TOK // rows))
+            )
+            operands.append(cot)
         out_specs = pl.BlockSpec((members, LANES), whole)
         out_shape = jax.ShapeDtypeStruct((members, LANES), jnp.float32)
         scratch = [pltpu.VMEM((total, LANES), jnp.float32)]
     flops = 2 * sum(len(t) for t in terms) * rows * extent * columns
     return pl.pallas_call(
-        functools.partial(stage_kernel, terms, sums is not None, score is not None),
+        functools.partial(stage_kernel, terms, slots, sums is not None, score is not None),
         grid_spec=pltpu.PrefetchScalarGridSpec(
             num_scalar_prefetch=1,
             grid=(columns // COLS,),
@@ -256,32 +265,44 @@
     )
 
     both = (True, False)
-    ways = (1, -1)
     idx = jnp.concatenate([sources(o) for o in both])
-
-    def send(arrays, o, sense):
+    tie = lax.optimization_barrier
+
+    def send(piece, o, way):
+        return shift(piece, 0, way) if o else shift(piece, way, 0)
+
+    def terms(h, *given):
         return [
-            shift(a, 0, sense * way) if o else shift(a, sense * way, 0)
-            for a, way in zip(arrays, ways)
+            [(arrays[o], base + SIDE * group) for arrays, group in given]
+            for base, o in ((0, True), (SIDE * SIDE, False))
         ]
 
-    def terms(*given):
-        out = []
-        for base, o in ((0, True), (SIDE * SIDE, False)):
-            for h in range(2):
-                out.append([(arrays[o][h], base + SIDE * groups[h]) for arrays, groups in given])
-        return out
-
-    near = {o: send(blocks[o], o, 1) for o in both}
-    near, blocks = lax.optimization_barrier((near, blocks))
-    other = {o: send(blocks[o], o, -1) for o in both}
-    sums = stage(terms((blocks, (0, 0)), (near, (1, 2))), idx, weight, left_own, VMEM_LIMITS[0])
-    other, sums, near = lax.optimization_barrier((other, sums, near))
-    far = {o: send(near[o], o, 1) for o in both}
-    sums = stage(terms((other, (2, 1))), idx, weight, left_own, VMEM_LIMITS[1], sums)
-    scores = stage(
-        terms((far, (3, 3))), idx, weight, left_own, VMEM_LIMITS[2], sums, (right_own, cotangent)
-    )
+    per = quarter // TOK
+    slots = [(h * per, (2 + h) * per) for h in range(2)]
+    work = (idx, weight, left_own)
+    own = [{o: blocks[o][h] for o in both} for h in range(2)]
+
+    back0 = {o: send(own[0][o], o, 1) for o in both}
+    ahead0 = {o: send(own[0][o], o, -1) for o in both}
+    far0 = {o: send(back0[o], o, 1) for o in both}
+    ahead1 = {}
+    for o in both:
+        ahead0[o], piece = tie((ahead0[o], own[1][o]))
+        ahead1[o] = send(piece, o, -1)
+    sums0 = stage(terms(0, (own[0], 0), (back0, 1), (ahead0, 2)), *work, VMEM_LIMITS[0])
+    far1, back1 = {}, {}
+    for o in both:
+        ahead1[o], _ = tie((ahead1[o], sums0))
+        far1[o] = send(ahead1[o], o, -1)
+        far0[o], piece, _ = tie((far0[o], own[1][o], sums0))
+        back1[o] = send(piece, o, 1)
+    score = (right_own, cotangent)
+    scores0 = stage(terms(0, (far0, 3)), *work, VMEM_LIMITS[1], sums0, score, slots[0])
+    sums1 = stage(terms(1, (own[1], 0), (ahead1, 2)), *work, VMEM_LIMITS[2])
+    scores1 = stage(
+        terms(1, (back1, 1), (far1, 3)), *work, VMEM_LIMITS[3], sums1, score, slots[1]
+    )
+    scores = scores0 + scores1
     partial = -jnp.sum(scores, axis=1) / math.sqrt(TOK * FF)
     seated = seat[:, :owned].astype(jnp.float32)
     table = jnp.sum(seated * partial[None, :], 1)

time: 141 us -> 150 us (1.064)
  local copies, waits for them, and re-layouts: 4.68 us -> 12.7 us
  starting transfers between devices: 43.1 us -> 37.5 us
  waiting for transfers between devices: 47 us -> 50.9 us
  other arithmetic: 2.88 us -> 5.23 us
    unnamed x20 -> x28, local copies, waits for them, and re-layouts: 2.27 us -> 7.94 us
    ppermute x20, starting transfers between devices: 27.7 us -> 23.8 us  [shift(): return lax.ppermute(piece, 'mp', perm)]
    ppermute x20, waiting for transfers between devices: 37.5 us -> 41.4 us  [shift(): return lax.ppermute(piece, 'mp', perm)]
    concatenate x4, other arithmetic: 2.47 us -> 4.82 us  [per_device(): jnp.concatenate([pieces[o][s], back[s], ahead[s], far], axis=1)]
    all_to_all x1, starting transfers between devices: 15.3 us -> 13.7 us  [per_device(): tables = lax.all_to_all(copies, everywhere, 0, 0, tiled=True)]
    pallas_call x3 -> x4, Pallas kernels: 38.7 us -> 39.3 us  [stage(): pl.pallas_call(functools.partial(stage_kernel, terms, slots, sums is not...]
  transfers between devices with their start and end apart: 21 -> 21, of which waited for: 9 -> 8; matrix products, arithmetic and copies ran while one was open for 3% -> 6% of each run, Pallas kernels for 20% -> 20%
where the time goes in v6:
time: 150 us
  waiting for transfers between devices  50.9 us (34%)
  Pallas kernels  41.9 us (28%)
  starting transfers between devices  37.5 us (25%)
  local copies, waits for them, and re-layouts  12.7 us (8%)
  other arithmetic  5.23 us (3%)
    ppermute x20, waiting for transfers between devices, shift(): return lax.ppermute(piece, 'mp', perm)  41.4 us
    pallas_call x4, Pallas kernels, stage(): pl.pallas_call(functools.partial(stage_kernel, terms, slots, sums is not...  39.3 us
    ppermute x20, starting transfers between devices, shift(): return lax.ppermute(piece, 'mp', perm)  23.8 us
    all_to_all x1, starting transfers between devices, per_device(): tables = lax.all_to_all(copies, everywhere, 0, 0, tiled=True)  13.7 us
    all_to_all x1, waiting for transfers between devices, per_device(): tables = lax.all_to_all(copies, everywhere, 0, 0, tiled=True)  9.5 us
    unnamed x28, local copies, waits for them, and re-layouts  7.94 us
    concatenate x4, other arithmetic, per_device(): jnp.concatenate([pieces[o][s], back[s], ahead[s], far], axis=1)  4.82 us
  transfers between devices with their start and end apart: 21, of which 8 were waited for; matrix products, arithmetic and copies ran while one was open for 6% of the time, Pallas kernels for 20%

profile of v6, /device:TPU:1, one launch (start us, length us, event | category | flops | bytes accessed | tf_op | source)
XLA Modules:
  0.0 149.8 jit_solution(15193472142650645931)
XLA Ops:
  2.0 2.1 %collective-permute-start = (bf16[1024,256]{1,0:T(8,128)(2,1)S(1)}, bf16[1024,256]{1,0:T(8,128)(2,1)S(1)}, u32[]{:S(2)}, u32[]{:S(2)}) collective-permute-start(bf16[1024,256]{1,0:T(8,128)(2,1)S(1)} %get-tuple-element.39), channel_id=1, source_target_pairs={{0,4},{1,5},{2,6},{3,7},{4,8},{5,9},{6,10},{7,11},{8,12},{9,13},{1... | collective-permute-start | bytes 1572872 | tf_op jit(solution)/shard_map/ppermute | solution.py:32
  5.4 1.5 collective-permute-start.1
  9.2 7.4 %collective-permute-done = bf16[1024,256]{1,0:T(8,128)(2,1)S(1)} collective-permute-done((bf16[1024,256]{1,0:T(8,128)(2,1)S(1)}, bf16[1024,256]{1,0:T(8,128)(2,1)S(1)}, u32[]{:S(2)}, u32[]{:S(2)}) %collective-permute-start) | collective-permute-done | bytes 524320 | tf_op jit(solution)/shard_map/ppermute | solution.py:32
  20.0 4.0 %collective-permute-done.2 = bf16[512,256]{1,0:T(8,128)(2,1)S(1)} collective-permute-done((bf16[512,256]{1,0:T(8,128)(2,1)S(1)}, bf16[512,256]{1,0:T(8,128)(2,1)S(1)}, u32[]{:S(2)}, u32[]{:S(2)}) %collective-permute-start.2) | collective-permute-done | bytes 262176 | tf_op jit(solution)/shard_map/ppermute | solution.py:32
  24.2 3.2 %collective-permute-start.6 = (bf16[512,1024]{1,0:T(8,128)(2,1)S(1)}, bf16[512,1024]{1,0:T(8,128)(2,1)}, u32[]{:S(2)}, u32[]{:S(2)}) collective-permute-start(bf16[512,1024]{1,0:T(8,128)(2,1)S(1)} %pad_maximum_fusion.refs_0_), channel_id=1, source_target_pairs={{0,3},{1,0},{2,1},{3,2},{4,7},{5,4},{6,5},{7,6},{8,11},{9,8},{10,9... | collective-permute-start | bytes 3145736 | tf_op jit(solution)/shard_map/ppermute | solution.py:32
  29.1 1.7 %collective-permute-start.5 = (bf16[512,256]{1,0:T(8,128)(2,1)S(1)}, bf16[512,256]{1,0:T(8,128)(2,1)S(1)}, u32[]{:S(2)}, u32[]{:S(2)}) collective-permute-start(bf16[512,256]{1,0:T(8,128)(2,1)S(1)} %get-tuple-element.46), channel_id=1, source_target_pairs={{0,12},{1,13},{2,14},{3,15},{4,0},{5,1},{6,2},{7,3},{8,4},{9,5},{1... | collective-permute-start | bytes 786440 | tf_op jit(solution)/shard_map/ppermute | solution.py:32
  30.9 24.4 %collective-permute-done.5 = bf16[512,256]{1,0:T(8,128)(2,1)S(1)} collective-permute-done((bf16[512,256]{1,0:T(8,128)(2,1)S(1)}, bf16[512,256]{1,0:T(8,128)(2,1)S(1)}, u32[]{:S(2)}, u32[]{:S(2)}) %collective-permute-start.5) | collective-permute-done | bytes 262176 | tf_op jit(solution)/shard_map/ppermute | solution.py:32
  56.0 2.3 %pad_maximum_fusion.1.refs_0_ = bf16[512,1024]{1,0:T(8,128)(2,1)} fusion(bf16[512,256]{1,0:T(8,128)(2,1)} %copy-done.11, bf16[512,256]{1,0:T(8,128)(2,1)} %copy-done.10, bf16[512,256]{1,0:T(8,128)(2,1)S(1)} %get-tuple-element.44, bf16[512,256]{1,0:T(8,128)(2,1)} %get-tuple-element.36), kind=kLoop, calls=%fused_computation.3 | loop fusion | flops 4194304 | bytes 2097152 | tf_op jit(solution)/shard_map/concatenate | solution.py:252
  58.3 2.4 %collective-permute-done.12 = bf16[512,256]{1,0:T(8,128)(2,1)S(1)} collective-permute-done((bf16[512,256]{1,0:T(8,128)(2,1)}, bf16[512,256]{1,0:T(8,128)(2,1)S(1)}, u32[]{:S(2)}, u32[]{:S(2)}) %collective-permute-start.12) | collective-permute-done | bytes 262176 | tf_op jit(solution)/shard_map/ppermute | solution.py:32
  60.7 2.2 %pad_maximum_fusion.3.refs_2_ = bf16[512,1024]{1,0:T(8,128)(2,1)} fusion(bf16[512,256]{1,0:T(8,128)(2,1)S(1)} %collective-permute-done.12, bf16[512,256]{1,0:T(8,128)(2,1)} %get-tuple-element.42, bf16[512,256]{1,0:T(8,128)(2,1)} %get-tuple-element.40, bf16[512,256]{1,0:T(8,128)(2,1)} %get-tuple-element.34), kind=kLoop, calls=%fused_computation.5 | loop fusion | flops 4194304 | bytes 2097152 | tf_op jit(solution)/shard_map/concatenate | solution.py:252
  62.9 1.7 %collective-permute-start.15 = (bf16[512,1024]{1,0:T(8,128)(2,1)}, bf16[512,1024]{1,0:T(8,128)(2,1)}, u32[]{:S(2)}, u32[]{:S(2)}) collective-permute-start(bf16[512,1024]{1,0:T(8,128)(2,1)} %pad_maximum_fusion.1.refs_0_), channel_id=1, source_target_pairs={{0,3},{1,0},{2,1},{3,2},{4,7},{5,4},{6,5},{7,6},{8,11},{9,8},{10,9... | collective-permute-start | bytes 3145736 | tf_op jit(solution)/shard_map/ppermute | solution.py:32
  64.7 2.5 %collective-permute-start.18 = (bf16[512,1024]{1,0:T(8,128)(2,1)}, bf16[512,1024]{1,0:T(8,128)(2,1)}, u32[]{:S(2)}, u32[]{:S(2)}) collective-permute-start(bf16[512,1024]{1,0:T(8,128)(2,1)} %pad_maximum_fusion.3.refs_2_), channel_id=1, source_target_pairs={{0,12},{1,13},{2,14},{3,15},{4,0},{5,1},{6,2},{7,3},{8,4},{9,5},{1... | collective-permute-start | bytes 3145736 | tf_op jit(solution)/shard_map/ppermute | solution.py:32
  69.1 3.4 %copy-done = bf16[4096,1024]{1,0:T(8,128)(2,1)S(1)} copy-done((bf16[4096,1024]{1,0:T(8,128)(2,1)S(1)}, bf16[4096,1024]{1,0:T(8,128)(2,1)}, u32[]{:S(2)}) %copy-start) | copy-done | bytes 8388632
  72.5 13.3 %shard_map.95 = (f32[1024,1024]{1,0:T(8,128)S(1)}, f32[1024,128]{1,0:T(8,128)S(1)}) custom-call(s32[32]{0:T(128)S(1)} %pad_add_fusion.idx_ref, bf16[512,1024]{1,0:T(8,128)(2,1)S(1)} %copy-done.5, bf16[512,1024]{1,0:T(8,128)(2,1)} %collective-permute-done.3.refs_1_, bf16[512,1024]{1,0:T(8,128)(2,1)} %collective-permute-done.6.refs_2_, ...), custom_call_target="tpu_custom_call" | custom-call | flops 6442450944 | bytes 25165824 | tf_op jit(solution)/shard_map/pallas_call | solution.py:158
  85.8 2.2 %collective-permute-done.4.refs_0_ = bf16[512,1024]{1,0:T(8,128)(2,1)S(1)} collective-permute-done((bf16[512,1024]{1,0:T(8,128)(2,1)}, bf16[512,1024]{1,0:T(8,128)(2,1)S(1)}, u32[]{:S(2)}, u32[]{:S(2)}) %collective-permute-start.4) | collective-permute-done | bytes 1048608 | tf_op jit(solution)/shard_map/ppermute | solution.py:32
  88.1 2.7 %collective-permute-start.16 = (bf16[512,1024]{1,0:T(8,128)(2,1)}, bf16[512,1024]{1,0:T(8,128)(2,1)S(1)}, u32[]{:S(2)}, u32[]{:S(2)}) collective-permute-start(bf16[512,1024]{1,0:T(8,128)(2,1)} %collective-permute-done.15.refs_1_), channel_id=1, source_target_pairs={{0,3},{1,0},{2,1},{3,2},{4,7},{5,4},{6,5},{7,6},{8,11},{9,8},{10,9... | collective-permute-start | bytes 3145736 | tf_op jit(solution)/shard_map/ppermute | solution.py:32
  90.8 2.7 %collective-permute-start.19 = (bf16[512,1024]{1,0:T(8,128)(2,1)}, bf16[512,1024]{1,0:T(8,128)(2,1)S(1)}, u32[]{:S(2)}, u32[]{:S(2)}) collective-permute-start(bf16[512,1024]{1,0:T(8,128)(2,1)} %collective-permute-done.18.refs_3_), channel_id=1, source_target_pairs={{0,12},{1,13},{2,14},{3,15},{4,0},{5,1},{6,2},{7,3},{8,4},{9,5},{1... | collective-permute-start | bytes 3145736 | tf_op jit(solution)/shard_map/ppermute | solution.py:32
  93.7 3.4 %copy-done.1 = bf16[4096,1024]{1,0:T(8,128)(2,1)S(1)} copy-done((bf16[4096,1024]{1,0:T(8,128)(2,1)S(1)}, bf16[4096,1024]{1,0:T(8,128)(2,1)}, u32[]{:S(2)}) %copy-start.1) | copy-done | bytes 8388632
  97.1 6.5 %shard_map.96 = f32[16,128]{1,0:T(8,128)S(1)} custom-call(s32[32]{0:T(128)S(1)} %pad_add_fusion.idx_ref, bf16[512,1024]{1,0:T(8,128)(2,1)S(1)} %collective-permute-done.4.refs_0_, bf16[512,1024]{1,0:T(8,128)(2,1)S(1)} %collective-permute-done.13.refs_1_, bf16[4096,1024]{1,0:T(8,128)(2,1)S(1)} %copy-done.1, bf16[4096,1024]{1,0:T(8,128)(2,1)S(1)} %copy-done.1, ...), custom_call_target="tpu_custom_call" | custom-call | flops 2147483648 | bytes 8388608 | tf_op jit(solution)/shard_map/pallas_call | solution.py:158
  103.5 10.2 %shard_map.97 = (f32[1024,1024]{1,0:T(8,128)S(1)}, f32[1024,128]{1,0:T(8,128)S(1)}) custom-call(s32[32]{0:T(128)S(1)} %pad_add_fusion.idx_ref, bf16[512,1024]{1,0:T(8,128)(2,1)} %pad_maximum_fusion.1.refs_0_, bf16[512,1024]{1,0:T(8,128)(2,1)} %collective-permute-done.15.refs_1_, bf16[512,1024]{1,0:T(8,128)(2,1)} %pad_maximum_fusion.3.refs_2_, ...), custom_call_target="tpu_custom_call" | custom-call | flops 4294967296 | bytes 16777216 | tf_op jit(solution)/shard_map/pallas_call | solution.py:158
  113.8 9.3 %shard_map.98 = f32[16,128]{1,0:T(8,128)S(1)} custom-call(s32[32]{0:T(128)S(1)} %pad_add_fusion.idx_ref, bf16[512,1024]{1,0:T(8,128)(2,1)S(1)} %collective-permute-done.14.refs_0_, bf16[512,1024]{1,0:T(8,128)(2,1)S(1)} %collective-permute-done.16.refs_1_, bf16[512,1024]{1,0:T(8,128)(2,1)S(1)} %collective-permute-done.17.refs_2_, ...), custom_call_target="tpu_custom_call" | custom-call | flops 4294967296 | bytes 16777216 | tf_op jit(solution)/shard_map/pallas_call | solution.py:158
  124.0 13.7 %all-to-all-start = ((f32[128,1,128]{2,1,0:T(1,128)}), f32[128,1,128]{2,1,0:T(1,128)S(1)}, u32[]{:S(2)}, u32[]{:S(2)}) async-start(f32[128,1,128]{2,1,0:T(1,128)} %broadcast_in_dim.2), calls=%async_computation | async-start | bytes 131072 | tf_op jit(solution)/shard_map/all_to_all | solution.py:313
  137.7 9.5 %all-to-all-done = f32[128,1,128]{2,1,0:T(1,128)S(1)} async-done(((f32[128,1,128]{2,1,0:T(1,128)}), f32[128,1,128]{2,1,0:T(1,128)S(1)}, u32[]{:S(2)}, u32[]{:S(2)}) %all-to-all-start) | async-done | bytes 65568 | tf_op jit(solution)/shard_map/all_to_all | solution.py:313
  147.2 2.6 %shard_map.99 = (f32[512,1024]{1,0:T(8,128)}, f32[1,16]{1,0:T(1,128)}) custom-call(s32[1]{0:T(128)} %bitcast.at_ref, f32[128,128]{1,0:T(8,128)S(1)} %bitcast.7, f32[128,128]{1,0:T(8,128)S(1)} %get-tuple-element.50.seat_ref, bf16[128,4096]{1,0:T(8,128)(2,1)S(1)} %copy-done.3, bf16[128,1024]{1,0:T(8,128)(2,1)S(1)} %copy-done.8), custom_call_target="tpu_custom_call" | custom-call | tf_op jit(solution)/shard_map/pallas_call | solution.py:205
  (74 shorter events, 14.0 us)
Async XLA Ops:
  2.0 14.6 %collective-permute-start = (bf16[1024,256]{1,0:T(8,128)(2,1)S(1)}, bf16[1024,256]{1,0:T(8,128)(2,1)S(1)}, u32[]{:S(2)}, u32[]{:S(2)}) collective-permute-start(bf16[1024,256]{1,0:T(8,128)(2,1)S(1)} %get-tuple-element.39), channel_id=1, source_target_pairs={{0,4},{1,5},{2,6},{3,7},{4,8},{5,9},{6,10},{7,11},{8,12},{9,13},{1... | collective-permute-start | bytes 1572872 | tf_op jit(solution)/shard_map/ppermute | solution.py:32
  4.1 13.8 %collective-permute-start.7 = (bf16[1024,256]{1,0:T(8,128)(2,1)S(1)}, bf16[1024,256]{1,0:T(8,128)(2,1)S(1)}, u32[]{:S(2)}, u32[]{:S(2)}) collective-permute-start(bf16[1024,256]{1,0:T(8,128)(2,1)S(1)} %get-tuple-element.38), channel_id=1, source_target_pairs={{0,1},{1,2},{2,3},{3,0},{4,5},{5,6},{6,7},{7,4},{8,9},{9,10},{10,1... | collective-permute-start | bytes 1572872 | tf_op jit(solution)/shard_map/ppermute | solution.py:32
  5.4 13.7 %collective-permute-start.1 = (bf16[1024,256]{1,0:T(8,128)(2,1)S(1)}, bf16[1024,256]{1,0:T(8,128)(2,1)S(1)}, u32[]{:S(2)}, u32[]{:S(2)}) collective-permute-start(bf16[1024,256]{1,0:T(8,128)(2,1)S(1)} %get-tuple-element.39), channel_id=1, source_target_pairs={{0,12},{1,13},{2,14},{3,15},{4,0},{5,1},{6,2},{7,3},{8,4},{9,5},{1... | collective-permute-start | bytes 1572872 | tf_op jit(solution)/shard_map/ppermute | solution.py:32
  6.9 12.3 %collective-permute-start.8 = (bf16[1024,256]{1,0:T(8,128)(2,1)S(1)}, bf16[1024,256]{1,0:T(8,128)(2,1)S(1)}, u32[]{:S(2)}, u32[]{:S(2)}) collective-permute-start(bf16[1024,256]{1,0:T(8,128)(2,1)S(1)} %get-tuple-element.38), channel_id=1, source_target_pairs={{0,3},{1,0},{2,1},{3,2},{4,7},{5,4},{6,5},{7,6},{8,11},{9,8},{10,9... | collective-permute-start | bytes 1572872 | tf_op jit(solution)/shard_map/ppermute | solution.py:32
  16.6 7.4 %collective-permute-start.2 = (bf16[512,256]{1,0:T(8,128)(2,1)S(1)}, bf16[512,256]{1,0:T(8,128)(2,1)S(1)}, u32[]{:S(2)}, u32[]{:S(2)}) collective-permute-start(bf16[512,256]{1,0:T(8,128)(2,1)S(1)} %get-tuple-element.45), channel_id=1, source_target_pairs={{0,4},{1,5},{2,6},{3,7},{4,8},{5,9},{6,10},{7,11},{8,12},{9,13},{1... | collective-permute-start | bytes 786440 | tf_op jit(solution)/shard_map/ppermute | solution.py:32
  18.7 8.7 %collective-permute-start.9 = (bf16[512,256]{1,0:T(8,128)(2,1)S(1)}, bf16[512,256]{1,0:T(8,128)(2,1)S(1)}, u32[]{:S(2)}, u32[]{:S(2)}) collective-permute-start(bf16[512,256]{1,0:T(8,128)(2,1)S(1)} %get-tuple-element.41), channel_id=1, source_target_pairs={{0,1},{1,2},{2,3},{3,0},{4,5},{5,6},{6,7},{7,4},{8,9},{9,10},{10,1... | collective-permute-start | bytes 786440 | tf_op jit(solution)/shard_map/ppermute | solution.py:32
  24.0 31.7 %copy-start.12 = (s32[4]{0:T(128)S(1)}, s32[4]{0:T(128)}, u32[]{:S(2)}) copy-start(s32[4]{0:T(128)} %constant.79) | copy-start | bytes 52
  24.2 34.1 %copy-start.4 = (bf16[512,1024]{1,0:T(8,128)(2,1)}, bf16[512,1024]{1,0:T(8,128)(2,1)S(1)}, u32[]{:S(2)}) copy-start(bf16[512,1024]{1,0:T(8,128)(2,1)S(1)} %pad_maximum_fusion.refs_0_) | copy-start | bytes 3145732
  24.2 38.8 %collective-permute-start.6 = (bf16[512,1024]{1,0:T(8,128)(2,1)S(1)}, bf16[512,1024]{1,0:T(8,128)(2,1)}, u32[]{:S(2)}, u32[]{:S(2)}) collective-permute-start(bf16[512,1024]{1,0:T(8,128)(2,1)S(1)} %pad_maximum_fusion.refs_0_), channel_id=1, source_target_pairs={{0,3},{1,0},{2,1},{3,2},{4,7},{5,4},{6,5},{7,6},{8,11},{9,8},{10,9... | collective-permute-start | bytes 3145736 | tf_op jit(solution)/shard_map/ppermute | solution.py:32
  27.6 35.4 %copy-start.6 = (bf16[512,1024]{1,0:T(8,128)(2,1)}, bf16[512,1024]{1,0:T(8,128)(2,1)S(1)}, u32[]{:S(2)}) copy-start(bf16[512,1024]{1,0:T(8,128)(2,1)S(1)} %pad_maximum_fusion.2.refs_3_) | copy-start | bytes 3145732
  27.6 35.4 %collective-permute-start.11 = (bf16[512,1024]{1,0:T(8,128)(2,1)S(1)}, bf16[512,1024]{1,0:T(8,128)(2,1)}, u32[]{:S(2)}, u32[]{:S(2)}) collective-permute-start(bf16[512,1024]{1,0:T(8,128)(2,1)S(1)} %pad_maximum_fusion.2.refs_3_), channel_id=1, source_target_pairs={{0,12},{1,13},{2,14},{3,15},{4,0},{5,1},{6,2},{7,3},{8,4},{9,5},{1... | collective-permute-start | bytes 3145736 | tf_op jit(solution)/shard_map/ppermute | solution.py:32
  28.2 39.0 %collective-permute-start.3 = (bf16[512,1024]{1,0:T(8,128)(2,1)S(1)}, bf16[512,1024]{1,0:T(8,128)(2,1)}, u32[]{:S(2)}, u32[]{:S(2)}) collective-permute-start(bf16[512,1024]{1,0:T(8,128)(2,1)S(1)} %pad_maximum_fusion.refs_0_), channel_id=1, source_target_pairs={{0,1},{1,2},{2,3},{3,0},{4,5},{5,6},{6,7},{7,4},{8,9},{9,10},{10,1... | collective-permute-start | bytes 3145736 | tf_op jit(solution)/shard_map/ppermute | solution.py:32
  28.2 39.0 %collective-permute-start.10 = (bf16[512,1024]{1,0:T(8,128)(2,1)S(1)}, bf16[512,1024]{1,0:T(8,128)(2,1)}, u32[]{:S(2)}, u32[]{:S(2)}) collective-permute-start(bf16[512,1024]{1,0:T(8,128)(2,1)S(1)} %pad_maximum_fusion.2.refs_3_), channel_id=1, source_target_pairs={{0,4},{1,5},{2,6},{3,7},{4,8},{5,9},{6,10},{7,11},{8,12},{9,13},{1... | collective-permute-start | bytes 3145736 | tf_op jit(solution)/shard_map/ppermute | solution.py:32
  29.1 26.2 %collective-permute-start.5 = (bf16[512,256]{1,0:T(8,128)(2,1)S(1)}, bf16[512,256]{1,0:T(8,128)(2,1)S(1)}, u32[]{:S(2)}, u32[]{:S(2)}) collective-permute-start(bf16[512,256]{1,0:T(8,128)(2,1)S(1)} %get-tuple-element.46), channel_id=1, source_target_pairs={{0,12},{1,13},{2,14},{3,15},{4,0},{5,1},{6,2},{7,3},{8,4},{9,5},{1... | collective-permute-start | bytes 786440 | tf_op jit(solution)/shard_map/ppermute | solution.py:32
  55.3 5.4 %collective-permute-start.12 = (bf16[512,256]{1,0:T(8,128)(2,1)}, bf16[512,256]{1,0:T(8,128)(2,1)S(1)}, u32[]{:S(2)}, u32[]{:S(2)}) collective-permute-start(bf16[512,256]{1,0:T(8,128)(2,1)} %get-tuple-element.42), channel_id=1, source_target_pairs={{0,3},{1,0},{2,1},{3,2},{4,7},{5,4},{6,5},{7,6},{8,11},{9,8},{10,9... | collective-permute-start | bytes 786440 | tf_op jit(solution)/shard_map/ppermute | solution.py:32
  62.9 25.1 %collective-permute-start.15 = (bf16[512,1024]{1,0:T(8,128)(2,1)}, bf16[512,1024]{1,0:T(8,128)(2,1)}, u32[]{:S(2)}, u32[]{:S(2)}) collective-permute-start(bf16[512,1024]{1,0:T(8,128)(2,1)} %pad_maximum_fusion.1.refs_0_), channel_id=1, source_target_pairs={{0,3},{1,0},{2,1},{3,2},{4,7},{5,4},{6,5},{7,6},{8,11},{9,8},{10,9... | collective-permute-start | bytes 3145736 | tf_op jit(solution)/shard_map/ppermute | solution.py:32
  64.7 26.1 %collective-permute-start.18 = (bf16[512,1024]{1,0:T(8,128)(2,1)}, bf16[512,1024]{1,0:T(8,128)(2,1)}, u32[]{:S(2)}, u32[]{:S(2)}) collective-permute-start(bf16[512,1024]{1,0:T(8,128)(2,1)} %pad_maximum_fusion.3.refs_2_), channel_id=1, source_target_pairs={{0,12},{1,13},{2,14},{3,15},{4,0},{5,1},{6,2},{7,3},{8,4},{9,5},{1... | collective-permute-start | bytes 3145736 | tf_op jit(solution)/shard_map/ppermute | solution.py:32
  67.2 20.8 %collective-permute-start.4 = (bf16[512,1024]{1,0:T(8,128)(2,1)}, bf16[512,1024]{1,0:T(8,128)(2,1)S(1)}, u32[]{:S(2)}, u32[]{:S(2)}) collective-permute-start(bf16[512,1024]{1,0:T(8,128)(2,1)} %collective-permute-done.3.refs_1_), channel_id=1, source_target_pairs={{0,1},{1,2},{2,3},{3,0},{4,5},{5,6},{6,7},{7,4},{8,9},{9,10},{10,1... | collective-permute-start | bytes 3145736 | tf_op jit(solution)/shard_map/ppermute | solution.py:32
  67.2 20.9 %collective-permute-start.13 = (bf16[512,1024]{1,0:T(8,128)(2,1)}, bf16[512,1024]{1,0:T(8,128)(2,1)S(1)}, u32[]{:S(2)}, u32[]{:S(2)}) collective-permute-start(bf16[512,1024]{1,0:T(8,128)(2,1)} %collective-permute-done.10.refs_4_), channel_id=1, source_target_pairs={{0,4},{1,5},{2,6},{3,7},{4,8},{5,9},{6,10},{7,11},{8,12},{9,13},{1... | collective-permute-start | bytes 3145736 | tf_op jit(solution)/shard_map/ppermute | solution.py:32
  88.1 25.6 %collective-permute-start.14 = (bf16[512,1024]{1,0:T(8,128)(2,1)}, bf16[512,1024]{1,0:T(8,128)(2,1)S(1)}, u32[]{:S(2)}, u32[]{:S(2)}) collective-permute-start(bf16[512,1024]{1,0:T(8,128)(2,1)} %pad_maximum_fusion.1.refs_0_), channel_id=1, source_target_pairs={{0,1},{1,2},{2,3},{3,0},{4,5},{5,6},{6,7},{7,4},{8,9},{9,10},{10,1... | collective-permute-start | bytes 3145736 | tf_op jit(solution)/shard_map/ppermute | solution.py:32
  88.1 25.7 %collective-permute-start.16 = (bf16[512,1024]{1,0:T(8,128)(2,1)}, bf16[512,1024]{1,0:T(8,128)(2,1)S(1)}, u32[]{:S(2)}, u32[]{:S(2)}) collective-permute-start(bf16[512,1024]{1,0:T(8,128)(2,1)} %collective-permute-done.15.refs_1_), channel_id=1, source_target_pairs={{0,3},{1,0},{2,1},{3,2},{4,7},{5,4},{6,5},{7,6},{8,11},{9,8},{10,9... | collective-permute-start | bytes 3145736 | tf_op jit(solution)/shard_map/ppermute | solution.py:32
  90.7 23.0 %collective-permute-start.17 = (bf16[512,1024]{1,0:T(8,128)(2,1)}, bf16[512,1024]{1,0:T(8,128)(2,1)S(1)}, u32[]{:S(2)}, u32[]{:S(2)}) collective-permute-start(bf16[512,1024]{1,0:T(8,128)(2,1)} %pad_maximum_fusion.3.refs_2_), channel_id=1, source_target_pairs={{0,4},{1,5},{2,6},{3,7},{4,8},{5,9},{6,10},{7,11},{8,12},{9,13},{1... | collective-permute-start | bytes 3145736 | tf_op jit(solution)/shard_map/ppermute | solution.py:32
  90.8 23.0 %collective-permute-start.19 = (bf16[512,1024]{1,0:T(8,128)(2,1)}, bf16[512,1024]{1,0:T(8,128)(2,1)S(1)}, u32[]{:S(2)}, u32[]{:S(2)}) collective-permute-start(bf16[512,1024]{1,0:T(8,128)(2,1)} %collective-permute-done.18.refs_3_), channel_id=1, source_target_pairs={{0,12},{1,13},{2,14},{3,15},{4,0},{5,1},{6,2},{7,3},{8,4},{9,5},{1... | collective-permute-start | bytes 3145736 | tf_op jit(solution)/shard_map/ppermute | solution.py:32
  124.0 23.2 %all-to-all-start = ((f32[128,1,128]{2,1,0:T(1,128)}), f32[128,1,128]{2,1,0:T(1,128)S(1)}, u32[]{:S(2)}, u32[]{:S(2)}) async-start(f32[128,1,128]{2,1,0:T(1,128)} %broadcast_in_dim.2), calls=%async_computation | async-start | bytes 131072 | tf_op jit(solution)/shard_map/all_to_all | solution.py:313
  (11 other events, 93.1 us)

commit v7 on v4

--- a/solution.py
+++ b/solution.py
@@ -19,7 +19,7 @@
 
 COLS = 256
 LANES = 128
-VMEM_LIMIT = 48 * 1024 * 1024
+VMEM_LIMITS = (36 << 20, 26 << 20, 20 << 20)
 
 
 def shift(piece, dx, dy):
@@ -80,10 +80,11 @@
         if final:
             out_ref[...] = jnp.zeros(out_ref.shape, jnp.float32)
 
+    here = pl.ds(pl.multiple_of(pl.program_id(0) * COLS, COLS), COLS) if final else slice(None)
     for b in range(len(terms)):
         base = product(b, w_ref)
         if started:
-            base += sum_ref[b * rows : (b + 1) * rows, :]
+            base += sum_ref[b * rows : (b + 1) * rows, here]
         if not final:
             out_ref[b * rows : (b + 1) * rows, :] = base
             continue
@@ -92,17 +93,18 @@
             token = slice(m * TOK, (m + 1) * TOK)
             there = slice(slot * TOK, (slot + 1) * TOK)
             proj = proj_ref[there, :]
-            right = right_ref[slot : slot + 1, :]
+            right = right_ref[slot : slot + 1, here]
+            cot = cot_ref[there, here].astype(jnp.float32)
             sums = jnp.zeros((1, LANES), jnp.float32)
             for g in range(COLS // LANES):
                 cols = slice(g * LANES, (g + 1) * LANES)
                 act = jnp.maximum(base[token, cols] + proj * right[:, cols], 0.0)
-                term = cot_ref[there, cols].astype(jnp.float32) * (act * act)
+                term = cot[:, cols] * (act * act)
                 sums += jnp.sum(term, axis=0, keepdims=True)
             out_ref[slot : slot + 1, :] += sums
 
 
-def stage(blocks, idx, weight, left_own, sums=None, score=None):
+def stage(blocks, idx, weight, left_own, limit, sums=None, score=None):
     terms = tuple(tuple(place for _, place in block) for block in blocks)
     rows, extent = blocks[0][0][0].shape
     total = rows * len(blocks)
@@ -111,15 +113,20 @@
     tile = lambda n, idx: (0, n)
     once = pl.Buffered(1)
     operands = [piece for block in blocks for piece, _ in block]
-    in_specs = [pl.BlockSpec((rows, extent), whole, pipeline_mode=once)] * len(operands)
+    placed = pl.BlockSpec(memory_space=pltpu.VMEM)
+    final = score is not None
+    in_specs = [
+        placed if final else pl.BlockSpec((rows, extent), whole, pipeline_mode=once)
+    ] * len(operands)
     in_specs += [
         pl.BlockSpec((depth, COLS), tile),
-        pl.BlockSpec((depth, LANES), whole, pipeline_mode=once),
+        placed if final else pl.BlockSpec((depth, LANES), whole, pipeline_mode=once),
     ]
     operands += [weight, left_own]
     block = pl.BlockSpec((total, COLS), tile)
     if sums is not None:
-        in_specs += [block, pl.BlockSpec((total, LANES), whole, pipeline_mode=once)]
+        carried = [block, pl.BlockSpec((total, LANES), whole, pipeline_mode=once)]
+        in_specs += [placed, placed] if final else carried
         operands += list(sums)
     if score is None:
         out_specs, scratch = [block, pl.BlockSpec((total, LANES), whole)], []
@@ -129,7 +136,7 @@
         ]
     else:
         members = total // TOK
-        in_specs += [pl.BlockSpec((members, COLS), tile), block]
+        in_specs += [placed, placed]
         operands += list(score)
         out_specs = pl.BlockSpec((members, LANES), whole)
         out_shape = jax.ShapeDtypeStruct((members, LANES), jnp.float32)
@@ -145,7 +152,7 @@
             scratch_shapes=scratch,
         ),
         out_shape=out_shape,
-        compiler_params=pltpu.CompilerParams(vmem_limit_bytes=VMEM_LIMIT),
+        compiler_params=pltpu.CompilerParams(vmem_limit_bytes=limit),
         cost_estimate=pl.CostEstimate(
             flops=flops, bytes_accessed=flops // 256, transcendentals=0
         ),
@@ -202,7 +209,7 @@
             jax.ShapeDtypeStruct((row_share, columns), jnp.float32),
             jax.ShapeDtypeStruct((1, owned), jnp.float32),
         ],
-        compiler_params=pltpu.CompilerParams(vmem_limit_bytes=VMEM_LIMIT),
+        compiler_params=pltpu.CompilerParams(vmem_limit_bytes=VMEM_LIMITS[2]),
     )(at, tables, seat, factor_left, factor_right)
 
 
@@ -263,12 +270,12 @@
 
     near = {o: send(blocks[o], o, 1) for o in both}
     far = {o: send(near[o], o, 1) for o in both}
-    sums = stage(terms((blocks, (0, 0)), (near, (1, 2))), idx, weight, left_own)
+    sums = stage(terms((blocks, (0, 0)), (near, (1, 2))), idx, weight, left_own, VMEM_LIMITS[0])
     far, sums, blocks = lax.optimization_barrier((far, sums, blocks))
     other = {o: send(blocks[o], o, -1) for o in both}
-    sums = stage(terms((far, (3, 3))), idx, weight, left_own, sums)
+    sums = stage(terms((far, (3, 3))), idx, weight, left_own, VMEM_LIMITS[1], sums)
     scores = stage(
-        terms((other, (2, 1))), idx, weight, left_own, sums, (right_own, cotangent)
+        terms((other, (2, 1))), idx, weight, left_own, VMEM_LIMITS[2], sums, (right_own, cotangent)
     )
     partial = -jnp.sum(scores, axis=1) / math.sqrt(TOK * FF)
     seated = seat[:, :owned].astype(jnp.float32)

time: 138 us -> 136 us (0.986)
  Pallas kernels: 47.4 us -> 40.3 us
  waiting for transfers between devices: 43.2 us -> 48.4 us
    pallas_call x3, Pallas kernels: 44.8 us -> 37.7 us  [stage(): pl.pallas_call(functools.partial(stage_kernel, terms, sums is not None, s...]
    ppermute x20, waiting for transfers between devices: 33.7 us -> 38.9 us  [shift(): return lax.ppermute(piece, 'mp', perm)]
    unnamed x16 -> x26, local copies, waits for them, and re-layouts: 2 us -> 2.76 us
  transfers between devices with their start and end apart: 21 -> 21, of which waited for: 8 -> 8; matrix products, arithmetic and copies ran while one was open for 3% -> 3% of each run, Pallas kernels for 23% -> 21%
where the time goes in v7:
time: 136 us
  waiting for transfers between devices  48.4 us (36%)
  Pallas kernels  40.3 us (30%)
  starting transfers between devices  37.7 us (28%)
  local copies, waits for them, and re-layouts  5.17 us (4%)
  other arithmetic  2.88 us (2%)
    ppermute x20, waiting for transfers between devices, shift(): return lax.ppermute(piece, 'mp', perm)  38.9 us
    pallas_call x3, Pallas kernels, stage(): pl.pallas_call(functools.partial(stage_kernel, terms, sums is not None, s...  37.7 us
    ppermute x20, starting transfers between devices, shift(): return lax.ppermute(piece, 'mp', perm)  25.1 us
    all_to_all x1, starting transfers between devices, per_device(): tables = lax.all_to_all(copies, everywhere, 0, 0, tiled=True)  12.6 us
    all_to_all x1, waiting for transfers between devices, per_device(): tables = lax.all_to_all(copies, everywhere, 0, 0, tiled=True)  9.5 us
    unnamed x26, local copies, waits for them, and re-layouts  2.76 us
  transfers between devices with their start and end apart: 21, of which 8 were waited for; matrix products, arithmetic and copies ran while one was open for 3% of the time, Pallas kernels for 21%

profile of v7, /device:TPU:1, one launch (start us, length us, event | category | flops | bytes accessed | tf_op | source)
XLA Modules:
  0.0 136.0 jit_solution(17918863116451758865)
XLA Ops:
  0.6 1.4 fusion.9
  2.0 2.1 %collective-permute-start.8 = (bf16[1024,256]{1,0:T(8,128)(2,1)S(1)}, bf16[1024,256]{1,0:T(8,128)(2,1)S(1)}, u32[]{:S(2)}, u32[]{:S(2)}) collective-permute-start(bf16[1024,256]{1,0:T(8,128)(2,1)S(1)} %get-tuple-element.38), channel_id=1, source_target_pairs={{0,4},{1,5},{2,6},{3,7},{4,8},{5,9},{6,10},{7,11},{8,12},{9,13},{1... | collective-permute-start | bytes 1572872 | tf_op jit(solution)/shard_map/ppermute | solution.py:31
  4.1 1.3 collective-permute-start.9
  5.5 2.9 %collective-permute-start.1 = (bf16[1024,256]{1,0:T(8,128)(2,1)S(1)}, bf16[1024,256]{1,0:T(8,128)(2,1)S(1)}, u32[]{:S(2)}, u32[]{:S(2)}) collective-permute-start(bf16[1024,256]{1,0:T(8,128)(2,1)S(1)} %get-tuple-element.39), channel_id=1, source_target_pairs={{0,3},{1,0},{2,1},{3,2},{4,7},{5,4},{6,5},{7,6},{8,11},{9,8},{10,9... | collective-permute-start | bytes 1572872 | tf_op jit(solution)/shard_map/ppermute | solution.py:31
  8.4 8.2 %collective-permute-done.8 = bf16[1024,256]{1,0:T(8,128)(2,1)S(1)} collective-permute-done((bf16[1024,256]{1,0:T(8,128)(2,1)S(1)}, bf16[1024,256]{1,0:T(8,128)(2,1)S(1)}, u32[]{:S(2)}, u32[]{:S(2)}) %collective-permute-start.8) | collective-permute-done | bytes 524320 | tf_op jit(solution)/shard_map/ppermute | solution.py:31
  17.1 2.4 %collective-permute-start.13 = (bf16[512,256]{1,0:T(8,128)(2,1)S(1)}, bf16[512,256]{1,0:T(8,128)(2,1)S(1)}, u32[]{:S(2)}, u32[]{:S(2)}) collective-permute-start(bf16[512,256]{1,0:T(8,128)(2,1)S(1)} %get-tuple-element.42), channel_id=1, source_target_pairs={{0,12},{1,13},{2,14},{3,15},{4,0},{5,1},{6,2},{7,3},{8,4},{9,5},{1... | collective-permute-start | bytes 786440 | tf_op jit(solution)/shard_map/ppermute | solution.py:31
  19.5 3.1 %collective-permute-start.5 = (bf16[512,256]{1,0:T(8,128)(2,1)S(1)}, bf16[512,256]{1,0:T(8,128)(2,1)S(1)}, u32[]{:S(2)}, u32[]{:S(2)}) collective-permute-start(bf16[512,256]{1,0:T(8,128)(2,1)S(1)} %get-tuple-element.46), channel_id=1, source_target_pairs={{0,3},{1,0},{2,1},{3,2},{4,7},{5,4},{6,5},{7,6},{8,11},{9,8},{10,9... | collective-permute-start | bytes 786440 | tf_op jit(solution)/shard_map/ppermute | solution.py:31
  22.8 1.3 collective-permute-done.10
  24.2 1.8 %collective-permute-start.11 = (bf16[512,1024]{1,0:T(8,128)(2,1)S(1)}, bf16[512,1024]{1,0:T(8,128)(2,1)}, u32[]{:S(2)}, u32[]{:S(2)}) collective-permute-start(bf16[512,1024]{1,0:T(8,128)(2,1)S(1)} %pad_maximum_fusion.2.refs_0_), channel_id=1, source_target_pairs={{0,1},{1,2},{2,3},{3,0},{4,5},{5,6},{6,7},{7,4},{8,9},{9,10},{10,1... | collective-permute-start | bytes 3145736 | tf_op jit(solution)/shard_map/ppermute | solution.py:31
  26.1 1.5 %collective-permute-start.14 = (bf16[512,1024]{1,0:T(8,128)(2,1)S(1)}, bf16[512,1024]{1,0:T(8,128)(2,1)}, u32[]{:S(2)}, u32[]{:S(2)}) collective-permute-start(bf16[512,1024]{1,0:T(8,128)(2,1)S(1)} %pad_maximum_fusion.3.refs_2_), channel_id=1, source_target_pairs={{0,3},{1,0},{2,1},{3,2},{4,7},{5,4},{6,5},{7,6},{8,11},{9,8},{10,9... | collective-permute-start | bytes 3145736 | tf_op jit(solution)/shard_map/ppermute | solution.py:31
  28.8 2.3 %collective-permute-start.6 = (bf16[512,1024]{1,0:T(8,128)(2,1)}, bf16[512,1024]{1,0:T(8,128)(2,1)}, u32[]{:S(2)}, u32[]{:S(2)}) collective-permute-start(bf16[512,1024]{1,0:T(8,128)(2,1)} %pad_maximum_fusion.1.refs_6_), channel_id=1, source_target_pairs={{0,12},{1,13},{2,14},{3,15},{4,0},{5,1},{6,2},{7,3},{8,4},{9,5},{1... | collective-permute-start | bytes 3145736 | tf_op jit(solution)/shard_map/ppermute | solution.py:31
  32.5 19.4 %collective-permute-done.11.refs_1_ = bf16[512,1024]{1,0:T(8,128)(2,1)} collective-permute-done((bf16[512,1024]{1,0:T(8,128)(2,1)S(1)}, bf16[512,1024]{1,0:T(8,128)(2,1)}, u32[]{:S(2)}, u32[]{:S(2)}) %collective-permute-start.11) | collective-permute-done | bytes 1048608 | tf_op jit(solution)/shard_map/ppermute | solution.py:31
  52.0 2.7 %collective-permute-start.15 = (bf16[512,1024]{1,0:T(8,128)(2,1)}, bf16[512,1024]{1,0:T(8,128)(2,1)S(1)}, u32[]{:S(2)}, u32[]{:S(2)}) collective-permute-start(bf16[512,1024]{1,0:T(8,128)(2,1)} %collective-permute-done.14.refs_3_), channel_id=1, source_target_pairs={{0,3},{1,0},{2,1},{3,2},{4,7},{5,4},{6,5},{7,6},{8,11},{9,8},{10,9... | collective-permute-start | bytes 3145736 | tf_op jit(solution)/shard_map/ppermute | solution.py:31
  56.7 1.5 %copy-done.3 = bf16[512,1024]{1,0:T(8,128)(2,1)S(1)} copy-done((bf16[512,1024]{1,0:T(8,128)(2,1)S(1)}, bf16[512,1024]{1,0:T(8,128)(2,1)}, u32[]{:S(2)}) %copy-start.3) | copy-done | bytes 1048600
  59.4 17.3 %shard_map.95 = (f32[2048,1024]{1,0:T(8,128)}, f32[2048,128]{1,0:T(8,128)S(1)}) custom-call(s32[32]{0:T(128)S(1)} %pad_add_fusion.idx_ref, bf16[512,1024]{1,0:T(8,128)(2,1)S(1)} %copy-done.3, bf16[512,1024]{1,0:T(8,128)(2,1)} %collective-permute-done.11.refs_1_, bf16[512,1024]{1,0:T(8,128)(2,1)S(1)} %copy-done.5, ...), custom_call_target="tpu_custom_call" | custom-call | flops 8589934592 | bytes 33554432 | tf_op jit(solution)/shard_map/pallas_call | solution.py:145
  78.3 1.5 %collective-permute-start.18 = (bf16[512,1024]{1,0:T(8,128)(2,1)}, bf16[512,1024]{1,0:T(8,128)(2,1)S(1)}, u32[]{:S(2)}, u32[]{:S(2)}) collective-permute-start(bf16[512,1024]{1,0:T(8,128)(2,1)} %pad_maximum_fusion.refs_4_), channel_id=1, source_target_pairs={{0,12},{1,13},{2,14},{3,15},{4,0},{5,1},{6,2},{7,3},{8,4},{9,5},{1... | collective-permute-start | bytes 3145736 | tf_op jit(solution)/shard_map/ppermute | solution.py:31
  80.1 10.6 %shard_map.96 = (f32[2048,1024]{1,0:T(8,128)S(1)}, f32[2048,128]{1,0:T(8,128)S(1)}) custom-call(s32[32]{0:T(128)S(1)} %pad_add_fusion.idx_ref, bf16[512,1024]{1,0:T(8,128)(2,1)S(1)} %collective-permute-done.12.refs_0_, bf16[512,1024]{1,0:T(8,128)(2,1)S(1)} %collective-permute-done.15.refs_1_, bf16[512,1024]{1,0:T(8,128)(2,1)S(1)} %collective-permute-done.4.refs_2_, ...), custom_call_target="tpu_custom_call" | custom-call | flops 4294967296 | bytes 16777216 | tf_op jit(solution)/shard_map/pallas_call | solution.py:145
  90.7 5.6 %collective-permute-done.16.refs_0_ = bf16[512,1024]{1,0:T(8,128)(2,1)S(1)} collective-permute-done((bf16[512,1024]{1,0:T(8,128)(2,1)S(1)}, bf16[512,1024]{1,0:T(8,128)(2,1)S(1)}, u32[]{:S(2)}, u32[]{:S(2)}) %collective-permute-start.16) | collective-permute-done | bytes 1048608 | tf_op jit(solution)/shard_map/ppermute | solution.py:31
  96.3 1.4 %collective-permute-done.17.refs_1_ = bf16[512,1024]{1,0:T(8,128)(2,1)S(1)} collective-permute-done((bf16[512,1024]{1,0:T(8,128)(2,1)S(1)}, bf16[512,1024]{1,0:T(8,128)(2,1)S(1)}, u32[]{:S(2)}, u32[]{:S(2)}) %collective-permute-start.17) | collective-permute-done | bytes 1048608 | tf_op jit(solution)/shard_map/ppermute | solution.py:31
  97.7 2.9 %collective-permute-done.19.refs_3_ = bf16[512,1024]{1,0:T(8,128)(2,1)S(1)} collective-permute-done((bf16[512,1024]{1,0:T(8,128)(2,1)}, bf16[512,1024]{1,0:T(8,128)(2,1)S(1)}, u32[]{:S(2)}, u32[]{:S(2)}) %collective-permute-start.19) | collective-permute-done | bytes 1048608 | tf_op jit(solution)/shard_map/ppermute | solution.py:31
  100.6 9.8 %shard_map.97 = f32[16,128]{1,0:T(8,128)S(1)} custom-call(s32[32]{0:T(128)S(1)} %pad_add_fusion.idx_ref, bf16[512,1024]{1,0:T(8,128)(2,1)S(1)} %collective-permute-done.16.refs_0_, bf16[512,1024]{1,0:T(8,128)(2,1)S(1)} %collective-permute-done.17.refs_1_, bf16[512,1024]{1,0:T(8,128)(2,1)S(1)} %collective-permute-done.18.refs_2_, ...), custom_call_target="tpu_custom_call" | custom-call | flops 4294967296 | bytes 16777216 | tf_op jit(solution)/shard_map/pallas_call | solution.py:145
  111.3 12.6 %all-to-all-start = ((f32[128,1,128]{2,1,0:T(1,128)}), f32[128,1,128]{2,1,0:T(1,128)S(1)}, u32[]{:S(2)}, u32[]{:S(2)}) async-start(f32[128,1,128]{2,1,0:T(1,128)} %broadcast_in_dim.2), calls=%async_computation | async-start | bytes 131072 | tf_op jit(solution)/shard_map/all_to_all | solution.py:287
  123.9 9.5 %all-to-all-done = f32[128,1,128]{2,1,0:T(1,128)S(1)} async-done(((f32[128,1,128]{2,1,0:T(1,128)}), f32[128,1,128]{2,1,0:T(1,128)S(1)}, u32[]{:S(2)}, u32[]{:S(2)}) %all-to-all-start) | async-done | bytes 65568 | tf_op jit(solution)/shard_map/all_to_all | solution.py:287
  133.4 2.6 %shard_map.98 = (f32[512,1024]{1,0:T(8,128)}, f32[1,16]{1,0:T(1,128)}) custom-call(s32[1]{0:T(128)} %bitcast.at_ref, f32[128,128]{1,0:T(8,128)S(1)} %bitcast.9, f32[128,128]{1,0:T(8,128)S(1)} %get-tuple-element.50.seat_ref, bf16[128,4096]{1,0:T(8,128)(2,1)S(1)} %copy-done, bf16[128,1024]{1,0:T(8,128)(2,1)S(1)} %copy-done.7), custom_call_target="tpu_custom_call" | custom-call | tf_op jit(solution)/shard_map/pallas_call | solution.py:192
  (72 shorter events, 9.5 us)
Async XLA Ops:
  2.0 14.6 %collective-permute-start.8 = (bf16[1024,256]{1,0:T(8,128)(2,1)S(1)}, bf16[1024,256]{1,0:T(8,128)(2,1)S(1)}, u32[]{:S(2)}, u32[]{:S(2)}) collective-permute-start(bf16[1024,256]{1,0:T(8,128)(2,1)S(1)} %get-tuple-element.38), channel_id=1, source_target_pairs={{0,4},{1,5},{2,6},{3,7},{4,8},{5,9},{6,10},{7,11},{8,12},{9,13},{1... | collective-permute-start | bytes 1572872 | tf_op jit(solution)/shard_map/ppermute | solution.py:31
  4.1 12.9 %collective-permute-start.9 = (bf16[1024,256]{1,0:T(8,128)(2,1)S(1)}, bf16[1024,256]{1,0:T(8,128)(2,1)S(1)}, u32[]{:S(2)}, u32[]{:S(2)}) collective-permute-start(bf16[1024,256]{1,0:T(8,128)(2,1)S(1)} %get-tuple-element.38), channel_id=1, source_target_pairs={{0,12},{1,13},{2,14},{3,15},{4,0},{5,1},{6,2},{7,3},{8,4},{9,5},{1... | collective-permute-start | bytes 1572872 | tf_op jit(solution)/shard_map/ppermute | solution.py:31
  5.5 14.0 %collective-permute-start.1 = (bf16[1024,256]{1,0:T(8,128)(2,1)S(1)}, bf16[1024,256]{1,0:T(8,128)(2,1)S(1)}, u32[]{:S(2)}, u32[]{:S(2)}) collective-permute-start(bf16[1024,256]{1,0:T(8,128)(2,1)S(1)} %get-tuple-element.39), channel_id=1, source_target_pairs={{0,3},{1,0},{2,1},{3,2},{4,7},{5,4},{6,5},{7,6},{8,11},{9,8},{10,9... | collective-permute-start | bytes 1572872 | tf_op jit(solution)/shard_map/ppermute | solution.py:31
  8.3 14.3 %collective-permute-start = (bf16[1024,256]{1,0:T(8,128)(2,1)S(1)}, bf16[1024,256]{1,0:T(8,128)(2,1)S(1)}, u32[]{:S(2)}, u32[]{:S(2)}) collective-permute-start(bf16[1024,256]{1,0:T(8,128)(2,1)S(1)} %get-tuple-element.39), channel_id=1, source_target_pairs={{0,1},{1,2},{2,3},{3,0},{4,5},{5,6},{6,7},{7,4},{8,9},{9,10},{10,1... | collective-permute-start | bytes 1572872 | tf_op jit(solution)/shard_map/ppermute | solution.py:31
  16.6 7.4 %collective-permute-start.10 = (bf16[512,256]{1,0:T(8,128)(2,1)S(1)}, bf16[512,256]{1,0:T(8,128)(2,1)S(1)}, u32[]{:S(2)}, u32[]{:S(2)}) collective-permute-start(bf16[512,256]{1,0:T(8,128)(2,1)S(1)} %get-tuple-element.41), channel_id=1, source_target_pairs={{0,4},{1,5},{2,6},{3,7},{4,8},{5,9},{6,10},{7,11},{8,12},{9,13},{1... | collective-permute-start | bytes 786440 | tf_op jit(solution)/shard_map/ppermute | solution.py:31
  17.1 8.9 %collective-permute-start.13 = (bf16[512,256]{1,0:T(8,128)(2,1)S(1)}, bf16[512,256]{1,0:T(8,128)(2,1)S(1)}, u32[]{:S(2)}, u32[]{:S(2)}) collective-permute-start(bf16[512,256]{1,0:T(8,128)(2,1)S(1)} %get-tuple-element.42), channel_id=1, source_target_pairs={{0,12},{1,13},{2,14},{3,15},{4,0},{5,1},{6,2},{7,3},{8,4},{9,5},{1... | collective-permute-start | bytes 786440 | tf_op jit(solution)/shard_map/ppermute | solution.py:31
  19.5 8.1 %collective-permute-start.5 = (bf16[512,256]{1,0:T(8,128)(2,1)S(1)}, bf16[512,256]{1,0:T(8,128)(2,1)S(1)}, u32[]{:S(2)}, u32[]{:S(2)}) collective-permute-start(bf16[512,256]{1,0:T(8,128)(2,1)S(1)} %get-tuple-element.46), channel_id=1, source_target_pairs={{0,3},{1,0},{2,1},{3,2},{4,7},{5,4},{6,5},{7,6},{8,11},{9,8},{10,9... | collective-permute-start | bytes 786440 | tf_op jit(solution)/shard_map/ppermute | solution.py:31
  22.7 8.4 %collective-permute-start.2 = (bf16[512,256]{1,0:T(8,128)(2,1)S(1)}, bf16[512,256]{1,0:T(8,128)(2,1)S(1)}, u32[]{:S(2)}, u32[]{:S(2)}) collective-permute-start(bf16[512,256]{1,0:T(8,128)(2,1)S(1)} %get-tuple-element.45), channel_id=1, source_target_pairs={{0,1},{1,2},{2,3},{3,0},{4,5},{5,6},{6,7},{7,4},{8,9},{9,10},{10,1... | collective-permute-start | bytes 786440 | tf_op jit(solution)/shard_map/ppermute | solution.py:31
  24.2 27.8 %collective-permute-start.11 = (bf16[512,1024]{1,0:T(8,128)(2,1)S(1)}, bf16[512,1024]{1,0:T(8,128)(2,1)}, u32[]{:S(2)}, u32[]{:S(2)}) collective-permute-start(bf16[512,1024]{1,0:T(8,128)(2,1)S(1)} %pad_maximum_fusion.2.refs_0_), channel_id=1, source_target_pairs={{0,1},{1,2},{2,3},{3,0},{4,5},{5,6},{6,7},{7,4},{8,9},{9,10},{10,1... | collective-permute-start | bytes 3145736 | tf_op jit(solution)/shard_map/ppermute | solution.py:31
  26.1 25.8 %collective-permute-start.14 = (bf16[512,1024]{1,0:T(8,128)(2,1)S(1)}, bf16[512,1024]{1,0:T(8,128)(2,1)}, u32[]{:S(2)}, u32[]{:S(2)}) collective-permute-start(bf16[512,1024]{1,0:T(8,128)(2,1)S(1)} %pad_maximum_fusion.3.refs_2_), channel_id=1, source_target_pairs={{0,3},{1,0},{2,1},{3,2},{4,7},{5,4},{6,5},{7,6},{8,11},{9,8},{10,9... | collective-permute-start | bytes 3145736 | tf_op jit(solution)/shard_map/ppermute | solution.py:31
  27.7 28.4 %copy-start = (bf16[128,4096]{1,0:T(8,128)(2,1)S(1)}, bf16[128,4096]{1,0:T(8,128)(2,1)}, u32[]{:S(2)}) copy-start(bf16[128,4096]{1,0:T(8,128)(2,1)} %left_ref.1) | copy-start | bytes 3145732
  28.8 25.8 %collective-permute-start.6 = (bf16[512,1024]{1,0:T(8,128)(2,1)}, bf16[512,1024]{1,0:T(8,128)(2,1)}, u32[]{:S(2)}, u32[]{:S(2)}) collective-permute-start(bf16[512,1024]{1,0:T(8,128)(2,1)} %pad_maximum_fusion.1.refs_6_), channel_id=1, source_target_pairs={{0,12},{1,13},{2,14},{3,15},{4,0},{5,1},{6,2},{7,3},{8,4},{9,5},{1... | collective-permute-start | bytes 3145736 | tf_op jit(solution)/shard_map/ppermute | solution.py:31
  32.2 22.8 %collective-permute-start.3 = (bf16[512,1024]{1,0:T(8,128)(2,1)}, bf16[512,1024]{1,0:T(8,128)(2,1)}, u32[]{:S(2)}, u32[]{:S(2)}) collective-permute-start(bf16[512,1024]{1,0:T(8,128)(2,1)} %pad_maximum_fusion.refs_4_), channel_id=1, source_target_pairs={{0,4},{1,5},{2,6},{3,7},{4,8},{5,9},{6,10},{7,11},{8,12},{9,13},{1... | collective-permute-start | bytes 3145736 | tf_op jit(solution)/shard_map/ppermute | solution.py:31
  52.0 24.7 %collective-permute-start.12 = (bf16[512,1024]{1,0:T(8,128)(2,1)}, bf16[512,1024]{1,0:T(8,128)(2,1)S(1)}, u32[]{:S(2)}, u32[]{:S(2)}) collective-permute-start(bf16[512,1024]{1,0:T(8,128)(2,1)} %collective-permute-done.11.refs_1_), channel_id=1, source_target_pairs={{0,1},{1,2},{2,3},{3,0},{4,5},{5,6},{6,7},{7,4},{8,9},{9,10},{10,1... | collective-permute-start | bytes 3145736 | tf_op jit(solution)/shard_map/ppermute | solution.py:31
  52.0 24.7 %collective-permute-start.15 = (bf16[512,1024]{1,0:T(8,128)(2,1)}, bf16[512,1024]{1,0:T(8,128)(2,1)S(1)}, u32[]{:S(2)}, u32[]{:S(2)}) collective-permute-start(bf16[512,1024]{1,0:T(8,128)(2,1)} %collective-permute-done.14.refs_3_), channel_id=1, source_target_pairs={{0,3},{1,0},{2,1},{3,2},{4,7},{5,4},{6,5},{7,6},{8,11},{9,8},{10,9... | collective-permute-start | bytes 3145736 | tf_op jit(solution)/shard_map/ppermute | solution.py:31
  54.6 22.1 %collective-permute-start.7 = (bf16[512,1024]{1,0:T(8,128)(2,1)}, bf16[512,1024]{1,0:T(8,128)(2,1)S(1)}, u32[]{:S(2)}, u32[]{:S(2)}) collective-permute-start(bf16[512,1024]{1,0:T(8,128)(2,1)} %collective-permute-done.6.refs_7_), channel_id=1, source_target_pairs={{0,12},{1,13},{2,14},{3,15},{4,0},{5,1},{6,2},{7,3},{8,4},{9,5},{1... | collective-permute-start | bytes 3145736 | tf_op jit(solution)/shard_map/ppermute | solution.py:31
  55.0 21.8 %collective-permute-start.4 = (bf16[512,1024]{1,0:T(8,128)(2,1)}, bf16[512,1024]{1,0:T(8,128)(2,1)S(1)}, u32[]{:S(2)}, u32[]{:S(2)}) collective-permute-start(bf16[512,1024]{1,0:T(8,128)(2,1)} %collective-permute-done.3.refs_5_), channel_id=1, source_target_pairs={{0,4},{1,5},{2,6},{3,7},{4,8},{5,9},{6,10},{7,11},{8,12},{9,13},{1... | collective-permute-start | bytes 3145736 | tf_op jit(solution)/shard_map/ppermute | solution.py:31
  56.1 24.0 %slice-start = ((s8[8388608]{0:T(1024)(128)(4,1)}), s8[4194304]{0:T(1024)(128)(4,1)S(1)}, s32[]{:S(2)}) async-start(s8[8388608]{0:T(1024)(128)(4,1)} %bitcast.7), calls=%async_computation.1 | async-start | bytes 8388608
  59.4 20.7 %slice-start.1 = ((s8[8388608]{0:T(1024)(128)(4,1)}), s8[4194304]{0:T(1024)(128)(4,1)S(1)}, s32[]{:S(2)}) async-start(s8[8388608]{0:T(1024)(128)(4,1)} %bitcast.7), calls=%async_computation.2 | async-start | bytes 8388608
  76.8 19.5 %collective-permute-start.16 = (bf16[512,1024]{1,0:T(8,128)(2,1)S(1)}, bf16[512,1024]{1,0:T(8,128)(2,1)S(1)}, u32[]{:S(2)}, u32[]{:S(2)}) collective-permute-start(bf16[512,1024]{1,0:T(8,128)(2,1)S(1)} %copy-done.3), channel_id=1, source_target_pairs={{0,3},{1,0},{2,1},{3,2},{4,7},{5,4},{6,5},{7,6},{8,11},{9,8},{10,9... | collective-permute-start | bytes 3145736 | tf_op jit(solution)/shard_map/ppermute | solution.py:31
  77.3 20.4 %collective-permute-start.17 = (bf16[512,1024]{1,0:T(8,128)(2,1)S(1)}, bf16[512,1024]{1,0:T(8,128)(2,1)S(1)}, u32[]{:S(2)}, u32[]{:S(2)}) collective-permute-start(bf16[512,1024]{1,0:T(8,128)(2,1)S(1)} %copy-done.6), channel_id=1, source_target_pairs={{0,1},{1,2},{2,3},{3,0},{4,5},{5,6},{6,7},{7,4},{8,9},{9,10},{10,1... | collective-permute-start | bytes 3145736 | tf_op jit(solution)/shard_map/ppermute | solution.py:31
  78.3 19.4 %collective-permute-start.18 = (bf16[512,1024]{1,0:T(8,128)(2,1)}, bf16[512,1024]{1,0:T(8,128)(2,1)S(1)}, u32[]{:S(2)}, u32[]{:S(2)}) collective-permute-start(bf16[512,1024]{1,0:T(8,128)(2,1)} %pad_maximum_fusion.refs_4_), channel_id=1, source_target_pairs={{0,12},{1,13},{2,14},{3,15},{4,0},{5,1},{6,2},{7,3},{8,4},{9,5},{1... | collective-permute-start | bytes 3145736 | tf_op jit(solution)/shard_map/ppermute | solution.py:31
  79.9 20.7 %collective-permute-start.19 = (bf16[512,1024]{1,0:T(8,128)(2,1)}, bf16[512,1024]{1,0:T(8,128)(2,1)S(1)}, u32[]{:S(2)}, u32[]{:S(2)}) collective-permute-start(bf16[512,1024]{1,0:T(8,128)(2,1)} %pad_maximum_fusion.1.refs_6_), channel_id=1, source_target_pairs={{0,4},{1,5},{2,6},{3,7},{4,8},{5,9},{6,10},{7,11},{8,12},{9,13},{1... | collective-permute-start | bytes 3145736 | tf_op jit(solution)/shard_map/ppermute | solution.py:31
  111.3 22.1 %all-to-all-start = ((f32[128,1,128]{2,1,0:T(1,128)}), f32[128,1,128]{2,1,0:T(1,128)S(1)}, u32[]{:S(2)}, u32[]{:S(2)}) async-start(f32[128,1,128]{2,1,0:T(1,128)} %broadcast_in_dim.2), calls=%async_computation | async-start | bytes 131072 | tf_op jit(solution)/shard_map/all_to_all | solution.py:287
  (10 other events, 89.2 us)

commit v8 on v7

--- a/solution.py
+++ b/solution.py
@@ -43,8 +43,11 @@
     xs = [[refs.pop(0) for _ in block] for block in terms]
     w_ref, left_ref = refs.pop(0), refs.pop(0)
     sum_ref, sum_proj_ref = (refs.pop(0), refs.pop(0)) if started else (None, None)
-    right_ref, cot_ref = (refs.pop(0), refs.pop(0)) if final else (None, None)
-    out_ref, proj_ref = refs
+    right_ref, cot_ref, seat_ref = [refs.pop(0) for _ in range(3)] if final else [None] * 3
+    if final:
+        table_ref, proj_ref, out_ref = refs
+    else:
+        out_ref, proj_ref = refs
     rows, extent = xs[0][0].shape
     width = extent // SIDE
     members = rows // TOK
@@ -102,6 +105,14 @@
                 term = cot[:, cols] * (act * act)
                 sums += jnp.sum(term, axis=0, keepdims=True)
             out_ref[slot : slot + 1, :] += sums
+
+    if final:
+
+        @pl.when(pl.program_id(0) == pl.num_programs(0) - 1)
+        def _():
+            fitness = jnp.sum(out_ref[...], axis=1, keepdims=True) / -math.sqrt(TOK * FF)
+            table = jnp.sum(seat_ref[...] * fitness, axis=0, keepdims=True)
+            table_ref[...] = jnp.broadcast_to(table[None], table_ref.shape)
 
 
 def stage(blocks, idx, weight, left_own, limit, sums=None, score=None):
@@ -136,11 +147,15 @@
         ]
     else:
         members = total // TOK
-        in_specs += [placed, placed]
-        operands += list(score)
-        out_specs = pl.BlockSpec((members, LANES), whole)
-        out_shape = jax.ShapeDtypeStruct((members, LANES), jnp.float32)
-        scratch = [pltpu.VMEM((total, LANES), jnp.float32)]
+        in_specs += [placed] * 3
+        operands += list(score[:3])
+        devices, table = score[3], score[2].shape[1]
+        out_specs = pl.BlockSpec((devices, 1, table), lambda n, idx: (0, 0, 0))
+        out_shape = jax.ShapeDtypeStruct((devices, 1, table), jnp.float32)
+        scratch = [
+            pltpu.VMEM((total, LANES), jnp.float32),
+            pltpu.VMEM((members, LANES), jnp.float32),
+        ]
     flops = 2 * sum(len(t) for t in terms) * rows * extent * columns
     return pl.pallas_call(
         functools.partial(stage_kernel, terms, sums is not None, score is not None),
@@ -274,17 +289,14 @@
     far, sums, blocks = lax.optimization_barrier((far, sums, blocks))
     other = {o: send(blocks[o], o, -1) for o in both}
     sums = stage(terms((far, (3, 3))), idx, weight, left_own, VMEM_LIMITS[1], sums)
-    scores = stage(
-        terms((other, (2, 1))), idx, weight, left_own, VMEM_LIMITS[2], sums, (right_own, cotangent)
-    )
-    partial = -jnp.sum(scores, axis=1) / math.sqrt(TOK * FF)
-    seated = seat[:, :owned].astype(jnp.float32)
-    table = jnp.sum(seated * partial[None, :], 1)
-
     everywhere = ("pop", "mp")
     devices = lax.axis_size("pop") * lax.axis_size("mp")
-    copies = jnp.broadcast_to(table[None, :], (devices, members))
-    tables = lax.all_to_all(copies, everywhere, 0, 0, tiled=True)
+    seated = (seeds[:, None] == jnp.arange(members, dtype=jnp.int32)[None, :]).astype(jnp.float32)
+    copies = stage(
+        terms((other, (2, 1))), idx, weight, left_own, VMEM_LIMITS[2], sums,
+        (right_own, cotangent, seated, devices),
+    )
+    tables = lax.all_to_all(copies, everywhere, 0, 0, tiled=True).reshape(devices, members)
     row_share = weight.shape[0] // lax.axis_size("pop")
     at = lax.axis_index("pop").astype(jnp.int32).reshape(1)
     estimate, fitness = finish(

time: 136 us -> 136 us (level)
  starting transfers between devices: 37.7 us -> 41.8 us
  waiting for transfers between devices: 48.4 us -> 45.2 us
  local copies, waits for them, and re-layouts: 5.17 us -> 3.28 us
    ppermute x20, waiting for transfers between devices: 38.9 us -> 35.7 us  [shift(): return lax.ppermute(piece, 'mp', perm)]
    ppermute x20, starting transfers between devices: 25.1 us -> 27.3 us  [shift(): return lax.ppermute(piece, 'mp', perm)]
    all_to_all x1, starting transfers between devices: 12.6 us -> 14.6 us  [per_device(): lax.all_to_all(copies, everywhere, 0, 0, tiled=True)]
    unnamed x26 -> x24, local copies, waits for them, and re-layouts: 2.76 us -> 1.55 us
  transfers between devices with their start and end apart: 21 -> 21, of which waited for: 8 -> 7; matrix products, arithmetic and copies ran while one was open for 3% -> 3% of each run, Pallas kernels for 21% -> 21%
where the time goes in v8:
time: 136 us
  waiting for transfers between devices  45.2 us (33%)
  starting transfers between devices  41.8 us (31%)
  Pallas kernels  41.1 us (30%)
  local copies, waits for them, and re-layouts  3.28 us (2%)
  other arithmetic  2.71 us (2%)
    pallas_call x3, Pallas kernels, stage(): pl.pallas_call(functools.partial(stage_kernel, terms, sums is not None, s...  38.5 us
    ppermute x20, waiting for transfers between devices, shift(): return lax.ppermute(piece, 'mp', perm)  35.7 us
    ppermute x20, starting transfers between devices, shift(): return lax.ppermute(piece, 'mp', perm)  27.3 us
    all_to_all x1, starting transfers between devices, per_device(): lax.all_to_all(copies, everywhere, 0, 0, tiled=True)  14.6 us
    all_to_all x1, waiting for transfers between devices, per_device(): lax.all_to_all(copies, everywhere, 0, 0, tiled=True)  9.5 us
  transfers between devices with their start and end apart: 21, of which 7 were waited for; matrix products, arithmetic and copies ran while one was open for 3% of the time, Pallas kernels for 21%

profile of v8, /device:TPU:1, one launch (start us, length us, event | category | flops | bytes accessed | tf_op | source)
XLA Modules:
  0.0 135.7 jit_solution(13108824616171847370)
XLA Ops:
  0.6 1.4 fusion.10
  2.0 2.2 %collective-permute-start = (bf16[1024,256]{1,0:T(8,128)(2,1)S(1)}, bf16[1024,256]{1,0:T(8,128)(2,1)S(1)}, u32[]{:S(2)}, u32[]{:S(2)}) collective-permute-start(bf16[1024,256]{1,0:T(8,128)(2,1)S(1)} %get-tuple-element.39), channel_id=1, source_target_pairs={{0,1},{1,2},{2,3},{3,0},{4,5},{5,6},{6,7},{7,4},{8,9},{9,10},{10,1... | collective-permute-start | bytes 1572872 | tf_op jit(solution)/shard_map/ppermute | solution.py:31
  4.2 1.5 %collective-permute-start.1 = (bf16[1024,256]{1,0:T(8,128)(2,1)S(1)}, bf16[1024,256]{1,0:T(8,128)(2,1)S(1)}, u32[]{:S(2)}, u32[]{:S(2)}) collective-permute-start(bf16[1024,256]{1,0:T(8,128)(2,1)S(1)} %get-tuple-element.39), channel_id=1, source_target_pairs={{0,3},{1,0},{2,1},{3,2},{4,7},{5,4},{6,5},{7,6},{8,11},{9,8},{10,9... | collective-permute-start | bytes 1572872 | tf_op jit(solution)/shard_map/ppermute | solution.py:31
  5.7 1.2 collective-permute-start.8
  6.9 1.5 %collective-permute-start.9 = (bf16[1024,256]{1,0:T(8,128)(2,1)S(1)}, bf16[1024,256]{1,0:T(8,128)(2,1)S(1)}, u32[]{:S(2)}, u32[]{:S(2)}) collective-permute-start(bf16[1024,256]{1,0:T(8,128)(2,1)S(1)} %get-tuple-element.38), channel_id=1, source_target_pairs={{0,12},{1,13},{2,14},{3,15},{4,0},{5,1},{6,2},{7,3},{8,4},{9,5},{1... | collective-permute-start | bytes 1572872 | tf_op jit(solution)/shard_map/ppermute | solution.py:31
  8.5 8.7 %collective-permute-done = bf16[1024,256]{1,0:T(8,128)(2,1)S(1)} collective-permute-done((bf16[1024,256]{1,0:T(8,128)(2,1)S(1)}, bf16[1024,256]{1,0:T(8,128)(2,1)S(1)}, u32[]{:S(2)}, u32[]{:S(2)}) %collective-permute-start) | collective-permute-done | bytes 524320 | tf_op jit(solution)/shard_map/ppermute | solution.py:31
  17.3 2.7 %collective-permute-start.5 = (bf16[512,256]{1,0:T(8,128)(2,1)S(1)}, bf16[512,256]{1,0:T(8,128)(2,1)S(1)}, u32[]{:S(2)}, u32[]{:S(2)}) collective-permute-start(bf16[512,256]{1,0:T(8,128)(2,1)S(1)} %get-tuple-element.46), channel_id=1, source_target_pairs={{0,3},{1,0},{2,1},{3,2},{4,7},{5,4},{6,5},{7,6},{8,11},{9,8},{10,9... | collective-permute-start | bytes 786440 | tf_op jit(solution)/shard_map/ppermute | solution.py:31
  21.3 1.6 %collective-permute-start.13 = (bf16[512,256]{1,0:T(8,128)(2,1)S(1)}, bf16[512,256]{1,0:T(8,128)(2,1)S(1)}, u32[]{:S(2)}, u32[]{:S(2)}) collective-permute-start(bf16[512,256]{1,0:T(8,128)(2,1)S(1)} %get-tuple-element.42), channel_id=1, source_target_pairs={{0,12},{1,13},{2,14},{3,15},{4,0},{5,1},{6,2},{7,3},{8,4},{9,5},{1... | collective-permute-start | bytes 786440 | tf_op jit(solution)/shard_map/ppermute | solution.py:31
  22.9 1.9 %collective-permute-done.2 = bf16[512,256]{1,0:T(8,128)(2,1)S(1)} collective-permute-done((bf16[512,256]{1,0:T(8,128)(2,1)S(1)}, bf16[512,256]{1,0:T(8,128)(2,1)S(1)}, u32[]{:S(2)}, u32[]{:S(2)}) %collective-permute-start.2) | collective-permute-done | bytes 262176 | tf_op jit(solution)/shard_map/ppermute | solution.py:31
  27.2 1.7 %collective-permute-start.6 = (bf16[512,1024]{1,0:T(8,128)(2,1)}, bf16[512,1024]{1,0:T(8,128)(2,1)}, u32[]{:S(2)}, u32[]{:S(2)}) collective-permute-start(bf16[512,1024]{1,0:T(8,128)(2,1)} %pad_maximum_fusion.1.refs_6_), channel_id=1, source_target_pairs={{0,12},{1,13},{2,14},{3,15},{4,0},{5,1},{6,2},{7,3},{8,4},{9,5},{1... | collective-permute-start | bytes 3145736 | tf_op jit(solution)/shard_map/ppermute | solution.py:31
  30.2 2.7 %collective-permute-start.14 = (bf16[512,1024]{1,0:T(8,128)(2,1)}, bf16[512,1024]{1,0:T(8,128)(2,1)}, u32[]{:S(2)}, u32[]{:S(2)}) collective-permute-start(bf16[512,1024]{1,0:T(8,128)(2,1)} %pad_maximum_fusion.3.refs_2_), channel_id=1, source_target_pairs={{0,3},{1,0},{2,1},{3,2},{4,7},{5,4},{6,5},{7,6},{8,11},{9,8},{10,9... | collective-permute-start | bytes 3145736 | tf_op jit(solution)/shard_map/ppermute | solution.py:31
  33.2 16.9 %collective-permute-done.3.refs_5_ = bf16[512,1024]{1,0:T(8,128)(2,1)} collective-permute-done((bf16[512,1024]{1,0:T(8,128)(2,1)S(1)}, bf16[512,1024]{1,0:T(8,128)(2,1)}, u32[]{:S(2)}, u32[]{:S(2)}) %collective-permute-start.3) | collective-permute-done | bytes 1048608 | tf_op jit(solution)/shard_map/ppermute | solution.py:31
  50.1 2.7 %collective-permute-start.7 = (bf16[512,1024]{1,0:T(8,128)(2,1)}, bf16[512,1024]{1,0:T(8,128)(2,1)S(1)}, u32[]{:S(2)}, u32[]{:S(2)}) collective-permute-start(bf16[512,1024]{1,0:T(8,128)(2,1)} %collective-permute-done.6.refs_7_), channel_id=1, source_target_pairs={{0,12},{1,13},{2,14},{3,15},{4,0},{5,1},{6,2},{7,3},{8,4},{9,5},{1... | collective-permute-start | bytes 3145736 | tf_op jit(solution)/shard_map/ppermute | solution.py:31
  52.8 3.1 %collective-permute-start.15 = (bf16[512,1024]{1,0:T(8,128)(2,1)}, bf16[512,1024]{1,0:T(8,128)(2,1)S(1)}, u32[]{:S(2)}, u32[]{:S(2)}) collective-permute-start(bf16[512,1024]{1,0:T(8,128)(2,1)} %collective-permute-done.14.refs_3_), channel_id=1, source_target_pairs={{0,3},{1,0},{2,1},{3,2},{4,7},{5,4},{6,5},{7,6},{8,11},{9,8},{10,9... | collective-permute-start | bytes 3145736 | tf_op jit(solution)/shard_map/ppermute | solution.py:31
  56.5 1.5 %copy-done.5 = bf16[512,1024]{1,0:T(8,128)(2,1)S(1)} copy-done((bf16[512,1024]{1,0:T(8,128)(2,1)S(1)}, bf16[512,1024]{1,0:T(8,128)(2,1)}, u32[]{:S(2)}) %copy-start.5) | copy-done | bytes 1048600
  58.0 17.4 %shard_map.95 = (f32[2048,1024]{1,0:T(8,128)}, f32[2048,128]{1,0:T(8,128)S(1)}) custom-call(s32[32]{0:T(128)S(1)} %pad_add_fusion.idx_ref, bf16[512,1024]{1,0:T(8,128)(2,1)S(1)} %copy-done.5, bf16[512,1024]{1,0:T(8,128)(2,1)} %collective-permute-done.11.refs_1_, bf16[512,1024]{1,0:T(8,128)(2,1)} %pad_maximum_fusion.3.refs_2_, ...), custom_call_target="tpu_custom_call" | custom-call | flops 8589934592 | bytes 33554432 | tf_op jit(solution)/shard_map/pallas_call | solution.py:160
  75.4 2.5 %collective-permute-start.16 = (bf16[512,1024]{1,0:T(8,128)(2,1)S(1)}, bf16[512,1024]{1,0:T(8,128)(2,1)S(1)}, u32[]{:S(2)}, u32[]{:S(2)}) collective-permute-start(bf16[512,1024]{1,0:T(8,128)(2,1)S(1)} %copy-done.5), channel_id=1, source_target_pairs={{0,3},{1,0},{2,1},{3,2},{4,7},{5,4},{6,5},{7,6},{8,11},{9,8},{10,9... | collective-permute-start | bytes 3145736 | tf_op jit(solution)/shard_map/ppermute | solution.py:31
  79.7 10.6 %shard_map.96 = (f32[2048,1024]{1,0:T(8,128)S(1)}, f32[2048,128]{1,0:T(8,128)S(1)}) custom-call(s32[32]{0:T(128)S(1)} %pad_add_fusion.idx_ref, bf16[512,1024]{1,0:T(8,128)(2,1)S(1)} %collective-permute-done.12.refs_0_, bf16[512,1024]{1,0:T(8,128)(2,1)S(1)} %collective-permute-done.15.refs_1_, bf16[512,1024]{1,0:T(8,128)(2,1)S(1)} %collective-permute-done.4.refs_2_, ...), custom_call_target="tpu_custom_call" | custom-call | flops 4294967296 | bytes 16777216 | tf_op jit(solution)/shard_map/pallas_call | solution.py:160
  90.3 5.8 %collective-permute-done.16.refs_0_ = bf16[512,1024]{1,0:T(8,128)(2,1)S(1)} collective-permute-done((bf16[512,1024]{1,0:T(8,128)(2,1)S(1)}, bf16[512,1024]{1,0:T(8,128)(2,1)S(1)}, u32[]{:S(2)}, u32[]{:S(2)}) %collective-permute-start.16) | collective-permute-done | bytes 1048608 | tf_op jit(solution)/shard_map/ppermute | solution.py:31
  96.1 2.0 %collective-permute-done.17.refs_1_ = bf16[512,1024]{1,0:T(8,128)(2,1)S(1)} collective-permute-done((bf16[512,1024]{1,0:T(8,128)(2,1)}, bf16[512,1024]{1,0:T(8,128)(2,1)S(1)}, u32[]{:S(2)}, u32[]{:S(2)}) %collective-permute-start.17) | collective-permute-done | bytes 1048608 | tf_op jit(solution)/shard_map/ppermute | solution.py:31
  98.6 10.5 %shard_map.97 = f32[128,1,128]{2,1,0:T(1,128)} custom-call(s32[32]{0:T(128)S(1)} %pad_add_fusion.idx_ref, bf16[512,1024]{1,0:T(8,128)(2,1)S(1)} %collective-permute-done.16.refs_0_, bf16[512,1024]{1,0:T(8,128)(2,1)S(1)} %collective-permute-done.17.refs_1_, bf16[512,1024]{1,0:T(8,128)(2,1)S(1)} %collective-permute-done.18.refs_2_, ...), custom_call_target="tpu_custom_call" | custom-call | flops 4294967296 | bytes 16777216 | tf_op jit(solution)/shard_map/pallas_call | solution.py:160
  109.1 14.6 %all-to-all-start = ((f32[128,1,128]{2,1,0:T(1,128)}), f32[128,1,128]{2,1,0:T(1,128)S(1)}, u32[]{:S(2)}, u32[]{:S(2)}) async-start(f32[128,1,128]{2,1,0:T(1,128)} %shard_map.97), calls=%async_computation | async-start | bytes 131072 | tf_op jit(solution)/shard_map/all_to_all | solution.py:299
  123.6 9.5 %all-to-all-done = f32[128,1,128]{2,1,0:T(1,128)S(1)} async-done(((f32[128,1,128]{2,1,0:T(1,128)}), f32[128,1,128]{2,1,0:T(1,128)S(1)}, u32[]{:S(2)}, u32[]{:S(2)}) %all-to-all-start) | async-done | bytes 65568 | tf_op jit(solution)/shard_map/all_to_all | solution.py:299
  133.1 2.6 %shard_map.98 = (f32[512,1024]{1,0:T(8,128)}, f32[1,16]{1,0:T(1,128)}) custom-call(s32[1]{0:T(128)} %bitcast.at_ref, f32[128,128]{1,0:T(8,128)S(1)} %bitcast.9, f32[128,128]{1,0:T(8,128)S(1)} %get-tuple-element.50.seat_ref, bf16[128,4096]{1,0:T(8,128)(2,1)S(1)} %copy-done, bf16[128,1024]{1,0:T(8,128)(2,1)S(1)} %copy-done.6), custom_call_target="tpu_custom_call" | custom-call | tf_op jit(solution)/shard_map/pallas_call | solution.py:207
  (67 shorter events, 8.3 us)
Async XLA Ops:
  2.0 15.1 %collective-permute-start = (bf16[1024,256]{1,0:T(8,128)(2,1)S(1)}, bf16[1024,256]{1,0:T(8,128)(2,1)S(1)}, u32[]{:S(2)}, u32[]{:S(2)}) collective-permute-start(bf16[1024,256]{1,0:T(8,128)(2,1)S(1)} %get-tuple-element.39), channel_id=1, source_target_pairs={{0,1},{1,2},{2,3},{3,0},{4,5},{5,6},{6,7},{7,4},{8,9},{9,10},{10,1... | collective-permute-start | bytes 1572872 | tf_op jit(solution)/shard_map/ppermute | solution.py:31
  4.2 13.1 %collective-permute-start.1 = (bf16[1024,256]{1,0:T(8,128)(2,1)S(1)}, bf16[1024,256]{1,0:T(8,128)(2,1)S(1)}, u32[]{:S(2)}, u32[]{:S(2)}) collective-permute-start(bf16[1024,256]{1,0:T(8,128)(2,1)S(1)} %get-tuple-element.39), channel_id=1, source_target_pairs={{0,3},{1,0},{2,1},{3,2},{4,7},{5,4},{6,5},{7,6},{8,11},{9,8},{10,9... | collective-permute-start | bytes 1572872 | tf_op jit(solution)/shard_map/ppermute | solution.py:31
  5.7 14.3 %collective-permute-start.8 = (bf16[1024,256]{1,0:T(8,128)(2,1)S(1)}, bf16[1024,256]{1,0:T(8,128)(2,1)S(1)}, u32[]{:S(2)}, u32[]{:S(2)}) collective-permute-start(bf16[1024,256]{1,0:T(8,128)(2,1)S(1)} %get-tuple-element.38), channel_id=1, source_target_pairs={{0,4},{1,5},{2,6},{3,7},{4,8},{5,9},{6,10},{7,11},{8,12},{9,13},{1... | collective-permute-start | bytes 1572872 | tf_op jit(solution)/shard_map/ppermute | solution.py:31
  6.9 14.3 %collective-permute-start.9 = (bf16[1024,256]{1,0:T(8,128)(2,1)S(1)}, bf16[1024,256]{1,0:T(8,128)(2,1)S(1)}, u32[]{:S(2)}, u32[]{:S(2)}) collective-permute-start(bf16[1024,256]{1,0:T(8,128)(2,1)S(1)} %get-tuple-element.38), channel_id=1, source_target_pairs={{0,12},{1,13},{2,14},{3,15},{4,0},{5,1},{6,2},{7,3},{8,4},{9,5},{1... | collective-permute-start | bytes 1572872 | tf_op jit(solution)/shard_map/ppermute | solution.py:31
  17.2 7.7 %collective-permute-start.2 = (bf16[512,256]{1,0:T(8,128)(2,1)S(1)}, bf16[512,256]{1,0:T(8,128)(2,1)S(1)}, u32[]{:S(2)}, u32[]{:S(2)}) collective-permute-start(bf16[512,256]{1,0:T(8,128)(2,1)S(1)} %get-tuple-element.45), channel_id=1, source_target_pairs={{0,1},{1,2},{2,3},{3,0},{4,5},{5,6},{6,7},{7,4},{8,9},{9,10},{10,1... | collective-permute-start | bytes 786440 | tf_op jit(solution)/shard_map/ppermute | solution.py:31
  17.3 8.8 %collective-permute-start.5 = (bf16[512,256]{1,0:T(8,128)(2,1)S(1)}, bf16[512,256]{1,0:T(8,128)(2,1)S(1)}, u32[]{:S(2)}, u32[]{:S(2)}) collective-permute-start(bf16[512,256]{1,0:T(8,128)(2,1)S(1)} %get-tuple-element.46), channel_id=1, source_target_pairs={{0,3},{1,0},{2,1},{3,2},{4,7},{5,4},{6,5},{7,6},{8,11},{9,8},{10,9... | collective-permute-start | bytes 786440 | tf_op jit(solution)/shard_map/ppermute | solution.py:31
  20.1 8.8 %collective-permute-start.10 = (bf16[512,256]{1,0:T(8,128)(2,1)S(1)}, bf16[512,256]{1,0:T(8,128)(2,1)S(1)}, u32[]{:S(2)}, u32[]{:S(2)}) collective-permute-start(bf16[512,256]{1,0:T(8,128)(2,1)S(1)} %get-tuple-element.41), channel_id=1, source_target_pairs={{0,4},{1,5},{2,6},{3,7},{4,8},{5,9},{6,10},{7,11},{8,12},{9,13},{1... | collective-permute-start | bytes 786440 | tf_op jit(solution)/shard_map/ppermute | solution.py:31
  21.3 7.8 %collective-permute-start.13 = (bf16[512,256]{1,0:T(8,128)(2,1)S(1)}, bf16[512,256]{1,0:T(8,128)(2,1)S(1)}, u32[]{:S(2)}, u32[]{:S(2)}) collective-permute-start(bf16[512,256]{1,0:T(8,128)(2,1)S(1)} %get-tuple-element.42), channel_id=1, source_target_pairs={{0,12},{1,13},{2,14},{3,15},{4,0},{5,1},{6,2},{7,3},{8,4},{9,5},{1... | collective-permute-start | bytes 786440 | tf_op jit(solution)/shard_map/ppermute | solution.py:31
  25.0 27.8 %copy-start.2 = (bf16[512,1024]{1,0:T(8,128)(2,1)}, bf16[512,1024]{1,0:T(8,128)(2,1)S(1)}, u32[]{:S(2)}) copy-start(bf16[512,1024]{1,0:T(8,128)(2,1)S(1)} %pad_maximum_fusion.refs_4_) | copy-start | bytes 3145732
  25.0 25.1 %collective-permute-start.3 = (bf16[512,1024]{1,0:T(8,128)(2,1)S(1)}, bf16[512,1024]{1,0:T(8,128)(2,1)}, u32[]{:S(2)}, u32[]{:S(2)}) collective-permute-start(bf16[512,1024]{1,0:T(8,128)(2,1)S(1)} %pad_maximum_fusion.refs_4_), channel_id=1, source_target_pairs={{0,4},{1,5},{2,6},{3,7},{4,8},{5,9},{6,10},{7,11},{8,12},{9,13},{1... | collective-permute-start | bytes 3145736 | tf_op jit(solution)/shard_map/ppermute | solution.py:31
  27.2 22.9 %collective-permute-start.6 = (bf16[512,1024]{1,0:T(8,128)(2,1)}, bf16[512,1024]{1,0:T(8,128)(2,1)}, u32[]{:S(2)}, u32[]{:S(2)}) collective-permute-start(bf16[512,1024]{1,0:T(8,128)(2,1)} %pad_maximum_fusion.1.refs_6_), channel_id=1, source_target_pairs={{0,12},{1,13},{2,14},{3,15},{4,0},{5,1},{6,2},{7,3},{8,4},{9,5},{1... | collective-permute-start | bytes 3145736 | tf_op jit(solution)/shard_map/ppermute | solution.py:31
  28.9 27.1 %copy-start = (bf16[128,4096]{1,0:T(8,128)(2,1)S(1)}, bf16[128,4096]{1,0:T(8,128)(2,1)}, u32[]{:S(2)}) copy-start(bf16[128,4096]{1,0:T(8,128)(2,1)} %left_ref.1) | copy-start | bytes 3145732
  29.0 26.9 %copy-start.4 = (bf16[512,1024]{1,0:T(8,128)(2,1)}, bf16[512,1024]{1,0:T(8,128)(2,1)S(1)}, u32[]{:S(2)}) copy-start(bf16[512,1024]{1,0:T(8,128)(2,1)S(1)} %pad_maximum_fusion.2.refs_0_) | copy-start | bytes 3145732
  29.0 23.8 %collective-permute-start.11 = (bf16[512,1024]{1,0:T(8,128)(2,1)S(1)}, bf16[512,1024]{1,0:T(8,128)(2,1)}, u32[]{:S(2)}, u32[]{:S(2)}) collective-permute-start(bf16[512,1024]{1,0:T(8,128)(2,1)S(1)} %pad_maximum_fusion.2.refs_0_), channel_id=1, source_target_pairs={{0,1},{1,2},{2,3},{3,0},{4,5},{5,6},{6,7},{7,4},{8,9},{9,10},{10,1... | collective-permute-start | bytes 3145736 | tf_op jit(solution)/shard_map/ppermute | solution.py:31
  30.2 22.6 %collective-permute-start.14 = (bf16[512,1024]{1,0:T(8,128)(2,1)}, bf16[512,1024]{1,0:T(8,128)(2,1)}, u32[]{:S(2)}, u32[]{:S(2)}) collective-permute-start(bf16[512,1024]{1,0:T(8,128)(2,1)} %pad_maximum_fusion.3.refs_2_), channel_id=1, source_target_pairs={{0,3},{1,0},{2,1},{3,2},{4,7},{5,4},{6,5},{7,6},{8,11},{9,8},{10,9... | collective-permute-start | bytes 3145736 | tf_op jit(solution)/shard_map/ppermute | solution.py:31
  50.1 25.3 %collective-permute-start.4 = (bf16[512,1024]{1,0:T(8,128)(2,1)}, bf16[512,1024]{1,0:T(8,128)(2,1)S(1)}, u32[]{:S(2)}, u32[]{:S(2)}) collective-permute-start(bf16[512,1024]{1,0:T(8,128)(2,1)} %collective-permute-done.3.refs_5_), channel_id=1, source_target_pairs={{0,4},{1,5},{2,6},{3,7},{4,8},{5,9},{6,10},{7,11},{8,12},{9,13},{1... | collective-permute-start | bytes 3145736 | tf_op jit(solution)/shard_map/ppermute | solution.py:31
  50.1 25.3 %collective-permute-start.7 = (bf16[512,1024]{1,0:T(8,128)(2,1)}, bf16[512,1024]{1,0:T(8,128)(2,1)S(1)}, u32[]{:S(2)}, u32[]{:S(2)}) collective-permute-start(bf16[512,1024]{1,0:T(8,128)(2,1)} %collective-permute-done.6.refs_7_), channel_id=1, source_target_pairs={{0,12},{1,13},{2,14},{3,15},{4,0},{5,1},{6,2},{7,3},{8,4},{9,5},{1... | collective-permute-start | bytes 3145736 | tf_op jit(solution)/shard_map/ppermute | solution.py:31
  52.8 22.6 %collective-permute-start.12 = (bf16[512,1024]{1,0:T(8,128)(2,1)}, bf16[512,1024]{1,0:T(8,128)(2,1)S(1)}, u32[]{:S(2)}, u32[]{:S(2)}) collective-permute-start(bf16[512,1024]{1,0:T(8,128)(2,1)} %collective-permute-done.11.refs_1_), channel_id=1, source_target_pairs={{0,1},{1,2},{2,3},{3,0},{4,5},{5,6},{6,7},{7,4},{8,9},{9,10},{10,1... | collective-permute-start | bytes 3145736 | tf_op jit(solution)/shard_map/ppermute | solution.py:31
  52.8 22.6 %collective-permute-start.15 = (bf16[512,1024]{1,0:T(8,128)(2,1)}, bf16[512,1024]{1,0:T(8,128)(2,1)S(1)}, u32[]{:S(2)}, u32[]{:S(2)}) collective-permute-start(bf16[512,1024]{1,0:T(8,128)(2,1)} %collective-permute-done.14.refs_3_), channel_id=1, source_target_pairs={{0,3},{1,0},{2,1},{3,2},{4,7},{5,4},{6,5},{7,6},{8,11},{9,8},{10,9... | collective-permute-start | bytes 3145736 | tf_op jit(solution)/shard_map/ppermute | solution.py:31
  75.4 20.7 %collective-permute-start.16 = (bf16[512,1024]{1,0:T(8,128)(2,1)S(1)}, bf16[512,1024]{1,0:T(8,128)(2,1)S(1)}, u32[]{:S(2)}, u32[]{:S(2)}) collective-permute-start(bf16[512,1024]{1,0:T(8,128)(2,1)S(1)} %copy-done.5), channel_id=1, source_target_pairs={{0,3},{1,0},{2,1},{3,2},{4,7},{5,4},{6,5},{7,6},{8,11},{9,8},{10,9... | collective-permute-start | bytes 3145736 | tf_op jit(solution)/shard_map/ppermute | solution.py:31
  77.9 20.2 %collective-permute-start.17 = (bf16[512,1024]{1,0:T(8,128)(2,1)}, bf16[512,1024]{1,0:T(8,128)(2,1)S(1)}, u32[]{:S(2)}, u32[]{:S(2)}) collective-permute-start(bf16[512,1024]{1,0:T(8,128)(2,1)} %pad_maximum_fusion.3.refs_2_), channel_id=1, source_target_pairs={{0,1},{1,2},{2,3},{3,0},{4,5},{5,6},{6,7},{7,4},{8,9},{9,10},{10,1... | collective-permute-start | bytes 3145736 | tf_op jit(solution)/shard_map/ppermute | solution.py:31
  77.9 20.2 %collective-permute-start.18 = (bf16[512,1024]{1,0:T(8,128)(2,1)S(1)}, bf16[512,1024]{1,0:T(8,128)(2,1)S(1)}, u32[]{:S(2)}, u32[]{:S(2)}) collective-permute-start(bf16[512,1024]{1,0:T(8,128)(2,1)S(1)} %copy-done.3), channel_id=1, source_target_pairs={{0,12},{1,13},{2,14},{3,15},{4,0},{5,1},{6,2},{7,3},{8,4},{9,5},{1... | collective-permute-start | bytes 3145736 | tf_op jit(solution)/shard_map/ppermute | solution.py:31
  78.8 19.7 %collective-permute-start.19 = (bf16[512,1024]{1,0:T(8,128)(2,1)}, bf16[512,1024]{1,0:T(8,128)(2,1)S(1)}, u32[]{:S(2)}, u32[]{:S(2)}) collective-permute-start(bf16[512,1024]{1,0:T(8,128)(2,1)} %pad_maximum_fusion.1.refs_6_), channel_id=1, source_target_pairs={{0,4},{1,5},{2,6},{3,7},{4,8},{5,9},{6,10},{7,11},{8,12},{9,13},{1... | collective-permute-start | bytes 3145736 | tf_op jit(solution)/shard_map/ppermute | solution.py:31
  109.1 24.1 %all-to-all-start = ((f32[128,1,128]{2,1,0:T(1,128)}), f32[128,1,128]{2,1,0:T(1,128)S(1)}, u32[]{:S(2)}, u32[]{:S(2)}) async-start(f32[128,1,128]{2,1,0:T(1,128)} %shard_map.97), calls=%async_computation | async-start | bytes 131072 | tf_op jit(solution)/shard_map/all_to_all | solution.py:299
  (9 other events, 107.1 us)

commit v9 on v8

--- a/solution.py
+++ b/solution.py
@@ -84,9 +84,12 @@
             out_ref[...] = jnp.zeros(out_ref.shape, jnp.float32)
 
     here = pl.ds(pl.multiple_of(pl.program_id(0) * COLS, COLS), COLS) if final else slice(None)
+    ahead = product(0, w_ref)
     for b in range(len(terms)):
-        base = product(b, w_ref)
-        if started:
+        base = ahead
+        if b + 1 < len(terms):
+            ahead = product(b + 1, w_ref)
+        if started and not final:
             base += sum_ref[b * rows : (b + 1) * rows, here]
         if not final:
             out_ref[b * rows : (b + 1) * rows, :] = base
@@ -98,10 +101,12 @@
             proj = proj_ref[there, :]
             right = right_ref[slot : slot + 1, here]
             cot = cot_ref[there, here].astype(jnp.float32)
+            carried = sum_ref[there, here]
             sums = jnp.zeros((1, LANES), jnp.float32)
             for g in range(COLS // LANES):
                 cols = slice(g * LANES, (g + 1) * LANES)
-                act = jnp.maximum(base[token, cols] + proj * right[:, cols], 0.0)
+                rest = carried[:, cols] + proj * right[:, cols]
+                act = jnp.maximum(base[token, cols] + rest, 0.0)
                 term = cot[:, cols] * (act * act)
                 sums += jnp.sum(term, axis=0, keepdims=True)
             out_ref[slot : slot + 1, :] += sums

time: 136 us -> 136 us (level)
  no operation moved by 1% of the time
where the time goes in v9:
time: 136 us
  waiting for transfers between devices  45.2 us (33%)
  starting transfers between devices  41.8 us (31%)
  Pallas kernels  41.1 us (30%)
  local copies, waits for them, and re-layouts  3.28 us (2%)
  other arithmetic  2.71 us (2%)
    pallas_call x3, Pallas kernels, stage(): pl.pallas_call(functools.partial(stage_kernel, terms, sums is not None, s...  38.5 us
    ppermute x20, waiting for transfers between devices, shift(): return lax.ppermute(piece, 'mp', perm)  35.7 us
    ppermute x20, starting transfers between devices, shift(): return lax.ppermute(piece, 'mp', perm)  27.3 us
    all_to_all x1, starting transfers between devices, per_device(): lax.all_to_all(copies, everywhere, 0, 0, tiled=True)  14.6 us
    all_to_all x1, waiting for transfers between devices, per_device(): lax.all_to_all(copies, everywhere, 0, 0, tiled=True)  9.5 us
  transfers between devices with their start and end apart: 21, of which 7 were waited for; matrix products, arithmetic and copies ran while one was open for 3% of the time, Pallas kernels for 21%

profile of v9, /device:TPU:1, one launch (start us, length us, event | category | flops | bytes accessed | tf_op | source)
XLA Modules:
  0.0 135.8 jit_solution(16978899484470654067)
XLA Ops:
  0.6 1.4 fusion.10
  2.0 2.2 %collective-permute-start = (bf16[1024,256]{1,0:T(8,128)(2,1)S(1)}, bf16[1024,256]{1,0:T(8,128)(2,1)S(1)}, u32[]{:S(2)}, u32[]{:S(2)}) collective-permute-start(bf16[1024,256]{1,0:T(8,128)(2,1)S(1)} %get-tuple-element.39), channel_id=1, source_target_pairs={{0,1},{1,2},{2,3},{3,0},{4,5},{5,6},{6,7},{7,4},{8,9},{9,10},{10,1... | collective-permute-start | bytes 1572872 | tf_op jit(solution)/shard_map/ppermute | solution.py:31
  4.2 1.5 %collective-permute-start.1 = (bf16[1024,256]{1,0:T(8,128)(2,1)S(1)}, bf16[1024,256]{1,0:T(8,128)(2,1)S(1)}, u32[]{:S(2)}, u32[]{:S(2)}) collective-permute-start(bf16[1024,256]{1,0:T(8,128)(2,1)S(1)} %get-tuple-element.39), channel_id=1, source_target_pairs={{0,3},{1,0},{2,1},{3,2},{4,7},{5,4},{6,5},{7,6},{8,11},{9,8},{10,9... | collective-permute-start | bytes 1572872 | tf_op jit(solution)/shard_map/ppermute | solution.py:31
  5.7 1.2 collective-permute-start.8
  6.9 1.5 %collective-permute-start.9 = (bf16[1024,256]{1,0:T(8,128)(2,1)S(1)}, bf16[1024,256]{1,0:T(8,128)(2,1)S(1)}, u32[]{:S(2)}, u32[]{:S(2)}) collective-permute-start(bf16[1024,256]{1,0:T(8,128)(2,1)S(1)} %get-tuple-element.38), channel_id=1, source_target_pairs={{0,12},{1,13},{2,14},{3,15},{4,0},{5,1},{6,2},{7,3},{8,4},{9,5},{1... | collective-permute-start | bytes 1572872 | tf_op jit(solution)/shard_map/ppermute | solution.py:31
  8.5 8.7 %collective-permute-done = bf16[1024,256]{1,0:T(8,128)(2,1)S(1)} collective-permute-done((bf16[1024,256]{1,0:T(8,128)(2,1)S(1)}, bf16[1024,256]{1,0:T(8,128)(2,1)S(1)}, u32[]{:S(2)}, u32[]{:S(2)}) %collective-permute-start) | collective-permute-done | bytes 524320 | tf_op jit(solution)/shard_map/ppermute | solution.py:31
  17.3 2.7 %collective-permute-start.5 = (bf16[512,256]{1,0:T(8,128)(2,1)S(1)}, bf16[512,256]{1,0:T(8,128)(2,1)S(1)}, u32[]{:S(2)}, u32[]{:S(2)}) collective-permute-start(bf16[512,256]{1,0:T(8,128)(2,1)S(1)} %get-tuple-element.46), channel_id=1, source_target_pairs={{0,3},{1,0},{2,1},{3,2},{4,7},{5,4},{6,5},{7,6},{8,11},{9,8},{10,9... | collective-permute-start | bytes 786440 | tf_op jit(solution)/shard_map/ppermute | solution.py:31
  21.3 1.6 %collective-permute-start.13 = (bf16[512,256]{1,0:T(8,128)(2,1)S(1)}, bf16[512,256]{1,0:T(8,128)(2,1)S(1)}, u32[]{:S(2)}, u32[]{:S(2)}) collective-permute-start(bf16[512,256]{1,0:T(8,128)(2,1)S(1)} %get-tuple-element.42), channel_id=1, source_target_pairs={{0,12},{1,13},{2,14},{3,15},{4,0},{5,1},{6,2},{7,3},{8,4},{9,5},{1... | collective-permute-start | bytes 786440 | tf_op jit(solution)/shard_map/ppermute | solution.py:31
  22.9 1.9 %collective-permute-done.2 = bf16[512,256]{1,0:T(8,128)(2,1)S(1)} collective-permute-done((bf16[512,256]{1,0:T(8,128)(2,1)S(1)}, bf16[512,256]{1,0:T(8,128)(2,1)S(1)}, u32[]{:S(2)}, u32[]{:S(2)}) %collective-permute-start.2) | collective-permute-done | bytes 262176 | tf_op jit(solution)/shard_map/ppermute | solution.py:31
  27.2 1.7 %collective-permute-start.6 = (bf16[512,1024]{1,0:T(8,128)(2,1)}, bf16[512,1024]{1,0:T(8,128)(2,1)}, u32[]{:S(2)}, u32[]{:S(2)}) collective-permute-start(bf16[512,1024]{1,0:T(8,128)(2,1)} %pad_maximum_fusion.1.refs_6_), channel_id=1, source_target_pairs={{0,12},{1,13},{2,14},{3,15},{4,0},{5,1},{6,2},{7,3},{8,4},{9,5},{1... | collective-permute-start | bytes 3145736 | tf_op jit(solution)/shard_map/ppermute | solution.py:31
  30.2 2.7 %collective-permute-start.14 = (bf16[512,1024]{1,0:T(8,128)(2,1)}, bf16[512,1024]{1,0:T(8,128)(2,1)}, u32[]{:S(2)}, u32[]{:S(2)}) collective-permute-start(bf16[512,1024]{1,0:T(8,128)(2,1)} %pad_maximum_fusion.3.refs_2_), channel_id=1, source_target_pairs={{0,3},{1,0},{2,1},{3,2},{4,7},{5,4},{6,5},{7,6},{8,11},{9,8},{10,9... | collective-permute-start | bytes 3145736 | tf_op jit(solution)/shard_map/ppermute | solution.py:31
  33.2 16.9 %collective-permute-done.3.refs_5_ = bf16[512,1024]{1,0:T(8,128)(2,1)} collective-permute-done((bf16[512,1024]{1,0:T(8,128)(2,1)S(1)}, bf16[512,1024]{1,0:T(8,128)(2,1)}, u32[]{:S(2)}, u32[]{:S(2)}) %collective-permute-start.3) | collective-permute-done | bytes 1048608 | tf_op jit(solution)/shard_map/ppermute | solution.py:31
  50.1 2.7 %collective-permute-start.7 = (bf16[512,1024]{1,0:T(8,128)(2,1)}, bf16[512,1024]{1,0:T(8,128)(2,1)S(1)}, u32[]{:S(2)}, u32[]{:S(2)}) collective-permute-start(bf16[512,1024]{1,0:T(8,128)(2,1)} %collective-permute-done.6.refs_7_), channel_id=1, source_target_pairs={{0,12},{1,13},{2,14},{3,15},{4,0},{5,1},{6,2},{7,3},{8,4},{9,5},{1... | collective-permute-start | bytes 3145736 | tf_op jit(solution)/shard_map/ppermute | solution.py:31
  52.8 3.1 %collective-permute-start.15 = (bf16[512,1024]{1,0:T(8,128)(2,1)}, bf16[512,1024]{1,0:T(8,128)(2,1)S(1)}, u32[]{:S(2)}, u32[]{:S(2)}) collective-permute-start(bf16[512,1024]{1,0:T(8,128)(2,1)} %collective-permute-done.14.refs_3_), channel_id=1, source_target_pairs={{0,3},{1,0},{2,1},{3,2},{4,7},{5,4},{6,5},{7,6},{8,11},{9,8},{10,9... | collective-permute-start | bytes 3145736 | tf_op jit(solution)/shard_map/ppermute | solution.py:31
  56.5 1.5 %copy-done.5 = bf16[512,1024]{1,0:T(8,128)(2,1)S(1)} copy-done((bf16[512,1024]{1,0:T(8,128)(2,1)S(1)}, bf16[512,1024]{1,0:T(8,128)(2,1)}, u32[]{:S(2)}) %copy-start.5) | copy-done | bytes 1048600
  58.0 17.4 %shard_map.95 = (f32[2048,1024]{1,0:T(8,128)}, f32[2048,128]{1,0:T(8,128)S(1)}) custom-call(s32[32]{0:T(128)S(1)} %pad_add_fusion.idx_ref, bf16[512,1024]{1,0:T(8,128)(2,1)S(1)} %copy-done.5, bf16[512,1024]{1,0:T(8,128)(2,1)} %collective-permute-done.11.refs_1_, bf16[512,1024]{1,0:T(8,128)(2,1)} %pad_maximum_fusion.3.refs_2_, ...), custom_call_target="tpu_custom_call" | custom-call | flops 8589934592 | bytes 33554432 | tf_op jit(solution)/shard_map/pallas_call | solution.py:165
  75.4 2.5 %collective-permute-start.16 = (bf16[512,1024]{1,0:T(8,128)(2,1)S(1)}, bf16[512,1024]{1,0:T(8,128)(2,1)S(1)}, u32[]{:S(2)}, u32[]{:S(2)}) collective-permute-start(bf16[512,1024]{1,0:T(8,128)(2,1)S(1)} %copy-done.5), channel_id=1, source_target_pairs={{0,3},{1,0},{2,1},{3,2},{4,7},{5,4},{6,5},{7,6},{8,11},{9,8},{10,9... | collective-permute-start | bytes 3145736 | tf_op jit(solution)/shard_map/ppermute | solution.py:31
  79.7 10.6 %shard_map.96 = (f32[2048,1024]{1,0:T(8,128)S(1)}, f32[2048,128]{1,0:T(8,128)S(1)}) custom-call(s32[32]{0:T(128)S(1)} %pad_add_fusion.idx_ref, bf16[512,1024]{1,0:T(8,128)(2,1)S(1)} %collective-permute-done.12.refs_0_, bf16[512,1024]{1,0:T(8,128)(2,1)S(1)} %collective-permute-done.15.refs_1_, bf16[512,1024]{1,0:T(8,128)(2,1)S(1)} %collective-permute-done.4.refs_2_, ...), custom_call_target="tpu_custom_call" | custom-call | flops 4294967296 | bytes 16777216 | tf_op jit(solution)/shard_map/pallas_call | solution.py:165
  90.3 5.8 %collective-permute-done.16.refs_0_ = bf16[512,1024]{1,0:T(8,128)(2,1)S(1)} collective-permute-done((bf16[512,1024]{1,0:T(8,128)(2,1)S(1)}, bf16[512,1024]{1,0:T(8,128)(2,1)S(1)}, u32[]{:S(2)}, u32[]{:S(2)}) %collective-permute-start.16) | collective-permute-done | bytes 1048608 | tf_op jit(solution)/shard_map/ppermute | solution.py:31
  96.1 2.0 %collective-permute-done.17.refs_1_ = bf16[512,1024]{1,0:T(8,128)(2,1)S(1)} collective-permute-done((bf16[512,1024]{1,0:T(8,128)(2,1)}, bf16[512,1024]{1,0:T(8,128)(2,1)S(1)}, u32[]{:S(2)}, u32[]{:S(2)}) %collective-permute-start.17) | collective-permute-done | bytes 1048608 | tf_op jit(solution)/shard_map/ppermute | solution.py:31
  98.6 10.5 %shard_map.97 = f32[128,1,128]{2,1,0:T(1,128)} custom-call(s32[32]{0:T(128)S(1)} %pad_add_fusion.idx_ref, bf16[512,1024]{1,0:T(8,128)(2,1)S(1)} %collective-permute-done.16.refs_0_, bf16[512,1024]{1,0:T(8,128)(2,1)S(1)} %collective-permute-done.17.refs_1_, bf16[512,1024]{1,0:T(8,128)(2,1)S(1)} %collective-permute-done.18.refs_2_, ...), custom_call_target="tpu_custom_call" | custom-call | flops 4294967296 | bytes 16777216 | tf_op jit(solution)/shard_map/pallas_call | solution.py:165
  109.1 14.6 %all-to-all-start = ((f32[128,1,128]{2,1,0:T(1,128)}), f32[128,1,128]{2,1,0:T(1,128)S(1)}, u32[]{:S(2)}, u32[]{:S(2)}) async-start(f32[128,1,128]{2,1,0:T(1,128)} %shard_map.97), calls=%async_computation | async-start | bytes 131072 | tf_op jit(solution)/shard_map/all_to_all | solution.py:304
  123.7 9.5 %all-to-all-done = f32[128,1,128]{2,1,0:T(1,128)S(1)} async-done(((f32[128,1,128]{2,1,0:T(1,128)}), f32[128,1,128]{2,1,0:T(1,128)S(1)}, u32[]{:S(2)}, u32[]{:S(2)}) %all-to-all-start) | async-done | bytes 65568 | tf_op jit(solution)/shard_map/all_to_all | solution.py:304
  133.1 2.6 %shard_map.98 = (f32[512,1024]{1,0:T(8,128)}, f32[1,16]{1,0:T(1,128)}) custom-call(s32[1]{0:T(128)} %bitcast.at_ref, f32[128,128]{1,0:T(8,128)S(1)} %bitcast.9, f32[128,128]{1,0:T(8,128)S(1)} %get-tuple-element.50.seat_ref, bf16[128,4096]{1,0:T(8,128)(2,1)S(1)} %copy-done, bf16[128,1024]{1,0:T(8,128)(2,1)S(1)} %copy-done.6), custom_call_target="tpu_custom_call" | custom-call | tf_op jit(solution)/shard_map/pallas_call | solution.py:212
  (67 shorter events, 8.3 us)
Async XLA Ops:
  2.0 15.1 %collective-permute-start = (bf16[1024,256]{1,0:T(8,128)(2,1)S(1)}, bf16[1024,256]{1,0:T(8,128)(2,1)S(1)}, u32[]{:S(2)}, u32[]{:S(2)}) collective-permute-start(bf16[1024,256]{1,0:T(8,128)(2,1)S(1)} %get-tuple-element.39), channel_id=1, source_target_pairs={{0,1},{1,2},{2,3},{3,0},{4,5},{5,6},{6,7},{7,4},{8,9},{9,10},{10,1... | collective-permute-start | bytes 1572872 | tf_op jit(solution)/shard_map/ppermute | solution.py:31
  4.2 13.1 %collective-permute-start.1 = (bf16[1024,256]{1,0:T(8,128)(2,1)S(1)}, bf16[1024,256]{1,0:T(8,128)(2,1)S(1)}, u32[]{:S(2)}, u32[]{:S(2)}) collective-permute-start(bf16[1024,256]{1,0:T(8,128)(2,1)S(1)} %get-tuple-element.39), channel_id=1, source_target_pairs={{0,3},{1,0},{2,1},{3,2},{4,7},{5,4},{6,5},{7,6},{8,11},{9,8},{10,9... | collective-permute-start | bytes 1572872 | tf_op jit(solution)/shard_map/ppermute | solution.py:31
  5.7 14.3 %collective-permute-start.8 = (bf16[1024,256]{1,0:T(8,128)(2,1)S(1)}, bf16[1024,256]{1,0:T(8,128)(2,1)S(1)}, u32[]{:S(2)}, u32[]{:S(2)}) collective-permute-start(bf16[1024,256]{1,0:T(8,128)(2,1)S(1)} %get-tuple-element.38), channel_id=1, source_target_pairs={{0,4},{1,5},{2,6},{3,7},{4,8},{5,9},{6,10},{7,11},{8,12},{9,13},{1... | collective-permute-start | bytes 1572872 | tf_op jit(solution)/shard_map/ppermute | solution.py:31
  6.9 14.3 %collective-permute-start.9 = (bf16[1024,256]{1,0:T(8,128)(2,1)S(1)}, bf16[1024,256]{1,0:T(8,128)(2,1)S(1)}, u32[]{:S(2)}, u32[]{:S(2)}) collective-permute-start(bf16[1024,256]{1,0:T(8,128)(2,1)S(1)} %get-tuple-element.38), channel_id=1, source_target_pairs={{0,12},{1,13},{2,14},{3,15},{4,0},{5,1},{6,2},{7,3},{8,4},{9,5},{1... | collective-permute-start | bytes 1572872 | tf_op jit(solution)/shard_map/ppermute | solution.py:31
  17.2 7.7 %collective-permute-start.2 = (bf16[512,256]{1,0:T(8,128)(2,1)S(1)}, bf16[512,256]{1,0:T(8,128)(2,1)S(1)}, u32[]{:S(2)}, u32[]{:S(2)}) collective-permute-start(bf16[512,256]{1,0:T(8,128)(2,1)S(1)} %get-tuple-element.45), channel_id=1, source_target_pairs={{0,1},{1,2},{2,3},{3,0},{4,5},{5,6},{6,7},{7,4},{8,9},{9,10},{10,1... | collective-permute-start | bytes 786440 | tf_op jit(solution)/shard_map/ppermute | solution.py:31
  17.3 8.8 %collective-permute-start.5 = (bf16[512,256]{1,0:T(8,128)(2,1)S(1)}, bf16[512,256]{1,0:T(8,128)(2,1)S(1)}, u32[]{:S(2)}, u32[]{:S(2)}) collective-permute-start(bf16[512,256]{1,0:T(8,128)(2,1)S(1)} %get-tuple-element.46), channel_id=1, source_target_pairs={{0,3},{1,0},{2,1},{3,2},{4,7},{5,4},{6,5},{7,6},{8,11},{9,8},{10,9... | collective-permute-start | bytes 786440 | tf_op jit(solution)/shard_map/ppermute | solution.py:31
  20.1 8.8 %collective-permute-start.10 = (bf16[512,256]{1,0:T(8,128)(2,1)S(1)}, bf16[512,256]{1,0:T(8,128)(2,1)S(1)}, u32[]{:S(2)}, u32[]{:S(2)}) collective-permute-start(bf16[512,256]{1,0:T(8,128)(2,1)S(1)} %get-tuple-element.41), channel_id=1, source_target_pairs={{0,4},{1,5},{2,6},{3,7},{4,8},{5,9},{6,10},{7,11},{8,12},{9,13},{1... | collective-permute-start | bytes 786440 | tf_op jit(solution)/shard_map/ppermute | solution.py:31
  21.3 7.8 %collective-permute-start.13 = (bf16[512,256]{1,0:T(8,128)(2,1)S(1)}, bf16[512,256]{1,0:T(8,128)(2,1)S(1)}, u32[]{:S(2)}, u32[]{:S(2)}) collective-permute-start(bf16[512,256]{1,0:T(8,128)(2,1)S(1)} %get-tuple-element.42), channel_id=1, source_target_pairs={{0,12},{1,13},{2,14},{3,15},{4,0},{5,1},{6,2},{7,3},{8,4},{9,5},{1... | collective-permute-start | bytes 786440 | tf_op jit(solution)/shard_map/ppermute | solution.py:31
  25.0 27.8 %copy-start.2 = (bf16[512,1024]{1,0:T(8,128)(2,1)}, bf16[512,1024]{1,0:T(8,128)(2,1)S(1)}, u32[]{:S(2)}) copy-start(bf16[512,1024]{1,0:T(8,128)(2,1)S(1)} %pad_maximum_fusion.refs_4_) | copy-start | bytes 3145732
  25.0 25.1 %collective-permute-start.3 = (bf16[512,1024]{1,0:T(8,128)(2,1)S(1)}, bf16[512,1024]{1,0:T(8,128)(2,1)}, u32[]{:S(2)}, u32[]{:S(2)}) collective-permute-start(bf16[512,1024]{1,0:T(8,128)(2,1)S(1)} %pad_maximum_fusion.refs_4_), channel_id=1, source_target_pairs={{0,4},{1,5},{2,6},{3,7},{4,8},{5,9},{6,10},{7,11},{8,12},{9,13},{1... | collective-permute-start | bytes 3145736 | tf_op jit(solution)/shard_map/ppermute | solution.py:31
  27.2 22.9 %collective-permute-start.6 = (bf16[512,1024]{1,0:T(8,128)(2,1)}, bf16[512,1024]{1,0:T(8,128)(2,1)}, u32[]{:S(2)}, u32[]{:S(2)}) collective-permute-start(bf16[512,1024]{1,0:T(8,128)(2,1)} %pad_maximum_fusion.1.refs_6_), channel_id=1, source_target_pairs={{0,12},{1,13},{2,14},{3,15},{4,0},{5,1},{6,2},{7,3},{8,4},{9,5},{1... | collective-permute-start | bytes 3145736 | tf_op jit(solution)/shard_map/ppermute | solution.py:31
  28.9 27.1 %copy-start = (bf16[128,4096]{1,0:T(8,128)(2,1)S(1)}, bf16[128,4096]{1,0:T(8,128)(2,1)}, u32[]{:S(2)}) copy-start(bf16[128,4096]{1,0:T(8,128)(2,1)} %left_ref.1) | copy-start | bytes 3145732
  29.0 26.9 %copy-start.4 = (bf16[512,1024]{1,0:T(8,128)(2,1)}, bf16[512,1024]{1,0:T(8,128)(2,1)S(1)}, u32[]{:S(2)}) copy-start(bf16[512,1024]{1,0:T(8,128)(2,1)S(1)} %pad_maximum_fusion.2.refs_0_) | copy-start | bytes 3145732
  29.0 23.8 %collective-permute-start.11 = (bf16[512,1024]{1,0:T(8,128)(2,1)S(1)}, bf16[512,1024]{1,0:T(8,128)(2,1)}, u32[]{:S(2)}, u32[]{:S(2)}) collective-permute-start(bf16[512,1024]{1,0:T(8,128)(2,1)S(1)} %pad_maximum_fusion.2.refs_0_), channel_id=1, source_target_pairs={{0,1},{1,2},{2,3},{3,0},{4,5},{5,6},{6,7},{7,4},{8,9},{9,10},{10,1... | collective-permute-start | bytes 3145736 | tf_op jit(solution)/shard_map/ppermute | solution.py:31
  30.2 22.6 %collective-permute-start.14 = (bf16[512,1024]{1,0:T(8,128)(2,1)}, bf16[512,1024]{1,0:T(8,128)(2,1)}, u32[]{:S(2)}, u32[]{:S(2)}) collective-permute-start(bf16[512,1024]{1,0:T(8,128)(2,1)} %pad_maximum_fusion.3.refs_2_), channel_id=1, source_target_pairs={{0,3},{1,0},{2,1},{3,2},{4,7},{5,4},{6,5},{7,6},{8,11},{9,8},{10,9... | collective-permute-start | bytes 3145736 | tf_op jit(solution)/shard_map/ppermute | solution.py:31
  50.1 25.2 %collective-permute-start.4 = (bf16[512,1024]{1,0:T(8,128)(2,1)}, bf16[512,1024]{1,0:T(8,128)(2,1)S(1)}, u32[]{:S(2)}, u32[]{:S(2)}) collective-permute-start(bf16[512,1024]{1,0:T(8,128)(2,1)} %collective-permute-done.3.refs_5_), channel_id=1, source_target_pairs={{0,4},{1,5},{2,6},{3,7},{4,8},{5,9},{6,10},{7,11},{8,12},{9,13},{1... | collective-permute-start | bytes 3145736 | tf_op jit(solution)/shard_map/ppermute | solution.py:31
  50.1 25.2 %collective-permute-start.7 = (bf16[512,1024]{1,0:T(8,128)(2,1)}, bf16[512,1024]{1,0:T(8,128)(2,1)S(1)}, u32[]{:S(2)}, u32[]{:S(2)}) collective-permute-start(bf16[512,1024]{1,0:T(8,128)(2,1)} %collective-permute-done.6.refs_7_), channel_id=1, source_target_pairs={{0,12},{1,13},{2,14},{3,15},{4,0},{5,1},{6,2},{7,3},{8,4},{9,5},{1... | collective-permute-start | bytes 3145736 | tf_op jit(solution)/shard_map/ppermute | solution.py:31
  52.8 22.6 %collective-permute-start.12 = (bf16[512,1024]{1,0:T(8,128)(2,1)}, bf16[512,1024]{1,0:T(8,128)(2,1)S(1)}, u32[]{:S(2)}, u32[]{:S(2)}) collective-permute-start(bf16[512,1024]{1,0:T(8,128)(2,1)} %collective-permute-done.11.refs_1_), channel_id=1, source_target_pairs={{0,1},{1,2},{2,3},{3,0},{4,5},{5,6},{6,7},{7,4},{8,9},{9,10},{10,1... | collective-permute-start | bytes 3145736 | tf_op jit(solution)/shard_map/ppermute | solution.py:31
  52.8 22.6 %collective-permute-start.15 = (bf16[512,1024]{1,0:T(8,128)(2,1)}, bf16[512,1024]{1,0:T(8,128)(2,1)S(1)}, u32[]{:S(2)}, u32[]{:S(2)}) collective-permute-start(bf16[512,1024]{1,0:T(8,128)(2,1)} %collective-permute-done.14.refs_3_), channel_id=1, source_target_pairs={{0,3},{1,0},{2,1},{3,2},{4,7},{5,4},{6,5},{7,6},{8,11},{9,8},{10,9... | collective-permute-start | bytes 3145736 | tf_op jit(solution)/shard_map/ppermute | solution.py:31
  75.4 20.7 %collective-permute-start.16 = (bf16[512,1024]{1,0:T(8,128)(2,1)S(1)}, bf16[512,1024]{1,0:T(8,128)(2,1)S(1)}, u32[]{:S(2)}, u32[]{:S(2)}) collective-permute-start(bf16[512,1024]{1,0:T(8,128)(2,1)S(1)} %copy-done.5), channel_id=1, source_target_pairs={{0,3},{1,0},{2,1},{3,2},{4,7},{5,4},{6,5},{7,6},{8,11},{9,8},{10,9... | collective-permute-start | bytes 3145736 | tf_op jit(solution)/shard_map/ppermute | solution.py:31
  77.9 20.2 %collective-permute-start.17 = (bf16[512,1024]{1,0:T(8,128)(2,1)}, bf16[512,1024]{1,0:T(8,128)(2,1)S(1)}, u32[]{:S(2)}, u32[]{:S(2)}) collective-permute-start(bf16[512,1024]{1,0:T(8,128)(2,1)} %pad_maximum_fusion.3.refs_2_), channel_id=1, source_target_pairs={{0,1},{1,2},{2,3},{3,0},{4,5},{5,6},{6,7},{7,4},{8,9},{9,10},{10,1... | collective-permute-start | bytes 3145736 | tf_op jit(solution)/shard_map/ppermute | solution.py:31
  77.9 20.2 %collective-permute-start.18 = (bf16[512,1024]{1,0:T(8,128)(2,1)S(1)}, bf16[512,1024]{1,0:T(8,128)(2,1)S(1)}, u32[]{:S(2)}, u32[]{:S(2)}) collective-permute-start(bf16[512,1024]{1,0:T(8,128)(2,1)S(1)} %copy-done.3), channel_id=1, source_target_pairs={{0,12},{1,13},{2,14},{3,15},{4,0},{5,1},{6,2},{7,3},{8,4},{9,5},{1... | collective-permute-start | bytes 3145736 | tf_op jit(solution)/shard_map/ppermute | solution.py:31
  78.8 19.7 %collective-permute-start.19 = (bf16[512,1024]{1,0:T(8,128)(2,1)}, bf16[512,1024]{1,0:T(8,128)(2,1)S(1)}, u32[]{:S(2)}, u32[]{:S(2)}) collective-permute-start(bf16[512,1024]{1,0:T(8,128)(2,1)} %pad_maximum_fusion.1.refs_6_), channel_id=1, source_target_pairs={{0,4},{1,5},{2,6},{3,7},{4,8},{5,9},{6,10},{7,11},{8,12},{9,13},{1... | collective-permute-start | bytes 3145736 | tf_op jit(solution)/shard_map/ppermute | solution.py:31
  109.1 24.1 %all-to-all-start = ((f32[128,1,128]{2,1,0:T(1,128)}), f32[128,1,128]{2,1,0:T(1,128)S(1)}, u32[]{:S(2)}, u32[]{:S(2)}) async-start(f32[128,1,128]{2,1,0:T(1,128)} %shard_map.97), calls=%async_computation | async-start | bytes 131072 | tf_op jit(solution)/shard_map/all_to_all | solution.py:304
  (9 other events, 107.1 us)

commit v10 on v9

--- a/solution.py
+++ b/solution.py
@@ -19,7 +19,7 @@
 
 COLS = 256
 LANES = 128
-VMEM_LIMITS = (36 << 20, 26 << 20, 20 << 20)
+VMEM_LIMITS = (50 << 20, 26 << 20, 16 << 20)
 
 
 def shift(piece, dx, dy):
@@ -290,10 +290,10 @@
 
     near = {o: send(blocks[o], o, 1) for o in both}
     far = {o: send(near[o], o, 1) for o in both}
-    sums = stage(terms((blocks, (0, 0)), (near, (1, 2))), idx, weight, left_own, VMEM_LIMITS[0])
+    sums = stage(terms((near, (1, 2))), idx, weight, left_own, VMEM_LIMITS[0])
     far, sums, blocks = lax.optimization_barrier((far, sums, blocks))
     other = {o: send(blocks[o], o, -1) for o in both}
-    sums = stage(terms((far, (3, 3))), idx, weight, left_own, VMEM_LIMITS[1], sums)
+    sums = stage(terms((blocks, (0, 0)), (far, (3, 3))), idx, weight, left_own, VMEM_LIMITS[1], sums)
     everywhere = ("pop", "mp")
     devices = lax.axis_size("pop") * lax.axis_size("mp")
     seated = (seeds[:, None] == jnp.arange(members, dtype=jnp.int32)[None, :]).astype(jnp.float32)

time: 136 us -> 138 us (1.015)
  starting transfers between devices: 41.8 us -> 38.2 us
  local copies, waits for them, and re-layouts: 3.28 us -> 6.45 us
  Pallas kernels: 41.1 us -> 44 us
  waiting for transfers between devices: 45.2 us -> 43.5 us
    unnamed x24 -> x30, local copies, waits for them, and re-layouts: 1.55 us -> 4.72 us
    pallas_call x3, Pallas kernels: 38.5 us -> 41.4 us  [stage(): pl.pallas_call(functools.partial(stage_kernel, terms, sums is not None, s...]
    ppermute x20, starting transfers between devices: 27.3 us -> 25 us  [shift(): return lax.ppermute(piece, 'mp', perm)]
    ppermute x20, waiting for transfers between devices: 35.7 us -> 34 us  [shift(): return lax.ppermute(piece, 'mp', perm)]
  transfers between devices with their start and end apart: 21 -> 21, of which waited for: 7 -> 7; matrix products, arithmetic and copies ran while one was open for 3% -> 4% of each run, Pallas kernels for 21% -> 22%
where the time goes in v10:
time: 138 us; the launch traced here: 137 us
  Pallas kernels  44 us (32%)
  waiting for transfers between devices  43.5 us (32%)
  starting transfers between devices  38.2 us (28%)
  local copies, waits for them, and re-layouts  6.45 us (5%)
  other arithmetic  2.72 us (2%)
  matrix products  1.72 us (1%)
    pallas_call x3, Pallas kernels, stage(): pl.pallas_call(functools.partial(stage_kernel, terms, sums is not None, s...  41.4 us
    ppermute x20, waiting for transfers between devices, shift(): return lax.ppermute(piece, 'mp', perm)  34 us
    ppermute x20, starting transfers between devices, shift(): return lax.ppermute(piece, 'mp', perm)  25 us
    all_to_all x1, starting transfers between devices, per_device(): lax.all_to_all(copies, everywhere, 0, 0, tiled=True)  13.2 us
    all_to_all x1, waiting for transfers between devices, per_device(): lax.all_to_all(copies, everywhere, 0, 0, tiled=True)  9.5 us
    unnamed x30, local copies, waits for them, and re-layouts  4.72 us
  transfers between devices with their start and end apart: 21, of which 7 were waited for; matrix products, arithmetic and copies ran while one was open for 4% of the time, Pallas kernels for 22%

profile of v10, /device:TPU:1, one launch (start us, length us, event | category | flops | bytes accessed | tf_op | source)
XLA Modules:
  0.0 137.5 jit_solution(7697870117667838053)
XLA Ops:
  0.6 1.4 fusion.10
  2.0 2.1 %collective-permute-start.8 = (bf16[1024,256]{1,0:T(8,128)(2,1)S(1)}, bf16[1024,256]{1,0:T(8,128)(2,1)S(1)}, u32[]{:S(2)}, u32[]{:S(2)}) collective-permute-start(bf16[1024,256]{1,0:T(8,128)(2,1)S(1)} %get-tuple-element.38), channel_id=1, source_target_pairs={{0,4},{1,5},{2,6},{3,7},{4,8},{5,9},{6,10},{7,11},{8,12},{9,13},{1... | collective-permute-start | bytes 1572872 | tf_op jit(solution)/shard_map/ppermute | solution.py:31
  4.1 1.3 collective-permute-start.9
  5.5 2.9 %collective-permute-start.1 = (bf16[1024,256]{1,0:T(8,128)(2,1)S(1)}, bf16[1024,256]{1,0:T(8,128)(2,1)S(1)}, u32[]{:S(2)}, u32[]{:S(2)}) collective-permute-start(bf16[1024,256]{1,0:T(8,128)(2,1)S(1)} %get-tuple-element.39), channel_id=1, source_target_pairs={{0,3},{1,0},{2,1},{3,2},{4,7},{5,4},{6,5},{7,6},{8,11},{9,8},{10,9... | collective-permute-start | bytes 1572872 | tf_op jit(solution)/shard_map/ppermute | solution.py:31
  8.4 8.2 %collective-permute-done.8 = bf16[1024,256]{1,0:T(8,128)(2,1)S(1)} collective-permute-done((bf16[1024,256]{1,0:T(8,128)(2,1)S(1)}, bf16[1024,256]{1,0:T(8,128)(2,1)S(1)}, u32[]{:S(2)}, u32[]{:S(2)}) %collective-permute-start.8) | collective-permute-done | bytes 524320 | tf_op jit(solution)/shard_map/ppermute | solution.py:31
  17.1 2.4 %collective-permute-start.13 = (bf16[512,256]{1,0:T(8,128)(2,1)S(1)}, bf16[512,256]{1,0:T(8,128)(2,1)S(1)}, u32[]{:S(2)}, u32[]{:S(2)}) collective-permute-start(bf16[512,256]{1,0:T(8,128)(2,1)S(1)} %get-tuple-element.42), channel_id=1, source_target_pairs={{0,12},{1,13},{2,14},{3,15},{4,0},{5,1},{6,2},{7,3},{8,4},{9,5},{1... | collective-permute-start | bytes 786440 | tf_op jit(solution)/shard_map/ppermute | solution.py:31
  19.5 3.1 %collective-permute-start.5 = (bf16[512,256]{1,0:T(8,128)(2,1)S(1)}, bf16[512,256]{1,0:T(8,128)(2,1)S(1)}, u32[]{:S(2)}, u32[]{:S(2)}) collective-permute-start(bf16[512,256]{1,0:T(8,128)(2,1)S(1)} %get-tuple-element.46), channel_id=1, source_target_pairs={{0,3},{1,0},{2,1},{3,2},{4,7},{5,4},{6,5},{7,6},{8,11},{9,8},{10,9... | collective-permute-start | bytes 786440 | tf_op jit(solution)/shard_map/ppermute | solution.py:31
  22.8 1.3 collective-permute-done.10
  24.2 1.8 %collective-permute-start.11 = (bf16[512,1024]{1,0:T(8,128)(2,1)S(1)}, bf16[512,1024]{1,0:T(8,128)(2,1)}, u32[]{:S(2)}, u32[]{:S(2)}) collective-permute-start(bf16[512,1024]{1,0:T(8,128)(2,1)S(1)} %pad_maximum_fusion.2.refs_0_), channel_id=1, source_target_pairs={{0,1},{1,2},{2,3},{3,0},{4,5},{5,6},{6,7},{7,4},{8,9},{9,10},{10,1... | collective-permute-start | bytes 3145736 | tf_op jit(solution)/shard_map/ppermute | solution.py:31
  26.1 1.5 %collective-permute-start.14 = (bf16[512,1024]{1,0:T(8,128)(2,1)S(1)}, bf16[512,1024]{1,0:T(8,128)(2,1)}, u32[]{:S(2)}, u32[]{:S(2)}) collective-permute-start(bf16[512,1024]{1,0:T(8,128)(2,1)S(1)} %pad_maximum_fusion.3.refs_2_), channel_id=1, source_target_pairs={{0,3},{1,0},{2,1},{3,2},{4,7},{5,4},{6,5},{7,6},{8,11},{9,8},{10,9... | collective-permute-start | bytes 3145736 | tf_op jit(solution)/shard_map/ppermute | solution.py:31
  28.8 2.3 %collective-permute-start.6 = (bf16[512,1024]{1,0:T(8,128)(2,1)}, bf16[512,1024]{1,0:T(8,128)(2,1)}, u32[]{:S(2)}, u32[]{:S(2)}) collective-permute-start(bf16[512,1024]{1,0:T(8,128)(2,1)} %pad_maximum_fusion.1.refs_6_), channel_id=1, source_target_pairs={{0,12},{1,13},{2,14},{3,15},{4,0},{5,1},{6,2},{7,3},{8,4},{9,5},{1... | collective-permute-start | bytes 3145736 | tf_op jit(solution)/shard_map/ppermute | solution.py:31
  32.2 19.8 %collective-permute-done.11.refs_0_ = bf16[512,1024]{1,0:T(8,128)(2,1)} collective-permute-done((bf16[512,1024]{1,0:T(8,128)(2,1)S(1)}, bf16[512,1024]{1,0:T(8,128)(2,1)}, u32[]{:S(2)}, u32[]{:S(2)}) %collective-permute-start.11) | collective-permute-done | bytes 1048608 | tf_op jit(solution)/shard_map/ppermute | solution.py:31
  52.0 2.7 %collective-permute-start.15 = (bf16[512,1024]{1,0:T(8,128)(2,1)}, bf16[512,1024]{1,0:T(8,128)(2,1)}, u32[]{:S(2)}, u32[]{:S(2)}) collective-permute-start(bf16[512,1024]{1,0:T(8,128)(2,1)} %collective-permute-done.14.refs_1_), channel_id=1, source_target_pairs={{0,3},{1,0},{2,1},{3,2},{4,7},{5,4},{6,5},{7,6},{8,11},{9,8},{10,9... | collective-permute-start | bytes 3145736 | tf_op jit(solution)/shard_map/ppermute | solution.py:31
  56.5 1.5 %fusion.refs_5_.refs_9_ = bf16[4096,128]{1,0:T(8,128)(2,1)} fusion(bf16[128,4096]{1,0:T(8,128)(2,1)S(1)} %copy-done.1, s32[128]{0:T(128)S(1)} %pad.4), kind=kOutput, calls=%fused_computation.1 | convolution fusion | flops 134758400 | bytes 2097664 | tf_op jit(solution)/shard_map/dot_general | solution.py:267
  58.0 13.1 %shard_map.95 = (f32[2048,1024]{1,0:T(8,128)}, f32[2048,128]{1,0:T(8,128)S(1)}) custom-call(s32[32]{0:T(128)S(1)} %pad_add_fusion.idx_ref, bf16[512,1024]{1,0:T(8,128)(2,1)} %collective-permute-done.11.refs_0_, bf16[512,1024]{1,0:T(8,128)(2,1)} %collective-permute-done.14.refs_1_, bf16[512,1024]{1,0:T(8,128)(2,1)} %collective-permute-done.3.refs_2_, ...), custom_call_target="tpu_custom_call" | custom-call | flops 4294967296 | bytes 16777216 | tf_op jit(solution)/shard_map/pallas_call | solution.py:165
  72.1 2.7 %collective-permute-done.12.refs_1_ = bf16[512,1024]{1,0:T(8,128)(2,1)} collective-permute-done((bf16[512,1024]{1,0:T(8,128)(2,1)}, bf16[512,1024]{1,0:T(8,128)(2,1)}, u32[]{:S(2)}, u32[]{:S(2)}) %collective-permute-start.12) | collective-permute-done | bytes 1048608 | tf_op jit(solution)/shard_map/ppermute | solution.py:31
  80.2 1.2 copy-done.4
  81.4 1.2 copy-done.6
  82.6 1.2 copy-done.9
  83.9 17.7 %shard_map.96 = (f32[2048,1024]{1,0:T(8,128)S(1)}, f32[2048,128]{1,0:T(8,128)S(1)}) custom-call(s32[32]{0:T(128)S(1)} %pad_add_fusion.idx_ref, bf16[512,1024]{1,0:T(8,128)(2,1)S(1)} %copy-done.4, bf16[512,1024]{1,0:T(8,128)(2,1)} %collective-permute-done.12.refs_1_, bf16[512,1024]{1,0:T(8,128)(2,1)S(1)} %copy-done.6, ...), custom_call_target="tpu_custom_call" | custom-call | flops 8589934592 | bytes 33554432 | tf_op jit(solution)/shard_map/pallas_call | solution.py:165
  101.6 10.5 %shard_map.97 = f32[128,1,128]{2,1,0:T(1,128)} custom-call(s32[32]{0:T(128)S(1)} %pad_add_fusion.idx_ref, bf16[512,1024]{1,0:T(8,128)(2,1)S(1)} %collective-permute-done.16.refs_0_, bf16[512,1024]{1,0:T(8,128)(2,1)S(1)} %collective-permute-done.17.refs_1_, bf16[512,1024]{1,0:T(8,128)(2,1)S(1)} %collective-permute-done.18.refs_2_, ...), custom_call_target="tpu_custom_call" | custom-call | flops 4294967296 | bytes 16777216 | tf_op jit(solution)/shard_map/pallas_call | solution.py:165
  112.1 13.2 %all-to-all-start = ((f32[128,1,128]{2,1,0:T(1,128)}), f32[128,1,128]{2,1,0:T(1,128)S(1)}, u32[]{:S(2)}, u32[]{:S(2)}) async-start(f32[128,1,128]{2,1,0:T(1,128)} %shard_map.97), calls=%async_computation | async-start | bytes 131072 | tf_op jit(solution)/shard_map/all_to_all | solution.py:304
  125.4 9.5 %all-to-all-done = f32[128,1,128]{2,1,0:T(1,128)S(1)} async-done(((f32[128,1,128]{2,1,0:T(1,128)}), f32[128,1,128]{2,1,0:T(1,128)S(1)}, u32[]{:S(2)}, u32[]{:S(2)}) %all-to-all-start) | async-done | bytes 65568 | tf_op jit(solution)/shard_map/all_to_all | solution.py:304
  134.9 2.6 %shard_map.98 = (f32[512,1024]{1,0:T(8,128)}, f32[1,16]{1,0:T(1,128)}) custom-call(s32[1]{0:T(128)} %bitcast.at_ref, f32[128,128]{1,0:T(8,128)S(1)} %bitcast.9, f32[128,128]{1,0:T(8,128)S(1)} %get-tuple-element.50.seat_ref, bf16[128,4096]{1,0:T(8,128)(2,1)S(1)} %copy-done.1, bf16[128,1024]{1,0:T(8,128)(2,1)S(1)} %copy-done.7), custom_call_target="tpu_custom_call" | custom-call | tf_op jit(solution)/shard_map/pallas_call | solution.py:212
  (73 shorter events, 11.4 us)
Async XLA Ops:
  2.0 14.6 %collective-permute-start.8 = (bf16[1024,256]{1,0:T(8,128)(2,1)S(1)}, bf16[1024,256]{1,0:T(8,128)(2,1)S(1)}, u32[]{:S(2)}, u32[]{:S(2)}) collective-permute-start(bf16[1024,256]{1,0:T(8,128)(2,1)S(1)} %get-tuple-element.38), channel_id=1, source_target_pairs={{0,4},{1,5},{2,6},{3,7},{4,8},{5,9},{6,10},{7,11},{8,12},{9,13},{1... | collective-permute-start | bytes 1572872 | tf_op jit(solution)/shard_map/ppermute | solution.py:31
  4.1 12.9 %collective-permute-start.9 = (bf16[1024,256]{1,0:T(8,128)(2,1)S(1)}, bf16[1024,256]{1,0:T(8,128)(2,1)S(1)}, u32[]{:S(2)}, u32[]{:S(2)}) collective-permute-start(bf16[1024,256]{1,0:T(8,128)(2,1)S(1)} %get-tuple-element.38), channel_id=1, source_target_pairs={{0,12},{1,13},{2,14},{3,15},{4,0},{5,1},{6,2},{7,3},{8,4},{9,5},{1... | collective-permute-start | bytes 1572872 | tf_op jit(solution)/shard_map/ppermute | solution.py:31
  5.5 14.0 %collective-permute-start.1 = (bf16[1024,256]{1,0:T(8,128)(2,1)S(1)}, bf16[1024,256]{1,0:T(8,128)(2,1)S(1)}, u32[]{:S(2)}, u32[]{:S(2)}) collective-permute-start(bf16[1024,256]{1,0:T(8,128)(2,1)S(1)} %get-tuple-element.39), channel_id=1, source_target_pairs={{0,3},{1,0},{2,1},{3,2},{4,7},{5,4},{6,5},{7,6},{8,11},{9,8},{10,9... | collective-permute-start | bytes 1572872 | tf_op jit(solution)/shard_map/ppermute | solution.py:31
  8.3 14.3 %collective-permute-start = (bf16[1024,256]{1,0:T(8,128)(2,1)S(1)}, bf16[1024,256]{1,0:T(8,128)(2,1)S(1)}, u32[]{:S(2)}, u32[]{:S(2)}) collective-permute-start(bf16[1024,256]{1,0:T(8,128)(2,1)S(1)} %get-tuple-element.39), channel_id=1, source_target_pairs={{0,1},{1,2},{2,3},{3,0},{4,5},{5,6},{6,7},{7,4},{8,9},{9,10},{10,1... | collective-permute-start | bytes 1572872 | tf_op jit(solution)/shard_map/ppermute | solution.py:31
  16.6 7.4 %collective-permute-start.10 = (bf16[512,256]{1,0:T(8,128)(2,1)S(1)}, bf16[512,256]{1,0:T(8,128)(2,1)S(1)}, u32[]{:S(2)}, u32[]{:S(2)}) collective-permute-start(bf16[512,256]{1,0:T(8,128)(2,1)S(1)} %get-tuple-element.41), channel_id=1, source_target_pairs={{0,4},{1,5},{2,6},{3,7},{4,8},{5,9},{6,10},{7,11},{8,12},{9,13},{1... | collective-permute-start | bytes 786440 | tf_op jit(solution)/shard_map/ppermute | solution.py:31
  17.1 8.9 %collective-permute-start.13 = (bf16[512,256]{1,0:T(8,128)(2,1)S(1)}, bf16[512,256]{1,0:T(8,128)(2,1)S(1)}, u32[]{:S(2)}, u32[]{:S(2)}) collective-permute-start(bf16[512,256]{1,0:T(8,128)(2,1)S(1)} %get-tuple-element.42), channel_id=1, source_target_pairs={{0,12},{1,13},{2,14},{3,15},{4,0},{5,1},{6,2},{7,3},{8,4},{9,5},{1... | collective-permute-start | bytes 786440 | tf_op jit(solution)/shard_map/ppermute | solution.py:31
  19.5 8.1 %collective-permute-start.5 = (bf16[512,256]{1,0:T(8,128)(2,1)S(1)}, bf16[512,256]{1,0:T(8,128)(2,1)S(1)}, u32[]{:S(2)}, u32[]{:S(2)}) collective-permute-start(bf16[512,256]{1,0:T(8,128)(2,1)S(1)} %get-tuple-element.46), channel_id=1, source_target_pairs={{0,3},{1,0},{2,1},{3,2},{4,7},{5,4},{6,5},{7,6},{8,11},{9,8},{10,9... | collective-permute-start | bytes 786440 | tf_op jit(solution)/shard_map/ppermute | solution.py:31
  22.7 8.4 %collective-permute-start.2 = (bf16[512,256]{1,0:T(8,128)(2,1)S(1)}, bf16[512,256]{1,0:T(8,128)(2,1)S(1)}, u32[]{:S(2)}, u32[]{:S(2)}) collective-permute-start(bf16[512,256]{1,0:T(8,128)(2,1)S(1)} %get-tuple-element.45), channel_id=1, source_target_pairs={{0,1},{1,2},{2,3},{3,0},{4,5},{5,6},{6,7},{7,4},{8,9},{9,10},{10,1... | collective-permute-start | bytes 786440 | tf_op jit(solution)/shard_map/ppermute | solution.py:31
  24.2 27.8 %collective-permute-start.11 = (bf16[512,1024]{1,0:T(8,128)(2,1)S(1)}, bf16[512,1024]{1,0:T(8,128)(2,1)}, u32[]{:S(2)}, u32[]{:S(2)}) collective-permute-start(bf16[512,1024]{1,0:T(8,128)(2,1)S(1)} %pad_maximum_fusion.2.refs_0_), channel_id=1, source_target_pairs={{0,1},{1,2},{2,3},{3,0},{4,5},{5,6},{6,7},{7,4},{8,9},{9,10},{10,1... | collective-permute-start | bytes 3145736 | tf_op jit(solution)/shard_map/ppermute | solution.py:31
  26.1 25.8 %collective-permute-start.14 = (bf16[512,1024]{1,0:T(8,128)(2,1)S(1)}, bf16[512,1024]{1,0:T(8,128)(2,1)}, u32[]{:S(2)}, u32[]{:S(2)}) collective-permute-start(bf16[512,1024]{1,0:T(8,128)(2,1)S(1)} %pad_maximum_fusion.3.refs_2_), channel_id=1, source_target_pairs={{0,3},{1,0},{2,1},{3,2},{4,7},{5,4},{6,5},{7,6},{8,11},{9,8},{10,9... | collective-permute-start | bytes 3145736 | tf_op jit(solution)/shard_map/ppermute | solution.py:31
  27.7 28.7 %copy-start.11 = (s32[16]{0:T(128)S(1)}, s32[16]{0:T(128)}, u32[]{:S(2)}) copy-start(s32[16]{0:T(128)} %param.13) | copy-start | bytes 196
  27.7 28.8 %copy-start.1 = (bf16[128,4096]{1,0:T(8,128)(2,1)S(1)}, bf16[128,4096]{1,0:T(8,128)(2,1)}, u32[]{:S(2)}) copy-start(bf16[128,4096]{1,0:T(8,128)(2,1)} %left_ref.1) | copy-start | bytes 3145732
  28.8 25.8 %collective-permute-start.6 = (bf16[512,1024]{1,0:T(8,128)(2,1)}, bf16[512,1024]{1,0:T(8,128)(2,1)}, u32[]{:S(2)}, u32[]{:S(2)}) collective-permute-start(bf16[512,1024]{1,0:T(8,128)(2,1)} %pad_maximum_fusion.1.refs_6_), channel_id=1, source_target_pairs={{0,12},{1,13},{2,14},{3,15},{4,0},{5,1},{6,2},{7,3},{8,4},{9,5},{1... | collective-permute-start | bytes 3145736 | tf_op jit(solution)/shard_map/ppermute | solution.py:31
  32.2 22.8 %collective-permute-start.3 = (bf16[512,1024]{1,0:T(8,128)(2,1)}, bf16[512,1024]{1,0:T(8,128)(2,1)}, u32[]{:S(2)}, u32[]{:S(2)}) collective-permute-start(bf16[512,1024]{1,0:T(8,128)(2,1)} %pad_maximum_fusion.refs_4_), channel_id=1, source_target_pairs={{0,4},{1,5},{2,6},{3,7},{4,8},{5,9},{6,10},{7,11},{8,12},{9,13},{1... | collective-permute-start | bytes 3145736 | tf_op jit(solution)/shard_map/ppermute | solution.py:31
  52.0 22.9 %collective-permute-start.12 = (bf16[512,1024]{1,0:T(8,128)(2,1)}, bf16[512,1024]{1,0:T(8,128)(2,1)}, u32[]{:S(2)}, u32[]{:S(2)}) collective-permute-start(bf16[512,1024]{1,0:T(8,128)(2,1)} %collective-permute-done.11.refs_0_), channel_id=1, source_target_pairs={{0,1},{1,2},{2,3},{3,0},{4,5},{5,6},{6,7},{7,4},{8,9},{9,10},{10,1... | collective-permute-start | bytes 3145736 | tf_op jit(solution)/shard_map/ppermute | solution.py:31
  52.0 22.9 %collective-permute-start.15 = (bf16[512,1024]{1,0:T(8,128)(2,1)}, bf16[512,1024]{1,0:T(8,128)(2,1)}, u32[]{:S(2)}, u32[]{:S(2)}) collective-permute-start(bf16[512,1024]{1,0:T(8,128)(2,1)} %collective-permute-done.14.refs_1_), channel_id=1, source_target_pairs={{0,3},{1,0},{2,1},{3,2},{4,7},{5,4},{6,5},{7,6},{8,11},{9,8},{10,9... | collective-permute-start | bytes 3145736 | tf_op jit(solution)/shard_map/ppermute | solution.py:31
  54.6 21.1 %collective-permute-start.7 = (bf16[512,1024]{1,0:T(8,128)(2,1)}, bf16[512,1024]{1,0:T(8,128)(2,1)}, u32[]{:S(2)}, u32[]{:S(2)}) collective-permute-start(bf16[512,1024]{1,0:T(8,128)(2,1)} %collective-permute-done.6.refs_3_), channel_id=1, source_target_pairs={{0,12},{1,13},{2,14},{3,15},{4,0},{5,1},{6,2},{7,3},{8,4},{9,5},{1... | collective-permute-start | bytes 3145736 | tf_op jit(solution)/shard_map/ppermute | solution.py:31
  55.0 21.9 %collective-permute-start.4 = (bf16[512,1024]{1,0:T(8,128)(2,1)}, bf16[512,1024]{1,0:T(8,128)(2,1)}, u32[]{:S(2)}, u32[]{:S(2)}) collective-permute-start(bf16[512,1024]{1,0:T(8,128)(2,1)} %collective-permute-done.3.refs_2_), channel_id=1, source_target_pairs={{0,4},{1,5},{2,6},{3,7},{4,8},{5,9},{6,10},{7,11},{8,12},{9,13},{1... | collective-permute-start | bytes 3145736 | tf_op jit(solution)/shard_map/ppermute | solution.py:31
  56.5 23.7 %slice-start = ((s8[8388608]{0:T(1024)(128)(4,1)}), s8[4194304]{0:T(1024)(128)(4,1)S(1)}, s32[]{:S(2)}) async-start(s8[8388608]{0:T(1024)(128)(4,1)} %bitcast.7), calls=%async_computation.1 | async-start | bytes 8388608
  76.9 24.6 %collective-permute-start.16 = (bf16[512,1024]{1,0:T(8,128)(2,1)}, bf16[512,1024]{1,0:T(8,128)(2,1)S(1)}, u32[]{:S(2)}, u32[]{:S(2)}) collective-permute-start(bf16[512,1024]{1,0:T(8,128)(2,1)} %copy-done.3), channel_id=1, source_target_pairs={{0,3},{1,0},{2,1},{3,2},{4,7},{5,4},{6,5},{7,6},{8,11},{9,8},{10,9... | collective-permute-start | bytes 3145736 | tf_op jit(solution)/shard_map/ppermute | solution.py:31
  77.4 24.2 %collective-permute-start.17 = (bf16[512,1024]{1,0:T(8,128)(2,1)}, bf16[512,1024]{1,0:T(8,128)(2,1)S(1)}, u32[]{:S(2)}, u32[]{:S(2)}) collective-permute-start(bf16[512,1024]{1,0:T(8,128)(2,1)} %copy-done.5), channel_id=1, source_target_pairs={{0,1},{1,2},{2,3},{3,0},{4,5},{5,6},{6,7},{7,4},{8,9},{9,10},{10,1... | collective-permute-start | bytes 3145736 | tf_op jit(solution)/shard_map/ppermute | solution.py:31
  78.4 23.2 %collective-permute-start.18 = (bf16[512,1024]{1,0:T(8,128)(2,1)}, bf16[512,1024]{1,0:T(8,128)(2,1)S(1)}, u32[]{:S(2)}, u32[]{:S(2)}) collective-permute-start(bf16[512,1024]{1,0:T(8,128)(2,1)} %pad_maximum_fusion.refs_4_), channel_id=1, source_target_pairs={{0,12},{1,13},{2,14},{3,15},{4,0},{5,1},{6,2},{7,3},{8,4},{9,5},{1... | collective-permute-start | bytes 3145736 | tf_op jit(solution)/shard_map/ppermute | solution.py:31
  78.7 22.8 %collective-permute-start.19 = (bf16[512,1024]{1,0:T(8,128)(2,1)}, bf16[512,1024]{1,0:T(8,128)(2,1)S(1)}, u32[]{:S(2)}, u32[]{:S(2)}) collective-permute-start(bf16[512,1024]{1,0:T(8,128)(2,1)} %pad_maximum_fusion.1.refs_6_), channel_id=1, source_target_pairs={{0,4},{1,5},{2,6},{3,7},{4,8},{5,9},{6,10},{7,11},{8,12},{9,13},{1... | collective-permute-start | bytes 3145736 | tf_op jit(solution)/shard_map/ppermute | solution.py:31
  112.1 22.7 %all-to-all-start = ((f32[128,1,128]{2,1,0:T(1,128)}), f32[128,1,128]{2,1,0:T(1,128)S(1)}, u32[]{:S(2)}, u32[]{:S(2)}) async-start(f32[128,1,128]{2,1,0:T(1,128)} %shard_map.97), calls=%async_computation | async-start | bytes 131072 | tf_op jit(solution)/shard_map/all_to_all | solution.py:304
  (12 other events, 111.6 us)

commit v11 on v10

--- a/solution.py
+++ b/solution.py
@@ -19,7 +19,7 @@
 
 COLS = 256
 LANES = 128
-VMEM_LIMITS = (50 << 20, 26 << 20, 16 << 20)
+VMEM_LIMITS = (52 << 20, 24 << 20, 24 << 20)
 
 
 def shift(piece, dx, dy):

time: 138 us -> 140 us (1.014)
  local copies, waits for them, and re-layouts: 6.45 us -> 8.63 us
    unnamed x30, local copies, waits for them, and re-layouts: 4.72 us -> 6.9 us
  transfers between devices with their start and end apart: 21 -> 21, of which waited for: 7 -> 7; matrix products, arithmetic and copies ran while one was open for 4% -> 3% of each run, Pallas kernels for 22% -> 22%
where the time goes in v11:
time: 140 us; the launch traced here: 139 us
  waiting for transfers between devices  43.5 us (31%)
  Pallas kernels  43.5 us (31%)
  starting transfers between devices  38.2 us (27%)
  local copies, waits for them, and re-layouts  8.63 us (6%)
  other arithmetic  2.72 us (2%)
  matrix products  1.72 us (1%)
    pallas_call x3, Pallas kernels, stage(): pl.pallas_call(functools.partial(stage_kernel, terms, sums is not None, s...  40.9 us
    ppermute x20, waiting for transfers between devices, shift(): return lax.ppermute(piece, 'mp', perm)  34 us
    ppermute x20, starting transfers between devices, shift(): return lax.ppermute(piece, 'mp', perm)  25 us
    all_to_all x1, starting transfers between devices, per_device(): lax.all_to_all(copies, everywhere, 0, 0, tiled=True)  13.2 us
    all_to_all x1, waiting for transfers between devices, per_device(): lax.all_to_all(copies, everywhere, 0, 0, tiled=True)  9.5 us
    unnamed x30, local copies, waits for them, and re-layouts  6.9 us
  transfers between devices with their start and end apart: 21, of which 7 were waited for; matrix products, arithmetic and copies ran while one was open for 3% of the time, Pallas kernels for 22%

profile of v11, /device:TPU:1, one launch (start us, length us, event | category | flops | bytes accessed | tf_op | source)
XLA Modules:
  0.0 139.2 jit_solution(3374686220457358186)
XLA Ops:
  0.6 1.4 fusion.10
  2.0 2.1 %collective-permute-start.8 = (bf16[1024,256]{1,0:T(8,128)(2,1)S(1)}, bf16[1024,256]{1,0:T(8,128)(2,1)S(1)}, u32[]{:S(2)}, u32[]{:S(2)}) collective-permute-start(bf16[1024,256]{1,0:T(8,128)(2,1)S(1)} %get-tuple-element.38), channel_id=1, source_target_pairs={{0,4},{1,5},{2,6},{3,7},{4,8},{5,9},{6,10},{7,11},{8,12},{9,13},{1... | collective-permute-start | bytes 1572872 | tf_op jit(solution)/shard_map/ppermute | solution.py:31
  4.1 1.3 collective-permute-start.9
  5.5 2.9 %collective-permute-start.1 = (bf16[1024,256]{1,0:T(8,128)(2,1)S(1)}, bf16[1024,256]{1,0:T(8,128)(2,1)S(1)}, u32[]{:S(2)}, u32[]{:S(2)}) collective-permute-start(bf16[1024,256]{1,0:T(8,128)(2,1)S(1)} %get-tuple-element.39), channel_id=1, source_target_pairs={{0,3},{1,0},{2,1},{3,2},{4,7},{5,4},{6,5},{7,6},{8,11},{9,8},{10,9... | collective-permute-start | bytes 1572872 | tf_op jit(solution)/shard_map/ppermute | solution.py:31
  8.4 8.2 %collective-permute-done.8 = bf16[1024,256]{1,0:T(8,128)(2,1)S(1)} collective-permute-done((bf16[1024,256]{1,0:T(8,128)(2,1)S(1)}, bf16[1024,256]{1,0:T(8,128)(2,1)S(1)}, u32[]{:S(2)}, u32[]{:S(2)}) %collective-permute-start.8) | collective-permute-done | bytes 524320 | tf_op jit(solution)/shard_map/ppermute | solution.py:31
  17.1 2.4 %collective-permute-start.13 = (bf16[512,256]{1,0:T(8,128)(2,1)S(1)}, bf16[512,256]{1,0:T(8,128)(2,1)S(1)}, u32[]{:S(2)}, u32[]{:S(2)}) collective-permute-start(bf16[512,256]{1,0:T(8,128)(2,1)S(1)} %get-tuple-element.42), channel_id=1, source_target_pairs={{0,12},{1,13},{2,14},{3,15},{4,0},{5,1},{6,2},{7,3},{8,4},{9,5},{1... | collective-permute-start | bytes 786440 | tf_op jit(solution)/shard_map/ppermute | solution.py:31
  19.5 3.1 %collective-permute-start.5 = (bf16[512,256]{1,0:T(8,128)(2,1)S(1)}, bf16[512,256]{1,0:T(8,128)(2,1)S(1)}, u32[]{:S(2)}, u32[]{:S(2)}) collective-permute-start(bf16[512,256]{1,0:T(8,128)(2,1)S(1)} %get-tuple-element.46), channel_id=1, source_target_pairs={{0,3},{1,0},{2,1},{3,2},{4,7},{5,4},{6,5},{7,6},{8,11},{9,8},{10,9... | collective-permute-start | bytes 786440 | tf_op jit(solution)/shard_map/ppermute | solution.py:31
  22.8 1.3 collective-permute-done.10
  24.2 1.8 %collective-permute-start.11 = (bf16[512,1024]{1,0:T(8,128)(2,1)S(1)}, bf16[512,1024]{1,0:T(8,128)(2,1)}, u32[]{:S(2)}, u32[]{:S(2)}) collective-permute-start(bf16[512,1024]{1,0:T(8,128)(2,1)S(1)} %pad_maximum_fusion.2.refs_0_), channel_id=1, source_target_pairs={{0,1},{1,2},{2,3},{3,0},{4,5},{5,6},{6,7},{7,4},{8,9},{9,10},{10,1... | collective-permute-start | bytes 3145736 | tf_op jit(solution)/shard_map/ppermute | solution.py:31
  26.1 1.5 %collective-permute-start.14 = (bf16[512,1024]{1,0:T(8,128)(2,1)S(1)}, bf16[512,1024]{1,0:T(8,128)(2,1)}, u32[]{:S(2)}, u32[]{:S(2)}) collective-permute-start(bf16[512,1024]{1,0:T(8,128)(2,1)S(1)} %pad_maximum_fusion.3.refs_2_), channel_id=1, source_target_pairs={{0,3},{1,0},{2,1},{3,2},{4,7},{5,4},{6,5},{7,6},{8,11},{9,8},{10,9... | collective-permute-start | bytes 3145736 | tf_op jit(solution)/shard_map/ppermute | solution.py:31
  28.8 2.3 %collective-permute-start.6 = (bf16[512,1024]{1,0:T(8,128)(2,1)}, bf16[512,1024]{1,0:T(8,128)(2,1)}, u32[]{:S(2)}, u32[]{:S(2)}) collective-permute-start(bf16[512,1024]{1,0:T(8,128)(2,1)} %pad_maximum_fusion.1.refs_6_), channel_id=1, source_target_pairs={{0,12},{1,13},{2,14},{3,15},{4,0},{5,1},{6,2},{7,3},{8,4},{9,5},{1... | collective-permute-start | bytes 3145736 | tf_op jit(solution)/shard_map/ppermute | solution.py:31
  32.2 19.8 %collective-permute-done.11.refs_0_ = bf16[512,1024]{1,0:T(8,128)(2,1)} collective-permute-done((bf16[512,1024]{1,0:T(8,128)(2,1)S(1)}, bf16[512,1024]{1,0:T(8,128)(2,1)}, u32[]{:S(2)}, u32[]{:S(2)}) %collective-permute-start.11) | collective-permute-done | bytes 1048608 | tf_op jit(solution)/shard_map/ppermute | solution.py:31
  52.0 2.7 %collective-permute-start.15 = (bf16[512,1024]{1,0:T(8,128)(2,1)}, bf16[512,1024]{1,0:T(8,128)(2,1)}, u32[]{:S(2)}, u32[]{:S(2)}) collective-permute-start(bf16[512,1024]{1,0:T(8,128)(2,1)} %collective-permute-done.14.refs_1_), channel_id=1, source_target_pairs={{0,3},{1,0},{2,1},{3,2},{4,7},{5,4},{6,5},{7,6},{8,11},{9,8},{10,9... | collective-permute-start | bytes 3145736 | tf_op jit(solution)/shard_map/ppermute | solution.py:31
  56.5 1.5 %fusion.refs_5_.refs_9_ = bf16[4096,128]{1,0:T(8,128)(2,1)} fusion(bf16[128,4096]{1,0:T(8,128)(2,1)S(1)} %copy-done.1, s32[128]{0:T(128)S(1)} %pad.4), kind=kOutput, calls=%fused_computation.1 | convolution fusion | flops 134758400 | bytes 2097664 | tf_op jit(solution)/shard_map/dot_general | solution.py:267
  58.0 13.1 %shard_map.95 = (f32[2048,1024]{1,0:T(8,128)}, f32[2048,128]{1,0:T(8,128)S(1)}) custom-call(s32[32]{0:T(128)S(1)} %pad_add_fusion.idx_ref, bf16[512,1024]{1,0:T(8,128)(2,1)} %collective-permute-done.11.refs_0_, bf16[512,1024]{1,0:T(8,128)(2,1)} %collective-permute-done.14.refs_1_, bf16[512,1024]{1,0:T(8,128)(2,1)} %collective-permute-done.3.refs_2_, ...), custom_call_target="tpu_custom_call" | custom-call | flops 4294967296 | bytes 16777216 | tf_op jit(solution)/shard_map/pallas_call | solution.py:165
  72.1 2.7 %collective-permute-done.12.refs_1_ = bf16[512,1024]{1,0:T(8,128)(2,1)} collective-permute-done((bf16[512,1024]{1,0:T(8,128)(2,1)}, bf16[512,1024]{1,0:T(8,128)(2,1)}, u32[]{:S(2)}, u32[]{:S(2)}) %collective-permute-start.12) | collective-permute-done | bytes 1048608 | tf_op jit(solution)/shard_map/ppermute | solution.py:31
  81.4 1.2 copy-done.6
  82.6 1.2 copy-done.9
  83.9 17.3 %shard_map.96 = (f32[2048,1024]{1,0:T(8,128)S(1)}, f32[2048,128]{1,0:T(8,128)S(1)}) custom-call(s32[32]{0:T(128)S(1)} %pad_add_fusion.idx_ref, bf16[512,1024]{1,0:T(8,128)(2,1)S(1)} %copy-done.4, bf16[512,1024]{1,0:T(8,128)(2,1)} %collective-permute-done.12.refs_1_, bf16[512,1024]{1,0:T(8,128)(2,1)S(1)} %copy-done.6, ...), custom_call_target="tpu_custom_call" | custom-call | flops 8589934592 | bytes 33554432 | tf_op jit(solution)/shard_map/pallas_call | solution.py:165
  101.2 2.2 %copy-done.2 = bf16[2048,1024]{1,0:T(8,128)(2,1)S(1)} copy-done((bf16[2048,1024]{1,0:T(8,128)(2,1)S(1)}, bf16[2048,1024]{1,0:T(8,128)(2,1)}, u32[]{:S(2)}) %copy-start.2) | copy-done | bytes 4194328
  103.4 10.5 %shard_map.97 = f32[128,1,128]{2,1,0:T(1,128)} custom-call(s32[32]{0:T(128)S(1)} %pad_add_fusion.idx_ref, bf16[512,1024]{1,0:T(8,128)(2,1)S(1)} %collective-permute-done.16.refs_0_, bf16[512,1024]{1,0:T(8,128)(2,1)S(1)} %collective-permute-done.17.refs_1_, bf16[512,1024]{1,0:T(8,128)(2,1)S(1)} %collective-permute-done.18.refs_2_, ...), custom_call_target="tpu_custom_call" | custom-call | flops 4294967296 | bytes 16777216 | tf_op jit(solution)/shard_map/pallas_call | solution.py:165
  113.8 13.2 %all-to-all-start = ((f32[128,1,128]{2,1,0:T(1,128)}), f32[128,1,128]{2,1,0:T(1,128)S(1)}, u32[]{:S(2)}, u32[]{:S(2)}) async-start(f32[128,1,128]{2,1,0:T(1,128)} %shard_map.97), calls=%async_computation | async-start | bytes 131072 | tf_op jit(solution)/shard_map/all_to_all | solution.py:304
  127.1 9.5 %all-to-all-done = f32[128,1,128]{2,1,0:T(1,128)S(1)} async-done(((f32[128,1,128]{2,1,0:T(1,128)}), f32[128,1,128]{2,1,0:T(1,128)S(1)}, u32[]{:S(2)}, u32[]{:S(2)}) %all-to-all-start) | async-done | bytes 65568 | tf_op jit(solution)/shard_map/all_to_all | solution.py:304
  136.6 2.6 %shard_map.98 = (f32[512,1024]{1,0:T(8,128)}, f32[1,16]{1,0:T(1,128)}) custom-call(s32[1]{0:T(128)} %bitcast.at_ref, f32[128,128]{1,0:T(8,128)S(1)} %bitcast.9, f32[128,128]{1,0:T(8,128)S(1)} %get-tuple-element.50.seat_ref, bf16[128,4096]{1,0:T(8,128)(2,1)S(1)} %copy-done.1, bf16[128,1024]{1,0:T(8,128)(2,1)S(1)} %copy-done.7), custom_call_target="tpu_custom_call" | custom-call | tf_op jit(solution)/shard_map/pallas_call | solution.py:212
  (73 shorter events, 12.6 us)
Async XLA Ops:
  2.0 14.6 %collective-permute-start.8 = (bf16[1024,256]{1,0:T(8,128)(2,1)S(1)}, bf16[1024,256]{1,0:T(8,128)(2,1)S(1)}, u32[]{:S(2)}, u32[]{:S(2)}) collective-permute-start(bf16[1024,256]{1,0:T(8,128)(2,1)S(1)} %get-tuple-element.38), channel_id=1, source_target_pairs={{0,4},{1,5},{2,6},{3,7},{4,8},{5,9},{6,10},{7,11},{8,12},{9,13},{1... | collective-permute-start | bytes 1572872 | tf_op jit(solution)/shard_map/ppermute | solution.py:31
  4.1 12.9 %collective-permute-start.9 = (bf16[1024,256]{1,0:T(8,128)(2,1)S(1)}, bf16[1024,256]{1,0:T(8,128)(2,1)S(1)}, u32[]{:S(2)}, u32[]{:S(2)}) collective-permute-start(bf16[1024,256]{1,0:T(8,128)(2,1)S(1)} %get-tuple-element.38), channel_id=1, source_target_pairs={{0,12},{1,13},{2,14},{3,15},{4,0},{5,1},{6,2},{7,3},{8,4},{9,5},{1... | collective-permute-start | bytes 1572872 | tf_op jit(solution)/shard_map/ppermute | solution.py:31
  5.5 14.0 %collective-permute-start.1 = (bf16[1024,256]{1,0:T(8,128)(2,1)S(1)}, bf16[1024,256]{1,0:T(8,128)(2,1)S(1)}, u32[]{:S(2)}, u32[]{:S(2)}) collective-permute-start(bf16[1024,256]{1,0:T(8,128)(2,1)S(1)} %get-tuple-element.39), channel_id=1, source_target_pairs={{0,3},{1,0},{2,1},{3,2},{4,7},{5,4},{6,5},{7,6},{8,11},{9,8},{10,9... | collective-permute-start | bytes 1572872 | tf_op jit(solution)/shard_map/ppermute | solution.py:31
  8.3 14.3 %collective-permute-start = (bf16[1024,256]{1,0:T(8,128)(2,1)S(1)}, bf16[1024,256]{1,0:T(8,128)(2,1)S(1)}, u32[]{:S(2)}, u32[]{:S(2)}) collective-permute-start(bf16[1024,256]{1,0:T(8,128)(2,1)S(1)} %get-tuple-element.39), channel_id=1, source_target_pairs={{0,1},{1,2},{2,3},{3,0},{4,5},{5,6},{6,7},{7,4},{8,9},{9,10},{10,1... | collective-permute-start | bytes 1572872 | tf_op jit(solution)/shard_map/ppermute | solution.py:31
  16.6 7.4 %collective-permute-start.10 = (bf16[512,256]{1,0:T(8,128)(2,1)S(1)}, bf16[512,256]{1,0:T(8,128)(2,1)S(1)}, u32[]{:S(2)}, u32[]{:S(2)}) collective-permute-start(bf16[512,256]{1,0:T(8,128)(2,1)S(1)} %get-tuple-element.41), channel_id=1, source_target_pairs={{0,4},{1,5},{2,6},{3,7},{4,8},{5,9},{6,10},{7,11},{8,12},{9,13},{1... | collective-permute-start | bytes 786440 | tf_op jit(solution)/shard_map/ppermute | solution.py:31
  17.1 8.9 %collective-permute-start.13 = (bf16[512,256]{1,0:T(8,128)(2,1)S(1)}, bf16[512,256]{1,0:T(8,128)(2,1)S(1)}, u32[]{:S(2)}, u32[]{:S(2)}) collective-permute-start(bf16[512,256]{1,0:T(8,128)(2,1)S(1)} %get-tuple-element.42), channel_id=1, source_target_pairs={{0,12},{1,13},{2,14},{3,15},{4,0},{5,1},{6,2},{7,3},{8,4},{9,5},{1... | collective-permute-start | bytes 786440 | tf_op jit(solution)/shard_map/ppermute | solution.py:31
  19.5 8.1 %collective-permute-start.5 = (bf16[512,256]{1,0:T(8,128)(2,1)S(1)}, bf16[512,256]{1,0:T(8,128)(2,1)S(1)}, u32[]{:S(2)}, u32[]{:S(2)}) collective-permute-start(bf16[512,256]{1,0:T(8,128)(2,1)S(1)} %get-tuple-element.46), channel_id=1, source_target_pairs={{0,3},{1,0},{2,1},{3,2},{4,7},{5,4},{6,5},{7,6},{8,11},{9,8},{10,9... | collective-permute-start | bytes 786440 | tf_op jit(solution)/shard_map/ppermute | solution.py:31
  22.7 8.4 %collective-permute-start.2 = (bf16[512,256]{1,0:T(8,128)(2,1)S(1)}, bf16[512,256]{1,0:T(8,128)(2,1)S(1)}, u32[]{:S(2)}, u32[]{:S(2)}) collective-permute-start(bf16[512,256]{1,0:T(8,128)(2,1)S(1)} %get-tuple-element.45), channel_id=1, source_target_pairs={{0,1},{1,2},{2,3},{3,0},{4,5},{5,6},{6,7},{7,4},{8,9},{9,10},{10,1... | collective-permute-start | bytes 786440 | tf_op jit(solution)/shard_map/ppermute | solution.py:31
  24.2 27.8 %collective-permute-start.11 = (bf16[512,1024]{1,0:T(8,128)(2,1)S(1)}, bf16[512,1024]{1,0:T(8,128)(2,1)}, u32[]{:S(2)}, u32[]{:S(2)}) collective-permute-start(bf16[512,1024]{1,0:T(8,128)(2,1)S(1)} %pad_maximum_fusion.2.refs_0_), channel_id=1, source_target_pairs={{0,1},{1,2},{2,3},{3,0},{4,5},{5,6},{6,7},{7,4},{8,9},{9,10},{10,1... | collective-permute-start | bytes 3145736 | tf_op jit(solution)/shard_map/ppermute | solution.py:31
  26.1 25.8 %collective-permute-start.14 = (bf16[512,1024]{1,0:T(8,128)(2,1)S(1)}, bf16[512,1024]{1,0:T(8,128)(2,1)}, u32[]{:S(2)}, u32[]{:S(2)}) collective-permute-start(bf16[512,1024]{1,0:T(8,128)(2,1)S(1)} %pad_maximum_fusion.3.refs_2_), channel_id=1, source_target_pairs={{0,3},{1,0},{2,1},{3,2},{4,7},{5,4},{6,5},{7,6},{8,11},{9,8},{10,9... | collective-permute-start | bytes 3145736 | tf_op jit(solution)/shard_map/ppermute | solution.py:31
  27.7 28.7 %copy-start.11 = (s32[16]{0:T(128)S(1)}, s32[16]{0:T(128)}, u32[]{:S(2)}) copy-start(s32[16]{0:T(128)} %param.13) | copy-start | bytes 196
  27.7 28.8 %copy-start.1 = (bf16[128,4096]{1,0:T(8,128)(2,1)S(1)}, bf16[128,4096]{1,0:T(8,128)(2,1)}, u32[]{:S(2)}) copy-start(bf16[128,4096]{1,0:T(8,128)(2,1)} %left_ref.1) | copy-start | bytes 3145732
  28.8 25.8 %collective-permute-start.6 = (bf16[512,1024]{1,0:T(8,128)(2,1)}, bf16[512,1024]{1,0:T(8,128)(2,1)}, u32[]{:S(2)}, u32[]{:S(2)}) collective-permute-start(bf16[512,1024]{1,0:T(8,128)(2,1)} %pad_maximum_fusion.1.refs_6_), channel_id=1, source_target_pairs={{0,12},{1,13},{2,14},{3,15},{4,0},{5,1},{6,2},{7,3},{8,4},{9,5},{1... | collective-permute-start | bytes 3145736 | tf_op jit(solution)/shard_map/ppermute | solution.py:31
  32.2 22.8 %collective-permute-start.3 = (bf16[512,1024]{1,0:T(8,128)(2,1)}, bf16[512,1024]{1,0:T(8,128)(2,1)}, u32[]{:S(2)}, u32[]{:S(2)}) collective-permute-start(bf16[512,1024]{1,0:T(8,128)(2,1)} %pad_maximum_fusion.refs_4_), channel_id=1, source_target_pairs={{0,4},{1,5},{2,6},{3,7},{4,8},{5,9},{6,10},{7,11},{8,12},{9,13},{1... | collective-permute-start | bytes 3145736 | tf_op jit(solution)/shard_map/ppermute | solution.py:31
  52.0 22.9 %collective-permute-start.12 = (bf16[512,1024]{1,0:T(8,128)(2,1)}, bf16[512,1024]{1,0:T(8,128)(2,1)}, u32[]{:S(2)}, u32[]{:S(2)}) collective-permute-start(bf16[512,1024]{1,0:T(8,128)(2,1)} %collective-permute-done.11.refs_0_), channel_id=1, source_target_pairs={{0,1},{1,2},{2,3},{3,0},{4,5},{5,6},{6,7},{7,4},{8,9},{9,10},{10,1... | collective-permute-start | bytes 3145736 | tf_op jit(solution)/shard_map/ppermute | solution.py:31
  52.0 22.9 %collective-permute-start.15 = (bf16[512,1024]{1,0:T(8,128)(2,1)}, bf16[512,1024]{1,0:T(8,128)(2,1)}, u32[]{:S(2)}, u32[]{:S(2)}) collective-permute-start(bf16[512,1024]{1,0:T(8,128)(2,1)} %collective-permute-done.14.refs_1_), channel_id=1, source_target_pairs={{0,3},{1,0},{2,1},{3,2},{4,7},{5,4},{6,5},{7,6},{8,11},{9,8},{10,9... | collective-permute-start | bytes 3145736 | tf_op jit(solution)/shard_map/ppermute | solution.py:31
  54.6 21.1 %collective-permute-start.7 = (bf16[512,1024]{1,0:T(8,128)(2,1)}, bf16[512,1024]{1,0:T(8,128)(2,1)}, u32[]{:S(2)}, u32[]{:S(2)}) collective-permute-start(bf16[512,1024]{1,0:T(8,128)(2,1)} %collective-permute-done.6.refs_3_), channel_id=1, source_target_pairs={{0,12},{1,13},{2,14},{3,15},{4,0},{5,1},{6,2},{7,3},{8,4},{9,5},{1... | collective-permute-start | bytes 3145736 | tf_op jit(solution)/shard_map/ppermute | solution.py:31
  55.0 21.9 %collective-permute-start.4 = (bf16[512,1024]{1,0:T(8,128)(2,1)}, bf16[512,1024]{1,0:T(8,128)(2,1)}, u32[]{:S(2)}, u32[]{:S(2)}) collective-permute-start(bf16[512,1024]{1,0:T(8,128)(2,1)} %collective-permute-done.3.refs_2_), channel_id=1, source_target_pairs={{0,4},{1,5},{2,6},{3,7},{4,8},{5,9},{6,10},{7,11},{8,12},{9,13},{1... | collective-permute-start | bytes 3145736 | tf_op jit(solution)/shard_map/ppermute | solution.py:31
  56.5 23.7 %slice-start = ((s8[8388608]{0:T(1024)(128)(4,1)}), s8[4194304]{0:T(1024)(128)(4,1)S(1)}, s32[]{:S(2)}) async-start(s8[8388608]{0:T(1024)(128)(4,1)} %bitcast.7), calls=%async_computation.1 | async-start | bytes 8388608
  76.9 24.2 %collective-permute-start.16 = (bf16[512,1024]{1,0:T(8,128)(2,1)}, bf16[512,1024]{1,0:T(8,128)(2,1)S(1)}, u32[]{:S(2)}, u32[]{:S(2)}) collective-permute-start(bf16[512,1024]{1,0:T(8,128)(2,1)} %copy-done.3), channel_id=1, source_target_pairs={{0,3},{1,0},{2,1},{3,2},{4,7},{5,4},{6,5},{7,6},{8,11},{9,8},{10,9... | collective-permute-start | bytes 3145736 | tf_op jit(solution)/shard_map/ppermute | solution.py:31
  77.4 23.7 %collective-permute-start.17 = (bf16[512,1024]{1,0:T(8,128)(2,1)}, bf16[512,1024]{1,0:T(8,128)(2,1)S(1)}, u32[]{:S(2)}, u32[]{:S(2)}) collective-permute-start(bf16[512,1024]{1,0:T(8,128)(2,1)} %copy-done.5), channel_id=1, source_target_pairs={{0,1},{1,2},{2,3},{3,0},{4,5},{5,6},{6,7},{7,4},{8,9},{9,10},{10,1... | collective-permute-start | bytes 3145736 | tf_op jit(solution)/shard_map/ppermute | solution.py:31
  78.4 22.7 %collective-permute-start.18 = (bf16[512,1024]{1,0:T(8,128)(2,1)}, bf16[512,1024]{1,0:T(8,128)(2,1)S(1)}, u32[]{:S(2)}, u32[]{:S(2)}) collective-permute-start(bf16[512,1024]{1,0:T(8,128)(2,1)} %pad_maximum_fusion.refs_4_), channel_id=1, source_target_pairs={{0,12},{1,13},{2,14},{3,15},{4,0},{5,1},{6,2},{7,3},{8,4},{9,5},{1... | collective-permute-start | bytes 3145736 | tf_op jit(solution)/shard_map/ppermute | solution.py:31
  78.7 22.4 %collective-permute-start.19 = (bf16[512,1024]{1,0:T(8,128)(2,1)}, bf16[512,1024]{1,0:T(8,128)(2,1)S(1)}, u32[]{:S(2)}, u32[]{:S(2)}) collective-permute-start(bf16[512,1024]{1,0:T(8,128)(2,1)} %pad_maximum_fusion.1.refs_6_), channel_id=1, source_target_pairs={{0,4},{1,5},{2,6},{3,7},{4,8},{5,9},{6,10},{7,11},{8,12},{9,13},{1... | collective-permute-start | bytes 3145736 | tf_op jit(solution)/shard_map/ppermute | solution.py:31
  113.8 22.7 %all-to-all-start = ((f32[128,1,128]{2,1,0:T(1,128)}), f32[128,1,128]{2,1,0:T(1,128)S(1)}, u32[]{:S(2)}, u32[]{:S(2)}) async-start(f32[128,1,128]{2,1,0:T(1,128)} %shard_map.97), calls=%async_computation | async-start | bytes 131072 | tf_op jit(solution)/shard_map/all_to_all | solution.py:304
  (12 other events, 96.0 us)
